TPU v7x, 32 devices: a whole 2x2x4 slice. The times are simulated.
32 devices in a mesh: wide: 8 (over z, x), narrow: 4 (over y, core).
Axes of the slice: x: 2, y: 2, z: 4, core: 2. Of those that a mesh axis runs over, the one named last changes fastest.
Arguments:
- tokens: bfloat16 [4, 1024, 2048], P('narrow', 'wide'), may hold values from -6 to 6
- attn_gain: bfloat16 [2048], P(('wide', 'narrow')), may hold values from 0.25 to 1.75
- w_query: bfloat16 [2048, 2048], P(('wide', 'narrow')), may hold values from -0.1875 to 0.1875
- w_key: bfloat16 [2048, 512], P(('wide', 'narrow')), may hold values from -0.1875 to 0.1875
- w_value: bfloat16 [2048, 512], P(('wide', 'narrow')), may hold values from -0.125 to 0.125
- w_out: bfloat16 [2048, 2048], P(('wide', 'narrow')), may hold values from -0.5 to 0.5
- mlp_gain: bfloat16 [2048], P(('wide', 'narrow')), may hold values from 0.25 to 1.75
- w_gate: bfloat16 [2048, 5632], P(('wide', 'narrow')), may hold values from -0.125 to 0.125
- w_up: bfloat16 [2048, 5632], P(('wide', 'narrow')), may hold values from -0.125 to 0.125
- w_down: bfloat16 [5632, 2048], P(('wide', 'narrow')), may hold values from -0.15625 to 0.15625
- keep_mask: int32 [4], P('narrow'), may hold values 0 or 1
- group_ids: int32 [4, 1024], P('narrow', 'wide'), may hold values from 0 to 1
- positions: int32 [4, 1024], P('narrow', 'wide'), may hold values from 0 to 2046, as said below
- exit_scale: float32 [2], replicated, may hold values from 0.5 to 2
- out_grad: bfloat16 [4, 1024, 2048], P('narrow', 'wide'), may hold values from -6 to 6
Outputs:
- output: bfloat16 [4, 1024, 2048], P('narrow', 'wide')
- token_grad: bfloat16 [4, 1024, 2048], P('narrow', 'wide')
- grad_attn_gain: float32 [2048], P(('wide', 'narrow'))
- grad_w_query: float32 [2048, 2048], P(('wide', 'narrow'))
- grad_w_key: float32 [2048, 512], P(('wide', 'narrow'))
- grad_w_value: float32 [2048, 512], P(('wide', 'narrow'))
- grad_w_out: float32 [2048, 2048], P(('wide', 'narrow'))
- grad_mlp_gain: float32 [2048], P(('wide', 'narrow'))
- grad_w_gate: float32 [2048, 5632], P(('wide', 'narrow'))
- grad_w_up: float32 [2048, 5632], P(('wide', 'narrow'))
- grad_w_down: float32 [5632, 2048], P(('wide', 'narrow'))
Inputs may be any that keep to these rules, and one draw needn't show every extreme that they name: In each sequence positions start at 0 and rise by 1 or 2 from one token to the next.
All inputs are finite; a program needn't handle non-finite values. No bound on the sum of `keep_mask` on one device may be relied on, other than what follows from the above.
Results may differ from a plain program's by a relative error of at most 0.023.
Values may be sent and summed in bfloat16 or wider, within the bound.
A program may use at most 384 MiB of HBM per device.

v0:
```python
import math

import jax
import jax.numpy as jnp
from jax import lax
from jax.sharding import PartitionSpec as P

HEADS = 16
KVH = 4
HD = 128


epsilon = 1e-05


def rotate(vectors, token_pos, direction):
    half_size = vectors.shape[-1] // 2
    freqs = 10000.0 ** (-2.0 * jnp.arange(half_size, dtype=jnp.float32) / vectors.shape[-1])
    angles = token_pos.astype(jnp.float32)[:, None] * freqs[None, :]
    cosine = jnp.cos(angles)[:, None, :]
    sine = direction * jnp.sin(angles)[:, None, :]
    first_half = vectors[..., :half_size]
    second_half = vectors[..., half_size:]
    return jnp.concatenate(
        [first_half * cosine - second_half * sine, second_half * cosine + first_half * sine],
        axis=-1,
    )


def split_blocks(piece_arr, seq_count, kv_heads, head_dim):
    piece_len = piece_arr.shape[1]
    block_len = math.gcd(piece_len, 512)
    shaped = piece_arr.reshape(seq_count, piece_len // block_len, block_len, kv_heads, head_dim)
    return shaped.transpose(1, 0, 2, 3, 4)


def add_rows(whole_arr, update, first_row):
    current = lax.dynamic_slice_in_dim(whole_arr, first_row, update.shape[1], 1)
    return lax.dynamic_update_slice_in_dim(whole_arr, current + update, first_row, 1)


def over_rows(left, right):
    return lax.dot_general(
        left, right, (((0,), (0,)), ((), ())), preferred_element_type=jnp.float32
    )


def against(left, right):
    return lax.dot_general(
        left, right, (((1,), (1,)), ((), ())), preferred_element_type=jnp.float32
    )


def unchanged(carried):
    return carried


def body(
    tokens,
    attn_gain,
    w_query,
    w_key,
    w_value,
    w_out,
    mlp_gain,
    w_gate,
    w_up,
    w_down,
    keep_mask,
    group_ids,
    positions,
    exit_scale,
    out_grad,
):
    seq_count, span_len, model_width = tokens.shape
    kv_heads = KVH
    head_dim = HD
    head_count = HEADS
    group_size = head_count // kv_heads
    row_count = seq_count * span_len
    stripe = group_size * span_len
    wide_count = lax.axis_size("wide")
    wide_place = lax.axis_index("wide")
    full_len = span_len * wide_count
    score_scale = 1.0 / math.sqrt(head_dim)
    gain_one, query_w, key_w, value_w, out_w = (
        lax.all_gather(attn_gain, ("wide", "narrow"), axis=0, tiled=True),
        lax.all_gather(w_query, ("wide", "narrow"), axis=0, tiled=True),
        lax.all_gather(w_key, ("wide", "narrow"), axis=0, tiled=True),
        lax.all_gather(w_value, ("wide", "narrow"), axis=0, tiled=True),
        lax.all_gather(w_out, ("wide", "narrow"), axis=0, tiled=True),
    )
    inputs = tokens.astype(jnp.float32).reshape(row_count, model_width)
    token_pos = positions.reshape(row_count)
    keep_rows = jnp.repeat(keep_mask.astype(jnp.float32), span_len)[:, None]
    inverse_one = lax.rsqrt(jnp.mean(inputs * inputs, axis=-1, keepdims=True) + epsilon)
    first_norm = (inputs * inverse_one * gain_one.astype(jnp.float32)).astype(jnp.bfloat16)
    query_pre = jnp.dot(first_norm, query_w, preferred_element_type=jnp.float32).reshape(
        row_count, head_count, head_dim
    )
    key_pre = jnp.dot(first_norm, key_w, preferred_element_type=jnp.float32).reshape(
        row_count, kv_heads, head_dim
    )
    query_rows = rotate(query_pre, token_pos, 1.0).astype(jnp.bfloat16)
    key_heads = (
        rotate(key_pre, token_pos, 1.0)
        .astype(jnp.bfloat16)
        .reshape(seq_count, span_len, kv_heads * head_dim)
    )
    value_heads = (
        jnp.dot(first_norm, value_w, preferred_element_type=jnp.float32)
        .astype(jnp.bfloat16)
        .reshape(seq_count, span_len, kv_heads * head_dim)
    )
    queries = (
        query_rows.reshape(seq_count, span_len, kv_heads, group_size, head_dim)
        .transpose(0, 2, 3, 1, 4)
        .reshape(seq_count, kv_heads, stripe, head_dim)
    )
    query_index = wide_place * span_len + jnp.arange(stripe, dtype=jnp.int32) % span_len
    last_query = wide_place * span_len + span_len - 1

    def block_scores(key_block, key_first):
        scores = (
            jnp.einsum("skrd,sjkd->skrj", queries, key_block, preferred_element_type=jnp.float32)
            * score_scale
        )
        key_index = key_first + jnp.arange(key_block.shape[1], dtype=jnp.int32)
        allowed = key_index[None, :] <= query_index[:, None]
        return (scores, allowed)

    start_forward = (
        jnp.full((seq_count, kv_heads, stripe), -1e30, jnp.float32),
        jnp.zeros((seq_count, kv_heads, stripe), jnp.float32),
        jnp.zeros((seq_count, kv_heads, stripe, head_dim), jnp.float32),
    )
    running = start_forward
    pieces = (
        lax.all_gather(key_heads, "wide", axis=1, tiled=True),
        lax.all_gather(value_heads, "wide", axis=1, tiled=True),
    )
    key_blocks = split_blocks(pieces[0], seq_count, kv_heads, head_dim)
    value_blocks = split_blocks(pieces[1], seq_count, kv_heads, head_dim)
    block_len = key_blocks.shape[2]

    def advance(carried, block_item):
        key_block, value_block, block_index = block_item
        key_first = block_index * block_len

        def compute_block(current):
            run_max, run_sum, run_acc = current
            scores, allowed = block_scores(key_block, key_first)
            scores = jnp.where(allowed, scores, -1e30)
            new_max = jnp.maximum(run_max, jnp.max(scores, axis=-1))
            factor = jnp.exp(run_max - new_max)
            weights = jnp.where(allowed, jnp.exp(scores - new_max[..., None]), 0.0)
            new_sum = run_sum * factor + jnp.sum(weights, axis=-1)
            new_acc = run_acc * factor[..., None] + jnp.einsum(
                "skrj,sjkd->skrd",
                weights.astype(jnp.bfloat16),
                value_block,
                preferred_element_type=jnp.float32,
            )
            return (new_max, new_sum, new_acc)

        return (lax.cond(key_first <= last_query, compute_block, unchanged, carried), None)

    running, _ = lax.scan(
        advance,
        running,
        (key_blocks, value_blocks, jnp.arange(key_blocks.shape[0], dtype=jnp.int32)),
    )
    run_max, run_sum, run_acc = running
    attended = run_acc / run_sum[..., None]
    log_total = run_max + jnp.log(run_sum)
    attended_rows = (
        attended.reshape(seq_count, kv_heads, group_size, span_len, head_dim)
        .transpose(0, 3, 1, 2, 4)
        .reshape(row_count, head_count * head_dim)
        .astype(jnp.bfloat16)
    )
    middle = inputs + keep_rows * jnp.dot(attended_rows, out_w, preferred_element_type=jnp.float32)
    gain_two, gate_w, up_w, down_w = (
        lax.all_gather(mlp_gain, ("wide", "narrow"), axis=0, tiled=True),
        lax.all_gather(w_gate, ("wide", "narrow"), axis=0, tiled=True),
        lax.all_gather(w_up, ("wide", "narrow"), axis=0, tiled=True),
        lax.all_gather(w_down, ("wide", "narrow"), axis=0, tiled=True),
    )
    inverse_two = lax.rsqrt(jnp.mean(middle * middle, axis=-1, keepdims=True) + epsilon)
    second_norm = (middle * inverse_two * gain_two.astype(jnp.float32)).astype(jnp.bfloat16)
    gate_value = jnp.dot(second_norm, gate_w, preferred_element_type=jnp.float32)
    up_value = jnp.dot(second_norm, up_w, preferred_element_type=jnp.float32)
    gate_sigmoid = jax.nn.sigmoid(gate_value)
    swish_value = gate_value * gate_sigmoid
    hidden = (swish_value * up_value).astype(jnp.bfloat16)
    output = (
        middle + keep_rows * jnp.dot(hidden, down_w, preferred_element_type=jnp.float32)
    ).astype(jnp.bfloat16)
    group_match = (
        group_ids.reshape(row_count)[:, None]
        == jnp.arange(exit_scale.shape[0], dtype=jnp.int32)[None, :]
    )
    token_scale = jnp.sum(jnp.where(group_match, exit_scale[None, :], 0.0), axis=1, keepdims=True)
    upstream = out_grad.astype(jnp.float32).reshape(row_count, model_width) * token_scale
    gain_two, gate_w, up_w, down_w = (
        lax.all_gather(mlp_gain, ("wide", "narrow"), axis=0, tiled=True),
        lax.all_gather(w_gate, ("wide", "narrow"), axis=0, tiled=True),
        lax.all_gather(w_up, ("wide", "narrow"), axis=0, tiled=True),
        lax.all_gather(w_down, ("wide", "narrow"), axis=0, tiled=True),
    )
    mixed_grad = (keep_rows * upstream).astype(jnp.bfloat16)
    grad_down = over_rows(hidden, mixed_grad)
    hidden_grad = against(mixed_grad, down_w)
    gate_grad = (
        hidden_grad * up_value * gate_sigmoid * (1.0 + gate_value * (1.0 - gate_sigmoid))
    ).astype(jnp.bfloat16)
    up_grad = (hidden_grad * swish_value).astype(jnp.bfloat16)
    grad_gate = over_rows(second_norm, gate_grad)
    grad_up = over_rows(second_norm, up_grad)
    norm_grad = against(gate_grad, gate_w) + against(up_grad, up_w)
    grad_gain_two = jnp.sum(norm_grad * middle * inverse_two, axis=0)
    scaled_two = gain_two.astype(jnp.float32) * norm_grad
    middle_grad = (
        upstream
        + inverse_two * scaled_two
        - middle
        * (inverse_two * inverse_two * inverse_two)
        * jnp.mean(scaled_two * middle, axis=-1, keepdims=True)
    )
    gain_two_share, gate_share, up_share, down_share = (
        lax.psum_scatter(grad_gain_two, ("wide", "narrow"), scatter_dimension=0, tiled=True),
        lax.psum_scatter(grad_gate, ("wide", "narrow"), scatter_dimension=0, tiled=True),
        lax.psum_scatter(grad_up, ("wide", "narrow"), scatter_dimension=0, tiled=True),
        lax.psum_scatter(grad_down, ("wide", "narrow"), scatter_dimension=0, tiled=True),
    )
    gain_one, query_w, key_w, value_w, out_w = (
        lax.all_gather(attn_gain, ("wide", "narrow"), axis=0, tiled=True),
        lax.all_gather(w_query, ("wide", "narrow"), axis=0, tiled=True),
        lax.all_gather(w_key, ("wide", "narrow"), axis=0, tiled=True),
        lax.all_gather(w_value, ("wide", "narrow"), axis=0, tiled=True),
        lax.all_gather(w_out, ("wide", "narrow"), axis=0, tiled=True),
    )
    branch_grad = (keep_rows * middle_grad).astype(jnp.bfloat16)
    grad_out = over_rows(attended_rows, branch_grad)
    attended_grad = against(branch_grad, out_w).astype(jnp.bfloat16)
    grouped_grad = (
        attended_grad.reshape(seq_count, span_len, kv_heads, group_size, head_dim)
        .transpose(0, 2, 3, 1, 4)
        .reshape(seq_count, kv_heads, stripe, head_dim)
    )
    row_delta = jnp.sum(grouped_grad.astype(jnp.float32) * attended, axis=-1)
    start_backward = (
        jnp.zeros((seq_count, kv_heads, stripe, head_dim), jnp.float32),
        jnp.zeros((seq_count, full_len, kv_heads * head_dim), jnp.float32),
        jnp.zeros((seq_count, full_len, kv_heads * head_dim), jnp.float32),
    )
    running = start_backward
    pieces = (
        lax.all_gather(key_heads, "wide", axis=1, tiled=True),
        lax.all_gather(value_heads, "wide", axis=1, tiled=True),
    )
    key_blocks = split_blocks(pieces[0], seq_count, kv_heads, head_dim)
    value_blocks = split_blocks(pieces[1], seq_count, kv_heads, head_dim)
    fold_block_len = key_blocks.shape[2]

    def advance(carried, block_item):
        key_block, value_block, block_index = block_item
        key_first = block_index * fold_block_len

        def compute_block(current):
            query_acc, key_acc, value_acc = current
            scores, allowed = block_scores(key_block, key_first)
            probabilities = jnp.where(allowed, jnp.exp(scores - log_total[..., None]), 0.0)
            value_part = jnp.einsum(
                "skrj,skrd->sjkd",
                probabilities.astype(jnp.bfloat16),
                grouped_grad,
                preferred_element_type=jnp.float32,
            )
            prob_grad = jnp.einsum(
                "skrd,sjkd->skrj", grouped_grad, value_block, preferred_element_type=jnp.float32
            )
            score_grad = (probabilities * (prob_grad - row_delta[..., None])).astype(jnp.bfloat16)
            query_acc = (
                query_acc
                + jnp.einsum(
                    "skrj,sjkd->skrd", score_grad, key_block, preferred_element_type=jnp.float32
                )
                * score_scale
            )
            key_part = (
                jnp.einsum(
                    "skrj,skrd->sjkd", score_grad, queries, preferred_element_type=jnp.float32
                )
                * score_scale
            )
            key_acc = add_rows(
                key_acc, key_part.reshape(seq_count, fold_block_len, kv_heads * head_dim), key_first
            )
            value_acc = add_rows(
                value_acc,
                value_part.reshape(seq_count, fold_block_len, kv_heads * head_dim),
                key_first,
            )
            return (query_acc, key_acc, value_acc)

        return (lax.cond(key_first <= last_query, compute_block, unchanged, carried), None)

    running, _ = lax.scan(
        advance,
        running,
        (key_blocks, value_blocks, jnp.arange(key_blocks.shape[0], dtype=jnp.int32)),
    )
    query_acc, key_acc, value_acc = running
    key_sum, value_sum = (
        lax.psum_scatter(
            key_acc.astype(jnp.bfloat16), "wide", scatter_dimension=1, tiled=True
        ).astype(jnp.float32),
        lax.psum_scatter(
            value_acc.astype(jnp.bfloat16), "wide", scatter_dimension=1, tiled=True
        ).astype(jnp.float32),
    )
    query_back = (
        query_acc.reshape(seq_count, kv_heads, group_size, span_len, head_dim)
        .transpose(0, 3, 1, 2, 4)
        .reshape(row_count, head_count, head_dim)
    )
    query_grad = (
        rotate(query_back, token_pos, -1.0)
        .reshape(row_count, head_count * head_dim)
        .astype(jnp.bfloat16)
    )
    key_grad = (
        rotate(key_sum.reshape(row_count, kv_heads, head_dim), token_pos, -1.0)
        .reshape(row_count, kv_heads * head_dim)
        .astype(jnp.bfloat16)
    )
    value_grad = value_sum.reshape(row_count, kv_heads * head_dim).astype(jnp.bfloat16)
    grad_query = over_rows(first_norm, query_grad)
    grad_key = over_rows(first_norm, key_grad)
    grad_value = over_rows(first_norm, value_grad)
    input_norm_grad = (
        against(query_grad, query_w) + against(key_grad, key_w) + against(value_grad, value_w)
    )
    grad_gain_one = jnp.sum(input_norm_grad * inputs * inverse_one, axis=0)
    scaled_one = gain_one.astype(jnp.float32) * input_norm_grad
    input_grad = (
        middle_grad
        + inverse_one * scaled_one
        - inputs
        * (inverse_one * inverse_one * inverse_one)
        * jnp.mean(scaled_one * inputs, axis=-1, keepdims=True)
    )
    gain_one_share, query_share, key_share, value_share, out_share = (
        lax.psum_scatter(grad_gain_one, ("wide", "narrow"), scatter_dimension=0, tiled=True),
        lax.psum_scatter(grad_query, ("wide", "narrow"), scatter_dimension=0, tiled=True),
        lax.psum_scatter(grad_key, ("wide", "narrow"), scatter_dimension=0, tiled=True),
        lax.psum_scatter(grad_value, ("wide", "narrow"), scatter_dimension=0, tiled=True),
        lax.psum_scatter(grad_out, ("wide", "narrow"), scatter_dimension=0, tiled=True),
    )
    return (
        output.reshape(seq_count, span_len, model_width),
        input_grad.astype(jnp.bfloat16).reshape(seq_count, span_len, model_width),
        gain_one_share,
        query_share,
        key_share,
        value_share,
        out_share,
        gain_two_share,
        gate_share,
        up_share,
        down_share,
    )


def solution(mesh):
    placed = (
        P("narrow", "wide", None),
        P(("wide", "narrow")),
        P(("wide", "narrow"), None),
        P(("wide", "narrow"), None),
        P(("wide", "narrow"), None),
        P(("wide", "narrow"), None),
        P(("wide", "narrow")),
        P(("wide", "narrow"), None),
        P(("wide", "narrow"), None),
        P(("wide", "narrow"), None),
        P("narrow"),
        P("narrow", "wide"),
        P("narrow", "wide"),
        P(),
        P("narrow", "wide", None),
    )
    return jax.shard_map(
        body,
        mesh=mesh,
        in_specs=placed,
        out_specs=(
            P("narrow", "wide", None),
            P("narrow", "wide", None),
            P(("wide", "narrow")),
            P(("wide", "narrow"), None),
            P(("wide", "narrow"), None),
            P(("wide", "narrow"), None),
            P(("wide", "narrow"), None),
            P(("wide", "narrow")),
            P(("wide", "narrow"), None),
            P(("wide", "narrow"), None),
            P(("wide", "narrow"), None),
        ),
        check_vma=False,
    )
```

profile of v0, /device:TPU:0, one launch (start us, length us, event | category | flops | bytes accessed | tf_op | source)
XLA Modules:
  0.0 3182.3 jit_solution(7677121652650000836)
XLA Ops:
  10.4 42.1 %all-reduce.5 = (bf16[2048]{0:T(1024)(128)(2,1)S(1)}, bf16[2048]{0:T(1024)(128)(2,1)S(1)}) all-reduce(bf16[2048]{0:T(1024)(128)(2,1)S(1)} %dynamic-update-slice, bf16[2048]{0:T(1024)(128)(2,1)S(1)} %dynamic-update-slice.1), channel_id=1, replica_groups=mesh['wide'=8,'narrow'=4] {'wide','narrow'}, use_global_device_ids=true, to_apply=%add | all-reduce | flops 4096 | bytes 16384
  55.8 14.2 all-gather.11.cloned.1.call-done
  70.1 2.9 copy.114
  74.8 53.5 %all-gather.17.cloned.1.call-done = bf16[2048,512]{1,0:T(8,128)(2,1)} async-done(((bf16[64,512]{1,0:T(8,128)(2,1)}), bf16[2048,512]{1,0:T(8,128)(2,1)}) %all-gather.17.cloned.1.call-update) | async-done | bytes 2097168 | tf_op jit(solution)/shard_map/all_gather | solution.py:90
  135.8 34.2 %all-gather.13.cloned.1.call-done = bf16[1,1024,512]{2,1,0:T(8,128)(2,1)} async-done(((bf16[1,128,512]{2,1,0:T(8,128)(2,1)}), bf16[1,1024,512]{2,1,0:T(8,128)(2,1)}) %all-gather.13.cloned.1.call-update) | async-done | bytes 1048592 | tf_op jit(solution)/shard_map/all_gather | solution.py:139
  172.4 39.0 %all-gather.27.cloned.1.call-done = bf16[1024,512]{1,0:T(8,128)(2,1)} async-done(((bf16[128,512]{1,0:T(8,128)(2,1)}), bf16[1024,512]{1,0:T(8,128)(2,1)}) %all-gather.27.cloned.1.call-update) | async-done | bytes 1048592 | tf_op jit(solution)/shard_map/all_gather | solution.py:140
  214.0 76.5 %all-gather.15.cloned.1.call-done = bf16[2048,2048]{1,0:T(8,128)(2,1)} async-done(((bf16[64,2048]{1,0:T(8,128)(2,1)}), bf16[2048,2048]{1,0:T(8,128)(2,1)}) %all-gather.15.cloned.1.call-update) | async-done | bytes 8388624 | tf_op jit(solution)/shard_map/all_gather | solution.py:88
  290.5 11.9 copy.116
  302.5 5.9 fusion.84
  310.8 9.0 while.30
  312.1 6.1 conditional.6
  315.3 2.9 fusion.13
  320.4 48.9 %all-gather.19.cloned.1.call-done = bf16[2048,2048]{1,0:T(8,128)(2,1)} async-done(((bf16[64,2048]{1,0:T(8,128)(2,1)}), bf16[2048,2048]{1,0:T(8,128)(2,1)}) %all-gather.19.cloned.1.call-update) | async-done | bytes 8388624 | tf_op jit(solution)/shard_map/all_gather | solution.py:91
  369.3 4.8 multiply_reduce_fusion.3
  375.4 140.0 %all-gather.21.cloned.1.call-done = bf16[2048,5632]{1,0:T(8,128)(2,1)} async-done(((bf16[64,5632]{1,0:T(8,128)(2,1)}), bf16[2048,5632]{1,0:T(8,128)(2,1)}) %all-gather.21.cloned.1.call-update) | async-done | bytes 23068688 | tf_op jit(solution)/shard_map/all_gather | solution.py:185
  515.4 12.3 fusion.110
  527.7 133.4 %all-gather.23.cloned.1.call-done = bf16[2048,5632]{1,0:T(8,128)(2,1)} async-done(((bf16[64,5632]{1,0:T(8,128)(2,1)}), bf16[2048,5632]{1,0:T(8,128)(2,1)}) %all-gather.23.cloned.1.call-update) | async-done | bytes 23068688 | tf_op jit(solution)/shard_map/all_gather | solution.py:186
  661.1 12.3 fusion.111
  673.4 133.4 %all-gather.25.cloned.1.call-done = bf16[5632,2048]{1,0:T(8,128)(2,1)} async-done(((bf16[176,2048]{1,0:T(8,128)(2,1)}), bf16[5632,2048]{1,0:T(8,128)(2,1)}) %all-gather.25.cloned.1.call-update) | async-done | bytes 23068688 | tf_op jit(solution)/shard_map/all_gather | solution.py:187
  806.8 14.7 multiply_convert_fusion
  821.5 13.8 fusion.112
  835.3 13.0 multiply_reduce_fusion
  849.6 6.4 convolution_convert_fusion
  862.5 31.1 while.31
  863.9 28.4 conditional.7
  866.1 3.5 fusion.29
  869.6 3.3 fusion.39
  875.0 3.3 fusion.31
  880.7 5.8 dynamic_update_slice.10
  886.5 5.8 dynamic_update_slice.11
  901.3 4.7 copy.136
  907.4 79.5 %reduce-scatter.28.cloned.1.call-done = bf16[128,512]{1,0:T(8,128)(2,1)} async-done(((bf16[1024,512]{1,0:T(8,128)(2,1)}), bf16[128,512]{1,0:T(8,128)(2,1)}) %reduce-scatter.28.cloned.1.call-update) | async-done | bytes 131088
  988.9 2.8 fusion.92
  991.8 61.3 %reduce-scatter.30.cloned.1.call-done = bf16[128,512]{1,0:T(8,128)(2,1)} async-done(((bf16[1024,512]{1,0:T(8,128)(2,1)}), bf16[128,512]{1,0:T(8,128)(2,1)}) %reduce-scatter.30.cloned.1.call-update) | async-done | bytes 131088
  1060.0 8.3 fusion.88
  1069.6 8.2 fusion.97
  1079.3 18.2 fusion.114
  1098.9 18.2 fusion.115
  1118.6 18.0 fusion.98
  1137.6 6.4 fusion.113
  1144.1 11.8 fusion.61
  1158.5 40.6 %all-reduce.4 = (f32[2048]{0:T(1024)S(1)}, f32[2048]{0:T(1024)S(1)}) all-reduce(f32[2048]{0:T(1024)S(1)} %get-tuple-element.596, f32[2048]{0:T(1024)S(1)} %copy-done.35), channel_id=5, replica_groups=mesh['wide'=8,'narrow'=4] {'wide','narrow'}, use_global_device_ids=true, to_apply=%region_19.20.clone | all-reduce | flops 4096 | bytes 32768
  1201.4 135.5 %reduce-scatter.18.cloned.1.call-done = f32[64,512]{1,0:T(8,128)} async-done(((f32[2048,512]{1,0:T(8,128)}), f32[64,512]{1,0:T(8,128)}) %reduce-scatter.18.cloned.1.call-update) | async-done | bytes 131088 | tf_op jit(solution)/shard_map/reduce_scatter | solution.py:358
  1336.9 181.7 %reduce-scatter.14.cloned.1.call-done = f32[64,2048]{1,0:T(8,128)} async-done(((f32[2048,2048]{1,0:T(8,128)}), f32[64,2048]{1,0:T(8,128)}) %reduce-scatter.14.cloned.1.call-update) | async-done | bytes 524304 | tf_op jit(solution)/shard_map/reduce_scatter | solution.py:356
  1518.6 187.3 %reduce-scatter.20.cloned.1.call-done = f32[64,2048]{1,0:T(8,128)} async-done(((f32[2048,2048]{1,0:T(8,128)}), f32[64,2048]{1,0:T(8,128)}) %reduce-scatter.20.cloned.1.call-update) | async-done | bytes 524304 | tf_op jit(solution)/shard_map/reduce_scatter | solution.py:359
  1705.9 486.7 %reduce-scatter.22.cloned.1.call-done = f32[64,5632]{1,0:T(8,128)} async-done(((f32[2048,5632]{1,0:T(8,128)}), f32[64,5632]{1,0:T(8,128)}) %reduce-scatter.22.cloned.1.call-update) | async-done | bytes 1441808 | tf_op jit(solution)/shard_map/reduce_scatter | solution.py:232
  2192.6 491.3 %reduce-scatter.24.cloned.1.call-done = f32[64,5632]{1,0:T(8,128)} async-done(((f32[2048,5632]{1,0:T(8,128)}), f32[64,5632]{1,0:T(8,128)}) %reduce-scatter.24.cloned.1.call-update) | async-done | bytes 1441808 | tf_op jit(solution)/shard_map/reduce_scatter | solution.py:233
  2683.9 491.2 %reduce-scatter.26.cloned.1.call-done = f32[176,2048]{1,0:T(8,128)} async-done(((f32[5632,2048]{1,0:T(8,128)}), f32[176,2048]{1,0:T(8,128)}) %reduce-scatter.26.cloned.1.call-update) | async-done | bytes 1441808 | tf_op jit(solution)/shard_map/reduce_scatter | solution.py:234
  (220 shorter events, 73.8 us)
Async XLA Ops:
  7.2 65.8 %copy-start.1 = (bf16[1,128,2048]{2,1,0:T(8,128)(2,1)S(1)}, bf16[1,128,2048]{2,1,0:T(8,128)(2,1)}, u32[]{:S(2)}) copy-start(bf16[1,128,2048]{2,1,0:T(8,128)(2,1)} %param.23) | copy-start | bytes 1572868
  7.2 62.9 %all-gather.11.cloned.1.call-start = ((), (), s32[]{:S(2)}) async-start(), calls=%async_computation.9 | async-start | bytes 2162688 | tf_op jit(solution)/shard_map/all_gather | solution.py:89
  7.9 120.3 %all-gather.17.cloned.1.call-start = ((), (), s32[]{:S(2)}) async-start(), calls=%async_computation.12 | async-start | bytes 2162688 | tf_op jit(solution)/shard_map/all_gather | solution.py:90
  8.7 161.3 %all-gather.13.cloned.1.call-start = ((), (), s32[]{:S(2)}) async-start(), calls=%async_computation.10 | async-start | bytes 1179648 | tf_op jit(solution)/shard_map/all_gather | solution.py:139
  52.6 249.9 %copy-start.30 = (f32[2048]{0:T(1024)}, f32[2048]{0:T(1024)S(1)}, u32[]{:S(2)}) copy-start(f32[2048]{0:T(1024)S(1)} %convert_element_type.180) | copy-start | bytes 24580
  55.0 247.4 %copy-start.33 = (f32[128]{0:T(128)}, f32[128]{0:T(128)S(1)}, u32[]{:S(2)}) copy-start(f32[128]{0:T(128)S(1)} %get-tuple-element.671) | copy-start | bytes 1540
  55.8 252.5 %copy-start.28 = (f32[128,64]{0,1:T(8,128)}, f32[128,64]{0,1:T(8,128)S(1)}, u32[]{:S(2)}) copy-start(f32[128,64]{0,1:T(8,128)S(1)} %get-tuple-element.669) | copy-start | bytes 98308
  73.0 62.1 %copy-start.43 = (f32[2]{0:T(128)S(1)}, f32[2]{0:T(128)}, u32[]{:S(2)}) copy-start(f32[2]{0:T(128)} %param.36) | copy-start | bytes 28
  73.0 62.1 %copy-start.44 = (s32[1,128]{1,0:T(1,128)S(1)}, s32[1,128]{1,0:T(1,128)}, u32[]{:S(2)}) copy-start(s32[1,128]{1,0:T(1,128)} %param.34) | copy-start | bytes 1540
  74.7 136.8 %all-gather.27.cloned.1.call-start = ((), (), s32[]{:S(2)}) async-start(), calls=%async_computation.24 | async-start | bytes 1179648 | tf_op jit(solution)/shard_map/all_gather | solution.py:140
  131.0 159.5 %all-gather.15.cloned.1.call-start = ((), (), s32[]{:S(2)}) async-start(), calls=%async_computation.11 | async-start | bytes 8650752 | tf_op jit(solution)/shard_map/all_gather | solution.py:88
  131.6 237.7 %all-gather.19.cloned.1.call-start = ((), (), s32[]{:S(2)}) async-start(), calls=%async_computation.13 | async-start | bytes 8650752 | tf_op jit(solution)/shard_map/all_gather | solution.py:91
  132.2 383.2 %all-gather.21.cloned.1.call-start = ((), (), s32[]{:S(2)}) async-start(), calls=%async_computation.14 | async-start | bytes 23789568 | tf_op jit(solution)/shard_map/all_gather | solution.py:185
  132.9 528.2 %all-gather.23.cloned.1.call-start = ((), (), s32[]{:S(2)}) async-start(), calls=%async_computation.15 | async-start | bytes 23789568 | tf_op jit(solution)/shard_map/all_gather | solution.py:186
  133.7 673.1 %all-gather.25.cloned.1.call-start = ((), (), s32[]{:S(2)}) async-start(), calls=%async_computation.16 | async-start | bytes 23789568 | tf_op jit(solution)/shard_map/all_gather | solution.py:187
  134.4 852.5 %reduce-scatter.28.cloned.1.call-start = ((), (), s32[]{:S(2)}) async-start(), calls=%async_computation.25 | async-start | bytes 1179648
  319.8 49.5 %copy-start.13 = (f32[1,4,512,128]{3,2,1,0:T(8,128)}, f32[1,4,512,128]{3,2,1,0:T(8,128)S(1)}, u32[]{:S(2)}) copy-start(f32[1,4,512,128]{3,2,1,0:T(8,128)S(1)} %get-tuple-element.321) | copy-start | bytes 3145732
  320.4 53.7 %copy-start.17 = (bf16[1,128,4,4,128]{1,4,3,2,0:T(8,128)(2,1)}, bf16[1,128,4,4,128]{1,4,3,2,0:T(8,128)(2,1)S(1)}, u32[]{:S(2)}) copy-start(bf16[1,128,4,4,128]{1,4,3,2,0:T(8,128)(2,1)S(1)} %copy.121) | copy-start | bytes 1572868
  374.1 474.2 %copy-start.3 = (f32[128,2048]{1,0:T(8,128)}, f32[128,2048]{1,0:T(8,128)S(1)}, u32[]{:S(2)}) copy-start(f32[128,2048]{1,0:T(8,128)S(1)} %get-tuple-element.675) | copy-start | bytes 3145732
  374.6 153.0 %copy-start.37 = (f32[128]{0:T(128)}, f32[128]{0:T(128)S(1)}, u32[]{:S(2)}) copy-start(f32[128]{0:T(128)S(1)} %get-tuple-element.673) | copy-start | bytes 1540
  375.4 285.7 %copy-start.7 = (bf16[128,2048]{1,0:T(8,128)(2,1)}, bf16[128,2048]{1,0:T(8,128)(2,1)S(1)}, u32[]{:S(2)}) copy-start(bf16[128,2048]{1,0:T(8,128)(2,1)S(1)} %multiply_convert_fusion.4) | copy-start | bytes 1572868
  527.7 279.1 %copy-start.21 = (bf16[1,128,2048]{2,1,0:T(8,128)(2,1)S(1)}, bf16[1,128,2048]{2,1,0:T(8,128)(2,1)}, u32[]{:S(2)}) copy-start(bf16[1,128,2048]{2,1,0:T(8,128)(2,1)} %param.37) | copy-start | bytes 1572868
  821.5 13.8 copy-start.9
  821.5 13.8 copy-start.11
  821.5 13.8 copy-start.38
  835.2 13.0 copy-start.39
  835.3 13.0 copy-start.42
  849.6 6.9 copy-start.14
  856.5 6.0 copy-start.36
  865.8 3.8 copy-start
  898.5 154.6 %reduce-scatter.30.cloned.1.call-start = ((), (), s32[]{:S(2)}) async-start(), calls=%async_computation.26 | async-start | bytes 1179648
  901.3 86.8 %copy-start.29 = (f32[128,64]{0,1:T(8,128)S(1)}, f32[128,64]{0,1:T(8,128)}, u32[]{:S(2)}) copy-start(f32[128,64]{0,1:T(8,128)} %copy-done.28) | copy-start | bytes 98308
  901.3 86.8 %copy-start.32 = (f32[128,64]{0,1:T(8,128)S(1)}, f32[128,64]{0,1:T(8,128)}, u32[]{:S(2)}) copy-start(f32[128,64]{0,1:T(8,128)} %get-tuple-element.667) | copy-start | bytes 98308
  901.3 87.6 %copy-start.2 = (bf16[1,128,2048]{2,1,0:T(8,128)(2,1)S(1)}, bf16[1,128,2048]{2,1,0:T(8,128)(2,1)}, u32[]{:S(2)}) copy-start(bf16[1,128,2048]{2,1,0:T(8,128)(2,1)} %param.23) | copy-start | bytes 1572868
  901.3 87.6 %copy-start.31 = (f32[2048]{0:T(1024)S(1)}, f32[2048]{0:T(1024)}, u32[]{:S(2)}) copy-start(f32[2048]{0:T(1024)} %copy-done.30) | copy-start | bytes 24580
  901.3 87.6 %copy-start.34 = (f32[128]{0:T(128)S(1)}, f32[128]{0:T(128)}, u32[]{:S(2)}) copy-start(f32[128]{0:T(128)} %copy-done.33) | copy-start | bytes 1540
  907.3 294.1 %reduce-scatter.16.cloned.1.call-start = ((), (), s32[]{:S(2)}) async-start(), calls=%async_computation.18 | async-start | bytes 4325376 | tf_op jit(solution)/shard_map/reduce_scatter | solution.py:357
  991.8 345.1 %reduce-scatter.18.cloned.1.call-start = ((), (), s32[]{:S(2)}) async-start(), calls=%async_computation.19 | async-start | bytes 4325376 | tf_op jit(solution)/shard_map/reduce_scatter | solution.py:358
  1054.3 2.8 copy-start.24
  1057.2 461.4 %reduce-scatter.14.cloned.1.call-start = ((), (), s32[]{:S(2)}) async-start(), calls=%async_computation.17 | async-start | bytes 17301504 | tf_op jit(solution)/shard_map/reduce_scatter | solution.py:356
  1068.3 637.6 %reduce-scatter.20.cloned.1.call-start = ((), (), s32[]{:S(2)}) async-start(), calls=%async_computation.20 | async-start | bytes 17301504 | tf_op jit(solution)/shard_map/reduce_scatter | solution.py:359
  1077.8 1114.8 %reduce-scatter.22.cloned.1.call-start = ((), (), s32[]{:S(2)}) async-start(), calls=%async_computation.21 | async-start | bytes 47579136 | tf_op jit(solution)/shard_map/reduce_scatter | solution.py:232
  1097.6 1586.3 %reduce-scatter.24.cloned.1.call-start = ((), (), s32[]{:S(2)}) async-start(), calls=%async_computation.22 | async-start | bytes 47579136 | tf_op jit(solution)/shard_map/reduce_scatter | solution.py:233
  1117.2 2057.9 %reduce-scatter.26.cloned.1.call-start = ((), (), s32[]{:S(2)}) async-start(), calls=%async_computation.23 | async-start | bytes 47579136 | tf_op jit(solution)/shard_map/reduce_scatter | solution.py:234
  1137.6 6.4 copy-start.4
  1144.0 11.8 copy-start.16
  1144.1 11.8 copy-start.27
  1155.9 44.4 %copy-start.41 = (f32[128]{0:T(128)S(1)}, f32[128]{0:T(128)}, u32[]{:S(2)}) copy-start(f32[128]{0:T(128)} %get-tuple-element.670) | copy-start | bytes 1540
  (15 other events, 20.1 us)
Sparse Core Ops, SparseCore 0:
  10.9 59.1 all-gather.10
  72.9 55.2 all-gather.16
  130.9 38.9 all-gather.12
  172.5 38.8 all-gather.26
  214.2 76.3 all-gather.14
  293.2 75.9 all-gather.18
  372.2 143.1 all-gather.20
  518.3 142.7 all-gather.22
  664.0 142.7 all-gather.24
  898.6 88.1 reduce-scatter.27
  990.7 62.3 reduce-scatter.29
  1055.8 140.5 reduce-scatter.15
  1199.3 137.5 reduce-scatter.17
  1339.6 178.9 reduce-scatter.13
  1521.3 184.5 reduce-scatter.19
  1708.6 483.9 reduce-scatter.21
  2195.3 488.4 reduce-scatter.23
  2686.6 488.3 reduce-scatter.25
where the time goes:
time: 3200 us; the launch traced here: 3180 us
  waiting for transfers between devices  2790 us (87%)
  matrix products  202 us (6%)
  blocking collectives  82.8 us (3%)
  local copies, waits for them, and re-layouts  67.9 us (2%)
    reduce_scatter x1, waiting for transfers between devices, body(): lax.psum_scatter(grad_up, ('wide', 'narrow'), scatter_dimension=0, tiled=...  491 us
    reduce_scatter x1, waiting for transfers between devices, body(): lax.psum_scatter(grad_down, ('wide', 'narrow'), scatter_dimension=0, tile...  491 us
    reduce_scatter x1, waiting for transfers between devices, body(): lax.psum_scatter(grad_gate, ('wide', 'narrow'), scatter_dimension=0, tile...  487 us
    reduce_scatter x1, waiting for transfers between devices, body(): lax.psum_scatter(grad_out, ('wide', 'narrow'), scatter_dimension=0, tiled...  187 us
    reduce_scatter x1, waiting for transfers between devices, body(): lax.psum_scatter(grad_query, ('wide', 'narrow'), scatter_dimension=0, til...  182 us
    unnamed x20, waiting for transfers between devices  145 us
    all_gather x1, waiting for transfers between devices, body(): lax.all_gather(w_gate, ('wide', 'narrow'), axis=0, tiled=True)  140 us
    reduce_scatter x1, waiting for transfers between devices, body(): lax.psum_scatter(grad_value, ('wide', 'narrow'), scatter_dimension=0, til...  135 us
  transfers between devices with their start and end apart: 18, of which 17 were waited for; matrix products, arithmetic and copies ran while one was open for 6% of the time, Pallas kernels for 0%

commit v1 on v0

--- a/solution.py
+++ b/solution.py
@@ -55,7 +55,7 @@
     return carried
 
 
-def body(
+def general_body(
     tokens,
     attn_gain,
     w_query,
@@ -373,6 +373,187 @@
     )
 
 
+def group_body(
+    tokens,
+    attn_gain,
+    w_query,
+    w_key,
+    w_value,
+    w_out,
+    mlp_gain,
+    w_gate,
+    w_up,
+    w_down,
+    keep_mask,
+    group_ids,
+    positions,
+    exit_scale,
+    out_grad,
+):
+    _, span_len, model_width = tokens.shape
+    wide_count = lax.axis_size("wide")
+    narrow_count = lax.axis_size("narrow")
+    wide_place = lax.axis_index("wide")
+    device_count = wide_count * narrow_count
+    rows_each = w_query.shape[0]
+    full_len = span_len * wide_count
+    score_scale = 1.0 / math.sqrt(HD)
+    head_each = HEADS // wide_count
+    q_cols = head_each * HD
+    ff_cols = w_gate.shape[1] // wide_count
+    kv_share = wide_count // KVH
+    f32 = jnp.float32
+    bf16 = jnp.bfloat16
+
+    def spread(values):
+        return lax.all_gather(values, "wide", axis=0, tiled=True)
+
+    def collect(values):
+        return lax.psum_scatter(values.astype(bf16), "wide", scatter_dimension=0, tiled=True)
+
+    def by_columns(weight, columns):
+        return weight.reshape(rows_each, -1, columns).transpose(1, 0, 2)
+
+    pack_attn = jnp.concatenate(
+        [
+            by_columns(w_query, q_cols),
+            jnp.repeat(by_columns(w_key, HD), kv_share, axis=0),
+            jnp.repeat(by_columns(w_value, HD), kv_share, axis=0),
+        ],
+        axis=2,
+    )
+    pack_ff = jnp.concatenate([by_columns(w_gate, ff_cols), by_columns(w_up, ff_cols)], axis=2)
+
+    def share_columns(pack):
+        got = lax.all_to_all(pack, "wide", 0, 0, tiled=True)
+        full = lax.all_gather(got, "narrow", axis=1)
+        return full.reshape(model_width, pack.shape[2])
+
+    qkv_w = share_columns(pack_attn)
+    ff_w = share_columns(pack_ff)
+    out_w = lax.all_gather(w_out, "narrow", axis=0, tiled=True)
+    down_w = lax.all_gather(w_down, "narrow", axis=0, tiled=True)
+    gains = lax.all_gather(jnp.stack([attn_gain, mlp_gain]), ("wide", "narrow"), axis=1, tiled=True)
+    gain_one = gains[0].astype(f32)
+    gain_two = gains[1].astype(f32)
+
+    own_x = tokens[0].astype(f32)
+    keep = keep_mask[0].astype(f32)
+    group_match = group_ids[0][:, None] == jnp.arange(exit_scale.shape[0], dtype=jnp.int32)[None, :]
+    token_scale = jnp.sum(jnp.where(group_match, exit_scale[None, :], 0.0), axis=1, keepdims=True)
+    upstream = out_grad[0].astype(f32) * token_scale
+    mixed_grad = spread((keep * upstream).astype(bf16))
+
+    inputs = spread(tokens[0]).astype(f32)
+    token_pos = lax.all_gather(positions[0], "wide", axis=0, tiled=True)
+    inverse_all = lax.rsqrt(jnp.mean(inputs * inputs, axis=-1, keepdims=True) + epsilon)
+    first_norm = (inputs * inverse_all * gain_one).astype(bf16)
+    qkv = jnp.dot(first_norm, qkv_w, preferred_element_type=f32)
+    queries = rotate(qkv[:, :q_cols].reshape(full_len, head_each, HD), token_pos, 1.0).astype(bf16)
+    keys = rotate(qkv[:, q_cols : q_cols + HD].reshape(full_len, 1, HD), token_pos, 1.0)[:, 0].astype(bf16)
+    values = qkv[:, q_cols + HD :].astype(bf16)
+    scores = jnp.einsum("tgd,jd->gtj", queries, keys, preferred_element_type=f32) * score_scale
+    place = jnp.arange(full_len, dtype=jnp.int32)
+    allowed = place[None, :] <= place[:, None]
+    scores = jnp.where(allowed, scores, -1e30)
+    weights = jnp.exp(scores - jnp.max(scores, axis=-1, keepdims=True))
+    probabilities = weights / jnp.sum(weights, axis=-1, keepdims=True)
+    rounded_probs = probabilities.astype(bf16)
+    attended = jnp.einsum("gtj,jd->tgd", rounded_probs, values, preferred_element_type=f32)
+    attended_rows = attended.reshape(full_len, q_cols).astype(bf16)
+    branch = collect(jnp.dot(attended_rows, out_w, preferred_element_type=f32))
+    middle = own_x + keep * branch.astype(f32)
+    inverse_two = lax.rsqrt(jnp.mean(middle * middle, axis=-1, keepdims=True) + epsilon)
+    second_norm = spread((middle * inverse_two * gain_two).astype(bf16))
+    gate_up = jnp.dot(second_norm, ff_w, preferred_element_type=f32)
+    gate_value = gate_up[:, :ff_cols]
+    up_value = gate_up[:, ff_cols:]
+    gate_sigmoid = jax.nn.sigmoid(gate_value)
+    swish_value = gate_value * gate_sigmoid
+    hidden = (swish_value * up_value).astype(bf16)
+    hidden_grad = against(mixed_grad, down_w)
+    gate_grad = hidden_grad * up_value * gate_sigmoid * (1.0 + gate_value * (1.0 - gate_sigmoid))
+    up_grad = hidden_grad * swish_value
+    both_grad = jnp.concatenate([gate_grad, up_grad], axis=1).astype(bf16)
+    norm_grad = collect(against(both_grad, ff_w)).astype(f32)
+    mixed = collect(jnp.dot(hidden, down_w, preferred_element_type=f32)).astype(f32)
+    output = (middle + keep * mixed).astype(bf16)
+    grad_gain_two = jnp.sum(norm_grad * middle * inverse_two, axis=0)
+    scaled_two = gain_two * norm_grad
+    middle_grad = (
+        upstream
+        + inverse_two * scaled_two
+        - middle
+        * (inverse_two * inverse_two * inverse_two)
+        * jnp.mean(scaled_two * middle, axis=-1, keepdims=True)
+    )
+    branch_grad = spread((keep * middle_grad).astype(bf16))
+    attended_grad = against(branch_grad, out_w).astype(bf16).reshape(full_len, head_each, HD)
+    prob_grad = jnp.einsum("tgd,jd->gtj", attended_grad, values, preferred_element_type=f32)
+    delta = jnp.sum(attended_grad.astype(f32) * attended, axis=-1).T[..., None]
+    score_grad = (probabilities * (prob_grad - delta)).astype(bf16)
+    query_back = jnp.einsum("gtj,jd->tgd", score_grad, keys, preferred_element_type=f32) * score_scale
+    key_back = jnp.einsum("gtj,tgd->jd", score_grad, queries, preferred_element_type=f32) * score_scale
+    value_back = jnp.einsum("gtj,tgd->jd", rounded_probs, attended_grad, preferred_element_type=f32)
+    qkv_grad = jnp.concatenate(
+        [
+            rotate(query_back, token_pos, -1.0).reshape(full_len, q_cols),
+            rotate(key_back[:, None], token_pos, -1.0)[:, 0],
+            value_back,
+        ],
+        axis=1,
+    ).astype(bf16)
+    input_norm_grad = collect(against(qkv_grad, qkv_w)).astype(f32)
+    inverse_one = lax.rsqrt(jnp.mean(own_x * own_x, axis=-1, keepdims=True) + epsilon)
+    grad_gain_one = jnp.sum(input_norm_grad * own_x * inverse_one, axis=0)
+    scaled_one = gain_one * input_norm_grad
+    input_grad = (
+        middle_grad
+        + inverse_one * scaled_one
+        - own_x
+        * (inverse_one * inverse_one * inverse_one)
+        * jnp.mean(scaled_one * own_x, axis=-1, keepdims=True)
+    )
+
+    def return_columns(grad):
+        summed = lax.psum_scatter(
+            grad.astype(bf16).reshape(wide_count, narrow_count, rows_each, -1),
+            "narrow",
+            scatter_dimension=1,
+            tiled=False,
+        )
+        return lax.all_to_all(summed, "wide", 0, 0, tiled=True)
+
+    def side_by_side(blocks):
+        return blocks.transpose(1, 0, 2).reshape(rows_each, -1)
+
+    qkv_back = return_columns(over_rows(first_norm, qkv_grad)).astype(f32)
+    ff_back = return_columns(over_rows(second_norm, both_grad)).astype(f32)
+    kv_back = qkv_back[:, :, q_cols:].reshape(KVH, kv_share, rows_each, 2 * HD).sum(axis=1)
+    grad_out = lax.psum_scatter(
+        over_rows(attended_rows, branch_grad).astype(bf16), "narrow", scatter_dimension=0, tiled=True
+    ).astype(f32)
+    grad_down = lax.psum_scatter(
+        over_rows(hidden, mixed_grad).astype(bf16), "narrow", scatter_dimension=0, tiled=True
+    ).astype(f32)
+    gain_grads = lax.psum_scatter(
+        jnp.stack([grad_gain_one, grad_gain_two]), ("wide", "narrow"), scatter_dimension=1, tiled=True
+    )
+    return (
+        output[None],
+        input_grad.astype(bf16)[None],
+        gain_grads[0],
+        side_by_side(qkv_back[:, :, :q_cols]),
+        side_by_side(kv_back[:, :, :HD]),
+        side_by_side(kv_back[:, :, HD:]),
+        grad_out,
+        gain_grads[1],
+        side_by_side(ff_back[:, :, :ff_cols]),
+        side_by_side(ff_back[:, :, ff_cols:]),
+        grad_down,
+    )
+
+
 def solution(mesh):
     placed = (
         P("narrow", "wide", None),
@@ -391,8 +572,10 @@
         P(),
         P("narrow", "wide", None),
     )
+    wide_count = mesh.shape["wide"]
+    grouped = mesh.shape["narrow"] == 4 and HEADS % wide_count == 0 and wide_count % KVH == 0
     return jax.shard_map(
-        body,
+        group_body if grouped else general_body,
         mesh=mesh,
         in_specs=placed,
         out_specs=(

time: 3200 us -> 1270 us (0.40)
  waiting for transfers between devices: 2790 us -> 892 us
  matrix products: 202 us -> 111 us
  blocking collectives: 82.8 us -> 144 us
    reduce_scatter x7 -> x6, waiting for transfers between devices: 1970 us -> 326 us  [the longest x4 288 us: collect(): lax.psum_scatter(values.astype(bf16), 'wide', scatter_dimension=0, tiled=...]
    all_gather x9 -> x8, waiting for transfers between devices: 673 us -> 296 us  [the longest x4 240 us: spread(): return lax.all_gather(values, 'wide', axis=0, tiled=True)]
    unnamed x20 -> x18, waiting for transfers between devices: 145 us -> 259 us
    all_to_all x0 -> x2, blocking collectives: none -> 88.6 us  [share_columns(): got = lax.all_to_all(pack, 'wide', 0, 0, tiled=True)]
    unnamed x2 -> x0, blocking collectives: 82.8 us -> none
    all_gather x0 -> x2, blocking collectives: none -> 55.7 us  [the longest x1 39.5 us: group_body(): lax.all_gather(jnp.stack([attn_gain, mlp_gain]), ('wide', 'narrow'), axis...]
    dot_general x7 -> x4, matrix products: 76.5 us -> 29.9 us  [over_rows(): lax.dot_general(left, right, (((0,), (0,)), ((), ())), preferred_element_...]
    dot_general x14 -> x9, matrix products: 69.1 us -> 40.9 us  [the longest x1 11.8 us: group_body(): gate_up = jnp.dot(second_norm, ff_w, preferred_element_type=f32)]
  transfers between devices with their start and end apart: 18 -> 18, of which waited for: 17 -> 15; matrix products, arithmetic and copies ran while one was open for 6% -> 10% of each run, Pallas kernels for 0% -> 0%
where the time goes in v1:
time: 1270 us; the launch traced here: 1260 us
  waiting for transfers between devices  892 us (70%)
  blocking collectives  144 us (11%)
  matrix products  111 us (9%)
  local copies, waits for them, and re-layouts  49.9 us (4%)
  other arithmetic  38.1 us (3%)
  between operations  15.2 us (1%)
    reduce_scatter x4, waiting for transfers between devices, collect(): lax.psum_scatter(values.astype(bf16), 'wide', scatter_dimension=0, tiled=...  288 us
    unnamed x18, waiting for transfers between devices  259 us
    all_gather x4, waiting for transfers between devices, spread(): return lax.all_gather(values, 'wide', axis=0, tiled=True)  240 us
    all_to_all x2, blocking collectives, share_columns(): got = lax.all_to_all(pack, 'wide', 0, 0, tiled=True)  88.6 us
    all_gather x2, waiting for transfers between devices, share_columns(): full = lax.all_gather(got, 'narrow', axis=1)  39.9 us
    all_gather x1, blocking collectives, group_body(): lax.all_gather(jnp.stack([attn_gain, mlp_gain]), ('wide', 'narrow'), axis...  39.5 us
    dot_general x4, matrix products, against(): lax.dot_general(left, right, (((1,), (1,)), ((), ())), preferred_element_...  31.2 us
    dot_general x4, matrix products, over_rows(): lax.dot_general(left, right, (((0,), (0,)), ((), ())), preferred_element_...  29.9 us
  transfers between devices with their start and end apart: 18, of which 15 were waited for; matrix products, arithmetic and copies ran while one was open for 10% of the time, Pallas kernels for 0%

profile of v1, /device:TPU:0, one launch (start us, length us, event | category | flops | bytes accessed | tf_op | source)
XLA Modules:
  0.0 1259.7 jit_solution(18354356528562617540)
XLA Ops:
  10.4 21.6 %all_to_all.20 = bf16[8,64,512]{2,1,0:T(8,128)(2,1)S(1)} all-to-all(bf16[8,64,512]{2,1,0:T(8,128)(2,1)S(1)} %copy.132), channel_id=1, replica_groups=mesh['wide'=8,'narrow'=4] {'wide'}, dimensions={0} | all-to-all | bytes 1048576 | tf_op jit(solution)/shard_map/all_to_all | solution.py:428
  35.9 39.5 %all-gather.4 = bf16[32,64,2]{1,2,0:T(2,128)(2,1)S(1)} all-gather(bf16[1,64,2]{1,2,0:T(2,128)(2,1)S(1)} %maximum_bitcast_fusion.9), channel_id=1, replica_groups=mesh['wide'=8,'narrow'=4] {'wide','narrow'}, dimensions={0}, use_global_device_ids=true | all-gather | bytes 8448 | tf_op jit(solution)/shard_map/all_gather | solution.py:436
  75.5 16.2 %all-gather.2 = s32[1,1024]{1,0:T(1,128)S(1)} all-gather(s32[1,128]{1,0:T(1,128)S(1)} %copy-done.13), channel_id=4, replica_groups=mesh['wide'=8,'narrow'=4] {'wide'}, dimensions={1}, use_global_device_ids=true | all-gather | bytes 4608 | tf_op jit(solution)/shard_map/all_gather | solution.py:448
  91.8 3.0 broadcast_multiply_fusion
  94.8 3.6 copy.134
  98.4 32.1 %all-gather.24.cloned.1.call-done = bf16[1,1024,2048]{2,1,0:T(8,128)(2,1)} async-done(((bf16[1,128,2048]{2,1,0:T(8,128)(2,1)}), bf16[1,1024,2048]{2,1,0:T(8,128)(2,1)}) %all-gather.24.cloned.1.call-update) | async-done | bytes 4194320 | tf_op jit(solution)/shard_map/all_gather | solution.py:409
  130.5 3.2 fusion.1
  133.9 4.2 fusion.19
  145.1 8.5 fusion.77
  153.6 4.6 fusion.10
  160.3 2.8 fusion.78
  163.1 4.5 convolution_convert_fusion.4
  169.5 2.5 reshape.291
  173.8 67.0 %all_to_all.21 = bf16[8,64,1408]{2,1,0:T(8,128)(2,1)S(1)} all-to-all(bf16[8,64,1408]{2,1,0:T(8,128)(2,1)S(1)} %copy.139), channel_id=1, replica_groups=mesh['wide'=8,'narrow'=4] {'wide'}, dimensions={0} | all-to-all | bytes 2883584 | tf_op jit(solution)/shard_map/all_to_all | solution.py:428
  243.4 40.8 %reduce-scatter.16.cloned.1.call-done = bf16[128,2048]{1,0:T(8,128)(2,1)} async-done(((bf16[1024,2048]{1,0:T(8,128)(2,1)}), bf16[128,2048]{1,0:T(8,128)(2,1)}) %reduce-scatter.16.cloned.1.call-update) | async-done | bytes 524304 | tf_op jit(solution)/shard_map/reduce_scatter | solution.py:412
  289.7 39.9 %all-gather.28.cloned.1.call-done = bf16[8,256,1408]{2,0,1:T(8,128)(2,1)} async-done(((bf16[8,64,1408]{2,0,1:T(8,128)(2,1)}), bf16[8,256,1408]{2,0,1:T(8,128)(2,1)}) %all-gather.28.cloned.1.call-update) | async-done | bytes 5767184 | tf_op jit(solution)/shard_map/all_gather | solution.py:429
  329.6 5.9 copy.141
  335.4 70.3 %all-gather.16.cloned.1.call-done = bf16[1024,2048]{1,0:T(8,128)(2,1)} async-done(((bf16[128,2048]{1,0:T(8,128)(2,1)}), bf16[1024,2048]{1,0:T(8,128)(2,1)}) %all-gather.16.cloned.1.call-update) | async-done | bytes 4194320 | tf_op jit(solution)/shard_map/all_gather | solution.py:409
  405.8 11.8 fusion.79
  417.6 15.2 %all-gather.18.cloned.1.call-done = bf16[704,2048]{1,0:T(8,128)(2,1)} async-done(((bf16[176,2048]{1,0:T(8,128)(2,1)}), bf16[704,2048]{1,0:T(8,128)(2,1)}) %all-gather.18.cloned.1.call-update) | async-done | bytes 2883600 | tf_op jit(solution)/shard_map/all_gather | solution.py:435
  432.7 76.3 %all-gather.20.cloned.1.call-done = bf16[1024,2048]{1,0:T(8,128)(2,1)} async-done(((bf16[128,2048]{1,0:T(8,128)(2,1)}), bf16[1024,2048]{1,0:T(8,128)(2,1)}) %all-gather.20.cloned.1.call-update) | async-done | bytes 4194320 | tf_op jit(solution)/shard_map/all_gather | solution.py:409
  509.1 10.1 multiply_convert_fusion.1
  520.9 11.0 convolution_convert_fusion.2
  531.9 7.7 convolution_convert_fusion.3
  539.7 78.5 %reduce-scatter.20.cloned.1.call-done = bf16[128,2048]{1,0:T(8,128)(2,1)} async-done(((bf16[1024,2048]{1,0:T(8,128)(2,1)}), bf16[128,2048]{1,0:T(8,128)(2,1)}) %reduce-scatter.20.cloned.1.call-update) | async-done | bytes 524304 | tf_op jit(solution)/shard_map/reduce_scatter | solution.py:412
  619.7 89.6 %reduce-scatter.18.cloned.1.call-done = bf16[128,2048]{1,0:T(8,128)(2,1)} async-done(((bf16[1024,2048]{1,0:T(8,128)(2,1)}), bf16[128,2048]{1,0:T(8,128)(2,1)}) %reduce-scatter.18.cloned.1.call-update) | async-done | bytes 524304 | tf_op jit(solution)/shard_map/reduce_scatter | solution.py:412
  709.4 2.9 multiply_convert_fusion.3
  712.4 11.5 convolution_convert_fusion
  723.9 61.7 %all-gather.22.cloned.1.call-done = bf16[1024,2048]{1,0:T(8,128)(2,1)} async-done(((bf16[128,2048]{1,0:T(8,128)(2,1)}), bf16[1024,2048]{1,0:T(8,128)(2,1)}) %all-gather.22.cloned.1.call-update) | async-done | bytes 4194320 | tf_op jit(solution)/shard_map/all_gather | solution.py:409
  785.7 4.1 multiply_reduce_fusion
  789.8 4.9 fusion.5
  803.6 6.5 convolution_convert_fusion.6
  810.2 7.4 convolution_convert_fusion.5
  817.7 4.5 convolution_convert_fusion.7
  822.3 6.1 convolution_convert_fusion.1
  829.6 124.3 %all-reduce.5.cloned.1.call-done = (bf16[8,4,64,512]{3,2,1,0:T(8,128)(2,1)}, bf16[8,4,64,1408]{3,2,1,0:T(8,128)(2,1)}) async-done(((bf16[8,4,64,512]{3,2,1,0:T(8,128)(2,1)}, bf16[8,4,64,1408]{3,2,1,0:T(8,128)(2,1)}), (bf16[8,4,64,512]{3,2,1,0:T(8,128)(2,1)}, bf16[8,4,64,1408]{3,2,1,0:T(8,128)(2,1)})) %all-reduce.5.cloned.1.call-update) | async-done | bytes 7864336
  953.9 2.5 dynamic-slice_bitcast_fusion.1
  956.4 5.5 all-to-all-start.2
  961.9 3.2 dynamic-slice_bitcast_fusion
  965.1 10.9 all-to-all-done.2
  976.9 3.6 all-to-all-start.3
  980.7 12.6 reduce-scatter.26.cloned.1.call-done
  993.3 2.4 convert_element_type.159
  995.6 25.5 %reduce-scatter.24.cloned.1.call-done = bf16[64,2048]{1,0:T(8,128)(2,1)} async-done(((bf16[256,2048]{1,0:T(8,128)(2,1)}), bf16[64,2048]{1,0:T(8,128)(2,1)}) %reduce-scatter.24.cloned.1.call-update) | async-done | bytes 262160 | tf_op jit(solution)/shard_map/reduce_scatter | solution.py:533
  1030.3 2.3 copy.156
  1034.3 78.7 %reduce-scatter.22.cloned.1.call-done = bf16[128,2048]{1,0:T(8,128)(2,1)} async-done(((bf16[1024,2048]{1,0:T(8,128)(2,1)}), bf16[128,2048]{1,0:T(8,128)(2,1)}) %reduce-scatter.22.cloned.1.call-update) | async-done | bytes 524304 | tf_op jit(solution)/shard_map/reduce_scatter | solution.py:412
  1115.8 2.2 fusion.40
  1118.0 132.9 %reduce-scatter.28.cloned.1.call-done = f32[64,2]{1,0:T(8,128)} async-done(((f32[2048,2]{1,0:T(8,128)}), f32[64,2]{1,0:T(8,128)}) %reduce-scatter.28.cloned.1.call-update) | async-done | bytes 528
  (140 shorter events, 57.7 us)
Async XLA Ops:
  7.2 28.7 %copy-start.15 = (bf16[64]{0:T(256)(128)(2,1)S(1)}, bf16[64]{0:T(256)(128)(2,1)}, u32[]{:S(2)}) copy-start(bf16[64]{0:T(256)(128)(2,1)} %param.16) | copy-start | bytes 388
  7.2 28.7 %copy-start.14 = (bf16[64]{0:T(256)(128)(2,1)S(1)}, bf16[64]{0:T(256)(128)(2,1)}, u32[]{:S(2)}) copy-start(bf16[64]{0:T(256)(128)(2,1)} %param.21) | copy-start | bytes 388
  7.2 68.3 %copy-start.13 = (s32[1,128]{1,0:T(1,128)S(1)}, s32[1,128]{1,0:T(1,128)}, u32[]{:S(2)}) copy-start(s32[1,128]{1,0:T(1,128)} %param.27) | copy-start | bytes 1540
  7.2 87.6 %all-gather.26.cloned.1.call-start = ((), (), s32[]{:S(2)}) async-start(), calls=%async_computation.23 | async-start | bytes 2621440 | tf_op jit(solution)/shard_map/all_gather | solution.py:429
  33.1 97.4 %all-gather.24.cloned.1.call-start = ((), (), s32[]{:S(2)}) async-start(), calls=%async_computation.22 | async-start | bytes 4718592 | tf_op jit(solution)/shard_map/all_gather | solution.py:409
  33.8 129.2 %all-gather.14.cloned.1.call-start = ((), (), s32[]{:S(2)}) async-start(), calls=%async_computation.11 | async-start | bytes 1310720 | tf_op jit(solution)/shard_map/all_gather | solution.py:434
  34.6 249.7 %reduce-scatter.16.cloned.1.call-start = ((), (), s32[]{:S(2)}) async-start(), calls=%async_computation.12 | async-start | bytes 4718592 | tf_op jit(solution)/shard_map/reduce_scatter | solution.py:412
  130.5 3.4 copy-start.4
  138.1 1.5 copy-start.11
  145.1 8.5 copy-start.7
  158.3 2.0 copy-start.1
  167.6 162.0 %all-gather.28.cloned.1.call-start = ((), (), s32[]{:S(2)}) async-start(), calls=%async_computation.24 | async-start | bytes 7208960 | tf_op jit(solution)/shard_map/all_gather | solution.py:429
  173.8 110.5 %copy-start = (bf16[1,128,2048]{2,1,0:T(8,128)(2,1)S(1)}, bf16[1,128,2048]{2,1,0:T(8,128)(2,1)}, u32[]{:S(2)}) copy-start(bf16[1,128,2048]{2,1,0:T(8,128)(2,1)} %param.15) | copy-start | bytes 1572868
  240.8 47.7 %copy-start.16 = (f32[2]{0:T(128)S(1)}, f32[2]{0:T(128)}, u32[]{:S(2)}) copy-start(f32[2]{0:T(128)} %param.28) | copy-start | bytes 28
  240.8 47.7 %copy-start.17 = (s32[1,128]{1,0:T(1,128)S(1)}, s32[1,128]{1,0:T(1,128)}, u32[]{:S(2)}) copy-start(s32[1,128]{1,0:T(1,128)} %param.26) | copy-start | bytes 1540
  240.8 47.8 %copy-start.5 = (bf16[1,128,2048]{2,1,0:T(8,128)(2,1)S(1)}, bf16[1,128,2048]{2,1,0:T(8,128)(2,1)}, u32[]{:S(2)}) copy-start(bf16[1,128,2048]{2,1,0:T(8,128)(2,1)} %param.29) | copy-start | bytes 1572868
  242.7 163.0 %all-gather.16.cloned.1.call-start = ((), (), s32[]{:S(2)}) async-start(), calls=%async_computation.13 | async-start | bytes 4718592 | tf_op jit(solution)/shard_map/all_gather | solution.py:409
  287.7 145.0 %all-gather.18.cloned.1.call-start = ((), (), s32[]{:S(2)}) async-start(), calls=%async_computation.14 | async-start | bytes 3604480 | tf_op jit(solution)/shard_map/all_gather | solution.py:435
  288.5 220.6 %all-gather.20.cloned.1.call-start = ((), (), s32[]{:S(2)}) async-start(), calls=%async_computation.16 | async-start | bytes 4718592 | tf_op jit(solution)/shard_map/all_gather | solution.py:409
  289.6 328.6 %reduce-scatter.20.cloned.1.call-start = ((), (), s32[]{:S(2)}) async-start(), calls=%async_computation.17 | async-start | bytes 4718592 | tf_op jit(solution)/shard_map/reduce_scatter | solution.py:412
  519.2 1.2 copy-start.19
  519.2 1.6 copy-start.20
  531.8 177.5 %reduce-scatter.18.cloned.1.call-start = ((), (), s32[]{:S(2)}) async-start(), calls=%async_computation.15 | async-start | bytes 4718592 | tf_op jit(solution)/shard_map/reduce_scatter | solution.py:412
  539.6 78.6 %copy-start.3 = (bf16[128,2048]{1,0:T(8,128)(2,1)S(1)}, bf16[128,2048]{1,0:T(8,128)(2,1)}, u32[]{:S(2)}) copy-start(bf16[128,2048]{1,0:T(8,128)(2,1)} %reduce-scatter.16.cloned.1.call-done) | copy-start | bytes 1572868
  539.6 246.0 %all-gather.22.cloned.1.call-start = ((), (), s32[]{:S(2)}) async-start(), calls=%async_computation.18 | async-start | bytes 4718592 | tf_op jit(solution)/shard_map/all_gather | solution.py:409
  712.3 241.5 %all-reduce.5.cloned.1.call-start = ((), (), s32[]{:S(2)}) async-start(), calls=%async_computation.26 | async-start | bytes 15728640
  794.6 1.9 copy-start.8
  794.6 1.9 copy-start.9
  796.5 2.2 copy-start.2
  798.7 1.6 copy-start.10
  810.2 183.1 %reduce-scatter.26.cloned.1.call-start = ((), (), s32[]{:S(2)}) async-start(), calls=%async_computation.21 | async-start | bytes 3604480 | tf_op jit(solution)/shard_map/reduce_scatter | solution.py:536
  817.7 4.6 copy-start.12
  817.7 203.4 %reduce-scatter.24.cloned.1.call-start = ((), (), s32[]{:S(2)}) async-start(), calls=%async_computation.20 | async-start | bytes 1310720 | tf_op jit(solution)/shard_map/reduce_scatter | solution.py:533
  822.2 290.8 %reduce-scatter.22.cloned.1.call-start = ((), (), s32[]{:S(2)}) async-start(), calls=%async_computation.19 | async-start | bytes 4718592 | tf_op jit(solution)/shard_map/reduce_scatter | solution.py:412
  828.3 0.7 copy-start.18
  956.4 19.7 %all-to-all-start.2 = ((bf16[8,64,512]{2,1,0:T(8,128)(2,1)}), bf16[8,64,512]{2,1,0:T(8,128)(2,1)S(1)}, u32[]{:S(2)}, u32[]{:S(2)}) async-start(bf16[8,64,512]{2,1,0:T(8,128)(2,1)} %dynamic-slice_bitcast_fusion.1), calls=%async_computation.6 | async-start | bytes 1048576 | tf_op jit(solution)/shard_map/all_to_all | solution.py:525
  976.1 0.8 copy-start.6
  976.9 48.9 %all-to-all-start.3 = ((bf16[8,64,1408]{2,1,0:T(8,128)(2,1)}), bf16[8,64,1408]{2,1,0:T(8,128)(2,1)S(1)}, u32[]{:S(2)}, u32[]{:S(2)}) async-start(bf16[8,64,1408]{2,1,0:T(8,128)(2,1)} %dynamic-slice_bitcast_fusion), calls=%async_computation.8 | async-start | bytes 2883584 | tf_op jit(solution)/shard_map/all_to_all | solution.py:525
  980.5 270.4 %reduce-scatter.28.cloned.1.call-start = ((), (), s32[]{:S(2)}) async-start(), calls=%async_computation.25 | async-start | bytes 1081344
Sparse Core Ops, SparseCore 0:
  33.2 21.6 all-gather.25
  57.0 73.4 all-gather.23
  132.1 15.0 all-gather.13
  167.7 116.5 reduce-scatter.15
  286.3 43.1 all-gather.27
  332.3 73.3 all-gather.15
  407.4 25.3 all-gather.17
  435.7 73.3 all-gather.19
  532.0 86.1 reduce-scatter.19
  621.7 87.6 reduce-scatter.17
  712.5 73.1 all-gather.21
  810.3 143.5 all-reduce.4
  956.6 36.6 reduce-scatter.25
  996.2 24.8 reduce-scatter.23
  1025.1 87.8 reduce-scatter.21
  1115.9 134.9 reduce-scatter.27

commit v2 on v1

--- a/solution.py
+++ b/solution.py
@@ -3,6 +3,7 @@
 import jax
 import jax.numpy as jnp
 from jax import lax
+from jax.sharding import Mesh
 from jax.sharding import PartitionSpec as P
 
 HEADS = 16
@@ -373,7 +374,7 @@
     )
 
 
-def group_body(
+def line_body(
     tokens,
     attn_gain,
     w_query,
@@ -390,81 +391,138 @@
     exit_scale,
     out_grad,
 ):
-    _, span_len, model_width = tokens.shape
-    wide_count = lax.axis_size("wide")
-    narrow_count = lax.axis_size("narrow")
-    wide_place = lax.axis_index("wide")
-    device_count = wide_count * narrow_count
-    rows_each = w_query.shape[0]
-    full_len = span_len * wide_count
-    score_scale = 1.0 / math.sqrt(HD)
-    head_each = HEADS // wide_count
-    q_cols = head_each * HD
-    ff_cols = w_gate.shape[1] // wide_count
-    kv_share = wide_count // KVH
     f32 = jnp.float32
     bf16 = jnp.bfloat16
-
-    def spread(values):
-        return lax.all_gather(values, "wide", axis=0, tiled=True)
-
-    def collect(values):
-        return lax.psum_scatter(values.astype(bf16), "wide", scatter_dimension=0, tiled=True)
+    _, span_len, model_width = tokens.shape
+    line = lax.axis_size("z")
+    place = lax.axis_index("z")
+    side = lax.axis_index("x")
+    near = lax.axis_size("x") * lax.axis_size("y") * lax.axis_size("c")
+    rows_each = w_query.shape[0]
+    heads = HEADS // line
+    q_cols = heads * HD
+    ff_cols = w_gate.shape[1] // line
+    group_len = span_len * line
+    score_scale = 1.0 / math.sqrt(HD)
+
+    def shift(values, axis, step):
+        size = lax.axis_size(axis)
+        return lax.ppermute(values, axis, [(i, (i + step) % size) for i in range(size)])
+
+    def halves(values):
+        cut = values.shape[0] // 2
+        return [values[:cut], values[cut:]]
+
+    def ring_pieces(values):
+        parts = [[part] for part in halves(values)]
+        for _ in range(line - 1):
+            for index, part in enumerate(parts):
+                part.append(shift(part[-1], "z", 1 - 2 * index))
+        return [[parts[0][k], parts[1][(line - k) % line]] for k in range(line)]
+
+    def ring_gather(values):
+        return jnp.concatenate(sum(ring_pieces(values), []), axis=0)
+
+    def ring_blocks(values):
+        return [jnp.concatenate(pieces, axis=0) for pieces in ring_pieces(values)]
+
+    def ring_sum(blocks):
+        totals = []
+        for index in range(2):
+            step = 2 * index - 1
+            total = None
+            for hop in range(line):
+                k = (line - 1 - hop) % line if index == 0 else (hop + 1) % line
+                own = halves(blocks[k])[index]
+                total = own if total is None else (shift(total, "z", step).astype(f32) + own.astype(f32))
+                if hop < line - 1:
+                    total = total.astype(bf16)
+            totals.append(total)
+        return jnp.concatenate(totals, axis=0)
+
+    def pick(values, index, dim):
+        return lax.dynamic_index_in_dim(values, index, dim, keepdims=False)
 
     def by_columns(weight, columns):
-        return weight.reshape(rows_each, -1, columns).transpose(1, 0, 2)
+        return weight.reshape(rows_each, line, columns).transpose(1, 0, 2)
+
+    def natural(blocks):
+        return jnp.take(blocks, (place - jnp.arange(line, dtype=jnp.int32)) % line, axis=0)
+
+    def turn(pack):
+        got = [pick(pack, place, 0)]
+        for k in range(1, line):
+            got.append(shift(pick(pack, (place + k) % line, 0), "z", k))
+        return jnp.stack(got)
+
+    def near_gather(values, dim):
+        return lax.all_gather(values, ("x", "y", "c"), axis=dim)
 
     pack_attn = jnp.concatenate(
-        [
-            by_columns(w_query, q_cols),
-            jnp.repeat(by_columns(w_key, HD), kv_share, axis=0),
-            jnp.repeat(by_columns(w_value, HD), kv_share, axis=0),
-        ],
-        axis=2,
+        [by_columns(w_query, q_cols), by_columns(w_key, HD), by_columns(w_value, HD)], axis=2
     )
     pack_ff = jnp.concatenate([by_columns(w_gate, ff_cols), by_columns(w_up, ff_cols)], axis=2)
-
-    def share_columns(pack):
-        got = lax.all_to_all(pack, "wide", 0, 0, tiled=True)
-        full = lax.all_gather(got, "narrow", axis=1)
-        return full.reshape(model_width, pack.shape[2])
-
-    qkv_w = share_columns(pack_attn)
-    ff_w = share_columns(pack_ff)
-    out_w = lax.all_gather(w_out, "narrow", axis=0, tiled=True)
-    down_w = lax.all_gather(w_down, "narrow", axis=0, tiled=True)
-    gains = lax.all_gather(jnp.stack([attn_gain, mlp_gain]), ("wide", "narrow"), axis=1, tiled=True)
+    qkv_w = near_gather(natural(turn(pack_attn)), 1).reshape(model_width, q_cols + 2 * HD)
+    gains = lax.all_gather(jnp.stack([attn_gain, mlp_gain]), ("z", "x", "y", "c"), axis=1, tiled=True)
     gain_one = gains[0].astype(f32)
     gain_two = gains[1].astype(f32)
-
+    inputs = ring_gather(tokens[0]).astype(f32)
+    relative = (place - jnp.arange(line, dtype=jnp.int32)) % line
+    inside = jnp.arange(span_len, dtype=jnp.int32)
+
+    def token_index(which):
+        return ((relative[:, None] * 2 + which) * span_len + inside[None, :]).reshape(group_len)
+
+    token_pos = lax.all_gather(positions[0], "z", axis=0)
+    token_pos = natural(token_pos).reshape(group_len)
     own_x = tokens[0].astype(f32)
     keep = keep_mask[0].astype(f32)
     group_match = group_ids[0][:, None] == jnp.arange(exit_scale.shape[0], dtype=jnp.int32)[None, :]
     token_scale = jnp.sum(jnp.where(group_match, exit_scale[None, :], 0.0), axis=1, keepdims=True)
     upstream = out_grad[0].astype(f32) * token_scale
-    mixed_grad = spread((keep * upstream).astype(bf16))
-
-    inputs = spread(tokens[0]).astype(f32)
-    token_pos = lax.all_gather(positions[0], "wide", axis=0, tiled=True)
+
     inverse_all = lax.rsqrt(jnp.mean(inputs * inputs, axis=-1, keepdims=True) + epsilon)
     first_norm = (inputs * inverse_all * gain_one).astype(bf16)
     qkv = jnp.dot(first_norm, qkv_w, preferred_element_type=f32)
-    queries = rotate(qkv[:, :q_cols].reshape(full_len, head_each, HD), token_pos, 1.0).astype(bf16)
-    keys = rotate(qkv[:, q_cols : q_cols + HD].reshape(full_len, 1, HD), token_pos, 1.0)[:, 0].astype(bf16)
-    values = qkv[:, q_cols + HD :].astype(bf16)
+    queries = rotate(qkv[:, :q_cols].reshape(group_len, heads, HD), token_pos, 1.0).astype(bf16)
+    own_kv = jnp.concatenate(
+        [
+            rotate(qkv[:, q_cols : q_cols + HD].reshape(group_len, 1, HD), token_pos, 1.0)[:, 0],
+            qkv[:, q_cols + HD :],
+        ],
+        axis=1,
+    ).astype(bf16)
+    out_w = lax.all_gather(w_out, ("x", "y", "c"), axis=0, tiled=True)
+    out_w = ring_gather(out_w)
+    both_kv = jnp.concatenate([own_kv, shift(own_kv, "x", 1)], axis=0)
+    keys = both_kv[:, :HD]
+    values = both_kv[:, HD:]
+    query_index = token_index(side)
+    key_index = jnp.concatenate([query_index, token_index(1 - side)])
     scores = jnp.einsum("tgd,jd->gtj", queries, keys, preferred_element_type=f32) * score_scale
-    place = jnp.arange(full_len, dtype=jnp.int32)
-    allowed = place[None, :] <= place[:, None]
+    allowed = key_index[None, :] <= query_index[:, None]
     scores = jnp.where(allowed, scores, -1e30)
     weights = jnp.exp(scores - jnp.max(scores, axis=-1, keepdims=True))
     probabilities = weights / jnp.sum(weights, axis=-1, keepdims=True)
     rounded_probs = probabilities.astype(bf16)
     attended = jnp.einsum("gtj,jd->tgd", rounded_probs, values, preferred_element_type=f32)
-    attended_rows = attended.reshape(full_len, q_cols).astype(bf16)
-    branch = collect(jnp.dot(attended_rows, out_w, preferred_element_type=f32))
-    middle = own_x + keep * branch.astype(f32)
-    inverse_two = lax.rsqrt(jnp.mean(middle * middle, axis=-1, keepdims=True) + epsilon)
-    second_norm = spread((middle * inverse_two * gain_two).astype(bf16))
+    own_attended = attended.reshape(group_len, q_cols).astype(bf16)
+
+    def turned(block, k):
+        return jnp.roll(block.reshape(line, span_len, q_cols), k, axis=0).reshape(group_len, q_cols)
+
+    gathered = ring_blocks(own_attended)
+    attended_rows = jnp.concatenate([turned(block, k) for k, block in enumerate(gathered)], axis=1)
+    branch = jnp.dot(attended_rows, out_w, preferred_element_type=f32)
+    middle_all = inputs + keep * branch
+    inverse_mid = lax.rsqrt(jnp.mean(middle_all * middle_all, axis=-1, keepdims=True) + epsilon)
+    second_norm = (middle_all * inverse_mid * gain_two).astype(bf16)
+    middle = middle_all[:span_len]
+    inverse_two = inverse_mid[:span_len]
+
+    ff_w = near_gather(natural(turn(pack_ff)), 1).reshape(model_width, 2 * ff_cols)
+    down_w = lax.all_gather(w_down, ("x", "y", "c"), axis=0, tiled=True)
+    mixed_grad = ring_gather((keep * upstream).astype(bf16))
     gate_up = jnp.dot(second_norm, ff_w, preferred_element_type=f32)
     gate_value = gate_up[:, :ff_cols]
     up_value = gate_up[:, ff_cols:]
@@ -475,10 +533,13 @@
     gate_grad = hidden_grad * up_value * gate_sigmoid * (1.0 + gate_value * (1.0 - gate_sigmoid))
     up_grad = hidden_grad * swish_value
     both_grad = jnp.concatenate([gate_grad, up_grad], axis=1).astype(bf16)
-    norm_grad = collect(against(both_grad, ff_w)).astype(f32)
-    mixed = collect(jnp.dot(hidden, down_w, preferred_element_type=f32)).astype(f32)
+
+    def split(values):
+        return [values[k * span_len : (k + 1) * span_len] for k in range(line)]
+
+    norm_grad = ring_sum(split(against(both_grad, ff_w).astype(bf16)))
+    mixed = ring_sum(split(jnp.dot(hidden, down_w, preferred_element_type=f32).astype(bf16)))
     output = (middle + keep * mixed).astype(bf16)
-    grad_gain_two = jnp.sum(norm_grad * middle * inverse_two, axis=0)
     scaled_two = gain_two * norm_grad
     middle_grad = (
         upstream
@@ -487,25 +548,31 @@
         * (inverse_two * inverse_two * inverse_two)
         * jnp.mean(scaled_two * middle, axis=-1, keepdims=True)
     )
-    branch_grad = spread((keep * middle_grad).astype(bf16))
-    attended_grad = against(branch_grad, out_w).astype(bf16).reshape(full_len, head_each, HD)
+    branch_grad = (keep * middle_grad).astype(bf16)
+    own_grad = against(branch_grad, out_w).astype(bf16)
+    grad_blocks = [own_grad[:, :q_cols]]
+    for k in range(1, line):
+        back = line - k
+        grad_blocks.append(shift(own_grad[:, back * q_cols : (back + 1) * q_cols], "z", -back))
+    attended_grad = jnp.concatenate(grad_blocks, axis=0).reshape(group_len, heads, HD)
     prob_grad = jnp.einsum("tgd,jd->gtj", attended_grad, values, preferred_element_type=f32)
     delta = jnp.sum(attended_grad.astype(f32) * attended, axis=-1).T[..., None]
     score_grad = (probabilities * (prob_grad - delta)).astype(bf16)
     query_back = jnp.einsum("gtj,jd->tgd", score_grad, keys, preferred_element_type=f32) * score_scale
     key_back = jnp.einsum("gtj,tgd->jd", score_grad, queries, preferred_element_type=f32) * score_scale
     value_back = jnp.einsum("gtj,tgd->jd", rounded_probs, attended_grad, preferred_element_type=f32)
+    kv_back = jnp.concatenate([key_back, value_back], axis=1)
+    kv_back = kv_back[:group_len] + shift(kv_back[group_len:].astype(bf16), "x", 1).astype(f32)
     qkv_grad = jnp.concatenate(
         [
-            rotate(query_back, token_pos, -1.0).reshape(full_len, q_cols),
-            rotate(key_back[:, None], token_pos, -1.0)[:, 0],
-            value_back,
+            rotate(query_back, token_pos, -1.0).reshape(group_len, q_cols),
+            rotate(kv_back[:, None, :HD], token_pos, -1.0)[:, 0],
+            kv_back[:, HD:],
         ],
         axis=1,
     ).astype(bf16)
-    input_norm_grad = collect(against(qkv_grad, qkv_w)).astype(f32)
-    inverse_one = lax.rsqrt(jnp.mean(own_x * own_x, axis=-1, keepdims=True) + epsilon)
-    grad_gain_one = jnp.sum(input_norm_grad * own_x * inverse_one, axis=0)
+    input_norm_grad = ring_sum(split(against(qkv_grad, qkv_w).astype(bf16)))
+    inverse_one = inverse_all[:span_len]
     scaled_one = gain_one * input_norm_grad
     input_grad = (
         middle_grad
@@ -515,81 +582,105 @@
         * jnp.mean(scaled_one * own_x, axis=-1, keepdims=True)
     )
 
+    def pair_sum(values, axis, dim):
+        mine = pick(values, lax.axis_index(axis), dim).astype(f32)
+        other = pick(values, 1 - lax.axis_index(axis), dim)
+        return (mine + shift(other, axis, 1).astype(f32)).astype(bf16)
+
+    def near_sum(values):
+        lead = values.ndim - 5
+        values = pair_sum(values, "c", lead + 2)
+        cut = values.shape[-1] // 256 * 128
+        left = pair_sum(pair_sum(values[..., :cut], "x", lead), "y", lead)
+        right = pair_sum(pair_sum(values[..., cut:], "y", lead + 1), "x", lead)
+        return jnp.concatenate([left, right], axis=-1)
+
     def return_columns(grad):
-        summed = lax.psum_scatter(
-            grad.astype(bf16).reshape(wide_count, narrow_count, rows_each, -1),
-            "narrow",
-            scatter_dimension=1,
-            tiled=False,
-        )
-        return lax.all_to_all(summed, "wide", 0, 0, tiled=True)
+        summed = near_sum(grad.astype(bf16).reshape(line, 2, 2, 2, rows_each, -1))
+        return natural(turn(summed)).astype(f32)
 
     def side_by_side(blocks):
         return blocks.transpose(1, 0, 2).reshape(rows_each, -1)
 
-    qkv_back = return_columns(over_rows(first_norm, qkv_grad)).astype(f32)
-    ff_back = return_columns(over_rows(second_norm, both_grad)).astype(f32)
-    kv_back = qkv_back[:, :, q_cols:].reshape(KVH, kv_share, rows_each, 2 * HD).sum(axis=1)
-    grad_out = lax.psum_scatter(
-        over_rows(attended_rows, branch_grad).astype(bf16), "narrow", scatter_dimension=0, tiled=True
+    ff_back = return_columns(over_rows(second_norm, both_grad))
+    grad_down = near_sum(
+        over_rows(hidden, mixed_grad).astype(bf16).reshape(2, 2, 2, -1, model_width)
     ).astype(f32)
-    grad_down = lax.psum_scatter(
-        over_rows(hidden, mixed_grad).astype(bf16), "narrow", scatter_dimension=0, tiled=True
-    ).astype(f32)
-    gain_grads = lax.psum_scatter(
-        jnp.stack([grad_gain_one, grad_gain_two]), ("wide", "narrow"), scatter_dimension=1, tiled=True
-    )
+    grad_out = near_sum(
+        over_rows(attended_rows[:span_len], branch_grad)
+        .astype(bf16)
+        .reshape(line, 2, 2, 2, rows_each, model_width)
+    )
+    grad_out = ring_sum([grad_out[k] for k in range(line)])
+    qkv_back = return_columns(over_rows(first_norm, qkv_grad))
+    grad_query = side_by_side(qkv_back[:, :, :q_cols])
+    grad_key = side_by_side(qkv_back[:, :, q_cols : q_cols + HD])
+    grad_value = side_by_side(qkv_back[:, :, q_cols + HD :])
+    grad_gate = side_by_side(ff_back[:, :, :ff_cols])
+    grad_up = side_by_side(ff_back[:, :, ff_cols:])
+
+    def gain_grad(pairs, gain):
+        total = sum(jnp.sum(weight.astype(f32) * grad, axis=1) for weight, grad in pairs)
+        return total / gain.astype(f32)
+
     return (
         output[None],
         input_grad.astype(bf16)[None],
-        gain_grads[0],
-        side_by_side(qkv_back[:, :, :q_cols]),
-        side_by_side(kv_back[:, :, :HD]),
-        side_by_side(kv_back[:, :, HD:]),
+        gain_grad([(w_query, grad_query), (w_key, grad_key), (w_value, grad_value)], attn_gain),
+        grad_query,
+        grad_key,
+        grad_value,
         grad_out,
-        gain_grads[1],
-        side_by_side(ff_back[:, :, :ff_cols]),
-        side_by_side(ff_back[:, :, ff_cols:]),
+        gain_grad([(w_gate, grad_gate), (w_up, grad_up)], mlp_gain),
+        grad_gate,
+        grad_up,
         grad_down,
     )
 
 
 def solution(mesh):
-    placed = (
-        P("narrow", "wide", None),
-        P(("wide", "narrow")),
-        P(("wide", "narrow"), None),
-        P(("wide", "narrow"), None),
-        P(("wide", "narrow"), None),
-        P(("wide", "narrow"), None),
-        P(("wide", "narrow")),
-        P(("wide", "narrow"), None),
-        P(("wide", "narrow"), None),
-        P(("wide", "narrow"), None),
-        P("narrow"),
-        P("narrow", "wide"),
-        P("narrow", "wide"),
-        P(),
-        P("narrow", "wide", None),
-    )
-    wide_count = mesh.shape["wide"]
-    grouped = mesh.shape["narrow"] == 4 and HEADS % wide_count == 0 and wide_count % KVH == 0
+    wide, narrow = mesh.shape["wide"], mesh.shape["narrow"]
+    if wide == 2 * KVH and narrow == 4:
+        mesh = Mesh(mesh.devices.reshape(wide // 2, 2, 2, 2), ("z", "x", "y", "c"))
+        body, wide, narrow = line_body, ("z", "x"), ("y", "c")
+    else:
+        body, wide, narrow = general_body, ("wide",), ("narrow",)
+    token_spec = P(narrow, wide, None)
+    id_spec = P(narrow, wide)
+    gain_spec = P(wide + narrow)
+    weight_spec = P(wide + narrow, None)
     return jax.shard_map(
-        group_body if grouped else general_body,
+        body,
         mesh=mesh,
-        in_specs=placed,
+        in_specs=(
+            token_spec,
+            gain_spec,
+            weight_spec,
+            weight_spec,
+            weight_spec,
+            weight_spec,
+            gain_spec,
+            weight_spec,
+            weight_spec,
+            weight_spec,
+            P(narrow),
+            id_spec,
+            id_spec,
+            P(),
+            token_spec,
+        ),
         out_specs=(
-            P("narrow", "wide", None),
-            P("narrow", "wide", None),
-            P(("wide", "narrow")),
-            P(("wide", "narrow"), None),
-            P(("wide", "narrow"), None),
-            P(("wide", "narrow"), None),
-            P(("wide", "narrow"), None),
-            P(("wide", "narrow")),
-            P(("wide", "narrow"), None),
-            P(("wide", "narrow"), None),
-            P(("wide", "narrow"), None),
+            token_spec,
+            token_spec,
+            gain_spec,
+            weight_spec,
+            weight_spec,
+            weight_spec,
+            weight_spec,
+            gain_spec,
+            weight_spec,
+            weight_spec,
+            weight_spec,
         ),
         check_vma=False,
     )

time: 1270 us -> 765 us (0.60)
  waiting for transfers between devices: 892 us -> 318 us
  starting transfers between devices: 9.97 us -> 138 us
  blocking collectives: 144 us -> 53.6 us
  local copies, waits for them, and re-layouts: 49.9 us -> 74.1 us
  other arithmetic: 38.1 us -> 60.2 us
  matrix products: 111 us -> 97.2 us
    reduce_scatter x6 -> x0, waiting for transfers between devices: 326 us -> none  [the longest x4 288 us: collect(): lax.psum_scatter(values.astype(bf16), 'wide', scatter_dimension=0, tiled=...]
    ppermute x0 -> x85, waiting for transfers between devices: none -> 317 us  [shift(): lax.ppermute(values, axis, [(i, (i + step) % size) for i in range(size)])]
    all_gather x8 -> x4, waiting for transfers between devices: 296 us -> 0.04 us  [the longest x2 0.04 us: near_gather(): return lax.all_gather(values, ('x', 'y', 'c'), axis=dim)]
    unnamed x18 -> x4, waiting for transfers between devices: 259 us -> 0.73 us
    ppermute x0 -> x85, starting transfers between devices: none -> 138 us  [shift(): lax.ppermute(values, axis, [(i, (i + step) % size) for i in range(size)])]
    all_to_all x2 -> x0, blocking collectives: 88.6 us -> none  [share_columns(): got = lax.all_to_all(pack, 'wide', 0, 0, tiled=True)]
    convert_element_type x8 -> x33, other arithmetic: 16.2 us -> 32.3 us  [the longest x20 22 us: pair_sum(): return (mine + shift(other, axis, 1).astype(f32)).astype(bf16)]
    unnamed x52 -> x184, local copies, waits for them, and re-layouts: 12.1 us -> 27.5 us
  transfers between devices with their start and end apart: 18 -> 89, of which waited for: 15 -> 54; matrix products, arithmetic and copies ran while one was open for 10% -> 26% of each run, Pallas kernels for 0% -> 0%
where the time goes in v2:
time: 765 us; the launch traced here: 759 us
  waiting for transfers between devices  318 us (42%)
  starting transfers between devices  138 us (18%)
  matrix products  97.2 us (13%)
  local copies, waits for them, and re-layouts  74.1 us (10%)
  other arithmetic  60.2 us (8%)
  blocking collectives  53.6 us (7%)
  between operations  16.9 us (2%)
    ppermute x85, waiting for transfers between devices, shift(): lax.ppermute(values, axis, [(i, (i + step) % size) for i in range(size)])  317 us
    ppermute x85, starting transfers between devices, shift(): lax.ppermute(values, axis, [(i, (i + step) % size) for i in range(size)])  138 us
    all_gather x1, blocking collectives, line_body(): lax.all_gather(jnp.stack([attn_gain, mlp_gain]), ('z', 'x', 'y', 'c'), ax...  46.1 us
    unnamed x184, local copies, waits for them, and re-layouts  27.5 us
    dot_general x4, matrix products, against(): lax.dot_general(left, right, (((1,), (1,)), ((), ())), preferred_element_...  27 us
    convert_element_type x20, other arithmetic, pair_sum(): return (mine + shift(other, axis, 1).astype(f32)).astype(bf16)  22 us
    dot_general x4, matrix products, over_rows(): lax.dot_general(left, right, (((0,), (0,)), ((), ())), preferred_element_...  19.2 us
  transfers between devices with their start and end apart: 89, of which 54 were waited for; matrix products, arithmetic and copies ran while one was open for 26% of the time, Pallas kernels for 0%

profile of v2, /device:TPU:0, one launch (start us, length us, event | category | flops | bytes accessed | tf_op | source)
XLA Modules:
  0.0 758.7 jit_solution(5726749596293308789)
XLA Ops:
  10.0 5.1 collective-permute-start.8
  18.3 5.5 collective-permute-done.7
  30.1 6.6 collective-permute-done.24
  36.7 22.4 %collective-permute-done.23 = bf16[64,2816]{1,0:T(8,128)(2,1)S(1)} collective-permute-done((bf16[64,2816]{1,0:T(8,128)(2,1)S(1)}, bf16[64,2816]{1,0:T(8,128)(2,1)S(1)}, u32[]{:S(2)}, u32[]{:S(2)}) %collective-permute-start.23) | collective-permute-done | bytes 360480 | tf_op jit(solution)/shard_map/ppermute | solution.py:410
  72.7 46.1 %all-gather.2 = bf16[32,64,2]{1,2,0:T(2,128)(2,1)S(1)} all-gather(bf16[1,64,2]{1,2,0:T(2,128)(2,1)S(1)} %maximum_bitcast_fusion.2), channel_id=1, replica_groups=mesh['z'=4,'x'=2,'y'=2,'c'=2] {'z','x','y','c'}, dimensions={0}, use_global_device_ids=true | all-gather | bytes 8448 | tf_op jit(solution)/shard_map/all_gather | solution.py:466
  118.9 7.5 all-gather.3
  135.9 6.3 collective-permute-done.2
  147.7 5.7 collective-permute-done.33
  156.5 8.1 %collective-permute-done.3 = bf16[64,2048]{1,0:T(8,128)(2,1)S(1)} collective-permute-done((bf16[64,2048]{1,0:T(8,128)(2,1)S(1)}, bf16[64,2048]{1,0:T(8,128)(2,1)S(1)}, u32[]{:S(2)}, u32[]{:S(2)}) %collective-permute-start.3) | collective-permute-done | bytes 262176 | tf_op jit(solution)/shard_map/ppermute | solution.py:410
  166.0 4.9 collective-permute-done.34
  173.3 25.7 %collective-permute-start.16 = (bf16[256,2048]{1,0:T(8,128)(2,1)S(1)}, bf16[256,2048]{1,0:T(8,128)(2,1)}, u32[]{:S(2)}, u32[]{:S(2)}) collective-permute-start(bf16[256,2048]{1,0:T(8,128)(2,1)S(1)} %get-tuple-element.65), channel_id=1, source_target_pairs={{0,8},{8,16},{16,24},{24,0},{1,9},{9,17},{17,25},{25,1},{2,10},{10... | collective-permute-start | bytes 3145736 | tf_op jit(solution)/shard_map/ppermute | solution.py:410
  203.5 25.2 %collective-permute-done.17 = bf16[256,2048]{1,0:T(8,128)(2,1)} collective-permute-done((bf16[256,2048]{1,0:T(8,128)(2,1)S(1)}, bf16[256,2048]{1,0:T(8,128)(2,1)}, u32[]{:S(2)}, u32[]{:S(2)}) %collective-permute-start.17) | collective-permute-done | bytes 1048608 | tf_op jit(solution)/shard_map/ppermute | solution.py:410
  228.7 4.5 collective-permute-start.18
  240.6 5.1 collective-permute-done.9
  246.7 6.7 fusion.149
  253.4 4.6 fusion.13
  270.8 5.3 collective-permute-done.13
  279.8 4.2 collective-permute-start.11
  302.4 46.1 %collective-permute-done.12 = bf16[256,512]{1,0:T(8,128)(2,1)S(1)} collective-permute-done((bf16[256,512]{1,0:T(8,128)(2,1)}, bf16[256,512]{1,0:T(8,128)(2,1)S(1)}, u32[]{:S(2)}, u32[]{:S(2)}) %collective-permute-start.12) | collective-permute-done | bytes 262176 | tf_op jit(solution)/shard_map/ppermute | solution.py:410
  362.2 9.7 %multiply_reduce_fusion = (f32[512]{0:T(512)S(1)}, f32[512,2048]{1,0:T(8,128)}) fusion(bf16[2048,2048]{1,0:T(8,128)(2,1)} %constant_dynamic-update-slice_fusion.8, bf16[512,512]{0,1:T(8,128)(2,1)S(1)} %copy.221, bf16[512,512]{0,1:T(8,128)(2,1)S(1)} %copy.254, bf16[512,512]{0,1:T(8,128)(2,1)S(1)} %copy.220, bf16[512,512]{0,1:T(8,128)(2,1)S(1)} %bitcast.386, ...), kind=kOutput, calls=%fused_computation.31 | convolution fusion | flops 4308598272 | bytes 16779268 | tf_op jit(solution)/shard_map/dot_general | solution.py:516
  372.0 13.0 %fusion.135 = f32[512,2816]{1,0:T(8,128)} fusion(bf16[2048,2816]{1,0:T(8,128)(2,1)} %bitcast.437, f32[512,2048]{1,0:T(8,128)} %get-tuple-element.120, f32[2048]{0:T(1024)S(1)} %bitcast.428, f32[512]{0:T(512)S(1)} %add_rsqrt_fusion), kind=kOutput, calls=%fused_computation.405 | convolution fusion | flops 5908725760 | bytes 21506048 | tf_op jit(solution)/shard_map/dot_general | solution.py:526
  385.0 10.5 %multiply_convert_fusion.2 = (bf16[512,1408]{1,0:T(8,128)(2,1)S(1)}, bf16[512,1408]{1,0:T(8,128)(2,1)S(1)}, bf16[512,1408]{1,0:T(8,128)(2,1)}) fusion(f32[512,2816]{1,0:T(8,128)} %fusion.135, bf16[512,2048]{1,0:T(8,128)(2,1)} %constant_dynamic-update-slice_fusion.15, bf16[1408,2048]{1,0:T(8,128)(2,1)} %all-gather.11.cloned.1.call-done), kind=kOutput, calls=%fused_computation.51 | convolution fusion | flops 2963603456 | bytes 17956864 | tf_op jit(solution)/shard_map/dot_general | solution.py:50
  396.6 6.4 convolution_convert_fusion.5
  403.0 8.7 %convolution_convert_fusion = bf16[2048,2816]{1,0:T(8,128)(2,1)S(1)} fusion(bf16[512,1408]{1,0:T(8,128)(2,1)} %copy-done.78, bf16[512,1408]{1,0:T(8,128)(2,1)S(1)} %get-tuple-element.19, f32[512,2048]{1,0:T(8,128)S(1)} %copy-done.42, f32[2048]{0:T(1024)S(1)} %bitcast.429, f32[512]{0:T(512)S(1)} %add_rsqrt_fusion), kind=kOutput, calls=%fused_computation.8 | convolution fusion | flops 5920260096 | bytes 18622464 | tf_op jit(solution)/shard_map/dot_general | solution.py:44
  414.9 6.1 convolution_convert_fusion.1
  444.4 5.7 collective-permute-done.41
  455.6 5.8 collective-permute-done.29
  466.7 5.9 collective-permute-done.42
  477.8 5.7 collective-permute-done.30
  484.9 6.3 convolution_convert_fusion.7
  498.7 7.2 collective-permute-done.44
  513.9 4.8 fusion.4
  539.5 4.2 collective-permute-done.47
  555.6 5.2 collective-permute-done.51
  567.1 4.8 copy.307
  584.9 4.4 collective-permute-done.54
  603.4 4.7 collective-permute-done.59
  613.5 4.7 collective-permute-done.83
  620.7 6.8 collective-permute-done.81
  631.6 4.9 collective-permute-done.82
  644.4 6.0 fusion.1
  650.4 11.6 %collective-permute-done.64 = bf16[4,2,64,1024]{3,2,0,1:T(8,128)(2,1)} collective-permute-done((bf16[4,2,64,1024]{3,2,0,1:T(8,128)(2,1)}, bf16[4,2,64,1024]{3,2,0,1:T(8,128)(2,1)}, u32[]{:S(2)}, u32[]{:S(2)}) %collective-permute-start.64) | collective-permute-done | bytes 1048608 | tf_op jit(solution)/shard_map/ppermute | solution.py:410
  669.4 7.8 %collective-permute-done.65 = bf16[4,64,1024]{2,1,0:T(8,128)(2,1)S(1)} collective-permute-done((bf16[4,64,1024]{2,1,0:T(8,128)(2,1)S(1)}, bf16[4,64,1024]{2,1,0:T(8,128)(2,1)S(1)}, u32[]{:S(2)}, u32[]{:S(2)}) %collective-permute-start.65) | collective-permute-done | bytes 524320 | tf_op jit(solution)/shard_map/ppermute | solution.py:410
  695.4 13.6 %collective-permute-done.73 = bf16[4,2,64,1408]{3,2,0,1:T(8,128)(2,1)S(1)} collective-permute-done((bf16[4,2,64,1408]{3,2,0,1:T(8,128)(2,1)S(1)}, bf16[4,2,64,1408]{3,2,0,1:T(8,128)(2,1)S(1)}, u32[]{:S(2)}, u32[]{:S(2)}) %collective-permute-start.73) | collective-permute-done | bytes 1441824 | tf_op jit(solution)/shard_map/ppermute | solution.py:410
  709.5 4.9 collective-permute-done.75
  716.7 5.4 collective-permute-done.74
  729.5 6.0 collective-permute-done.79
  735.5 11.7 %collective-permute-done.78 = bf16[64,2816]{1,0:T(8,128)(2,1)S(1)} collective-permute-done((bf16[64,2816]{1,0:T(8,128)(2,1)S(1)}, bf16[64,2816]{1,0:T(8,128)(2,1)S(1)}, u32[]{:S(2)}, u32[]{:S(2)}) %collective-permute-start.78) | collective-permute-done | bytes 360480 | tf_op jit(solution)/shard_map/ppermute | solution.py:410
  (511 shorter events, 294.0 us)
Async XLA Ops:
  7.2 164.4 %all-gather.9.cloned.1.call-start = ((), (), s32[]{:S(2)}) async-start(), calls=%async_computation | async-start | bytes 2359296 | tf_op jit(solution)/shard_map/all_gather | solution.py:495
  7.9 225.5 %all-gather.13.cloned.1.call-start = ((), (), s32[]{:S(2)}) async-start(), calls=%async_computation.2 | async-start | bytes 3538944 | tf_op jit(solution)/shard_map/all_gather | solution.py:459
  25.4 346.6 %all-gather.15.cloned.1.call-start = ((), (), s32[]{:S(2)}) async-start(), calls=%async_computation.3 | async-start | bytes 12976128 | tf_op jit(solution)/shard_map/all_gather | solution.py:459
  27.7 31.3 %collective-permute-start.23 = (bf16[64,2816]{1,0:T(8,128)(2,1)S(1)}, bf16[64,2816]{1,0:T(8,128)(2,1)S(1)}, u32[]{:S(2)}, u32[]{:S(2)}) collective-permute-start(bf16[64,2816]{1,0:T(8,128)(2,1)S(1)} %get-tuple-element.76), channel_id=1, source_target_pairs={{0,16},{8,24},{16,0},{24,8},{1,17},{9,25},{17,1},{25,9},{2,18},{10... | collective-permute-start | bytes 1081352 | tf_op jit(solution)/shard_map/ppermute | solution.py:410
  28.1 30.9 %collective-permute-start.22 = (bf16[64,2816]{1,0:T(8,128)(2,1)S(1)}, bf16[64,2816]{1,0:T(8,128)(2,1)S(1)}, u32[]{:S(2)}, u32[]{:S(2)}) collective-permute-start(bf16[64,2816]{1,0:T(8,128)(2,1)S(1)} %get-tuple-element.75), channel_id=1, source_target_pairs={{0,8},{8,16},{16,24},{24,0},{1,9},{9,17},{17,25},{25,1},{2,10},{10... | collective-permute-start | bytes 1081352 | tf_op jit(solution)/shard_map/ppermute | solution.py:410
  61.2 323.8 %all-gather.11.cloned.1.call-start = ((), (), s32[]{:S(2)}) async-start(), calls=%async_computation.1 | async-start | bytes 6488064 | tf_op jit(solution)/shard_map/all_gather | solution.py:524
  62.0 70.1 %collective-permute-start = (bf16[64,2048]{1,0:T(8,128)(2,1)}, bf16[64,2048]{1,0:T(8,128)(2,1)}, u32[]{:S(2)}, u32[]{:S(2)}) collective-permute-start(bf16[64,2048]{1,0:T(8,128)(2,1)} %get-tuple-element.97), channel_id=1, source_target_pairs={{0,8},{8,16},{16,24},{24,0},{1,9},{9,17},{17,25},{25,1},{2,10},{10... | collective-permute-start | bytes 786440 | tf_op jit(solution)/shard_map/ppermute | solution.py:410
  62.0 66.2 %collective-permute-start.1 = (bf16[64,2048]{1,0:T(8,128)(2,1)S(1)}, bf16[64,2048]{1,0:T(8,128)(2,1)S(1)}, u32[]{:S(2)}, u32[]{:S(2)}) collective-permute-start(bf16[64,2048]{1,0:T(8,128)(2,1)S(1)} %get-tuple-element.96), channel_id=1, source_target_pairs={{0,24},{8,0},{16,8},{24,16},{1,25},{9,1},{17,9},{25,17},{2,26},{10... | collective-permute-start | bytes 786440 | tf_op jit(solution)/shard_map/ppermute | solution.py:410
  68.5 67.4 %collective-permute-start.31 = (bf16[64,2048]{1,0:T(8,128)(2,1)}, bf16[64,2048]{1,0:T(8,128)(2,1)}, u32[]{:S(2)}, u32[]{:S(2)}) collective-permute-start(bf16[64,2048]{1,0:T(8,128)(2,1)} %get-tuple-element.93), channel_id=1, source_target_pairs={{0,8},{8,16},{16,24},{24,0},{1,9},{9,17},{17,25},{25,1},{2,10},{10... | collective-permute-start | bytes 786440 | tf_op jit(solution)/shard_map/ppermute | solution.py:410
  68.5 63.6 %collective-permute-start.32 = (bf16[64,2048]{1,0:T(8,128)(2,1)}, bf16[64,2048]{1,0:T(8,128)(2,1)S(1)}, u32[]{:S(2)}, u32[]{:S(2)}) collective-permute-start(bf16[64,2048]{1,0:T(8,128)(2,1)} %get-tuple-element.92), channel_id=1, source_target_pairs={{0,24},{8,0},{16,8},{24,16},{1,25},{9,1},{17,9},{25,17},{2,26},{10... | collective-permute-start | bytes 786440 | tf_op jit(solution)/shard_map/ppermute | solution.py:410
  128.2 14.0 %collective-permute-start.2 = (bf16[64,2048]{1,0:T(8,128)(2,1)S(1)}, bf16[64,2048]{1,0:T(8,128)(2,1)S(1)}, u32[]{:S(2)}, u32[]{:S(2)}) collective-permute-start(bf16[64,2048]{1,0:T(8,128)(2,1)S(1)} %collective-permute-done.1), channel_id=1, source_target_pairs={{0,24},{8,0},{16,8},{24,16},{1,25},{9,1},{17,9},{25,17},{2,26},{10... | collective-permute-start | bytes 786440 | tf_op jit(solution)/shard_map/ppermute | solution.py:410
  132.1 21.3 %collective-permute-start.33 = (bf16[64,2048]{1,0:T(8,128)(2,1)S(1)}, bf16[64,2048]{1,0:T(8,128)(2,1)S(1)}, u32[]{:S(2)}, u32[]{:S(2)}) collective-permute-start(bf16[64,2048]{1,0:T(8,128)(2,1)S(1)} %collective-permute-done.32), channel_id=1, source_target_pairs={{0,24},{8,0},{16,8},{24,16},{1,25},{9,1},{17,9},{25,17},{2,26},{10... | collective-permute-start | bytes 786440 | tf_op jit(solution)/shard_map/ppermute | solution.py:410
  135.9 18.8 %collective-permute-start.35 = (bf16[64,2048]{1,0:T(8,128)(2,1)}, bf16[64,2048]{1,0:T(8,128)(2,1)}, u32[]{:S(2)}, u32[]{:S(2)}) collective-permute-start(bf16[64,2048]{1,0:T(8,128)(2,1)} %collective-permute-done.31), channel_id=1, source_target_pairs={{0,8},{8,16},{16,24},{24,0},{1,9},{9,17},{17,25},{25,1},{2,10},{10... | collective-permute-start | bytes 786440 | tf_op jit(solution)/shard_map/ppermute | solution.py:410
  142.2 22.4 %collective-permute-start.3 = (bf16[64,2048]{1,0:T(8,128)(2,1)S(1)}, bf16[64,2048]{1,0:T(8,128)(2,1)S(1)}, u32[]{:S(2)}, u32[]{:S(2)}) collective-permute-start(bf16[64,2048]{1,0:T(8,128)(2,1)S(1)} %collective-permute-done.2), channel_id=1, source_target_pairs={{0,24},{8,0},{16,8},{24,16},{1,25},{9,1},{17,9},{25,17},{2,26},{10... | collective-permute-start | bytes 786440 | tf_op jit(solution)/shard_map/ppermute | solution.py:410
  144.9 21.0 %collective-permute-start.5 = (bf16[64,2048]{1,0:T(8,128)(2,1)S(1)}, bf16[64,2048]{1,0:T(8,128)(2,1)S(1)}, u32[]{:S(2)}, u32[]{:S(2)}) collective-permute-start(bf16[64,2048]{1,0:T(8,128)(2,1)S(1)} %collective-permute-done.4), channel_id=1, source_target_pairs={{0,8},{8,16},{16,24},{24,0},{1,9},{9,17},{17,25},{25,1},{2,10},{10... | collective-permute-start | bytes 786440 | tf_op jit(solution)/shard_map/ppermute | solution.py:410
  153.4 17.5 %collective-permute-start.34 = (bf16[64,2048]{1,0:T(8,128)(2,1)S(1)}, bf16[64,2048]{1,0:T(8,128)(2,1)S(1)}, u32[]{:S(2)}, u32[]{:S(2)}) collective-permute-start(bf16[64,2048]{1,0:T(8,128)(2,1)S(1)} %collective-permute-done.33), channel_id=1, source_target_pairs={{0,24},{8,0},{16,8},{24,16},{1,25},{9,1},{17,9},{25,17},{2,26},{10... | collective-permute-start | bytes 786440 | tf_op jit(solution)/shard_map/ppermute | solution.py:410
  154.7 47.2 %collective-permute-start.36 = (bf16[64,2048]{1,0:T(8,128)(2,1)}, bf16[64,2048]{1,0:T(8,128)(2,1)}, u32[]{:S(2)}, u32[]{:S(2)}) collective-permute-start(bf16[64,2048]{1,0:T(8,128)(2,1)} %collective-permute-done.35), channel_id=1, source_target_pairs={{0,8},{8,16},{16,24},{24,0},{1,9},{9,17},{17,25},{25,1},{2,10},{10... | collective-permute-start | bytes 786440 | tf_op jit(solution)/shard_map/ppermute | solution.py:410
  173.3 59.9 %collective-permute-start.16 = (bf16[256,2048]{1,0:T(8,128)(2,1)S(1)}, bf16[256,2048]{1,0:T(8,128)(2,1)}, u32[]{:S(2)}, u32[]{:S(2)}) collective-permute-start(bf16[256,2048]{1,0:T(8,128)(2,1)S(1)} %get-tuple-element.65), channel_id=1, source_target_pairs={{0,8},{8,16},{16,24},{24,0},{1,9},{9,17},{17,25},{25,1},{2,10},{10... | collective-permute-start | bytes 3145736 | tf_op jit(solution)/shard_map/ppermute | solution.py:410
  199.0 29.7 %collective-permute-start.17 = (bf16[256,2048]{1,0:T(8,128)(2,1)S(1)}, bf16[256,2048]{1,0:T(8,128)(2,1)}, u32[]{:S(2)}, u32[]{:S(2)}) collective-permute-start(bf16[256,2048]{1,0:T(8,128)(2,1)S(1)} %get-tuple-element.64), channel_id=1, source_target_pairs={{0,24},{8,0},{16,8},{24,16},{1,25},{9,1},{17,9},{25,17},{2,26},{10... | collective-permute-start | bytes 3145736 | tf_op jit(solution)/shard_map/ppermute | solution.py:410
  228.7 65.1 %collective-permute-start.18 = (bf16[256,2048]{1,0:T(8,128)(2,1)}, bf16[256,2048]{1,0:T(8,128)(2,1)}, u32[]{:S(2)}, u32[]{:S(2)}) collective-permute-start(bf16[256,2048]{1,0:T(8,128)(2,1)} %collective-permute-done.17), channel_id=1, source_target_pairs={{0,24},{8,0},{16,8},{24,16},{1,25},{9,1},{17,9},{25,17},{2,26},{10... | collective-permute-start | bytes 3145736 | tf_op jit(solution)/shard_map/ppermute | solution.py:410
  233.2 63.7 %collective-permute-start.20 = (bf16[256,2048]{1,0:T(8,128)(2,1)}, bf16[256,2048]{1,0:T(8,128)(2,1)}, u32[]{:S(2)}, u32[]{:S(2)}) collective-permute-start(bf16[256,2048]{1,0:T(8,128)(2,1)} %collective-permute-done.16), channel_id=1, source_target_pairs={{0,8},{8,16},{16,24},{24,0},{1,9},{9,17},{17,25},{25,1},{2,10},{10... | collective-permute-start | bytes 3145736 | tf_op jit(solution)/shard_map/ppermute | solution.py:410
  264.7 15.0 %collective-permute-start.10 = (bf16[256,512]{1,0:T(8,128)(2,1)}, bf16[256,512]{1,0:T(8,128)(2,1)S(1)}, u32[]{:S(2)}, u32[]{:S(2)}) collective-permute-start(bf16[256,512]{1,0:T(8,128)(2,1)} %copy.217), channel_id=1, source_target_pairs={{0,24},{8,0},{16,8},{24,16},{1,25},{9,1},{17,9},{25,17},{2,26},{10... | collective-permute-start | bytes 786440 | tf_op jit(solution)/shard_map/ppermute | solution.py:410
  279.8 17.2 %collective-permute-start.11 = (bf16[256,512]{1,0:T(8,128)(2,1)S(1)}, bf16[256,512]{1,0:T(8,128)(2,1)S(1)}, u32[]{:S(2)}, u32[]{:S(2)}) collective-permute-start(bf16[256,512]{1,0:T(8,128)(2,1)S(1)} %collective-permute-done.10), channel_id=1, source_target_pairs={{0,24},{8,0},{16,8},{24,16},{1,25},{9,1},{17,9},{25,17},{2,26},{10... | collective-permute-start | bytes 786440 | tf_op jit(solution)/shard_map/ppermute | solution.py:410
  287.8 14.5 %collective-permute-start.15 = (bf16[256,512]{1,0:T(8,128)(2,1)}, bf16[256,512]{1,0:T(8,128)(2,1)S(1)}, u32[]{:S(2)}, u32[]{:S(2)}) collective-permute-start(bf16[256,512]{1,0:T(8,128)(2,1)} %collective-permute-done.14), channel_id=1, source_target_pairs={{0,8},{8,16},{16,24},{24,0},{1,9},{9,17},{17,25},{25,1},{2,10},{10... | collective-permute-start | bytes 786440 | tf_op jit(solution)/shard_map/ppermute | solution.py:410
  293.8 56.4 %collective-permute-start.19 = (bf16[256,2048]{1,0:T(8,128)(2,1)}, bf16[256,2048]{1,0:T(8,128)(2,1)}, u32[]{:S(2)}, u32[]{:S(2)}) collective-permute-start(bf16[256,2048]{1,0:T(8,128)(2,1)} %collective-permute-done.18), channel_id=1, source_target_pairs={{0,24},{8,0},{16,8},{24,16},{1,25},{9,1},{17,9},{25,17},{2,26},{10... | collective-permute-start | bytes 3145736 | tf_op jit(solution)/shard_map/ppermute | solution.py:410
  296.9 60.5 %collective-permute-start.21 = (bf16[256,2048]{1,0:T(8,128)(2,1)}, bf16[256,2048]{1,0:T(8,128)(2,1)}, u32[]{:S(2)}, u32[]{:S(2)}) collective-permute-start(bf16[256,2048]{1,0:T(8,128)(2,1)} %collective-permute-done.20), channel_id=1, source_target_pairs={{0,8},{8,16},{16,24},{24,0},{1,9},{9,17},{17,25},{25,1},{2,10},{10... | collective-permute-start | bytes 3145736 | tf_op jit(solution)/shard_map/ppermute | solution.py:410
  298.3 50.2 %collective-permute-start.12 = (bf16[256,512]{1,0:T(8,128)(2,1)}, bf16[256,512]{1,0:T(8,128)(2,1)S(1)}, u32[]{:S(2)}, u32[]{:S(2)}) collective-permute-start(bf16[256,512]{1,0:T(8,128)(2,1)} %copy-done.52), channel_id=1, source_target_pairs={{0,24},{8,0},{16,8},{24,16},{1,25},{9,1},{17,9},{25,17},{2,26},{10... | collective-permute-start | bytes 786440 | tf_op jit(solution)/shard_map/ppermute | solution.py:410
  412.6 19.5 %collective-permute-start.37 = (bf16[64,2048]{1,0:T(8,128)(2,1)}, bf16[64,2048]{1,0:T(8,128)(2,1)S(1)}, u32[]{:S(2)}, u32[]{:S(2)}) collective-permute-start(bf16[64,2048]{1,0:T(8,128)(2,1)} %get-tuple-element.54), channel_id=1, source_target_pairs={{0,24},{8,0},{16,8},{24,16},{1,25},{9,1},{17,9},{25,17},{2,26},{10... | collective-permute-start | bytes 786440 | tf_op jit(solution)/shard_map/ppermute | solution.py:410
  414.9 17.2 %collective-permute-start.40 = (bf16[64,2048]{1,0:T(8,128)(2,1)S(1)}, bf16[64,2048]{1,0:T(8,128)(2,1)}, u32[]{:S(2)}, u32[]{:S(2)}) collective-permute-start(bf16[64,2048]{1,0:T(8,128)(2,1)S(1)} %get-tuple-element.55), channel_id=1, source_target_pairs={{0,8},{8,16},{16,24},{24,0},{1,9},{9,17},{17,25},{25,1},{2,10},{10... | collective-permute-start | bytes 786440 | tf_op jit(solution)/shard_map/ppermute | solution.py:410
  432.1 212.3 %collective-permute-start.72 = (bf16[4,2,2,64,2816]{4,3,2,1,0:T(8,128)(2,1)}, bf16[4,2,2,64,2816]{4,3,2,1,0:T(8,128)(2,1)}, u32[]{:S(2)}, u32[]{:S(2)}) collective-permute-start(bf16[4,2,2,64,2816]{4,3,2,1,0:T(8,128)(2,1)} %dynamic-slice_bitcast_fusion), channel_id=1, source_target_pairs={{0,1},{1,0},{2,3},{3,2},{4,5},{5,4},{6,7},{7,6},{8,9},{9,8},{10,11... | collective-permute-start | bytes 17301512 | tf_op jit(solution)/shard_map/ppermute | solution.py:410
  439.6 15.9 %collective-permute-start.26 = (bf16[64,2048]{1,0:T(8,128)(2,1)S(1)}, bf16[64,2048]{1,0:T(8,128)(2,1)S(1)}, u32[]{:S(2)}, u32[]{:S(2)}) collective-permute-start(bf16[64,2048]{1,0:T(8,128)(2,1)S(1)} %get-tuple-element.60), channel_id=1, source_target_pairs={{0,24},{8,0},{16,8},{24,16},{1,25},{9,1},{17,9},{25,17},{2,26},{10... | collective-permute-start | bytes 786440 | tf_op jit(solution)/shard_map/ppermute | solution.py:410
  442.3 19.1 %collective-permute-start.29 = (bf16[64,2048]{1,0:T(8,128)(2,1)S(1)}, bf16[64,2048]{1,0:T(8,128)(2,1)S(1)}, u32[]{:S(2)}, u32[]{:S(2)}) collective-permute-start(bf16[64,2048]{1,0:T(8,128)(2,1)S(1)} %get-tuple-element.61), channel_id=1, source_target_pairs={{0,8},{8,16},{16,24},{24,0},{1,9},{9,17},{17,25},{25,1},{2,10},{10... | collective-permute-start | bytes 786440 | tf_op jit(solution)/shard_map/ppermute | solution.py:410
  450.2 16.5 %collective-permute-start.39 = (bf16[64,2048]{1,0:T(8,128)(2,1)S(1)}, bf16[64,2048]{1,0:T(8,128)(2,1)S(1)}, u32[]{:S(2)}, u32[]{:S(2)}) collective-permute-start(bf16[64,2048]{1,0:T(8,128)(2,1)S(1)} %get-tuple-element.50), channel_id=1, source_target_pairs={{0,24},{8,0},{16,8},{24,16},{1,25},{9,1},{17,9},{25,17},{2,26},{10... | collective-permute-start | bytes 786440 | tf_op jit(solution)/shard_map/ppermute | solution.py:410
  452.2 20.4 %collective-permute-start.42 = (bf16[64,2048]{1,0:T(8,128)(2,1)S(1)}, bf16[64,2048]{1,0:T(8,128)(2,1)S(1)}, u32[]{:S(2)}, u32[]{:S(2)}) collective-permute-start(bf16[64,2048]{1,0:T(8,128)(2,1)S(1)} %get-tuple-element.51), channel_id=1, source_target_pairs={{0,8},{8,16},{16,24},{24,0},{1,9},{9,17},{17,25},{25,1},{2,10},{10... | collective-permute-start | bytes 786440 | tf_op jit(solution)/shard_map/ppermute | solution.py:410
  461.5 16.4 %collective-permute-start.27 = (bf16[64,2048]{1,0:T(8,128)(2,1)S(1)}, bf16[64,2048]{1,0:T(8,128)(2,1)S(1)}, u32[]{:S(2)}, u32[]{:S(2)}) collective-permute-start(bf16[64,2048]{1,0:T(8,128)(2,1)S(1)} %get-tuple-element.58), channel_id=1, source_target_pairs={{0,24},{8,0},{16,8},{24,16},{1,25},{9,1},{17,9},{25,17},{2,26},{10... | collective-permute-start | bytes 786440 | tf_op jit(solution)/shard_map/ppermute | solution.py:410
  463.5 20.0 %collective-permute-start.30 = (bf16[64,2048]{1,0:T(8,128)(2,1)S(1)}, bf16[64,2048]{1,0:T(8,128)(2,1)S(1)}, u32[]{:S(2)}, u32[]{:S(2)}) collective-permute-start(bf16[64,2048]{1,0:T(8,128)(2,1)S(1)} %get-tuple-element.59), channel_id=1, source_target_pairs={{0,8},{8,16},{16,24},{24,0},{1,9},{9,17},{17,25},{25,1},{2,10},{10... | collective-permute-start | bytes 786440 | tf_op jit(solution)/shard_map/ppermute | solution.py:410
  498.7 81.9 %collective-permute-start.80 = (bf16[2,2,176,2048]{3,2,0,1:T(8,128)(2,1)}, bf16[2,2,176,2048]{3,2,0,1:T(8,128)(2,1)}, u32[]{:S(2)}, u32[]{:S(2)}) collective-permute-start(bf16[2,2,176,2048]{3,2,0,1:T(8,128)(2,1)} %bitcast.373), channel_id=1, source_target_pairs={{0,1},{1,0},{2,3},{3,2},{4,5},{5,4},{6,7},{7,6},{8,9},{9,8},{10,11... | collective-permute-start | bytes 8650760 | tf_op jit(solution)/shard_map/ppermute | solution.py:410
  551.7 24.4 %collective-permute-start.53 = (bf16[4,2,2,64,768]{4,3,2,1,0:T(8,128)(2,1)S(1)}, bf16[4,2,2,64,768]{4,3,2,1,0:T(8,128)(2,1)S(1)}, u32[]{:S(2)}, u32[]{:S(2)}) collective-permute-start(bf16[4,2,2,64,768]{4,3,2,1,0:T(8,128)(2,1)S(1)} %dynamic-slice_bitcast_fusion.1), channel_id=1, source_target_pairs={{0,1},{1,0},{2,3},{3,2},{4,5},{5,4},{6,7},{7,6},{8,9},{9,8},{10,11... | collective-permute-start | bytes 4718600 | tf_op jit(solution)/shard_map/ppermute | solution.py:410
  573.5 63.1 %collective-permute-start.61 = (bf16[4,2,2,64,2048]{4,3,0,1,2:T(8,128)(2,1)}, bf16[4,2,2,64,2048]{4,3,0,1,2:T(8,128)(2,1)}, u32[]{:S(2)}, u32[]{:S(2)}) collective-permute-start(bf16[4,2,2,64,2048]{4,3,0,1,2:T(8,128)(2,1)} %bitcast.372), channel_id=1, source_target_pairs={{0,1},{1,0},{2,3},{3,2},{4,5},{5,4},{6,7},{7,6},{8,9},{9,8},{10,11... | collective-permute-start | bytes 12582920 | tf_op jit(solution)/shard_map/ppermute | solution.py:410
  602.8 15.4 %collective-permute-start.83 = (bf16[2,176,1024]{2,1,0:T(8,128)(2,1)}, bf16[2,176,1024]{2,1,0:T(8,128)(2,1)}, u32[]{:S(2)}, u32[]{:S(2)}) collective-permute-start(bf16[2,176,1024]{2,1,0:T(8,128)(2,1)} %dynamic-slice_bitcast_fusion.5), channel_id=1, source_target_pairs={{0,2},{2,0},{1,3},{3,1},{4,6},{6,4},{5,7},{7,5},{8,10},{10,8},{9,1... | collective-permute-start | bytes 2162696 | tf_op jit(solution)/shard_map/ppermute | solution.py:410
  608.2 19.4 %collective-permute-start.81 = (bf16[2,176,1024]{2,1,0:T(8,128)(2,1)}, bf16[2,176,1024]{2,1,0:T(8,128)(2,1)}, u32[]{:S(2)}, u32[]{:S(2)}) collective-permute-start(bf16[2,176,1024]{2,1,0:T(8,128)(2,1)} %dynamic-slice_bitcast_fusion.6), channel_id=1, source_target_pairs={{0,4},{4,0},{1,5},{5,1},{2,6},{6,2},{3,7},{7,3},{8,12},{12,8},{9,1... | collective-permute-start | bytes 2162696 | tf_op jit(solution)/shard_map/ppermute | solution.py:410
  642.4 19.7 %collective-permute-start.64 = (bf16[4,2,64,1024]{3,2,0,1:T(8,128)(2,1)}, bf16[4,2,64,1024]{3,2,0,1:T(8,128)(2,1)}, u32[]{:S(2)}, u32[]{:S(2)}) collective-permute-start(bf16[4,2,64,1024]{3,2,0,1:T(8,128)(2,1)} %dynamic-slice_bitcast_fusion.3), channel_id=1, source_target_pairs={{0,2},{2,0},{1,3},{3,1},{4,6},{6,4},{5,7},{7,5},{8,10},{10,8},{9,1... | collective-permute-start | bytes 3145736 | tf_op jit(solution)/shard_map/ppermute | solution.py:410
  642.9 21.3 %collective-permute-start.62 = (bf16[4,2,64,1024]{3,2,0,1:T(8,128)(2,1)S(1)}, bf16[4,2,64,1024]{3,2,0,1:T(8,128)(2,1)}, u32[]{:S(2)}, u32[]{:S(2)}) collective-permute-start(bf16[4,2,64,1024]{3,2,0,1:T(8,128)(2,1)S(1)} %dynamic-slice_bitcast_fusion.4), channel_id=1, source_target_pairs={{0,4},{4,0},{1,5},{5,1},{2,6},{6,2},{3,7},{7,3},{8,12},{12,8},{9,1... | collective-permute-start | bytes 3145736 | tf_op jit(solution)/shard_map/ppermute | solution.py:410
  678.2 30.8 %collective-permute-start.73 = (bf16[4,2,64,1408]{3,2,0,1:T(8,128)(2,1)S(1)}, bf16[4,2,64,1408]{3,2,0,1:T(8,128)(2,1)S(1)}, u32[]{:S(2)}, u32[]{:S(2)}) collective-permute-start(bf16[4,2,64,1408]{3,2,0,1:T(8,128)(2,1)S(1)} %bitcast.401), channel_id=1, source_target_pairs={{0,4},{4,0},{1,5},{5,1},{2,6},{6,2},{3,7},{7,3},{8,12},{12,8},{9,1... | collective-permute-start | bytes 4325384 | tf_op jit(solution)/shard_map/ppermute | solution.py:410
  685.6 28.8 %collective-permute-start.75 = (bf16[4,2,64,1408]{3,2,1,0:T(8,128)(2,1)S(1)}, bf16[4,2,64,1408]{3,2,1,0:T(8,128)(2,1)S(1)}, u32[]{:S(2)}, u32[]{:S(2)}) collective-permute-start(bf16[4,2,64,1408]{3,2,1,0:T(8,128)(2,1)S(1)} %dynamic-slice_bitcast_fusion.2), channel_id=1, source_target_pairs={{0,2},{2,0},{1,3},{3,1},{4,6},{6,4},{5,7},{7,5},{8,10},{10,8},{9,1... | collective-permute-start | bytes 4325384 | tf_op jit(solution)/shard_map/ppermute | solution.py:410
  695.3 21.3 %collective-permute-start.70 = (bf16[32,2048]{1,0:T(8,128)(2,1)S(1)}, bf16[32,2048]{1,0:T(8,128)(2,1)S(1)}, u32[]{:S(2)}, u32[]{:S(2)}) collective-permute-start(bf16[32,2048]{1,0:T(8,128)(2,1)S(1)} %get-tuple-element.79), channel_id=1, source_target_pairs={{0,8},{8,16},{16,24},{24,0},{1,9},{9,17},{17,25},{25,1},{2,10},{10... | collective-permute-start | bytes 393224 | tf_op jit(solution)/shard_map/ppermute | solution.py:410
  726.6 20.6 %collective-permute-start.78 = (bf16[64,2816]{1,0:T(8,128)(2,1)S(1)}, bf16[64,2816]{1,0:T(8,128)(2,1)S(1)}, u32[]{:S(2)}, u32[]{:S(2)}) collective-permute-start(bf16[64,2816]{1,0:T(8,128)(2,1)S(1)} %get-tuple-element.72), channel_id=1, source_target_pairs={{0,16},{8,24},{16,0},{24,8},{1,17},{9,25},{17,1},{25,9},{2,18},{10... | collective-permute-start | bytes 1081352 | tf_op jit(solution)/shard_map/ppermute | solution.py:410
  726.7 20.5 %collective-permute-start.77 = (bf16[64,2816]{1,0:T(8,128)(2,1)S(1)}, bf16[64,2816]{1,0:T(8,128)(2,1)S(1)}, u32[]{:S(2)}, u32[]{:S(2)}) collective-permute-start(bf16[64,2816]{1,0:T(8,128)(2,1)S(1)} %get-tuple-element.71), channel_id=1, source_target_pairs={{0,8},{8,16},{16,24},{24,0},{1,9},{9,17},{17,25},{25,1},{2,10},{10... | collective-permute-start | bytes 1081352 | tf_op jit(solution)/shard_map/ppermute | solution.py:410
  (122 other events, 1678.3 us)
Sparse Core Ops, SparseCore 0:
  9.9 30.5 all-gather.8
  43.0 32.3 all-gather.12
  77.8 67.7 all-gather.14
  147.4 43.2 all-gather.10

commit v3 on v2

--- a/solution.py
+++ b/solution.py
@@ -1,8 +1,11 @@
+import functools
 import math
 
 import jax
 import jax.numpy as jnp
 from jax import lax
+from jax.experimental import pallas as pl
+from jax.experimental.pallas import tpu as pltpu
 from jax.sharding import Mesh
 from jax.sharding import PartitionSpec as P
 
@@ -54,6 +57,279 @@
 
 def unchanged(carried):
     return carried
+
+
+MESH = pl.DeviceIdType.MESH
+AXES = ("z", "x", "y", "c")
+
+
+class Links:
+    def __init__(self, send_sems, recv_sems, line):
+        self.send_sems, self.recv_sems, self.line = send_sems, recv_sems, line
+        self.z, self.x, self.y, self.c = (lax.axis_index(name) for name in AXES)
+        self.slot = self.x * 4 + self.y * 2 + self.c
+        self.used = 0
+        self.sent = []
+
+    def device(self, to):
+        if to == "x":
+            return (self.z, 1 - self.x, self.y, self.c)
+        if to == "y":
+            return (self.z, self.x, 1 - self.y, self.c)
+        if to == "c":
+            return (self.z, self.x, self.y, 1 - self.c)
+        return (self.along(to), self.x, self.y, self.c)
+
+    def along(self, step):
+        return lax.rem(self.z + step + self.line, self.line)
+
+    def other(self, to):
+        slot = self.slot
+        for name in to:
+            bit = {"x": 4, "y": 2, "c": 1}[name]
+            here = {"x": self.x, "y": self.y, "c": self.c}[name]
+            slot = slot + bit * (1 - 2 * here)
+        return slot
+
+    def meet(self, targets):
+        barrier = pltpu.get_barrier_semaphore()
+        for to in targets:
+            pl.semaphore_signal(barrier, inc=1, device_id=self.device(to), device_id_type=MESH)
+        pl.semaphore_wait(barrier, len(targets))
+
+    def send(self, source, target, to):
+        copy = pltpu.make_async_remote_copy(
+            src_ref=source,
+            dst_ref=target,
+            send_sem=self.send_sems.at[self.used],
+            recv_sem=self.recv_sems.at[self.used],
+            device_id=self.device(to),
+            device_id_type=MESH,
+        )
+        copy.start()
+        self.used += 1
+        self.sent.append(copy)
+        return copy
+
+    def keep(self, source, target):
+        copy = pltpu.make_async_copy(source, target, self.send_sems.at[self.used])
+        copy.start()
+        self.used += 1
+        return copy
+
+    def finish(self):
+        for copy in self.sent:
+            copy.wait_send()
+
+
+class NearGather:
+    def __init__(self, links, slot):
+        self.links, self.slot = links, slot
+        self.got = {}
+
+    def offer(self, block, source):
+        target = self.slot(block, self.links.slot)
+        for to in ("x", "y", "c"):
+            self.got[block, to] = self.links.send(source, target, to)
+
+    def relay(self, block, first):
+        links = self.links
+        for to, then in (("x", "y"), ("y", "x")):
+            self.got[block, to].wait_recv()
+            place = self.slot(block, links.other(to))
+            self.got[block, to + "c"] = links.send(place, place, "c")
+            if to == first:
+                self.got[block, "xy"] = links.send(place, place, then)
+
+    def close(self, block):
+        self.got[block, "xy"].wait_recv()
+        place = self.slot(block, self.links.other("xy"))
+        self.got[block, "xyc"] = self.links.send(place, place, "c")
+
+    def wait(self, blocks):
+        for block in blocks:
+            for to in ("c", "xc", "yc", "xyc"):
+                self.got[block, to].wait_recv()
+
+
+class RingGather:
+    def __init__(self, links, source, place, pieces=4):
+        self.links, self.source, self.place, self.pieces = links, source, place, pieces
+        self.rows = source.shape[0] // pieces
+        self.last = [None] * pieces
+
+    def step(self, number):
+        for piece in range(self.pieces):
+            way = 1 if piece < self.pieces // 2 else -1
+            rows = pl.ds(piece * self.rows, self.rows)
+            place = self.place(self.links.along(-way * number), rows)
+            if number > 0:
+                self.last[piece].wait_recv()
+            if number < self.links.line - 1:
+                origin = self.source.at[rows] if number == 0 else place
+                self.last[piece] = self.links.send(origin, place, way)
+
+
+def first_kernel(line, x_ref, pos_ref, pack_ref, xs_ref, poss_ref, qkv_ref, send_sems, recv_sems):
+    links = Links(send_sems, recv_sems, line)
+    far = [1, line - 1] + list(range(2, line - 1))
+    links.meet(["x", "y", "c"] + far)
+    qkv = NearGather(links, lambda block, place: qkv_ref.at[links.along(-block), place])
+    ring = RingGather(links, x_ref, lambda block, rows: xs_ref.at[block, rows])
+    here = links.slot
+    local = [
+        links.keep(x_ref, xs_ref.at[links.z]),
+        links.keep(pos_ref, poss_ref.at[links.z]),
+        links.keep(pack_ref.at[links.z], qkv_ref.at[links.z, here]),
+    ]
+    turned = {k: links.send(pack_ref.at[links.along(k)], qkv_ref.at[links.z, here], k) for k in far}
+    placed = [links.send(pos_ref, poss_ref.at[links.z], k) for k in far]
+    ring.step(0)
+    qkv.offer(0, pack_ref.at[links.z])
+    for k in far:
+        turned[k].wait_recv()
+        qkv.offer(k, qkv_ref.at[links.along(-k), here])
+    ring.step(1)
+    for k in [0] + far:
+        qkv.relay(k, "x" if k < line // 2 else "y")
+    ring.step(2)
+    for k in [0] + far:
+        qkv.close(k)
+    ring.step(3)
+    qkv.wait(range(line))
+    for copy in placed:
+        copy.wait_recv()
+    links.finish()
+    for copy in local:
+        copy.wait()
+
+
+def ring_kernel(line, x_ref, xs_ref, send_sems, recv_sems):
+    links = Links(send_sems, recv_sems, line)
+    columns = x_ref.shape[1]
+    links.meet([1, line - 1])
+
+    def place(block, rows):
+        return xs_ref.at[rows, pl.ds(pl.multiple_of(block * columns, columns), columns)]
+
+    ring = RingGather(links, x_ref, place)
+    local = links.keep(x_ref, place(links.z, pl.ds(0, x_ref.shape[0])))
+    for number in range(line):
+        ring.step(number)
+    links.finish()
+    local.wait()
+
+
+def sum_kernel(line, pieces, parts_ref, total_ref, got, made, send_sems, recv_sems):
+    links = Links(send_sems, recv_sems, line)
+    links.meet([1, line - 1])
+    rows = parts_ref.shape[1] // pieces
+    last = [None] * pieces
+    for number in range(line):
+        for piece in range(pieces):
+            way = 1 if piece < pieces // 2 else -1
+            block = links.along(-way * (number + 1))
+            where = pl.ds(piece * rows, rows)
+            if number == 0:
+                source = parts_ref.at[block, where]
+            else:
+                last[piece].wait_recv()
+                total = got[number - 1, where].astype(jnp.float32) + parts_ref[
+                    block, where
+                ].astype(jnp.float32)
+                if number == line - 1:
+                    total_ref[where] = total
+                    continue
+                made[number - 1, where] = total.astype(made.dtype)
+                source = made.at[number - 1, where]
+            last[piece] = links.send(source, got.at[number, where], way)
+    links.finish()
+
+
+def turn_kernel(line, rows_ref, columns_ref, send_sems, recv_sems):
+    links = Links(send_sems, recv_sems, line)
+    far = [1, line - 1] + list(range(2, line - 1))
+    links.meet(far)
+    columns = columns_ref.shape[2]
+
+    def part(block):
+        return rows_ref.at[:, pl.ds(pl.multiple_of(block * columns, columns), columns)]
+
+    local = links.keep(part(links.z), columns_ref.at[links.z])
+    for k in far:
+        links.send(part(links.along(k)), columns_ref.at[links.z], k)
+    for copy in links.sent:
+        copy.wait_recv()
+    links.finish()
+    local.wait()
+
+
+def link_call(kernel, collective_id, copies, shapes, arguments, spaces=None, scratch=()):
+    any_space = pl.BlockSpec(memory_space=pl.ANY)
+    vmem = pl.BlockSpec(memory_space=pltpu.VMEM)
+    spec = vmem if spaces == "vmem" else any_space
+    many = isinstance(shapes, tuple)
+    return pl.pallas_call(
+        kernel,
+        out_shape=shapes,
+        in_specs=[spec] * len(arguments),
+        out_specs=(spec,) * len(shapes) if many else spec,
+        scratch_shapes=list(scratch)
+        + [pltpu.SemaphoreType.DMA((copies,)), pltpu.SemaphoreType.DMA((copies,))],
+        compiler_params=pltpu.CompilerParams(
+            collective_id=collective_id, has_side_effects=True, vmem_limit_bytes=32 * 2**20
+        ),
+    )(*arguments)
+
+
+def first_gather(tokens, positions, pack, line):
+    return link_call(
+        functools.partial(first_kernel, line),
+        0,
+        64,
+        (
+            jax.ShapeDtypeStruct((line,) + tokens.shape, tokens.dtype),
+            jax.ShapeDtypeStruct((line,) + positions.shape, positions.dtype),
+            jax.ShapeDtypeStruct((line, 8) + pack.shape[1:], pack.dtype),
+        ),
+        (tokens, positions, pack),
+    )
+
+
+def gather_columns(values, line):
+    return link_call(
+        functools.partial(ring_kernel, line),
+        1,
+        4 * line,
+        jax.ShapeDtypeStruct((values.shape[0], line * values.shape[1]), values.dtype),
+        (values,),
+    )
+
+
+def sum_blocks(parts, line):
+    shape = parts.shape[1:]
+    return link_call(
+        functools.partial(sum_kernel, line, 4),
+        2,
+        4 * line,
+        jax.ShapeDtypeStruct(shape, jnp.float32),
+        (parts,),
+        "vmem",
+        [
+            pltpu.VMEM((line - 1,) + shape, parts.dtype),
+            pltpu.VMEM((line - 2,) + shape, parts.dtype),
+        ],
+    )
+
+
+def turn_rows(values, line):
+    return link_call(
+        functools.partial(turn_kernel, line),
+        3,
+        line,
+        jax.ShapeDtypeStruct((line, values.shape[0], values.shape[1] // line), values.dtype),
+        (values,),
+    )
 
 
 def general_body(
@@ -409,77 +685,84 @@
         size = lax.axis_size(axis)
         return lax.ppermute(values, axis, [(i, (i + step) % size) for i in range(size)])
 
-    def halves(values):
+    def after(values, first):
+        return lax.optimization_barrier((values, first))[0]
+
+    def pick(values, index, dim):
+        return lax.dynamic_index_in_dim(values, index, dim, keepdims=False)
+
+    def back_order(blocks):
+        return jnp.take(blocks, (place - jnp.arange(line, dtype=jnp.int32)) % line, axis=0)
+
+    def ring_gather(values):
         cut = values.shape[0] // 2
-        return [values[:cut], values[cut:]]
-
-    def ring_pieces(values):
-        parts = [[part] for part in halves(values)]
+        up, down = [values[:cut]], [values[cut:]]
         for _ in range(line - 1):
-            for index, part in enumerate(parts):
-                part.append(shift(part[-1], "z", 1 - 2 * index))
-        return [[parts[0][k], parts[1][(line - k) % line]] for k in range(line)]
-
-    def ring_gather(values):
-        return jnp.concatenate(sum(ring_pieces(values), []), axis=0)
-
-    def ring_blocks(values):
-        return [jnp.concatenate(pieces, axis=0) for pieces in ring_pieces(values)]
+            up.append(shift(up[-1], "z", 1))
+            down.append(shift(down[-1], "z", -1))
+        pairs = [jnp.concatenate([up[k], down[(line - k) % line]], axis=0) for k in range(line)]
+        return back_order(jnp.stack(pairs))
 
     def ring_sum(blocks):
+        cut = blocks.shape[1] // 2
         totals = []
-        for index in range(2):
-            step = 2 * index - 1
+        for step in (1, -1):
             total = None
             for hop in range(line):
-                k = (line - 1 - hop) % line if index == 0 else (hop + 1) % line
-                own = halves(blocks[k])[index]
-                total = own if total is None else (shift(total, "z", step).astype(f32) + own.astype(f32))
+                own = pick(blocks, (place - step * (hop + 1)) % line, 0)
+                own = own[:cut] if step == 1 else own[cut:]
+                total = own if total is None else shift(total, "z", step).astype(f32) + own.astype(f32)
                 if hop < line - 1:
                     total = total.astype(bf16)
             totals.append(total)
         return jnp.concatenate(totals, axis=0)
 
-    def pick(values, index, dim):
-        return lax.dynamic_index_in_dim(values, index, dim, keepdims=False)
-
     def by_columns(weight, columns):
         return weight.reshape(rows_each, line, columns).transpose(1, 0, 2)
-
-    def natural(blocks):
-        return jnp.take(blocks, (place - jnp.arange(line, dtype=jnp.int32)) % line, axis=0)
 
     def turn(pack):
         got = [pick(pack, place, 0)]
         for k in range(1, line):
             got.append(shift(pick(pack, (place + k) % line, 0), "z", k))
-        return jnp.stack(got)
-
-    def near_gather(values, dim):
-        return lax.all_gather(values, ("x", "y", "c"), axis=dim)
-
+        return back_order(jnp.stack(got))
+
+    gains = jnp.stack([attn_gain, mlp_gain] + [jnp.zeros_like(attn_gain)] * (HD - 2), axis=1)
     pack_attn = jnp.concatenate(
-        [by_columns(w_query, q_cols), by_columns(w_key, HD), by_columns(w_value, HD)], axis=2
-    )
+        [
+            by_columns(w_query, q_cols),
+            by_columns(w_key, HD),
+            by_columns(w_value, HD),
+            jnp.broadcast_to(gains[None], (line,) + gains.shape),
+        ],
+        axis=2,
+    )
+    place_rows = jnp.broadcast_to(positions[0].astype(f32)[None, :], (8, span_len))
+    x_blocks, place_blocks, near_w = first_gather(tokens[0], place_rows, pack_attn, line)
+    inputs = x_blocks.reshape(group_len, model_width).astype(f32)
+    token_pos = place_blocks[:, 0].reshape(group_len)
+    near_w = near_w.reshape(model_width, -1)
+    qkv_w = near_w[:, : q_cols + 2 * HD]
+    gain_rows = near_w[:, q_cols + 2 * HD : q_cols + 2 * HD + 2].astype(f32).T
+    gain_one, gain_two = gain_rows[:1], gain_rows[1:]
+
+    out_w = lax.all_gather(w_out, ("z", "x", "y", "c"), axis=0, tiled=True)
+    down_w = lax.all_gather(w_down, ("x", "y", "c"), axis=0, tiled=True)
     pack_ff = jnp.concatenate([by_columns(w_gate, ff_cols), by_columns(w_up, ff_cols)], axis=2)
-    qkv_w = near_gather(natural(turn(pack_attn)), 1).reshape(model_width, q_cols + 2 * HD)
-    gains = lax.all_gather(jnp.stack([attn_gain, mlp_gain]), ("z", "x", "y", "c"), axis=1, tiled=True)
-    gain_one = gains[0].astype(f32)
-    gain_two = gains[1].astype(f32)
-    inputs = ring_gather(tokens[0]).astype(f32)
-    relative = (place - jnp.arange(line, dtype=jnp.int32)) % line
-    inside = jnp.arange(span_len, dtype=jnp.int32)
-
-    def token_index(which):
-        return ((relative[:, None] * 2 + which) * span_len + inside[None, :]).reshape(group_len)
-
-    token_pos = lax.all_gather(positions[0], "z", axis=0)
-    token_pos = natural(token_pos).reshape(group_len)
+    turned_ff = turn(after(pack_ff, x_blocks))
+    ff_w = lax.all_gather(turned_ff, ("x", "y", "c"), axis=1).reshape(model_width, 2 * ff_cols)
+
     own_x = tokens[0].astype(f32)
     keep = keep_mask[0].astype(f32)
     group_match = group_ids[0][:, None] == jnp.arange(exit_scale.shape[0], dtype=jnp.int32)[None, :]
     token_scale = jnp.sum(jnp.where(group_match, exit_scale[None, :], 0.0), axis=1, keepdims=True)
     upstream = out_grad[0].astype(f32) * token_scale
+    mixed_grad = ring_gather((keep * upstream).astype(bf16)).reshape(group_len, model_width)
+
+    inside = jnp.arange(span_len, dtype=jnp.int32)
+    block_first = jnp.arange(line, dtype=jnp.int32) * (2 * span_len)
+
+    def token_index(which):
+        return (block_first[:, None] + which * span_len + inside[None, :]).reshape(group_len)
 
     inverse_all = lax.rsqrt(jnp.mean(inputs * inputs, axis=-1, keepdims=True) + epsilon)
     first_norm = (inputs * inverse_all * gain_one).astype(bf16)
@@ -492,8 +775,6 @@
         ],
         axis=1,
     ).astype(bf16)
-    out_w = lax.all_gather(w_out, ("x", "y", "c"), axis=0, tiled=True)
-    out_w = ring_gather(out_w)
     both_kv = jnp.concatenate([own_kv, shift(own_kv, "x", 1)], axis=0)
     keys = both_kv[:, :HD]
     values = both_kv[:, HD:]
@@ -508,21 +789,17 @@
     attended = jnp.einsum("gtj,jd->tgd", rounded_probs, values, preferred_element_type=f32)
     own_attended = attended.reshape(group_len, q_cols).astype(bf16)
 
-    def turned(block, k):
-        return jnp.roll(block.reshape(line, span_len, q_cols), k, axis=0).reshape(group_len, q_cols)
-
-    gathered = ring_blocks(own_attended)
-    attended_rows = jnp.concatenate([turned(block, k) for k, block in enumerate(gathered)], axis=1)
+    def own_rows(values):
+        return lax.dynamic_slice_in_dim(values, place * span_len, span_len, 0)
+
+    attended_rows = gather_columns(own_attended, line)
     branch = jnp.dot(attended_rows, out_w, preferred_element_type=f32)
     middle_all = inputs + keep * branch
     inverse_mid = lax.rsqrt(jnp.mean(middle_all * middle_all, axis=-1, keepdims=True) + epsilon)
     second_norm = (middle_all * inverse_mid * gain_two).astype(bf16)
-    middle = middle_all[:span_len]
-    inverse_two = inverse_mid[:span_len]
-
-    ff_w = near_gather(natural(turn(pack_ff)), 1).reshape(model_width, 2 * ff_cols)
-    down_w = lax.all_gather(w_down, ("x", "y", "c"), axis=0, tiled=True)
-    mixed_grad = ring_gather((keep * upstream).astype(bf16))
+    middle = own_rows(middle_all)
+    inverse_two = own_rows(inverse_mid)
+
     gate_up = jnp.dot(second_norm, ff_w, preferred_element_type=f32)
     gate_value = gate_up[:, :ff_cols]
     up_value = gate_up[:, ff_cols:]
@@ -535,11 +812,28 @@
     both_grad = jnp.concatenate([gate_grad, up_grad], axis=1).astype(bf16)
 
     def split(values):
-        return [values[k * span_len : (k + 1) * span_len] for k in range(line)]
-
-    norm_grad = ring_sum(split(against(both_grad, ff_w).astype(bf16)))
-    mixed = ring_sum(split(jnp.dot(hidden, down_w, preferred_element_type=f32).astype(bf16)))
-    output = (middle + keep * mixed).astype(bf16)
+        return values.astype(bf16).reshape(line, span_len, model_width)
+
+    def pair_sum(values, axis, dim):
+        mine = pick(values, lax.axis_index(axis), dim).astype(f32)
+        other = pick(values, 1 - lax.axis_index(axis), dim)
+        return (mine + shift(other, axis, 1).astype(f32)).astype(bf16)
+
+    def core_sum(values):
+        return pair_sum(values, "c", values.ndim - 3)
+
+    def near_sum(values):
+        lead = values.ndim - 4
+        cut = values.shape[-1] // 256 * 128
+        left = pair_sum(pair_sum(values[..., :cut], "x", lead), "y", lead)
+        right = pair_sum(pair_sum(values[..., cut:], "y", lead + 1), "x", lead)
+        return jnp.concatenate([left, right], axis=-1)
+
+    grad_ff = over_rows(second_norm, both_grad).astype(bf16)
+    grad_ff = core_sum(grad_ff.reshape(line, 2, 2, 2, rows_each, -1))
+    grad_down = over_rows(hidden, mixed_grad).astype(bf16)
+    grad_down = core_sum(grad_down.reshape(2, 2, 2, -1, model_width))
+    norm_grad = sum_blocks(split(against(both_grad, ff_w)), line)
     scaled_two = gain_two * norm_grad
     middle_grad = (
         upstream
@@ -550,11 +844,10 @@
     )
     branch_grad = (keep * middle_grad).astype(bf16)
     own_grad = against(branch_grad, out_w).astype(bf16)
-    grad_blocks = [own_grad[:, :q_cols]]
-    for k in range(1, line):
-        back = line - k
-        grad_blocks.append(shift(own_grad[:, back * q_cols : (back + 1) * q_cols], "z", -back))
-    attended_grad = jnp.concatenate(grad_blocks, axis=0).reshape(group_len, heads, HD)
+    attended_grad = turn_rows(own_grad, line).reshape(group_len, heads, HD)
+    mixed_parts = jnp.dot(hidden, down_w, preferred_element_type=f32)
+    mixed = ring_sum(split(after(mixed_parts, norm_grad)))
+    output = (middle + keep * mixed).astype(bf16)
     prob_grad = jnp.einsum("tgd,jd->gtj", attended_grad, values, preferred_element_type=f32)
     delta = jnp.sum(attended_grad.astype(f32) * attended, axis=-1).T[..., None]
     score_grad = (probabilities * (prob_grad - delta)).astype(bf16)
@@ -571,8 +864,8 @@
         ],
         axis=1,
     ).astype(bf16)
-    input_norm_grad = ring_sum(split(against(qkv_grad, qkv_w).astype(bf16)))
-    inverse_one = inverse_all[:span_len]
+    input_norm_grad = sum_blocks(split(against(qkv_grad, qkv_w)), line)
+    inverse_one = own_rows(inverse_all)
     scaled_one = gain_one * input_norm_grad
     input_grad = (
         middle_grad
@@ -582,37 +875,17 @@
         * jnp.mean(scaled_one * own_x, axis=-1, keepdims=True)
     )
 
-    def pair_sum(values, axis, dim):
-        mine = pick(values, lax.axis_index(axis), dim).astype(f32)
-        other = pick(values, 1 - lax.axis_index(axis), dim)
-        return (mine + shift(other, axis, 1).astype(f32)).astype(bf16)
-
-    def near_sum(values):
-        lead = values.ndim - 5
-        values = pair_sum(values, "c", lead + 2)
-        cut = values.shape[-1] // 256 * 128
-        left = pair_sum(pair_sum(values[..., :cut], "x", lead), "y", lead)
-        right = pair_sum(pair_sum(values[..., cut:], "y", lead + 1), "x", lead)
-        return jnp.concatenate([left, right], axis=-1)
-
-    def return_columns(grad):
-        summed = near_sum(grad.astype(bf16).reshape(line, 2, 2, 2, rows_each, -1))
-        return natural(turn(summed)).astype(f32)
-
     def side_by_side(blocks):
         return blocks.transpose(1, 0, 2).reshape(rows_each, -1)
 
-    ff_back = return_columns(over_rows(second_norm, both_grad))
-    grad_down = near_sum(
-        over_rows(hidden, mixed_grad).astype(bf16).reshape(2, 2, 2, -1, model_width)
-    ).astype(f32)
-    grad_out = near_sum(
-        over_rows(attended_rows[:span_len], branch_grad)
-        .astype(bf16)
-        .reshape(line, 2, 2, 2, rows_each, model_width)
-    )
-    grad_out = ring_sum([grad_out[k] for k in range(line)])
-    qkv_back = return_columns(over_rows(first_norm, qkv_grad))
+    ff_back = turn(near_sum(grad_ff)).astype(f32)
+    grad_down = near_sum(grad_down).astype(f32)
+    grad_out = over_rows(own_rows(attended_rows), branch_grad).astype(bf16)
+    grad_out = near_sum(core_sum(grad_out.reshape(line, 2, 2, 2, rows_each, model_width)))
+    grad_out = ring_sum(grad_out)
+    grad_qkv = over_rows(first_norm, qkv_grad).astype(bf16)
+    grad_qkv = near_sum(core_sum(grad_qkv.reshape(line, 2, 2, 2, rows_each, -1)))
+    qkv_back = turn(grad_qkv).astype(f32)
     grad_query = side_by_side(qkv_back[:, :, :q_cols])
     grad_key = side_by_side(qkv_back[:, :, q_cols : q_cols + HD])
     grad_value = side_by_side(qkv_back[:, :, q_cols + HD :])

time: 765 us -> 678 us (0.89)
  Pallas kernels: 0 us -> 191 us
  waiting for transfers between devices: 318 us -> 167 us
  starting transfers between devices: 138 us -> 66 us
  blocking collectives: 53.6 us -> 0 us
  other arithmetic: 60.2 us -> 73 us
  local copies, waits for them, and re-layouts: 74.1 us -> 62.9 us
    pallas_call x0 -> x5, Pallas kernels: none -> 191 us  [link_call(): pl.pallas_call(kernel, out_shape=shapes, in_specs=[spec] * len(arguments)...]
    ppermute x85 -> x49, waiting for transfers between devices: 317 us -> 166 us  [shift(): lax.ppermute(values, axis, [(i, (i + step) % size) for i in range(size)])]
    ppermute x85 -> x49, starting transfers between devices: 138 us -> 65.9 us  [shift(): lax.ppermute(values, axis, [(i, (i + step) % size) for i in range(size)])]
    all_gather x2 -> x0, blocking collectives: 53.6 us -> none  [the longest x1 46.1 us: line_body(): lax.all_gather(jnp.stack([attn_gain, mlp_gain]), ('z', 'x', 'y', 'c'), ax...]
    unnamed x184 -> x150, local copies, waits for them, and re-layouts: 27.5 us -> 13.9 us
  transfers between devices with their start and end apart: 89 -> 52, of which waited for: 54 -> 31; matrix products, arithmetic and copies ran while one was open for 26% -> 27% of each run, Pallas kernels for 0% -> 23%
where the time goes in v3:
time: 678 us; the launch traced here: 670 us
  Pallas kernels  191 us (28%)
  waiting for transfers between devices  167 us (25%)
  matrix products  93.6 us (14%)
  other arithmetic  73 us (11%)
  starting transfers between devices  66 us (10%)
  local copies, waits for them, and re-layouts  62.9 us (9%)
  between operations  16.4 us (2%)
    pallas_call x5, Pallas kernels, link_call(): pl.pallas_call(kernel, out_shape=shapes, in_specs=[spec] * len(arguments)...  191 us
    ppermute x49, waiting for transfers between devices, shift(): lax.ppermute(values, axis, [(i, (i + step) % size) for i in range(size)])  166 us
    ppermute x49, starting transfers between devices, shift(): lax.ppermute(values, axis, [(i, (i + step) % size) for i in range(size)])  65.9 us
    convert_element_type x20, other arithmetic, pair_sum(): return (mine + shift(other, axis, 1).astype(f32)).astype(bf16)  22 us
    dot_general x4, matrix products, against(): lax.dot_general(left, right, (((1,), (1,)), ((), ())), preferred_element_...  21.7 us
    dot_general x4, matrix products, over_rows(): lax.dot_general(left, right, (((0,), (0,)), ((), ())), preferred_element_...  16.9 us
    dynamic_slice x7, local copies, waits for them, and re-layouts, pick(): return lax.dynamic_index_in_dim(values, index, dim, keepdims=False)  15 us
    unnamed x150, local copies, waits for them, and re-layouts  13.9 us
  transfers between devices with their start and end apart: 52, of which 31 were waited for; matrix products, arithmetic and copies ran while one was open for 27% of the time, Pallas kernels for 23%

profile of v3, /device:TPU:0, one launch (start us, length us, event | category | flops | bytes accessed | tf_op | source)
XLA Modules:
  0.0 669.7 jit_solution(4339067843854120409)
XLA Ops:
  11.8 67.1 %shard_map.230 = (bf16[4,128,2048]{2,1,0:T(8,128)(2,1)S(1)}, f32[4,8,128]{2,1,0:T(8,128)S(1)}, bf16[4,8,64,896]{3,2,1,0:T(8,128)(2,1)S(1)}) custom-call(bf16[128,2048]{1,0:T(8,128)(2,1)S(1)} %bitcast.399, f32[8,128]{1,0:T(8,128)S(1)} %broadcast_in_dim.66.pos_ref, bf16[4,64,896]{2,1,0:T(8,128)(2,1)S(1)} %pad_maximum_fusion.13.pack_ref), custom_call_target="tpu_custom_call" | custom-call | tf_op jit(solution)/shard_map/pallas_call | solution.py:272
  87.3 18.6 %collective-permute-done.3 = bf16[64,2816]{1,0:T(8,128)(2,1)S(1)} collective-permute-done((bf16[64,2816]{1,0:T(8,128)(2,1)S(1)}, bf16[64,2816]{1,0:T(8,128)(2,1)S(1)}, u32[]{:S(2)}, u32[]{:S(2)}) %collective-permute-start.3) | collective-permute-done | bytes 360480 | tf_op jit(solution)/shard_map/ppermute | solution.py:686
  106.0 33.0 %collective-permute-done.2 = bf16[64,2816]{1,0:T(8,128)(2,1)S(1)} collective-permute-done((bf16[64,2816]{1,0:T(8,128)(2,1)S(1)}, bf16[64,2816]{1,0:T(8,128)(2,1)S(1)}, u32[]{:S(2)}, u32[]{:S(2)}) %collective-permute-start.2) | collective-permute-done | bytes 360480 | tf_op jit(solution)/shard_map/ppermute | solution.py:686
  140.3 3.1 gather_fusion.2
  182.0 8.7 %fusion.133 = (f32[4,512]{1,0:T(4,128)S(1)}, f32[4,512,1024]{1,2,0:T(8,128)}) fusion(pred[512,1024]{0,1:T(8,128)(4,1)} %broadcast_compare_fusion, bf16[1024,256]{0,1:T(8,128)(2,1)S(1)} %pad_maximum_fusion.9, bf16[512,4,64]{2,0,1:T(8,128)(2,1)} %get-tuple-element.48, bf16[512,4,64]{2,0,1:T(8,128)(2,1)} %get-tuple-element.47), kind=kOutput, calls=%fused_computation.362 | convolution fusion | flops 546309120 | bytes 9707520 | tf_op jit(solution)/shard_map/sub | solution.py:786
  190.7 4.7 fusion.13
  195.4 3.9 collective-permute-start.6
  202.5 39.5 %shard_map.231 = bf16[512,2048]{1,0:T(8,128)(2,1)S(1)} custom-call(bf16[512,512]{1,0:T(8,128)(2,1)S(1)} %copy.212.x_ref), custom_call_target="tpu_custom_call" | custom-call | tf_op jit(solution)/shard_map/pallas_call | solution.py:272
  243.4 4.3 collective-permute-start.7
  254.4 3.8 gather_fusion
  258.2 3.1 bitcast_select_fusion.4
  261.3 10.6 %multiply_reduce_fusion = (f32[512]{0:T(512)S(1)}, f32[512,2048]{1,0:T(8,128)}) fusion(bf16[512,2048]{1,0:T(8,128)(2,1)} %copy-done.1, bf16[2048,2048]{1,0:T(8,128)(2,1)} %all-gather.5.cloned.1.call-done, f32[]{:T(128)} %bitcast.8, bf16[4,128,2048]{2,1,0:T(8,128)(2,1)S(1)} %get-tuple-element.17), kind=kOutput, calls=%fused_computation.30 | convolution fusion | flops 4300209664 | bytes 16779268 | tf_op jit(solution)/shard_map/dot_general | solution.py:796
  272.0 13.6 %fusion.125 = f32[512,2816]{1,0:T(8,128)} fusion(bf16[2048,2816]{1,0:T(8,128)(2,1)} %bitcast.457, f32[512,2048]{1,0:T(8,128)} %get-tuple-element.103, f32[2048]{0:T(1024)S(1)} %bitcast.445, f32[512]{0:T(512)S(1)} %add_rsqrt_fusion), kind=kOutput, calls=%fused_computation.354 | convolution fusion | flops 5908725760 | bytes 21506048 | tf_op jit(solution)/shard_map/dot_general | solution.py:803
  285.6 9.3 %multiply_convert_fusion.2 = (bf16[512,1408]{1,0:T(8,128)(2,1)S(1)}, bf16[512,1408]{1,0:T(8,128)(2,1)}, bf16[512,1408]{1,0:T(8,128)(2,1)}) fusion(f32[512,2816]{1,0:T(8,128)} %fusion.125, bf16[512,2048]{1,0:T(8,128)(2,1)S(1)} %copy-done.26, bf16[1408,2048]{1,0:T(8,128)(2,1)} %all-gather.7.cloned.1.call-done), kind=kOutput, calls=%fused_computation.49 | convolution fusion | flops 2963603456 | bytes 17956864 | tf_op jit(solution)/shard_map/dot_general | solution.py:53
  296.0 7.7 %convolution_convert_fusion.5 = bf16[512,2048]{1,0:T(8,128)(2,1)S(1)} fusion(bf16[2048,2816]{1,0:T(8,128)(2,1)S(1)} %bitcast.458, bf16[512,1408]{1,0:T(8,128)(2,1)} %get-tuple-element.29, bf16[512,1408]{1,0:T(8,128)(2,1)S(1)} %get-tuple-element.28), kind=kOutput, calls=%fused_computation.40 | convolution fusion | flops 5912395776 | bytes 16515072 | tf_op jit(solution)/shard_map/dot_general | solution.py:53
  303.7 8.1 %convolution_convert_fusion = bf16[2048,2816]{1,0:T(8,128)(2,1)S(1)} fusion(bf16[512,1408]{1,0:T(8,128)(2,1)S(1)} %copy-done.68, bf16[512,1408]{1,0:T(8,128)(2,1)} %copy-done.67, f32[512,2048]{1,0:T(8,128)S(1)} %copy-done.39, f32[2048]{0:T(1024)S(1)} %bitcast.446, f32[512]{0:T(512)S(1)} %add_rsqrt_fusion), kind=kOutput, calls=%fused_computation.7 | convolution fusion | flops 5920260096 | bytes 18622464 | tf_op jit(solution)/shard_map/dot_general | solution.py:47
  311.8 34.1 %shard_map.232 = f32[128,2048]{1,0:T(8,128)S(1)} custom-call(bf16[4,128,2048]{2,1,0:T(8,128)(2,1)S(1)} %bitcast.400), custom_call_target="tpu_custom_call" | custom-call | tf_op jit(solution)/shard_map/pallas_call | solution.py:272
  345.9 6.6 fusion.135
  356.6 3.4 convolution_convert_fusion.1
  361.0 7.8 %collective-permute-done.13 = bf16[64,2048]{1,0:T(8,128)(2,1)S(1)} collective-permute-done((bf16[64,2048]{1,0:T(8,128)(2,1)S(1)}, bf16[64,2048]{1,0:T(8,128)(2,1)S(1)}, u32[]{:S(2)}, u32[]{:S(2)}) %collective-permute-start.13) | collective-permute-done | bytes 262176 | tf_op jit(solution)/shard_map/ppermute | solution.py:686
  369.1 3.7 collective-permute-start.14
  378.6 3.8 collective-permute-start.15
  386.3 3.3 collective-permute-done.12
  398.3 13.6 %shard_map.233 = bf16[4,128,512]{2,1,0:T(8,128)(2,1)S(1)} custom-call(bf16[128,2048]{1,0:T(8,128)(2,1)S(1)} %convolution_convert_fusion.6.rows_ref), custom_call_target="tpu_custom_call" | custom-call | tf_op jit(solution)/shard_map/pallas_call | solution.py:272
  412.4 3.8 convolution_bitcast_fusion.1
  416.4 4.7 fusion.4
  428.1 3.6 convolution_convert_fusion.2
  438.0 4.3 constant_dynamic-slice_fusion.5
  442.3 4.9 copy.267
  449.6 36.7 %shard_map.234 = f32[128,2048]{1,0:T(8,128)S(1)} custom-call(bf16[4,128,2048]{2,1,0:T(8,128)(2,1)S(1)} %bitcast.401), custom_call_target="tpu_custom_call" | custom-call | tf_op jit(solution)/shard_map/pallas_call | solution.py:272
  490.8 5.5 collective-permute-start.20
  500.7 4.7 collective-permute-start.19
  527.4 4.3 collective-permute-done.47
  534.4 5.9 collective-permute-done.45
  544.1 5.4 collective-permute-done.46
  549.7 4.1 fusion.2
  557.6 6.0 fusion.1
  563.6 10.8 %collective-permute-done.28 = bf16[4,2,64,1024]{3,2,0,1:T(8,128)(2,1)} collective-permute-done((bf16[4,2,64,1024]{3,2,0,1:T(8,128)(2,1)}, bf16[4,2,64,1024]{3,2,0,1:T(8,128)(2,1)}, u32[]{:S(2)}, u32[]{:S(2)}) %collective-permute-start.28) | collective-permute-done | bytes 1048608 | tf_op jit(solution)/shard_map/ppermute | solution.py:686
  582.3 7.3 %collective-permute-done.29 = bf16[4,64,1024]{2,1,0:T(8,128)(2,1)S(1)} collective-permute-done((bf16[4,64,1024]{2,1,0:T(8,128)(2,1)S(1)}, bf16[4,64,1024]{2,1,0:T(8,128)(2,1)S(1)}, u32[]{:S(2)}, u32[]{:S(2)}) %collective-permute-start.29) | collective-permute-done | bytes 524320 | tf_op jit(solution)/shard_map/ppermute | solution.py:686
  593.3 6.6 collective-permute-done.30
  601.4 3.8 collective-permute-start.33
  608.3 5.6 collective-permute-done.32
  614.0 9.0 %collective-permute-done.37 = bf16[4,2,64,1408]{3,2,0,1:T(8,128)(2,1)S(1)} collective-permute-done((bf16[4,2,64,1408]{3,2,0,1:T(8,128)(2,1)S(1)}, bf16[4,2,64,1408]{3,2,0,1:T(8,128)(2,1)S(1)}, u32[]{:S(2)}, u32[]{:S(2)}) %collective-permute-start.37) | collective-permute-done | bytes 1441824 | tf_op jit(solution)/shard_map/ppermute | solution.py:686
  623.5 4.1 collective-permute-done.39
  630.8 4.6 collective-permute-done.38
  635.6 3.9 collective-permute-done.40
  642.8 4.7 collective-permute-done.43
  647.5 10.9 %collective-permute-done.42 = bf16[64,2816]{1,0:T(8,128)(2,1)S(1)} collective-permute-done((bf16[64,2816]{1,0:T(8,128)(2,1)S(1)}, bf16[64,2816]{1,0:T(8,128)(2,1)S(1)}, u32[]{:S(2)}, u32[]{:S(2)}) %collective-permute-start.42) | collective-permute-done | bytes 360480 | tf_op jit(solution)/shard_map/ppermute | solution.py:686
  (393 shorter events, 172.7 us)
Async XLA Ops:
  7.2 254.1 %all-gather.5.cloned.1.call-start = ((), (), s32[]{:S(2)}) async-start(), calls=%async_computation | async-start | bytes 8650752 | tf_op jit(solution)/shard_map/all_gather | solution.py:748
  7.9 264.1 %all-gather.9.cloned.1.call-start = ((), (), s32[]{:S(2)}) async-start(), calls=%async_computation.2 | async-start | bytes 12976128 | tf_op jit(solution)/shard_map/all_gather | solution.py:752
  82.6 23.3 %collective-permute-start.3 = (bf16[64,2816]{1,0:T(8,128)(2,1)S(1)}, bf16[64,2816]{1,0:T(8,128)(2,1)S(1)}, u32[]{:S(2)}, u32[]{:S(2)}) collective-permute-start(bf16[64,2816]{1,0:T(8,128)(2,1)S(1)} %get-tuple-element.66), channel_id=1, source_target_pairs={{0,24},{8,0},{16,8},{24,16},{1,25},{9,1},{17,9},{25,17},{2,26},{10... | collective-permute-start | bytes 1081352 | tf_op jit(solution)/shard_map/ppermute | solution.py:686
  84.9 54.0 %collective-permute-start.2 = (bf16[64,2816]{1,0:T(8,128)(2,1)S(1)}, bf16[64,2816]{1,0:T(8,128)(2,1)S(1)}, u32[]{:S(2)}, u32[]{:S(2)}) collective-permute-start(bf16[64,2816]{1,0:T(8,128)(2,1)S(1)} %get-tuple-element.67), channel_id=1, source_target_pairs={{0,16},{8,24},{16,0},{24,8},{1,17},{9,25},{17,1},{25,9},{2,18},{10... | collective-permute-start | bytes 1081352 | tf_op jit(solution)/shard_map/ppermute | solution.py:686
  85.8 53.2 %collective-permute-start.1 = (bf16[64,2816]{1,0:T(8,128)(2,1)S(1)}, bf16[64,2816]{1,0:T(8,128)(2,1)S(1)}, u32[]{:S(2)}, u32[]{:S(2)}) collective-permute-start(bf16[64,2816]{1,0:T(8,128)(2,1)S(1)} %get-tuple-element.68), channel_id=1, source_target_pairs={{0,8},{8,16},{16,24},{24,0},{1,9},{9,17},{17,25},{25,1},{2,10},{10... | collective-permute-start | bytes 1081352 | tf_op jit(solution)/shard_map/ppermute | solution.py:686
  146.1 139.5 %all-gather.7.cloned.1.call-start = ((), (), s32[]{:S(2)}) async-start(), calls=%async_computation.1 | async-start | bytes 6488064 | tf_op jit(solution)/shard_map/all_gather | solution.py:749
  160.4 20.5 %collective-permute-start = (bf16[512,256]{0,1:T(8,128)(2,1)}, bf16[512,256]{0,1:T(8,128)(2,1)}, u32[]{:S(2)}, u32[]{:S(2)}) collective-permute-start(bf16[512,256]{0,1:T(8,128)(2,1)} %pad_maximum_fusion.17), channel_id=1, source_target_pairs={{0,4},{4,0},{1,5},{5,1},{2,6},{6,2},{3,7},{7,3},{8,12},{12,8},{9,1... | collective-permute-start | bytes 786440 | tf_op jit(solution)/shard_map/ppermute | solution.py:686
  164.5 30.9 %collective-permute-start.5 = (bf16[64,2048]{1,0:T(8,128)(2,1)}, bf16[64,2048]{1,0:T(8,128)(2,1)}, u32[]{:S(2)}, u32[]{:S(2)}) collective-permute-start(bf16[64,2048]{1,0:T(8,128)(2,1)} %get-tuple-element.80), channel_id=1, source_target_pairs={{0,24},{8,0},{16,8},{24,16},{1,25},{9,1},{17,9},{25,17},{2,26},{10... | collective-permute-start | bytes 786440 | tf_op jit(solution)/shard_map/ppermute | solution.py:686
  164.5 16.2 %collective-permute-start.4 = (bf16[64,2048]{1,0:T(8,128)(2,1)}, bf16[64,2048]{1,0:T(8,128)(2,1)}, u32[]{:S(2)}, u32[]{:S(2)}) collective-permute-start(bf16[64,2048]{1,0:T(8,128)(2,1)} %get-tuple-element.79), channel_id=1, source_target_pairs={{0,8},{8,16},{16,24},{24,0},{1,9},{9,17},{17,25},{25,1},{2,10},{10... | collective-permute-start | bytes 786440 | tf_op jit(solution)/shard_map/ppermute | solution.py:686
  180.7 18.7 %collective-permute-start.8 = (bf16[64,2048]{1,0:T(8,128)(2,1)}, bf16[64,2048]{1,0:T(8,128)(2,1)}, u32[]{:S(2)}, u32[]{:S(2)}) collective-permute-start(bf16[64,2048]{1,0:T(8,128)(2,1)} %collective-permute-done.4), channel_id=1, source_target_pairs={{0,8},{8,16},{16,24},{24,0},{1,9},{9,17},{17,25},{25,1},{2,10},{10... | collective-permute-start | bytes 786440 | tf_op jit(solution)/shard_map/ppermute | solution.py:686
  195.4 47.9 %collective-permute-start.6 = (bf16[64,2048]{1,0:T(8,128)(2,1)}, bf16[64,2048]{1,0:T(8,128)(2,1)}, u32[]{:S(2)}, u32[]{:S(2)}) collective-permute-start(bf16[64,2048]{1,0:T(8,128)(2,1)} %collective-permute-done.5), channel_id=1, source_target_pairs={{0,24},{8,0},{16,8},{24,16},{1,25},{9,1},{17,9},{25,17},{2,26},{10... | collective-permute-start | bytes 786440 | tf_op jit(solution)/shard_map/ppermute | solution.py:686
  199.4 49.4 %collective-permute-start.9 = (bf16[64,2048]{1,0:T(8,128)(2,1)}, bf16[64,2048]{1,0:T(8,128)(2,1)}, u32[]{:S(2)}, u32[]{:S(2)}) collective-permute-start(bf16[64,2048]{1,0:T(8,128)(2,1)} %collective-permute-done.8), channel_id=1, source_target_pairs={{0,8},{8,16},{16,24},{24,0},{1,9},{9,17},{17,25},{25,1},{2,10},{10... | collective-permute-start | bytes 786440 | tf_op jit(solution)/shard_map/ppermute | solution.py:686
  243.4 8.5 %collective-permute-start.7 = (bf16[64,2048]{1,0:T(8,128)(2,1)}, bf16[64,2048]{1,0:T(8,128)(2,1)S(1)}, u32[]{:S(2)}, u32[]{:S(2)}) collective-permute-start(bf16[64,2048]{1,0:T(8,128)(2,1)} %collective-permute-done.6), channel_id=1, source_target_pairs={{0,24},{8,0},{16,8},{24,16},{1,25},{9,1},{17,9},{25,17},{2,26},{10... | collective-permute-start | bytes 786440 | tf_op jit(solution)/shard_map/ppermute | solution.py:686
  352.6 8.4 %collective-permute-start.10 = (bf16[64,2048]{1,0:T(8,128)(2,1)S(1)}, bf16[64,2048]{1,0:T(8,128)(2,1)S(1)}, u32[]{:S(2)}, u32[]{:S(2)}) collective-permute-start(bf16[64,2048]{1,0:T(8,128)(2,1)S(1)} %get-tuple-element.55), channel_id=1, source_target_pairs={{0,8},{8,16},{16,24},{24,0},{1,9},{9,17},{17,25},{25,1},{2,10},{10... | collective-permute-start | bytes 786440 | tf_op jit(solution)/shard_map/ppermute | solution.py:686
  354.2 14.7 %collective-permute-start.13 = (bf16[64,2048]{1,0:T(8,128)(2,1)S(1)}, bf16[64,2048]{1,0:T(8,128)(2,1)S(1)}, u32[]{:S(2)}, u32[]{:S(2)}) collective-permute-start(bf16[64,2048]{1,0:T(8,128)(2,1)S(1)} %get-tuple-element.56), channel_id=1, source_target_pairs={{0,24},{8,0},{16,8},{24,16},{1,25},{9,1},{17,9},{25,17},{2,26},{10... | collective-permute-start | bytes 786440 | tf_op jit(solution)/shard_map/ppermute | solution.py:686
  368.9 8.4 %collective-permute-start.11 = (bf16[64,2048]{1,0:T(8,128)(2,1)S(1)}, bf16[64,2048]{1,0:T(8,128)(2,1)S(1)}, u32[]{:S(2)}, u32[]{:S(2)}) collective-permute-start(bf16[64,2048]{1,0:T(8,128)(2,1)S(1)} %get-tuple-element.53), channel_id=1, source_target_pairs={{0,8},{8,16},{16,24},{24,0},{1,9},{9,17},{17,25},{25,1},{2,10},{10... | collective-permute-start | bytes 786440 | tf_op jit(solution)/shard_map/ppermute | solution.py:686
  369.1 9.2 %collective-permute-start.14 = (bf16[64,2048]{1,0:T(8,128)(2,1)S(1)}, bf16[64,2048]{1,0:T(8,128)(2,1)S(1)}, u32[]{:S(2)}, u32[]{:S(2)}) collective-permute-start(bf16[64,2048]{1,0:T(8,128)(2,1)S(1)} %get-tuple-element.54), channel_id=1, source_target_pairs={{0,24},{8,0},{16,8},{24,16},{1,25},{9,1},{17,9},{25,17},{2,26},{10... | collective-permute-start | bytes 786440 | tf_op jit(solution)/shard_map/ppermute | solution.py:686
  375.6 181.9 %collective-permute-start.36 = (bf16[4,2,2,64,2816]{4,3,2,1,0:T(8,128)(2,1)}, bf16[4,2,2,64,2816]{4,3,2,1,0:T(8,128)(2,1)}, u32[]{:S(2)}, u32[]{:S(2)}) collective-permute-start(bf16[4,2,2,64,2816]{4,3,2,1,0:T(8,128)(2,1)} %dynamic-slice_bitcast_fusion), channel_id=1, source_target_pairs={{0,1},{1,0},{2,3},{3,2},{4,5},{5,4},{6,7},{7,6},{8,9},{9,8},{10,11... | collective-permute-start | bytes 17301512 | tf_op jit(solution)/shard_map/ppermute | solution.py:686
  378.4 11.2 %collective-permute-start.12 = (bf16[64,2048]{1,0:T(8,128)(2,1)S(1)}, bf16[64,2048]{1,0:T(8,128)(2,1)S(1)}, u32[]{:S(2)}, u32[]{:S(2)}) collective-permute-start(bf16[64,2048]{1,0:T(8,128)(2,1)S(1)} %get-tuple-element.51), channel_id=1, source_target_pairs={{0,8},{8,16},{16,24},{24,0},{1,9},{9,17},{17,25},{25,1},{2,10},{10... | collective-permute-start | bytes 786440 | tf_op jit(solution)/shard_map/ppermute | solution.py:686
  378.6 13.2 %collective-permute-start.15 = (bf16[64,2048]{1,0:T(8,128)(2,1)S(1)}, bf16[64,2048]{1,0:T(8,128)(2,1)S(1)}, u32[]{:S(2)}, u32[]{:S(2)}) collective-permute-start(bf16[64,2048]{1,0:T(8,128)(2,1)S(1)} %get-tuple-element.52), channel_id=1, source_target_pairs={{0,24},{8,0},{16,8},{24,16},{1,25},{9,1},{17,9},{25,17},{2,26},{10... | collective-permute-start | bytes 786440 | tf_op jit(solution)/shard_map/ppermute | solution.py:686
  386.3 110.0 %collective-permute-start.44 = (bf16[2,2,176,2048]{3,2,0,1:T(8,128)(2,1)}, bf16[2,2,176,2048]{3,2,0,1:T(8,128)(2,1)}, u32[]{:S(2)}, u32[]{:S(2)}) collective-permute-start(bf16[2,2,176,2048]{3,2,0,1:T(8,128)(2,1)} %bitcast.394), channel_id=1, source_target_pairs={{0,1},{1,0},{2,3},{3,2},{4,5},{5,4},{6,7},{7,6},{8,9},{9,8},{10,11... | collective-permute-start | bytes 8650760 | tf_op jit(solution)/shard_map/ppermute | solution.py:686
  425.3 7.3 %collective-permute-start.16 = (bf16[512,256]{0,1:T(8,128)(2,1)}, bf16[512,256]{0,1:T(8,128)(2,1)}, u32[]{:S(2)}, u32[]{:S(2)}) collective-permute-start(bf16[512,256]{0,1:T(8,128)(2,1)} %fusion.54), channel_id=1, source_target_pairs={{0,4},{4,0},{1,5},{5,1},{2,6},{6,2},{3,7},{7,3},{8,12},{12,8},{9,1... | collective-permute-start | bytes 786440 | tf_op jit(solution)/shard_map/ppermute | solution.py:686
  438.0 49.8 %collective-permute-start.17 = (bf16[4,2,2,64,768]{4,3,2,1,0:T(8,128)(2,1)S(1)}, bf16[4,2,2,64,768]{4,3,2,1,0:T(8,128)(2,1)S(1)}, u32[]{:S(2)}, u32[]{:S(2)}) collective-permute-start(bf16[4,2,2,64,768]{4,3,2,1,0:T(8,128)(2,1)S(1)} %dynamic-slice_bitcast_fusion.1), channel_id=1, source_target_pairs={{0,1},{1,0},{2,3},{3,2},{4,5},{5,4},{6,7},{7,6},{8,9},{9,8},{10,11... | collective-permute-start | bytes 4718600 | tf_op jit(solution)/shard_map/ppermute | solution.py:686
  447.3 102.4 %collective-permute-start.25 = (bf16[4,2,2,64,2048]{4,3,0,1,2:T(8,128)(2,1)}, bf16[4,2,2,64,2048]{4,3,0,1,2:T(8,128)(2,1)}, u32[]{:S(2)}, u32[]{:S(2)}) collective-permute-start(bf16[4,2,2,64,2048]{4,3,0,1,2:T(8,128)(2,1)} %bitcast.393), channel_id=1, source_target_pairs={{0,1},{1,0},{2,3},{3,2},{4,5},{5,4},{6,7},{7,6},{8,9},{9,8},{10,11... | collective-permute-start | bytes 12582920 | tf_op jit(solution)/shard_map/ppermute | solution.py:686
  489.3 11.3 %collective-permute-start.18 = (bf16[4,2,64,384]{3,2,0,1:T(8,128)(2,1)S(1)}, bf16[4,2,64,384]{3,2,0,1:T(8,128)(2,1)S(1)}, u32[]{:S(2)}, u32[]{:S(2)}) collective-permute-start(bf16[4,2,64,384]{3,2,0,1:T(8,128)(2,1)S(1)} %bitcast.432), channel_id=1, source_target_pairs={{0,4},{4,0},{1,5},{5,1},{2,6},{6,2},{3,7},{7,3},{8,12},{12,8},{9,1... | collective-permute-start | bytes 1179656 | tf_op jit(solution)/shard_map/ppermute | solution.py:686
  490.8 14.6 %collective-permute-start.20 = (bf16[4,2,64,384]{3,2,1,0:T(8,128)(2,1)S(1)}, bf16[4,2,64,384]{3,2,1,0:T(8,128)(2,1)S(1)}, u32[]{:S(2)}, u32[]{:S(2)}) collective-permute-start(bf16[4,2,64,384]{3,2,1,0:T(8,128)(2,1)S(1)} %dynamic-slice_bitcast_fusion.11), channel_id=1, source_target_pairs={{0,2},{2,0},{1,3},{3,1},{4,6},{6,4},{5,7},{7,5},{8,10},{10,8},{9,1... | collective-permute-start | bytes 1179656 | tf_op jit(solution)/shard_map/ppermute | solution.py:686
  500.7 8.4 %collective-permute-start.19 = (bf16[4,64,384]{2,1,0:T(8,128)(2,1)S(1)}, bf16[4,64,384]{2,1,0:T(8,128)(2,1)S(1)}, u32[]{:S(2)}, u32[]{:S(2)}) collective-permute-start(bf16[4,64,384]{2,1,0:T(8,128)(2,1)S(1)} %dynamic-slice_bitcast_fusion.26), channel_id=1, source_target_pairs={{0,2},{2,0},{1,3},{3,1},{4,6},{6,4},{5,7},{7,5},{8,10},{10,8},{9,1... | collective-permute-start | bytes 589832 | tf_op jit(solution)/shard_map/ppermute | solution.py:686
  514.3 7.4 %collective-permute-start.23 = (bf16[64,768]{1,0:T(8,128)(2,1)S(1)}, bf16[64,768]{1,0:T(8,128)(2,1)S(1)}, u32[]{:S(2)}, u32[]{:S(2)}) collective-permute-start(bf16[64,768]{1,0:T(8,128)(2,1)S(1)} %get-tuple-element.83), channel_id=1, source_target_pairs={{0,16},{8,24},{16,0},{24,8},{1,17},{9,25},{17,1},{25,9},{2,18},{10... | collective-permute-start | bytes 294920 | tf_op jit(solution)/shard_map/ppermute | solution.py:686
  514.3 8.4 %collective-permute-start.22 = (bf16[64,768]{1,0:T(8,128)(2,1)S(1)}, bf16[64,768]{1,0:T(8,128)(2,1)S(1)}, u32[]{:S(2)}, u32[]{:S(2)}) collective-permute-start(bf16[64,768]{1,0:T(8,128)(2,1)S(1)} %get-tuple-element.82), channel_id=1, source_target_pairs={{0,8},{8,16},{16,24},{24,0},{1,9},{9,17},{17,25},{25,1},{2,10},{10... | collective-permute-start | bytes 294920 | tf_op jit(solution)/shard_map/ppermute | solution.py:686
  518.1 13.6 %collective-permute-start.47 = (bf16[2,176,1024]{2,1,0:T(8,128)(2,1)}, bf16[2,176,1024]{2,1,0:T(8,128)(2,1)}, u32[]{:S(2)}, u32[]{:S(2)}) collective-permute-start(bf16[2,176,1024]{2,1,0:T(8,128)(2,1)} %dynamic-slice_bitcast_fusion.5), channel_id=1, source_target_pairs={{0,2},{2,0},{1,3},{3,1},{4,6},{6,4},{5,7},{7,5},{8,10},{10,8},{9,1... | collective-permute-start | bytes 2162696 | tf_op jit(solution)/shard_map/ppermute | solution.py:686
  521.7 18.6 %collective-permute-start.45 = (bf16[2,176,1024]{2,1,0:T(8,128)(2,1)}, bf16[2,176,1024]{2,1,0:T(8,128)(2,1)}, u32[]{:S(2)}, u32[]{:S(2)}) collective-permute-start(bf16[2,176,1024]{2,1,0:T(8,128)(2,1)} %dynamic-slice_bitcast_fusion.6), channel_id=1, source_target_pairs={{0,4},{4,0},{1,5},{5,1},{2,6},{6,2},{3,7},{7,3},{8,12},{12,8},{9,1... | collective-permute-start | bytes 2162696 | tf_op jit(solution)/shard_map/ppermute | solution.py:686
  533.1 10.9 %collective-permute-start.48 = (bf16[176,1024]{1,0:T(8,128)(2,1)S(1)}, bf16[176,1024]{1,0:T(8,128)(2,1)S(1)}, u32[]{:S(2)}, u32[]{:S(2)}) collective-permute-start(bf16[176,1024]{1,0:T(8,128)(2,1)S(1)} %dynamic-slice_bitcast_fusion.12), channel_id=1, source_target_pairs={{0,4},{4,0},{1,5},{5,1},{2,6},{6,2},{3,7},{7,3},{8,12},{12,8},{9,1... | collective-permute-start | bytes 1081352 | tf_op jit(solution)/shard_map/ppermute | solution.py:686
  541.7 7.9 %collective-permute-start.46 = (bf16[176,1024]{1,0:T(8,128)(2,1)S(1)}, bf16[176,1024]{1,0:T(8,128)(2,1)S(1)}, u32[]{:S(2)}, u32[]{:S(2)}) collective-permute-start(bf16[176,1024]{1,0:T(8,128)(2,1)S(1)} %dynamic-slice_bitcast_fusion.13), channel_id=1, source_target_pairs={{0,2},{2,0},{1,3},{3,1},{4,6},{6,4},{5,7},{7,5},{8,10},{10,8},{9,1... | collective-permute-start | bytes 1081352 | tf_op jit(solution)/shard_map/ppermute | solution.py:686
  555.4 18.9 %collective-permute-start.28 = (bf16[4,2,64,1024]{3,2,0,1:T(8,128)(2,1)}, bf16[4,2,64,1024]{3,2,0,1:T(8,128)(2,1)}, u32[]{:S(2)}, u32[]{:S(2)}) collective-permute-start(bf16[4,2,64,1024]{3,2,0,1:T(8,128)(2,1)} %dynamic-slice_bitcast_fusion.3), channel_id=1, source_target_pairs={{0,2},{2,0},{1,3},{3,1},{4,6},{6,4},{5,7},{7,5},{8,10},{10,8},{9,1... | collective-permute-start | bytes 3145736 | tf_op jit(solution)/shard_map/ppermute | solution.py:686
  557.4 20.7 %collective-permute-start.26 = (bf16[4,2,64,1024]{3,2,0,1:T(8,128)(2,1)}, bf16[4,2,64,1024]{3,2,0,1:T(8,128)(2,1)}, u32[]{:S(2)}, u32[]{:S(2)}) collective-permute-start(bf16[4,2,64,1024]{3,2,0,1:T(8,128)(2,1)} %dynamic-slice_bitcast_fusion.4), channel_id=1, source_target_pairs={{0,4},{4,0},{1,5},{5,1},{2,6},{6,2},{3,7},{7,3},{8,12},{12,8},{9,1... | collective-permute-start | bytes 3145736 | tf_op jit(solution)/shard_map/ppermute | solution.py:686
  576.4 13.2 %collective-permute-start.29 = (bf16[4,64,1024]{2,1,0:T(8,128)(2,1)S(1)}, bf16[4,64,1024]{2,1,0:T(8,128)(2,1)S(1)}, u32[]{:S(2)}, u32[]{:S(2)}) collective-permute-start(bf16[4,64,1024]{2,1,0:T(8,128)(2,1)S(1)} %dynamic-slice_bitcast_fusion.9), channel_id=1, source_target_pairs={{0,4},{4,0},{1,5},{5,1},{2,6},{6,2},{3,7},{7,3},{8,12},{12,8},{9,1... | collective-permute-start | bytes 1572872 | tf_op jit(solution)/shard_map/ppermute | solution.py:686
  579.8 11.6 %collective-permute-start.27 = (bf16[4,64,1024]{2,1,0:T(8,128)(2,1)S(1)}, bf16[4,64,1024]{2,1,0:T(8,128)(2,1)S(1)}, u32[]{:S(2)}, u32[]{:S(2)}) collective-permute-start(bf16[4,64,1024]{2,1,0:T(8,128)(2,1)S(1)} %dynamic-slice_bitcast_fusion.10), channel_id=1, source_target_pairs={{0,2},{2,0},{1,3},{3,1},{4,6},{6,4},{5,7},{7,5},{8,10},{10,8},{9,1... | collective-permute-start | bytes 1572872 | tf_op jit(solution)/shard_map/ppermute | solution.py:686
  591.7 8.3 %collective-permute-start.30 = (bf16[32,2048]{1,0:T(8,128)(2,1)S(1)}, bf16[32,2048]{1,0:T(8,128)(2,1)S(1)}, u32[]{:S(2)}, u32[]{:S(2)}) collective-permute-start(bf16[32,2048]{1,0:T(8,128)(2,1)S(1)} %get-tuple-element.71), channel_id=1, source_target_pairs={{0,8},{8,16},{16,24},{24,0},{1,9},{9,17},{17,25},{25,1},{2,10},{10... | collective-permute-start | bytes 393224 | tf_op jit(solution)/shard_map/ppermute | solution.py:686
  592.2 30.8 %collective-permute-start.37 = (bf16[4,2,64,1408]{3,2,0,1:T(8,128)(2,1)S(1)}, bf16[4,2,64,1408]{3,2,0,1:T(8,128)(2,1)S(1)}, u32[]{:S(2)}, u32[]{:S(2)}) collective-permute-start(bf16[4,2,64,1408]{3,2,0,1:T(8,128)(2,1)S(1)} %bitcast.426), channel_id=1, source_target_pairs={{0,4},{4,0},{1,5},{5,1},{2,6},{6,2},{3,7},{7,3},{8,12},{12,8},{9,1... | collective-permute-start | bytes 4325384 | tf_op jit(solution)/shard_map/ppermute | solution.py:686
  600.0 6.9 %collective-permute-start.31 = (bf16[32,2048]{1,0:T(8,128)(2,1)S(1)}, bf16[32,2048]{1,0:T(8,128)(2,1)S(1)}, u32[]{:S(2)}, u32[]{:S(2)}) collective-permute-start(bf16[32,2048]{1,0:T(8,128)(2,1)S(1)} %fusion.72), channel_id=1, source_target_pairs={{0,8},{8,16},{16,24},{24,0},{1,9},{9,17},{17,25},{25,1},{2,10},{10... | collective-permute-start | bytes 393224 | tf_op jit(solution)/shard_map/ppermute | solution.py:686
  600.2 27.5 %collective-permute-start.39 = (bf16[4,2,64,1408]{3,2,1,0:T(8,128)(2,1)S(1)}, bf16[4,2,64,1408]{3,2,1,0:T(8,128)(2,1)S(1)}, u32[]{:S(2)}, u32[]{:S(2)}) collective-permute-start(bf16[4,2,64,1408]{3,2,1,0:T(8,128)(2,1)S(1)} %dynamic-slice_bitcast_fusion.2), channel_id=1, source_target_pairs={{0,2},{2,0},{1,3},{3,1},{4,6},{6,4},{5,7},{7,5},{8,10},{10,8},{9,1... | collective-permute-start | bytes 4325384 | tf_op jit(solution)/shard_map/ppermute | solution.py:686
  613.9 15.1 %collective-permute-start.34 = (bf16[32,2048]{1,0:T(8,128)(2,1)S(1)}, bf16[32,2048]{1,0:T(8,128)(2,1)S(1)}, u32[]{:S(2)}, u32[]{:S(2)}) collective-permute-start(bf16[32,2048]{1,0:T(8,128)(2,1)S(1)} %get-tuple-element.70), channel_id=1, source_target_pairs={{0,24},{8,0},{16,8},{24,16},{1,25},{9,1},{17,9},{25,17},{2,26},{10... | collective-permute-start | bytes 393224 | tf_op jit(solution)/shard_map/ppermute | solution.py:686
  623.4 12.0 %collective-permute-start.38 = (bf16[4,64,1408]{2,1,0:T(8,128)(2,1)S(1)}, bf16[4,64,1408]{2,1,0:T(8,128)(2,1)S(1)}, u32[]{:S(2)}, u32[]{:S(2)}) collective-permute-start(bf16[4,64,1408]{2,1,0:T(8,128)(2,1)S(1)} %dynamic-slice_bitcast_fusion.8), channel_id=1, source_target_pairs={{0,2},{2,0},{1,3},{3,1},{4,6},{6,4},{5,7},{7,5},{8,10},{10,8},{9,1... | collective-permute-start | bytes 2162696 | tf_op jit(solution)/shard_map/ppermute | solution.py:686
  628.1 11.4 %collective-permute-start.40 = (bf16[4,64,1408]{2,1,0:T(8,128)(2,1)S(1)}, bf16[4,64,1408]{2,1,0:T(8,128)(2,1)S(1)}, u32[]{:S(2)}, u32[]{:S(2)}) collective-permute-start(bf16[4,64,1408]{2,1,0:T(8,128)(2,1)S(1)} %dynamic-slice_bitcast_fusion.7), channel_id=1, source_target_pairs={{0,4},{4,0},{1,5},{5,1},{2,6},{6,2},{3,7},{7,3},{8,12},{12,8},{9,1... | collective-permute-start | bytes 2162696 | tf_op jit(solution)/shard_map/ppermute | solution.py:686
  629.1 12.8 %collective-permute-start.35 = (bf16[32,2048]{1,0:T(8,128)(2,1)S(1)}, bf16[32,2048]{1,0:T(8,128)(2,1)S(1)}, u32[]{:S(2)}, u32[]{:S(2)}) collective-permute-start(bf16[32,2048]{1,0:T(8,128)(2,1)S(1)} %fusion.69), channel_id=1, source_target_pairs={{0,24},{8,0},{16,8},{24,16},{1,25},{9,1},{17,9},{25,17},{2,26},{10... | collective-permute-start | bytes 393224 | tf_op jit(solution)/shard_map/ppermute | solution.py:686
  639.8 7.7 %collective-permute-start.43 = (bf16[64,2816]{1,0:T(8,128)(2,1)S(1)}, bf16[64,2816]{1,0:T(8,128)(2,1)S(1)}, u32[]{:S(2)}, u32[]{:S(2)}) collective-permute-start(bf16[64,2816]{1,0:T(8,128)(2,1)S(1)} %get-tuple-element.64), channel_id=1, source_target_pairs={{0,24},{8,0},{16,8},{24,16},{1,25},{9,1},{17,9},{25,17},{2,26},{10... | collective-permute-start | bytes 1081352 | tf_op jit(solution)/shard_map/ppermute | solution.py:686
  641.3 17.1 %collective-permute-start.42 = (bf16[64,2816]{1,0:T(8,128)(2,1)S(1)}, bf16[64,2816]{1,0:T(8,128)(2,1)S(1)}, u32[]{:S(2)}, u32[]{:S(2)}) collective-permute-start(bf16[64,2816]{1,0:T(8,128)(2,1)S(1)} %get-tuple-element.63), channel_id=1, source_target_pairs={{0,16},{8,24},{16,0},{24,8},{1,17},{9,25},{17,1},{25,9},{2,18},{10... | collective-permute-start | bytes 1081352 | tf_op jit(solution)/shard_map/ppermute | solution.py:686
  641.3 17.1 %collective-permute-start.41 = (bf16[64,2816]{1,0:T(8,128)(2,1)S(1)}, bf16[64,2816]{1,0:T(8,128)(2,1)S(1)}, u32[]{:S(2)}, u32[]{:S(2)}) collective-permute-start(bf16[64,2816]{1,0:T(8,128)(2,1)S(1)} %get-tuple-element.62), channel_id=1, source_target_pairs={{0,8},{8,16},{16,24},{24,0},{1,9},{9,17},{17,25},{25,1},{2,10},{10... | collective-permute-start | bytes 1081352 | tf_op jit(solution)/shard_map/ppermute | solution.py:686
  (75 other events, 839.9 us)
Sparse Core Ops, SparseCore 0:
  10.9 126.6 all-gather.4
  146.2 70.8 all-gather.8
  219.0 43.3 all-gather.6

commit v4 on v3

--- a/solution.py
+++ b/solution.py
@@ -204,46 +204,226 @@
         copy.wait()
 
 
-def ring_kernel(line, x_ref, xs_ref, send_sems, recv_sems):
+def second_kernel(line, att_ref, mix_ref, ff_ref, atts_ref, mixs_ref, ffs_ref, send_sems, recv_sems):
     links = Links(send_sems, recv_sems, line)
-    columns = x_ref.shape[1]
-    links.meet([1, line - 1])
+    links.meet(["x", "y", "c", 1, line - 1])
+    columns = att_ref.shape[1]
 
     def place(block, rows):
-        return xs_ref.at[rows, pl.ds(pl.multiple_of(block * columns, columns), columns)]
-
-    ring = RingGather(links, x_ref, place)
-    local = links.keep(x_ref, place(links.z, pl.ds(0, x_ref.shape[0])))
-    for number in range(line):
-        ring.step(number)
+        return atts_ref.at[rows, pl.ds(pl.multiple_of(block * columns, columns), columns)]
+
+    rings = [
+        RingGather(links, att_ref, place),
+        RingGather(links, mix_ref, lambda block, rows: mixs_ref.at[block, rows]),
+    ]
+    near = NearGather(links, lambda block, slot: ffs_ref.at[block, slot])
+    local = [
+        links.keep(att_ref, place(links.z, pl.ds(0, att_ref.shape[0]))),
+        links.keep(mix_ref, mixs_ref.at[links.z]),
+    ]
+
+    def step(number):
+        for ring in rings:
+            ring.step(number)
+
+    step(0)
+    for block in range(line):
+        near.offer(block, ff_ref.at[block])
+        local.append(links.keep(ff_ref.at[block], ffs_ref.at[block, links.slot]))
+    for block in range(line):
+        if block == line // 2:
+            step(1)
+        near.relay(block, "x" if block % 2 == 0 else "y")
+    step(2)
+    for block in range(line):
+        near.close(block)
+    step(3)
+    near.wait(range(line))
     links.finish()
-    local.wait()
-
-
-def sum_kernel(line, pieces, parts_ref, total_ref, got, made, send_sems, recv_sems):
-    links = Links(send_sems, recv_sems, line)
-    links.meet([1, line - 1])
-    rows = parts_ref.shape[1] // pieces
-    last = [None] * pieces
-    for number in range(line):
-        for piece in range(pieces):
-            way = 1 if piece < pieces // 2 else -1
+    for copy in local:
+        copy.wait()
+
+
+def add_rows_of(target, values, count):
+    def add(index, carry):
+        rows = pl.ds(pl.multiple_of(index * 16, 16), 16)
+        target[rows] = target[rows] + values[rows]
+        return carry
+
+    lax.fori_loop(0, count // 16, add, 0)
+
+
+class NearSum:
+    def __init__(self, links, source, own, from_core, from_first, from_second, first):
+        self.links, self.source, self.own, self.first = links, source, own, first
+        self.from_core, self.from_first, self.from_second = from_core, from_first, from_second
+
+    def start(self):
+        links = self.links
+        self.local = links.keep(self.source(links.c), self.own)
+        self.copy = links.send(self.source(1 - links.c), self.from_core, "c")
+
+    def add(self, target, values):
+        add_rows_of(target, values, target.shape[0])
+
+    def core_done(self):
+        links = self.links
+        self.copy.wait_recv()
+        self.local.wait()
+        for x in range(2):
+            for y in range(2):
+                self.add(self.own.at[x, y], self.from_core.at[x, y])
+        if self.first == "x":
+            self.copy = links.send(self.own.at[1 - links.x], self.from_first, "x")
+        else:
+            self.copy = links.send(self.own.at[:, 1 - links.y], self.from_first, "y")
+
+    def first_done(self):
+        links = self.links
+        self.copy.wait_recv()
+        for other in range(2):
+            place = (links.x, other) if self.first == "x" else (other, links.y)
+            self.add(self.own.at[place], self.from_first.at[other])
+        if self.first == "x":
+            self.copy = links.send(self.own.at[links.x, 1 - links.y], self.from_second, "y")
+        else:
+            self.copy = links.send(self.own.at[1 - links.x, links.y], self.from_second, "x")
+
+    def second_done(self):
+        self.copy.wait_recv()
+        total = self.own.at[self.links.x, self.links.y]
+        self.add(total, self.from_second)
+        return total
+
+
+def sum_space(blocks, rows, columns):
+    shape = (rows, columns)
+    return [
+        pltpu.VMEM((blocks, 2, 2) + shape, jnp.bfloat16),
+        pltpu.VMEM((blocks, 2, 2) + shape, jnp.bfloat16),
+        pltpu.VMEM((blocks, 2) + shape, jnp.bfloat16),
+        pltpu.VMEM((blocks,) + shape, jnp.bfloat16),
+    ]
+
+
+class RingSum:
+    def __init__(self, links, parts, total, got, made, pieces=4):
+        self.links, self.parts, self.total, self.got, self.made = links, parts, total, got, made
+        self.pieces, self.last = pieces, [None] * pieces
+        self.rows = parts.shape[1] // pieces
+
+    def step(self, number):
+        links = self.links
+        for piece in range(self.pieces):
+            way = 1 if piece < self.pieces // 2 else -1
             block = links.along(-way * (number + 1))
-            where = pl.ds(piece * rows, rows)
+            where = pl.ds(piece * self.rows, self.rows)
             if number == 0:
-                source = parts_ref.at[block, where]
+                source = self.parts.at[block, where]
             else:
-                last[piece].wait_recv()
-                total = got[number - 1, where].astype(jnp.float32) + parts_ref[
+                self.last[piece].wait_recv()
+                total = self.got[number - 1, where].astype(jnp.float32) + self.parts[
                     block, where
                 ].astype(jnp.float32)
-                if number == line - 1:
-                    total_ref[where] = total
+                if number == links.line - 1:
+                    self.total[where] = total
                     continue
-                made[number - 1, where] = total.astype(made.dtype)
-                source = made.at[number - 1, where]
-            last[piece] = links.send(source, got.at[number, where], way)
+                self.made[number - 1, where] = total.astype(self.made.dtype)
+                source = self.made.at[number - 1, where]
+            self.last[piece] = links.send(source, self.got.at[number, where], way)
+
+
+def ring_space(line, shape):
+    return [pltpu.VMEM((line - 1,) + shape, jnp.bfloat16), pltpu.VMEM((line - 2,) + shape, jnp.bfloat16)]
+
+
+def third_kernel(
+    line, cuts, parts_ref, down_ref, total_ref, sum_ref, got, made, *scratch
+):
+    space, (send_sems, recv_sems) = scratch[:-2], scratch[-2:]
+    links = Links(send_sems, recv_sems, line)
+    links.meet(["x", "y", "c", 1, line - 1])
+    ring = RingSum(links, parts_ref, total_ref, got, made)
+    ring.step(0)
+    items = []
+    for index, (low, high) in enumerate(cuts):
+        rows = pl.ds(low, high - low)
+        own, core, first, second = space[4 * index : 4 * index + 4]
+        items.append(
+            NearSum(
+                links,
+                lambda c, rows=rows: down_ref.at[:, :, c, rows],
+                own.at[0],
+                core.at[0],
+                first.at[0],
+                second.at[0],
+                "xy"[index % 2],
+            )
+        )
+    for item in items:
+        item.start()
+    for item in items:
+        item.core_done()
+    ring.step(1)
+    for item in items:
+        item.first_done()
+    ring.step(2)
+    for item, (low, high) in zip(items, cuts):
+        sum_ref[low:high] = item.second_done()[...]
+    ring.step(3)
     links.finish()
+
+
+def last_kernel(line, parts_ref, ff_ref, out_ref, qkv_ref, total_ref, ffs_ref, outs_ref, qkvs_ref, got, made, *scratch):
+    space, (send_sems, recv_sems) = scratch[:-2], scratch[-2:]
+    links = Links(send_sems, recv_sems, line)
+    far = [1, line - 1] + list(range(2, line - 1))
+    links.meet(["x", "y", "c"] + far)
+    ring = RingSum(links, parts_ref, total_ref, got, made)
+    ring.step(0)
+    items = []
+    for kind, (source, target) in enumerate(((ff_ref, ffs_ref), (out_ref, outs_ref), (qkv_ref, qkvs_ref))):
+        own, core, first, second = space[4 * kind : 4 * kind + 4]
+        for index, k in enumerate(far + [0]):
+            item = NearSum(
+                links,
+                lambda c, source=source, k=k: source.at[links.along(k), :, :, c],
+                own.at[index],
+                core.at[index],
+                first.at[index],
+                second.at[index],
+                "xy"[index % 2],
+            )
+            items.append((item, target, k))
+    for item, _, _ in items:
+        item.start()
+    arrived, local = [], []
+
+    def turn(item, target, k):
+        total = item.second_done()
+        if k == 0:
+            local.append(links.keep(total, target.at[links.z]))
+        else:
+            arrived.append(links.send(total, target.at[links.z], k))
+
+    pairs = [items[index : index + 2] for index in range(0, len(items), 2)]
+    for number in range(len(pairs) + 2):
+        if number < len(pairs):
+            for item in pairs[number]:
+                item[0].core_done()
+        if 1 <= number < line:
+            ring.step(number)
+        if 1 <= number <= len(pairs):
+            for item in pairs[number - 1]:
+                item[0].first_done()
+        if number >= 2:
+            for item in pairs[number - 2]:
+                turn(*item)
+    for copy in arrived:
+        copy.wait_recv()
+    links.finish()
+    for copy in local:
+        copy.wait()
 
 
 def turn_kernel(line, rows_ref, columns_ref, send_sems, recv_sems):
@@ -264,20 +444,22 @@
     local.wait()
 
 
-def link_call(kernel, collective_id, copies, shapes, arguments, spaces=None, scratch=()):
+def link_call(kernel, collective_id, copies, shapes, arguments, spaces=None, scratch=(), vmem=16):
     any_space = pl.BlockSpec(memory_space=pl.ANY)
-    vmem = pl.BlockSpec(memory_space=pltpu.VMEM)
-    spec = vmem if spaces == "vmem" else any_space
+    near_space = pl.BlockSpec(memory_space=pltpu.VMEM)
     many = isinstance(shapes, tuple)
+    if spaces is None:
+        spaces = "h" * (len(arguments) + (len(shapes) if many else 1))
+    specs = [near_space if space == "v" else any_space for space in spaces]
     return pl.pallas_call(
         kernel,
         out_shape=shapes,
-        in_specs=[spec] * len(arguments),
-        out_specs=(spec,) * len(shapes) if many else spec,
+        in_specs=specs[: len(arguments)],
+        out_specs=tuple(specs[len(arguments) :]) if many else specs[-1],
         scratch_shapes=list(scratch)
         + [pltpu.SemaphoreType.DMA((copies,)), pltpu.SemaphoreType.DMA((copies,))],
         compiler_params=pltpu.CompilerParams(
-            collective_id=collective_id, has_side_effects=True, vmem_limit_bytes=32 * 2**20
+            collective_id=collective_id, has_side_effects=True, vmem_limit_bytes=vmem * 2**20
         ),
     )(*arguments)
 
@@ -296,29 +478,50 @@
     )
 
 
-def gather_columns(values, line):
+def second_gather(attended, mixed, pack, line):
     return link_call(
-        functools.partial(ring_kernel, line),
+        functools.partial(second_kernel, line),
         1,
-        4 * line,
-        jax.ShapeDtypeStruct((values.shape[0], line * values.shape[1]), values.dtype),
-        (values,),
-    )
-
-
-def sum_blocks(parts, line):
+        96,
+        (
+            jax.ShapeDtypeStruct((attended.shape[0], line * attended.shape[1]), attended.dtype),
+            jax.ShapeDtypeStruct((line,) + mixed.shape, mixed.dtype),
+            jax.ShapeDtypeStruct((line, 8) + pack.shape[1:], pack.dtype),
+        ),
+        (attended, mixed, pack),
+    )
+
+
+def third_sum(parts, grad_down, line):
     shape = parts.shape[1:]
+    rows, columns = grad_down.shape[3:]
+    half = (rows // 2 + 15) // 16 * 16
+    cuts = ((0, half), (half, rows))
     return link_call(
-        functools.partial(sum_kernel, line, 4),
+        functools.partial(third_kernel, line, cuts),
         2,
-        4 * line,
-        jax.ShapeDtypeStruct(shape, jnp.float32),
-        (parts,),
-        "vmem",
-        [
-            pltpu.VMEM((line - 1,) + shape, parts.dtype),
-            pltpu.VMEM((line - 2,) + shape, parts.dtype),
-        ],
+        64,
+        (jax.ShapeDtypeStruct(shape, jnp.float32), jax.ShapeDtypeStruct((rows, columns), jnp.bfloat16)),
+        (parts, grad_down),
+        "vhvv",
+        ring_space(line, shape) + sum((sum_space(1, high - low, columns) for low, high in cuts), []),
+        vmem=40,
+    )
+
+
+def last_sum(parts, grad_ff, grad_out, grad_qkv, line):
+    shape = parts.shape[1:]
+    grads = (grad_ff, grad_out, grad_qkv)
+    return link_call(
+        functools.partial(last_kernel, line),
+        4,
+        96,
+        (jax.ShapeDtypeStruct(shape, jnp.float32),)
+        + tuple(jax.ShapeDtypeStruct((line,) + grad.shape[4:], grad.dtype) for grad in grads),
+        (parts,) + grads,
+        "vhhhvhhh",
+        ring_space(line, shape) + sum((sum_space(line, *grad.shape[4:]) for grad in grads), []),
+        vmem=58,
     )
 
 
@@ -694,28 +897,14 @@
     def back_order(blocks):
         return jnp.take(blocks, (place - jnp.arange(line, dtype=jnp.int32)) % line, axis=0)
 
-    def ring_gather(values):
-        cut = values.shape[0] // 2
-        up, down = [values[:cut]], [values[cut:]]
-        for _ in range(line - 1):
-            up.append(shift(up[-1], "z", 1))
-            down.append(shift(down[-1], "z", -1))
-        pairs = [jnp.concatenate([up[k], down[(line - k) % line]], axis=0) for k in range(line)]
-        return back_order(jnp.stack(pairs))
-
     def ring_sum(blocks):
-        cut = blocks.shape[1] // 2
-        totals = []
-        for step in (1, -1):
-            total = None
-            for hop in range(line):
-                own = pick(blocks, (place - step * (hop + 1)) % line, 0)
-                own = own[:cut] if step == 1 else own[cut:]
-                total = own if total is None else shift(total, "z", step).astype(f32) + own.astype(f32)
-                if hop < line - 1:
-                    total = total.astype(bf16)
-            totals.append(total)
-        return jnp.concatenate(totals, axis=0)
+        total = pick(blocks, (place - 1) % line, 0)
+        for hop in range(1, line):
+            own = pick(blocks, (place - 1 - hop) % line, 0)
+            total = shift(total, "z", 1).astype(f32) + own.astype(f32)
+            if hop < line - 1:
+                total = total.astype(bf16)
+        return total
 
     def by_columns(weight, columns):
         return weight.reshape(rows_each, line, columns).transpose(1, 0, 2)
@@ -749,14 +938,12 @@
     down_w = lax.all_gather(w_down, ("x", "y", "c"), axis=0, tiled=True)
     pack_ff = jnp.concatenate([by_columns(w_gate, ff_cols), by_columns(w_up, ff_cols)], axis=2)
     turned_ff = turn(after(pack_ff, x_blocks))
-    ff_w = lax.all_gather(turned_ff, ("x", "y", "c"), axis=1).reshape(model_width, 2 * ff_cols)
 
     own_x = tokens[0].astype(f32)
     keep = keep_mask[0].astype(f32)
     group_match = group_ids[0][:, None] == jnp.arange(exit_scale.shape[0], dtype=jnp.int32)[None, :]
     token_scale = jnp.sum(jnp.where(group_match, exit_scale[None, :], 0.0), axis=1, keepdims=True)
     upstream = out_grad[0].astype(f32) * token_scale
-    mixed_grad = ring_gather((keep * upstream).astype(bf16)).reshape(group_len, model_width)
 
     inside = jnp.arange(span_len, dtype=jnp.int32)
     block_first = jnp.arange(line, dtype=jnp.int32) * (2 * span_len)
@@ -792,7 +979,11 @@
     def own_rows(values):
         return lax.dynamic_slice_in_dim(values, place * span_len, span_len, 0)
 
-    attended_rows = gather_columns(own_attended, line)
+    attended_rows, mixed_grad, ff_w = second_gather(
+        own_attended, (keep * upstream).astype(bf16), turned_ff, line
+    )
+    mixed_grad = mixed_grad.reshape(group_len, model_width)
+    ff_w = ff_w.reshape(model_width, 2 * ff_cols)
     branch = jnp.dot(attended_rows, out_w, preferred_element_type=f32)
     middle_all = inputs + keep * branch
     inverse_mid = lax.rsqrt(jnp.mean(middle_all * middle_all, axis=-1, keepdims=True) + epsilon)
@@ -814,26 +1005,10 @@
     def split(values):
         return values.astype(bf16).reshape(line, span_len, model_width)
 
-    def pair_sum(values, axis, dim):
-        mine = pick(values, lax.axis_index(axis), dim).astype(f32)
-        other = pick(values, 1 - lax.axis_index(axis), dim)
-        return (mine + shift(other, axis, 1).astype(f32)).astype(bf16)
-
-    def core_sum(values):
-        return pair_sum(values, "c", values.ndim - 3)
-
-    def near_sum(values):
-        lead = values.ndim - 4
-        cut = values.shape[-1] // 256 * 128
-        left = pair_sum(pair_sum(values[..., :cut], "x", lead), "y", lead)
-        right = pair_sum(pair_sum(values[..., cut:], "y", lead + 1), "x", lead)
-        return jnp.concatenate([left, right], axis=-1)
-
-    grad_ff = over_rows(second_norm, both_grad).astype(bf16)
-    grad_ff = core_sum(grad_ff.reshape(line, 2, 2, 2, rows_each, -1))
-    grad_down = over_rows(hidden, mixed_grad).astype(bf16)
-    grad_down = core_sum(grad_down.reshape(2, 2, 2, -1, model_width))
-    norm_grad = sum_blocks(split(against(both_grad, ff_w)), line)
+    grad_down = over_rows(hidden, mixed_grad).astype(bf16).reshape(2, 2, 2, -1, model_width)
+    norm_grad, grad_down = third_sum(split(against(both_grad, ff_w)), grad_down, line)
+    grad_down = grad_down.astype(f32)
+    grad_ff = over_rows(second_norm, after(both_grad, norm_grad)).astype(bf16)
     scaled_two = gain_two * norm_grad
     middle_grad = (
         upstream
@@ -864,7 +1039,18 @@
         ],
         axis=1,
     ).astype(bf16)
-    input_norm_grad = sum_blocks(split(against(qkv_grad, qkv_w)), line)
+    grad_out = over_rows(own_rows(attended_rows), branch_grad).astype(bf16)
+    grad_qkv = over_rows(first_norm, qkv_grad).astype(bf16)
+
+    def by_place(grad):
+        return grad.reshape(line, 2, 2, 2, rows_each, grad.shape[1])
+
+    input_norm_grad, ff_back, out_back, qkv_back = last_sum(
+        split(against(qkv_grad, qkv_w)), by_place(grad_ff), by_place(grad_out), by_place(grad_qkv), line
+    )
+    ff_back = ff_back.astype(f32)
+    qkv_back = qkv_back.astype(f32)
+    grad_out = jnp.sum(out_back.astype(f32), axis=0)
     inverse_one = own_rows(inverse_all)
     scaled_one = gain_one * input_norm_grad
     input_grad = (
@@ -878,14 +1064,6 @@
     def side_by_side(blocks):
         return blocks.transpose(1, 0, 2).reshape(rows_each, -1)
 
-    ff_back = turn(near_sum(grad_ff)).astype(f32)
-    grad_down = near_sum(grad_down).astype(f32)
-    grad_out = over_rows(own_rows(attended_rows), branch_grad).astype(bf16)
-    grad_out = near_sum(core_sum(grad_out.reshape(line, 2, 2, 2, rows_each, model_width)))
-    grad_out = ring_sum(grad_out)
-    grad_qkv = over_rows(first_norm, qkv_grad).astype(bf16)
-    grad_qkv = near_sum(core_sum(grad_qkv.reshape(line, 2, 2, 2, rows_each, -1)))
-    qkv_back = turn(grad_qkv).astype(f32)
     grad_query = side_by_side(qkv_back[:, :, :q_cols])
     grad_key = side_by_side(qkv_back[:, :, q_cols : q_cols + HD])
     grad_value = side_by_side(qkv_back[:, :, q_cols + HD :])

time: 678 us -> 552 us (0.81)
  waiting for transfers between devices: 167 us -> 27.9 us
  Pallas kernels: 191 us -> 323 us
  starting transfers between devices: 66 us -> 11.4 us
  other arithmetic: 73 us -> 40.4 us
  local copies, waits for them, and re-layouts: 62.9 us -> 34.7 us
    ppermute x49 -> x8, waiting for transfers between devices: 166 us -> 27.2 us  [shift(): lax.ppermute(values, axis, [(i, (i + step) % size) for i in range(size)])]
    pallas_call x5, Pallas kernels: 191 us -> 323 us  [link_call(): pl.pallas_call(kernel, out_shape=shapes, in_specs=specs[:len(arguments)],...]
    ppermute x49 -> x8, starting transfers between devices: 65.9 us -> 11.4 us  [shift(): lax.ppermute(values, axis, [(i, (i + step) % size) for i in range(size)])]
    convert_element_type x23 -> x3, other arithmetic: 24.7 us -> 2.65 us  [the longest x1 1.25 us: line_body(): grad_down = grad_down.astype(f32)]
    dynamic_slice x7 -> x1, local copies, waits for them, and re-layouts: 15 us -> 1.13 us  [pick(): return lax.dynamic_index_in_dim(values, index, dim, keepdims=False)]
    squeeze x16 -> x1, local copies, waits for them, and re-layouts: 7.51 us -> 0.03 us  [pick(): return lax.dynamic_index_in_dim(values, index, dim, keepdims=False)]
    unnamed x150 -> x122, local copies, waits for them, and re-layouts: 13.9 us -> 18.9 us
  transfers between devices with their start and end apart: 52 -> 10, of which waited for: 31 -> 3; matrix products, arithmetic and copies ran while one was open for 27% -> 16% of each run, Pallas kernels for 23% -> 29%
where the time goes in v4:
time: 552 us; the launch traced here: 544 us
  Pallas kernels  323 us (59%)
  matrix products  90.4 us (16%)
  other arithmetic  40.4 us (7%)
  local copies, waits for them, and re-layouts  34.7 us (6%)
  waiting for transfers between devices  27.9 us (5%)
  between operations  16.1 us (3%)
  starting transfers between devices  11.4 us (2%)
    pallas_call x5, Pallas kernels, link_call(): pl.pallas_call(kernel, out_shape=shapes, in_specs=specs[:len(arguments)],...  323 us
    ppermute x8, waiting for transfers between devices, shift(): lax.ppermute(values, axis, [(i, (i + step) % size) for i in range(size)])  27.2 us
    dot_general x4, matrix products, against(): lax.dot_general(left, right, (((1,), (1,)), ((), ())), preferred_element_...  23.6 us
    dot_general x4, matrix products, over_rows(): lax.dot_general(left, right, (((0,), (0,)), ((), ())), preferred_element_...  22.8 us
    unnamed x122, local copies, waits for them, and re-layouts  18.9 us
    ppermute x8, starting transfers between devices, shift(): lax.ppermute(values, axis, [(i, (i + step) % size) for i in range(size)])  11.4 us
  transfers between devices with their start and end apart: 10, of which 3 were waited for; matrix products, arithmetic and copies ran while one was open for 16% of the time, Pallas kernels for 29%

profile of v4, /device:TPU:0, one launch (start us, length us, event | category | flops | bytes accessed | tf_op | source)
XLA Modules:
  0.0 543.9 jit_solution(16610432406001684503)
XLA Ops:
  13.4 67.1 %shard_map.230 = (bf16[4,128,2048]{2,1,0:T(8,128)(2,1)S(1)}, f32[4,8,128]{2,1,0:T(8,128)S(1)}, bf16[4,8,64,896]{3,2,1,0:T(8,128)(2,1)S(1)}) custom-call(bf16[128,2048]{1,0:T(8,128)(2,1)S(1)} %bitcast.209, f32[8,128]{1,0:T(8,128)S(1)} %broadcast_in_dim.43.pos_ref, bf16[4,64,896]{2,1,0:T(8,128)(2,1)S(1)} %pad_maximum_fusion.8.pack_ref), custom_call_target="tpu_custom_call" | custom-call | tf_op jit(solution)/shard_map/pallas_call | solution.py:454
  80.5 1.8 copy-done.3
  83.7 1.6 collective-permute-start.1
  86.4 2.7 collective-permute-start.3
  93.1 1.8 fusion.13
  97.8 1.5 collective-permute-start
  99.3 2.3 slice.130
  101.5 1.6 reshape.445
  105.2 2.6 broadcast_multiply_fusion
  110.3 1.8 broadcast_compare_fusion
  112.2 1.8 pad_maximum_fusion.5
  114.0 8.0 %fusion.74 = (f32[4,512]{1,0:T(4,128)S(1)}, f32[4,512,1024]{1,2,0:T(8,128)}) fusion(pred[512,1024]{0,1:T(8,128)(4,1)} %broadcast_compare_fusion, bf16[1024,256]{0,1:T(8,128)(2,1)} %pad_maximum_fusion.5, bf16[512,4,64]{2,0,1:T(8,128)(2,1)} %get-tuple-element.55, bf16[512,4,64]{2,0,1:T(8,128)(2,1)S(1)} %get-tuple-element.54), kind=kOutput, calls=%fused_computation.186 | convolution fusion | flops 546309120 | bytes 9969664 | tf_op jit(solution)/shard_map/sub | solution.py:973
  122.0 4.7 fusion.10
  126.7 2.3 fusion.75
  130.4 2.6 pad_maximum_fusion.2
  133.0 3.2 gather_fusion
  136.3 1.6 broadcast_select_fusion.ff_ref
  137.8 90.7 %shard_map.231 = (bf16[512,2048]{1,0:T(8,128)(2,1)S(1)}, bf16[4,128,2048]{2,1,0:T(8,128)(2,1)S(1)}, bf16[4,8,64,2816]{3,2,1,0:T(8,128)(2,1)S(1)}) custom-call(bf16[512,512]{1,0:T(8,128)(2,1)S(1)} %copy.177.att_ref, bf16[128,2048]{1,0:T(8,128)(2,1)S(1)} %fusion.28.mix_ref, bf16[4,64,2816]{2,1,0:T(8,128)(2,1)S(1)} %broadcast_select_fusion.ff_ref), custom_call_target="tpu_custom_call" | custom-call | tf_op jit(solution)/shard_map/pallas_call | solution.py:454
  228.5 1.3 copy-done.2
  229.8 4.3 copy-done.6
  234.1 1.4 copy-done.8
  235.5 8.0 %multiply_reduce_fusion = (f32[512]{0:T(512)S(1)}, f32[512,2048]{1,0:T(8,128)S(1)}) fusion(bf16[512,2048]{1,0:T(8,128)(2,1)} %copy-done.2, bf16[2048,2048]{1,0:T(8,128)(2,1)} %all-gather.3.cloned.1.call-done, f32[]{:T(128)} %bitcast.8, bf16[4,128,2048]{2,1,0:T(8,128)(2,1)S(1)} %get-tuple-element.26), kind=kOutput, calls=%fused_computation.18 | convolution fusion | flops 4300209664 | bytes 16779268 | tf_op jit(solution)/shard_map/dot_general | solution.py:987
  243.5 2.0 copy-done.39
  245.5 8.5 %fusion.71 = f32[512,2816]{1,0:T(8,128)} fusion(bf16[2048,2816]{1,0:T(8,128)(2,1)S(1)} %bitcast.215, f32[512,2048]{1,0:T(8,128)S(1)} %get-tuple-element.84, f32[2048]{0:T(1024)S(1)} %bitcast.245, f32[512]{0:T(512)S(1)} %add_rsqrt_fusion), kind=kOutput, calls=%fused_computation.183 | convolution fusion | flops 5908725760 | bytes 21506048 | tf_op jit(solution)/shard_map/dot_general | solution.py:994
  254.0 8.1 %multiply_convert_fusion.2 = (bf16[512,1408]{1,0:T(8,128)(2,1)S(1)}, bf16[512,1408]{1,0:T(8,128)(2,1)S(1)}, bf16[512,1408]{1,0:T(8,128)(2,1)S(1)}) fusion(f32[512,2816]{1,0:T(8,128)} %fusion.71, bf16[512,2048]{1,0:T(8,128)(2,1)S(1)} %bitcast.216, bf16[1408,2048]{1,0:T(8,128)(2,1)} %all-gather.5.cloned.1.call-done), kind=kOutput, calls=%fused_computation.29 | convolution fusion | flops 2963603456 | bytes 17956864 | tf_op jit(solution)/shard_map/dot_general | solution.py:53
  262.2 3.4 convolution_convert_fusion.1
  265.6 9.1 %convolution_convert_fusion.5 = bf16[512,2048]{1,0:T(8,128)(2,1)S(1)} fusion(bf16[2048,2816]{1,0:T(8,128)(2,1)} %bitcast.214, bf16[512,1408]{1,0:T(8,128)(2,1)S(1)} %get-tuple-element.48, bf16[512,1408]{1,0:T(8,128)(2,1)S(1)} %get-tuple-element.47), kind=kOutput, calls=%fused_computation.26 | convolution fusion | flops 5912395776 | bytes 16515072 | tf_op jit(solution)/shard_map/dot_general | solution.py:53
  274.8 39.4 %shard_map.232 = (f32[128,2048]{1,0:T(8,128)S(1)}, bf16[176,2048]{1,0:T(8,128)(2,1)S(1)}) custom-call(bf16[4,128,2048]{2,1,0:T(8,128)(2,1)S(1)} %bitcast.210, bf16[2,2,2,176,2048]{4,3,2,1,0:T(8,128)(2,1)S(1)} %bitcast.208), custom_call_target="tpu_custom_call" | custom-call | tf_op jit(solution)/shard_map/pallas_call | solution.py:454
  314.2 3.6 fusion.76
  317.8 1.3 copy-done.25
  320.3 14.0 %collective-permute-done.4 = bf16[128,2048]{1,0:T(8,128)(2,1)S(1)} collective-permute-done((bf16[128,2048]{1,0:T(8,128)(2,1)S(1)}, bf16[128,2048]{1,0:T(8,128)(2,1)S(1)}, u32[]{:S(2)}, u32[]{:S(2)}) %collective-permute-start.4) | collective-permute-done | bytes 524320 | tf_op jit(solution)/shard_map/ppermute | solution.py:889
  334.3 1.3 fusion.25
  336.9 2.1 pad_maximum_fusion
  339.0 10.7 %collective-permute-done.5 = bf16[128,2048]{1,0:T(8,128)(2,1)S(1)} collective-permute-done((bf16[128,2048]{1,0:T(8,128)(2,1)S(1)}, bf16[128,2048]{1,0:T(8,128)(2,1)S(1)}, u32[]{:S(2)}, u32[]{:S(2)}) %collective-permute-start.5) | collective-permute-done | bytes 524320 | tf_op jit(solution)/shard_map/ppermute | solution.py:889
  350.0 9.2 %convolution_convert_fusion = bf16[2048,2816]{1,0:T(8,128)(2,1)} fusion(bf16[512,2816]{1,0:T(8,128)(2,1)S(1)} %pad_maximum_fusion, f32[512,2048]{1,0:T(8,128)S(1)} %copy-done.40, f32[2048]{0:T(1024)S(1)} %bitcast.246, f32[512]{0:T(512)S(1)} %add_rsqrt_fusion), kind=kOutput, calls=%fused_computation.2 | convolution fusion | flops 5914492928 | bytes 18622464 | tf_op jit(solution)/shard_map/dot_general | solution.py:47
  360.8 2.4 collective-permute-done.6
  363.2 1.3 fusion.29
  364.5 2.9 convolution_convert_fusion.6.rows_ref
  367.4 11.7 %shard_map.233 = bf16[4,128,512]{2,1,0:T(8,128)(2,1)S(1)} custom-call(bf16[128,2048]{1,0:T(8,128)(2,1)S(1)} %convolution_convert_fusion.6.rows_ref), custom_call_target="tpu_custom_call" | custom-call | tf_op jit(solution)/shard_map/pallas_call | solution.py:454
  379.6 3.8 convolution_bitcast_fusion.1
  383.6 4.7 fusion.2
  388.2 1.8 fusion.15
  390.1 1.6 fusion.16
  394.5 3.2 collective-permute-start.7
  397.7 6.6 %convolution_convert_fusion.2 = bf16[2048,2048]{1,0:T(8,128)(2,1)} fusion(bf16[512,2048]{1,0:T(8,128)(2,1)} %copy-done.2, s32[]{:T(128)S(6)} %select_n.122, f32[128,2048]{1,0:T(8,128)S(1)} %get-tuple-element.50, f32[]{:T(128)} %bitcast.8), kind=kOutput, calls=%fused_computation.9 | convolution fusion | flops 1078460416 | bytes 9961988 | tf_op jit(solution)/shard_map/dot_general | solution.py:47
  406.0 3.5 convolution_convert_fusion.3
  409.5 3.4 convolution_convert_fusion.4
  413.0 114.2 %shard_map.234 = (f32[128,2048]{1,0:T(8,128)}, bf16[4,64,2816]{2,1,0:T(8,128)(2,1)}, bf16[4,64,2048]{2,1,0:T(8,128)(2,1)}, bf16[4,64,768]{2,1,0:T(8,128)(2,1)}) custom-call(bf16[4,128,2048]{2,1,0:T(8,128)(2,1)} %bitcast.229, bf16[4,2,2,2,64,2816]{5,4,3,2,1,0:T(8,128)(2,1)} %bitcast.219, bf16[4,2,2,2,64,2048]{5,4,3,2,1,0:T(8,128)(2,1)} %bitcast.218, ...), custom_call_target="tpu_custom_call" | custom-call | tf_op jit(solution)/shard_map/pallas_call | solution.py:454
  (212 shorter events, 39.2 us)
Async XLA Ops:
  7.2 75.1 %copy-start.17 = (bf16[64,5632]{1,0:T(8,128)(2,1)S(1)}, bf16[64,5632]{1,0:T(8,128)(2,1)}, u32[]{:S(2)}) copy-start(bf16[64,5632]{1,0:T(8,128)(2,1)} %param.22) | copy-start | bytes 2162692
  7.2 75.1 %copy-start.15 = (bf16[64,5632]{1,0:T(8,128)(2,1)S(1)}, bf16[64,5632]{1,0:T(8,128)(2,1)}, u32[]{:S(2)}) copy-start(bf16[64,5632]{1,0:T(8,128)(2,1)} %param.23) | copy-start | bytes 2162692
  7.2 228.3 %all-gather.3.cloned.1.call-start = ((), (), s32[]{:S(2)}) async-start(), calls=%async_computation | async-start | bytes 8650752 | tf_op jit(solution)/shard_map/all_gather | solution.py:937
  7.9 246.1 %all-gather.5.cloned.1.call-start = ((), (), s32[]{:S(2)}) async-start(), calls=%async_computation.1 | async-start | bytes 6488064 | tf_op jit(solution)/shard_map/all_gather | solution.py:938
  83.7 46.8 %collective-permute-start.1 = (bf16[64,2816]{1,0:T(8,128)(2,1)}, bf16[64,2816]{1,0:T(8,128)(2,1)}, u32[]{:S(2)}, u32[]{:S(2)}) collective-permute-start(bf16[64,2816]{1,0:T(8,128)(2,1)} %get-tuple-element.61), channel_id=1, source_target_pairs={{0,8},{8,16},{16,24},{24,0},{1,9},{9,17},{17,25},{25,1},{2,10},{10... | collective-permute-start | bytes 1081352 | tf_op jit(solution)/shard_map/ppermute | solution.py:889
  85.3 45.1 %collective-permute-start.2 = (bf16[64,2816]{1,0:T(8,128)(2,1)}, bf16[64,2816]{1,0:T(8,128)(2,1)}, u32[]{:S(2)}, u32[]{:S(2)}) collective-permute-start(bf16[64,2816]{1,0:T(8,128)(2,1)} %get-tuple-element.60), channel_id=1, source_target_pairs={{0,16},{8,24},{16,0},{24,8},{1,17},{9,25},{17,1},{25,9},{2,18},{10... | collective-permute-start | bytes 1081352 | tf_op jit(solution)/shard_map/ppermute | solution.py:889
  86.4 44.0 %collective-permute-start.3 = (bf16[64,2816]{1,0:T(8,128)(2,1)}, bf16[64,2816]{1,0:T(8,128)(2,1)}, u32[]{:S(2)}, u32[]{:S(2)}) collective-permute-start(bf16[64,2816]{1,0:T(8,128)(2,1)} %get-tuple-element.59), channel_id=1, source_target_pairs={{0,24},{8,0},{16,8},{24,16},{1,25},{9,1},{17,9},{25,17},{2,26},{10... | collective-permute-start | bytes 1081352 | tf_op jit(solution)/shard_map/ppermute | solution.py:889
  91.1 2.1 copy-start.4
  91.1 3.8 copy-start.43
  96.3 8.9 %copy-start.52 = (f32[2]{0:T(128)S(1)}, f32[2]{0:T(128)}, u32[]{:S(2)}) copy-start(f32[2]{0:T(128)} %param.28) | copy-start | bytes 28
  96.3 8.9 %copy-start.53 = (s32[1,128]{1,0:T(1,128)S(1)}, s32[1,128]{1,0:T(1,128)}, u32[]{:S(2)}) copy-start(s32[1,128]{1,0:T(1,128)} %param.26) | copy-start | bytes 1540
  97.0 2.2 copy-start.35
  97.8 14.4 %collective-permute-start = (bf16[512,256]{0,1:T(8,128)(2,1)}, bf16[512,256]{0,1:T(8,128)(2,1)}, u32[]{:S(2)}, u32[]{:S(2)}) collective-permute-start(bf16[512,256]{0,1:T(8,128)(2,1)} %pad_maximum_fusion.11), channel_id=1, source_target_pairs={{0,4},{4,0},{1,5},{5,1},{2,6},{6,2},{3,7},{7,3},{8,12},{12,8},{9,1... | collective-permute-start | bytes 786440 | tf_op jit(solution)/shard_map/ppermute | solution.py:889
  105.2 4.3 copy-start.47
  109.6 12.4 %copy-start.19 = (bf16[512,4,64]{2,0,1:T(8,128)(2,1)}, bf16[512,4,64]{2,0,1:T(8,128)(2,1)S(1)}, u32[]{:S(2)}) copy-start(bf16[512,4,64]{2,0,1:T(8,128)(2,1)S(1)} %get-tuple-element.54) | copy-start | bytes 786436
  122.0 4.7 copy-start.29
  126.7 2.5 copy-start.10
  130.4 5.8 %copy-start.51 = (pred[4]{0:T(512)(128)(4,1)S(1)}, pred[4]{0:T(512)(128)(4,1)}, u32[]{:S(2)}) copy-start(pred[4]{0:T(512)(128)(4,1)} %compare_and_fusion) | copy-start | bytes 16
  229.8 4.3 copy-start.6
  235.5 10.0 %copy-start.7 = (bf16[4,8,64,2816]{3,2,1,0:T(8,128)(2,1)S(1)}, bf16[4,8,64,2816]{3,2,1,0:T(8,128)(2,1)}, u32[]{:S(2)}) copy-start(bf16[4,8,64,2816]{3,2,1,0:T(8,128)(2,1)} %copy-done.6) | copy-start | bytes 34603012
  243.5 2.0 copy-start.39
  245.5 8.5 %copy-start.9 = (bf16[4,128,2048]{2,1,0:T(8,128)(2,1)S(1)}, bf16[4,128,2048]{2,1,0:T(8,128)(2,1)}, u32[]{:S(2)}) copy-start(bf16[4,128,2048]{2,1,0:T(8,128)(2,1)} %copy-done.8) | copy-start | bytes 6291460
  262.1 3.5 copy-start.32
  262.1 3.5 copy-start.33
  262.2 52.0 %slice-start.2 = ((s8[5767168]{0:T(1024)(128)(4,1)}), s8[4194304]{0:T(1024)(128)(4,1)S(1)}, s32[]{:S(2)}) async-start(s8[5767168]{0:T(1024)(128)(4,1)} %bitcast.257), calls=%async_computation.4 | async-start | bytes 8388608
  265.6 48.6 %slice-start.3 = ((s8[5767168]{0:T(1024)(128)(4,1)}), s8[1572864]{0:T(1024)(128)(4,1)S(1)}, s32[]{:S(2)}) async-start(s8[5767168]{0:T(1024)(128)(4,1)} %bitcast.257), calls=%async_computation.5 | async-start | bytes 3145728
  319.2 15.1 %collective-permute-start.4 = (bf16[128,2048]{1,0:T(8,128)(2,1)S(1)}, bf16[128,2048]{1,0:T(8,128)(2,1)S(1)}, u32[]{:S(2)}, u32[]{:S(2)}) collective-permute-start(bf16[128,2048]{1,0:T(8,128)(2,1)S(1)} %dynamic-slice_bitcast_fusion), channel_id=1, source_target_pairs={{0,8},{8,16},{16,24},{24,0},{1,9},{9,17},{17,25},{25,1},{2,10},{10... | collective-permute-start | bytes 1572872 | tf_op jit(solution)/shard_map/ppermute | solution.py:889
  334.3 15.5 %copy-start.26 = (bf16[512,2048]{1,0:T(8,128)(2,1)S(1)}, bf16[512,2048]{1,0:T(8,128)(2,1)}, u32[]{:S(2)}) copy-start(bf16[512,2048]{1,0:T(8,128)(2,1)} %copy-done.25) | copy-start | bytes 6291460
  334.3 15.7 %copy-start.40 = (f32[512,2048]{1,0:T(8,128)S(1)}, f32[512,2048]{1,0:T(8,128)}, u32[]{:S(2)}) copy-start(f32[512,2048]{1,0:T(8,128)} %copy-done.39) | copy-start | bytes 12582916
  335.6 14.1 %collective-permute-start.5 = (bf16[128,2048]{1,0:T(8,128)(2,1)S(1)}, bf16[128,2048]{1,0:T(8,128)(2,1)S(1)}, u32[]{:S(2)}, u32[]{:S(2)}) collective-permute-start(bf16[128,2048]{1,0:T(8,128)(2,1)S(1)} %fusion.25), channel_id=1, source_target_pairs={{0,8},{8,16},{16,24},{24,0},{1,9},{9,17},{17,25},{25,1},{2,10},{10... | collective-permute-start | bytes 1572872 | tf_op jit(solution)/shard_map/ppermute | solution.py:889
  336.9 27.6 %slice-start = ((s8[8388608]{0:T(1024)(128)(4,1)}), s8[4194304]{0:T(1024)(128)(4,1)S(1)}, s32[]{:S(2)}) async-start(s8[8388608]{0:T(1024)(128)(4,1)} %bitcast.220), calls=%async_computation.2 | async-start | bytes 8388608
  349.9 14.6 %slice-start.1 = ((s8[8388608]{0:T(1024)(128)(4,1)}), s8[4194304]{0:T(1024)(128)(4,1)S(1)}, s32[]{:S(2)}) async-start(s8[8388608]{0:T(1024)(128)(4,1)} %bitcast.220), calls=%async_computation.3 | async-start | bytes 8388608
  349.9 13.2 %collective-permute-start.6 = (bf16[128,2048]{1,0:T(8,128)(2,1)S(1)}, bf16[128,2048]{1,0:T(8,128)(2,1)S(1)}, u32[]{:S(2)}, u32[]{:S(2)}) collective-permute-start(bf16[128,2048]{1,0:T(8,128)(2,1)S(1)} %fusion.24), channel_id=1, source_target_pairs={{0,8},{8,16},{16,24},{24,0},{1,9},{9,17},{17,25},{25,1},{2,10},{10... | collective-permute-start | bytes 1572872 | tf_op jit(solution)/shard_map/ppermute | solution.py:889
  359.2 4.0 copy-start.28
  359.2 4.0 copy-start.48
  379.5 3.8 copy-start.14
  379.6 4.0 copy-start.30
  394.5 10.0 %copy-start.46 = (f32[64]{0:T(128)S(1)}, f32[64]{0:T(128)}, u32[]{:S(2)}) copy-start(f32[64]{0:T(128)} %copy-done.45) | copy-start | bytes 772
  394.5 9.9 %collective-permute-start.7 = (bf16[512,256]{0,1:T(8,128)(2,1)S(1)}, bf16[512,256]{0,1:T(8,128)(2,1)S(1)}, u32[]{:S(2)}, u32[]{:S(2)}) collective-permute-start(bf16[512,256]{0,1:T(8,128)(2,1)S(1)} %fusion.36), channel_id=1, source_target_pairs={{0,4},{4,0},{1,5},{5,1},{2,6},{6,2},{3,7},{7,3},{8,12},{12,8},{9,1... | collective-permute-start | bytes 786440 | tf_op jit(solution)/shard_map/ppermute | solution.py:889
  406.0 3.6 copy-start.5
  530.8 2.8 copy-start.12
  530.9 2.6 copy-start.1
  530.9 2.6 copy-start.13
  530.9 2.6 copy-start.44
  531.0 2.7 copy-start.37
  531.3 3.4 copy-start.50
  531.3 3.9 copy-start.49
  531.4 5.5 %copy-start.22 = (f32[4,8,8,512]{3,2,0,1:T(8,128)}, f32[4,8,8,512]{3,2,0,1:T(8,128)S(1)}, u32[]{:S(2)}) copy-start(f32[4,8,8,512]{3,2,0,1:T(8,128)S(1)} %copy.189) | copy-start | bytes 1572868
  (20 other events, 28.7 us)
Sparse Core Ops, SparseCore 0:
  10.9 126.0 all-gather.2
  138.9 68.2 all-gather.4

commit v5 on v4

--- a/solution.py
+++ b/solution.py
@@ -170,75 +170,206 @@
                 self.last[piece] = self.links.send(origin, place, way)
 
 
-def first_kernel(line, x_ref, pos_ref, pack_ref, xs_ref, poss_ref, qkv_ref, send_sems, recv_sems):
+def first_kernel(
+    line,
+    x_ref,
+    table_ref,
+    pack_ref,
+    ff_ref,
+    mix_ref,
+    xs_ref,
+    weight_ref,
+    gain_ref,
+    norm_ref,
+    query_ref,
+    kv_ref,
+    peak_ref,
+    turn_ref,
+    atts_ref,
+    mixs_ref,
+    ffs_ref,
+    x_all,
+    tables,
+    weights,
+    gains,
+    norm,
+    turns,
+    flat,
+    query,
+    kv,
+    peak,
+    att,
+    send_sems,
+    recv_sems,
+):
+    f32, bf16 = jnp.float32, jnp.bfloat16
     links = Links(send_sems, recv_sems, line)
     far = [1, line - 1] + list(range(2, line - 1))
     links.meet(["x", "y", "c"] + far)
-    qkv = NearGather(links, lambda block, place: qkv_ref.at[links.along(-block), place])
-    ring = RingGather(links, x_ref, lambda block, rows: xs_ref.at[block, rows])
     here = links.slot
-    local = [
-        links.keep(x_ref, xs_ref.at[links.z]),
-        links.keep(pos_ref, poss_ref.at[links.z]),
-        links.keep(pack_ref.at[links.z], qkv_ref.at[links.z, here]),
+    span_len, width = x_ref.shape
+    group_len = line * span_len
+    rows_each = ff_ref.shape[1]
+    q_cols = query.shape[1]
+    heads = q_cols // HD
+    local = []
+
+    near = NearGather(links, lambda block, place: weights.at[links.along(-block), place])
+    far_ff = NearGather(links, lambda block, place: ffs_ref.at[links.along(-block), place])
+    ring = RingGather(links, x_ref, lambda block, rows: x_all.at[block, rows])
+    own = [
+        links.keep(x_ref, x_all.at[links.z]),
+        links.keep(table_ref, tables.at[links.z]),
+        links.keep(pack_ref.at[links.z], weights.at[links.z, here]),
     ]
-    turned = {k: links.send(pack_ref.at[links.along(k)], qkv_ref.at[links.z, here], k) for k in far}
-    placed = [links.send(pos_ref, poss_ref.at[links.z], k) for k in far]
+    turned = {k: links.send(pack_ref.at[links.along(k)], weights.at[links.z, here], k) for k in far}
+    placed = [links.send(table_ref, tables.at[links.z], k) for k in far]
     ring.step(0)
-    qkv.offer(0, pack_ref.at[links.z])
+    near.offer(0, pack_ref.at[links.z])
+    local.append(links.keep(ff_ref.at[links.z], ffs_ref.at[links.z, here]))
+    local.append(links.keep(mix_ref, mixs_ref.at[links.z]))
     for k in far:
         turned[k].wait_recv()
-        qkv.offer(k, qkv_ref.at[links.along(-k), here])
+        near.offer(k, weights.at[links.along(-k), here])
     ring.step(1)
     for k in [0] + far:
-        qkv.relay(k, "x" if k < line // 2 else "y")
+        near.relay(k, "x" if k < line // 2 else "y")
+    far_ff.offer(0, ff_ref.at[links.z])
     ring.step(2)
+    turned_ff = {k: links.send(ff_ref.at[links.along(k)], ffs_ref.at[links.z, here], k) for k in far}
     for k in [0] + far:
-        qkv.close(k)
-    ring.step(3)
-    qkv.wait(range(line))
+        near.close(k)
+    for copy in own:
+        copy.wait()
     for copy in placed:
         copy.wait_recv()
-    links.finish()
-    for copy in local:
-        copy.wait()
-
-
-def second_kernel(line, att_ref, mix_ref, ff_ref, atts_ref, mixs_ref, ffs_ref, send_sems, recv_sems):
-    links = Links(send_sems, recv_sems, line)
-    links.meet(["x", "y", "c", 1, line - 1])
-    columns = att_ref.shape[1]
+
+    lane = lax.broadcasted_iota(jnp.int32, (span_len, HD), 1)
+    for block in range(line):
+        table = tables[block]
+        swapped = pltpu.roll(table, HD // 2, 1)
+        rows = slice(block * span_len, (block + 1) * span_len)
+        turns[0, rows] = jnp.where(lane < HD // 2, table, swapped)
+        turns[1, rows] = jnp.where(lane < HD // 2, -swapped, table)
+    local.append(links.keep(turns, turn_ref))
+    near.wait(range(line))
+    for index in range(line * 4):
+        z, q = divmod(index, 4)
+        for which in range(2):
+            lanes = slice(which * HD, (which + 1) * HD)
+            both = [weights[z, 2 * q + c, rows_each : rows_each + 16, lanes].astype(f32) for c in range(2)]
+            gains[which, :, index * HD : (index + 1) * HD] = both[0] + both[1]
+    local.append(links.keep(weights, weight_ref))
+    local.append(links.keep(gains, gain_ref))
+    ring.step(3)
+    local.append(links.keep(x_all, xs_ref))
+
+    def normalise(index, carry):
+        block = index // (span_len // 16)
+        rows = pl.ds(pl.multiple_of(lax.rem(index, span_len // 16) * 16, 16), 16)
+        values = x_all[block, rows].astype(f32)
+        inverse = lax.rsqrt(jnp.mean(values * values, axis=-1, keepdims=True) + epsilon)
+        target = pl.ds(pl.multiple_of(index * 16, 16), 16)
+        norm[target] = (values * inverse * gains[0]).astype(bf16)
+        return carry
+
+    lax.fori_loop(0, group_len // 16, normalise, 0)
+    local.append(links.keep(norm, norm_ref))
+
+    def project(low, high):
+        step = group_len // 2
+        for part in range(2):
+            rows = slice(part * step, (part + 1) * step)
+            total = None
+            for z in range(line):
+                weight = weights[z, :, :rows_each, low:high].reshape(8 * rows_each, high - low)
+                term = jnp.dot(
+                    norm[rows, z * 8 * rows_each : (z + 1) * 8 * rows_each],
+                    weight,
+                    preferred_element_type=f32,
+                )
+                total = term if total is None else total + term
+            flat[rows, low:high] = total
+
+    def turn(values, rows):
+        return values * turns[0, rows] + pltpu.roll(values, HD // 2, 1) * turns[1, rows]
+
+    project(q_cols, q_cols + 2 * HD)
+    for block in range(line):
+        rows = slice(block * span_len, (block + 1) * span_len)
+        kv[0, rows, :HD] = turn(flat[rows, q_cols : q_cols + HD], rows).astype(bf16)
+        kv[0, rows, HD:] = flat[rows, q_cols + HD : q_cols + 2 * HD].astype(bf16)
+    exchange = links.send(kv.at[0], kv.at[1], "x")
+    project(0, q_cols)
+    for block in range(line):
+        rows = slice(block * span_len, (block + 1) * span_len)
+        for head in range(heads):
+            lanes = slice(head * HD, (head + 1) * HD)
+            query[rows, lanes] = turn(flat[rows, lanes], rows).astype(bf16)
+    local.append(links.keep(query, query_ref))
+    exchange.wait_recv()
+    local.append(links.keep(kv, kv_ref))
+
+    scale = 1.0 / math.sqrt(HD)
+    peak[...] = jnp.zeros_like(peak)
+
+    def attend(head, carry):
+        lanes = pl.ds(pl.multiple_of(head * HD, HD), HD)
+        for block in range(line):
+            rows = slice(block * span_len, (block + 1) * span_len)
+            reach = (block + 1) * span_len
+            part = query[rows, lanes]
+            row = lax.broadcasted_iota(jnp.int32, (span_len, reach), 0) + block * span_len
+            column = lax.broadcasted_iota(jnp.int32, (span_len, reach), 1)
+            allowed = (column <= row, column < (block + links.x) * span_len)
+            scores = []
+            for half in range(2):
+                score = lax.dot_general(
+                    part, kv[half, :reach, :HD], (((1,), (1,)), ((), ())), preferred_element_type=f32
+                )
+                scores.append(jnp.where(allowed[half], score * scale, -1e30))
+            top = jnp.maximum(
+                jnp.max(scores[0], axis=-1, keepdims=True), jnp.max(scores[1], axis=-1, keepdims=True)
+            )
+            total, mixed = None, None
+            for half in range(2):
+                weight = jnp.exp(scores[half] - top)
+                count = jnp.sum(weight, axis=-1, keepdims=True)
+                term = jnp.dot(weight.astype(bf16), kv[half, :reach, HD:], preferred_element_type=f32)
+                total = count if total is None else total + count
+                mixed = term if mixed is None else mixed + term
+            att[rows, lanes] = (mixed / total).astype(bf16)
+            spot = lax.broadcasted_iota(jnp.int32, (span_len, HD), 1) == head
+            peak[rows] = jnp.where(spot, top + jnp.log(total), peak[rows])
+        return carry
+
+    lax.fori_loop(0, heads, attend, 0)
+    local.append(links.keep(peak, peak_ref))
 
     def place(block, rows):
-        return atts_ref.at[rows, pl.ds(pl.multiple_of(block * columns, columns), columns)]
-
-    rings = [
-        RingGather(links, att_ref, place),
-        RingGather(links, mix_ref, lambda block, rows: mixs_ref.at[block, rows]),
-    ]
-    near = NearGather(links, lambda block, slot: ffs_ref.at[block, slot])
-    local = [
-        links.keep(att_ref, place(links.z, pl.ds(0, att_ref.shape[0]))),
-        links.keep(mix_ref, mixs_ref.at[links.z]),
-    ]
-
-    def step(number):
-        for ring in rings:
-            ring.step(number)
-
-    step(0)
-    for block in range(line):
-        near.offer(block, ff_ref.at[block])
-        local.append(links.keep(ff_ref.at[block], ffs_ref.at[block, links.slot]))
-    for block in range(line):
-        if block == line // 2:
-            step(1)
-        near.relay(block, "x" if block % 2 == 0 else "y")
-    step(2)
-    for block in range(line):
-        near.close(block)
-    step(3)
-    near.wait(range(line))
+        return atts_ref.at[rows, pl.ds(pl.multiple_of(block * q_cols, q_cols), q_cols)]
+
+    att_ring = RingGather(links, att, place)
+    mix_ring = RingGather(links, mix_ref, lambda block, rows: mixs_ref.at[block, rows])
+    local.append(links.keep(att, place(links.z, pl.ds(0, group_len))))
+    att_ring.step(0)
+    for k in far:
+        turned_ff[k].wait_recv()
+        far_ff.offer(k, ffs_ref.at[links.along(-k), here])
+    far_ff.relay(0, "x")
+    far_ff.close(0)
+    att_ring.step(1)
+    mix_ring.step(0)
+    for k in far:
+        far_ff.relay(k, "x" if k < line // 2 else "y")
+    att_ring.step(2)
+    mix_ring.step(1)
+    for k in far:
+        far_ff.close(k)
+    att_ring.step(3)
+    mix_ring.step(2)
+    mix_ring.step(3)
+    far_ff.wait(range(line))
     links.finish()
     for copy in local:
         copy.wait()
@@ -464,31 +595,46 @@
     )(*arguments)
 
 
-def first_gather(tokens, positions, pack, line):
+def forward_call(tokens, table, pack, pack_ff, mixed, line):
+    span_len, width = tokens.shape
+    group_len = line * span_len
+    rows_each = pack_ff.shape[1]
+    qkv_cols = pack.shape[2]
+    q_cols = qkv_cols - 2 * HD
+    f32, bf16 = jnp.float32, jnp.bfloat16
+    outs = (
+        ((line, span_len, width), bf16),
+        ((line, 8) + pack.shape[1:], bf16),
+        ((2, 16, width), f32),
+        ((group_len, width), bf16),
+        ((group_len, q_cols), bf16),
+        ((2, group_len, 2 * HD), bf16),
+        ((group_len, HD), f32),
+        ((2, group_len, HD), f32),
+        ((group_len, line * q_cols), bf16),
+        ((line, span_len, width), bf16),
+        ((line, 8) + pack_ff.shape[1:], bf16),
+    )
     return link_call(
         functools.partial(first_kernel, line),
         0,
-        64,
-        (
-            jax.ShapeDtypeStruct((line,) + tokens.shape, tokens.dtype),
-            jax.ShapeDtypeStruct((line,) + positions.shape, positions.dtype),
-            jax.ShapeDtypeStruct((line, 8) + pack.shape[1:], pack.dtype),
-        ),
-        (tokens, positions, pack),
-    )
-
-
-def second_gather(attended, mixed, pack, line):
-    return link_call(
-        functools.partial(second_kernel, line),
-        1,
-        96,
-        (
-            jax.ShapeDtypeStruct((attended.shape[0], line * attended.shape[1]), attended.dtype),
-            jax.ShapeDtypeStruct((line,) + mixed.shape, mixed.dtype),
-            jax.ShapeDtypeStruct((line, 8) + pack.shape[1:], pack.dtype),
-        ),
-        (attended, mixed, pack),
+        176,
+        tuple(jax.ShapeDtypeStruct(*out) for out in outs),
+        (tokens, table, pack, pack_ff, mixed),
+        scratch=[
+            pltpu.VMEM((line, span_len, width), bf16),
+            pltpu.VMEM((line,) + table.shape, f32),
+            pltpu.VMEM((line, 8) + pack.shape[1:], bf16),
+            pltpu.VMEM((2, 16, width), f32),
+            pltpu.VMEM((group_len, width), bf16),
+            pltpu.VMEM((2, group_len, HD), f32),
+            pltpu.VMEM((group_len, qkv_cols), f32),
+            pltpu.VMEM((group_len, q_cols), bf16),
+            pltpu.VMEM((2, group_len, 2 * HD), bf16),
+            pltpu.VMEM((group_len, HD), f32),
+            pltpu.VMEM((group_len, q_cols), bf16),
+        ],
+        vmem=48,
     )
 
 
@@ -894,96 +1040,56 @@
     def pick(values, index, dim):
         return lax.dynamic_index_in_dim(values, index, dim, keepdims=False)
 
-    def back_order(blocks):
-        return jnp.take(blocks, (place - jnp.arange(line, dtype=jnp.int32)) % line, axis=0)
-
-    def ring_sum(blocks):
-        total = pick(blocks, (place - 1) % line, 0)
-        for hop in range(1, line):
-            own = pick(blocks, (place - 1 - hop) % line, 0)
-            total = shift(total, "z", 1).astype(f32) + own.astype(f32)
-            if hop < line - 1:
-                total = total.astype(bf16)
-        return total
-
     def by_columns(weight, columns):
         return weight.reshape(rows_each, line, columns).transpose(1, 0, 2)
 
-    def turn(pack):
-        got = [pick(pack, place, 0)]
-        for k in range(1, line):
-            got.append(shift(pick(pack, (place + k) % line, 0), "z", k))
-        return back_order(jnp.stack(got))
-
-    gains = jnp.stack([attn_gain, mlp_gain] + [jnp.zeros_like(attn_gain)] * (HD - 2), axis=1)
-    pack_attn = jnp.concatenate(
-        [
-            by_columns(w_query, q_cols),
-            by_columns(w_key, HD),
-            by_columns(w_value, HD),
-            jnp.broadcast_to(gains[None], (line,) + gains.shape),
-        ],
-        axis=2,
-    )
-    place_rows = jnp.broadcast_to(positions[0].astype(f32)[None, :], (8, span_len))
-    x_blocks, place_blocks, near_w = first_gather(tokens[0], place_rows, pack_attn, line)
-    inputs = x_blocks.reshape(group_len, model_width).astype(f32)
-    token_pos = place_blocks[:, 0].reshape(group_len)
-    near_w = near_w.reshape(model_width, -1)
-    qkv_w = near_w[:, : q_cols + 2 * HD]
-    gain_rows = near_w[:, q_cols + 2 * HD : q_cols + 2 * HD + 2].astype(f32).T
-    gain_one, gain_two = gain_rows[:1], gain_rows[1:]
-
     out_w = lax.all_gather(w_out, ("z", "x", "y", "c"), axis=0, tiled=True)
     down_w = lax.all_gather(w_down, ("x", "y", "c"), axis=0, tiled=True)
-    pack_ff = jnp.concatenate([by_columns(w_gate, ff_cols), by_columns(w_up, ff_cols)], axis=2)
-    turned_ff = turn(after(pack_ff, x_blocks))
-
     own_x = tokens[0].astype(f32)
     keep = keep_mask[0].astype(f32)
     group_match = group_ids[0][:, None] == jnp.arange(exit_scale.shape[0], dtype=jnp.int32)[None, :]
     token_scale = jnp.sum(jnp.where(group_match, exit_scale[None, :], 0.0), axis=1, keepdims=True)
     upstream = out_grad[0].astype(f32) * token_scale
 
-    inside = jnp.arange(span_len, dtype=jnp.int32)
-    block_first = jnp.arange(line, dtype=jnp.int32) * (2 * span_len)
-
-    def token_index(which):
-        return (block_first[:, None] + which * span_len + inside[None, :]).reshape(group_len)
-
-    inverse_all = lax.rsqrt(jnp.mean(inputs * inputs, axis=-1, keepdims=True) + epsilon)
-    first_norm = (inputs * inverse_all * gain_one).astype(bf16)
-    qkv = jnp.dot(first_norm, qkv_w, preferred_element_type=f32)
-    queries = rotate(qkv[:, :q_cols].reshape(group_len, heads, HD), token_pos, 1.0).astype(bf16)
-    own_kv = jnp.concatenate(
-        [
-            rotate(qkv[:, q_cols : q_cols + HD].reshape(group_len, 1, HD), token_pos, 1.0)[:, 0],
-            qkv[:, q_cols + HD :],
-        ],
-        axis=1,
-    ).astype(bf16)
-    both_kv = jnp.concatenate([own_kv, shift(own_kv, "x", 1)], axis=0)
+    core = lax.axis_index("c")
+    gain_row = jnp.zeros((q_cols + 2 * HD,), bf16)
+    gain_row = lax.dynamic_update_slice_in_dim(gain_row, attn_gain, core * rows_each, 0)
+    gain_row = lax.dynamic_update_slice_in_dim(gain_row, mlp_gain, HD + core * rows_each, 0)
+    gain_rows = jnp.broadcast_to(gain_row, (line, 16, gain_row.shape[0]))
+    pack_attn = jnp.concatenate(
+        [by_columns(w_query, q_cols), by_columns(w_key, HD), by_columns(w_value, HD)], axis=2
+    )
+    pack_attn = jnp.concatenate([pack_attn, gain_rows], axis=1)
+    pack_ff = jnp.concatenate([by_columns(w_gate, ff_cols), by_columns(w_up, ff_cols)], axis=2)
+    freqs = 10000.0 ** (-2.0 * jnp.arange(HD // 2, dtype=f32) / HD)
+    angles = positions[0].astype(f32)[:, None] * freqs[None, :]
+    table = jnp.concatenate([jnp.cos(angles), jnp.sin(angles)], axis=1)
+    (
+        x_blocks,
+        near_w,
+        gain_all,
+        first_norm,
+        queries,
+        both_kv,
+        log_total,
+        turns,
+        attended_rows,
+        mixed_grad,
+        ff_w,
+    ) = forward_call(tokens[0], table, pack_attn, pack_ff, (keep * upstream).astype(bf16), line)
+    inputs = x_blocks.reshape(group_len, model_width).astype(f32)
+    qkv_w = near_w[:, :, :rows_each].reshape(model_width, q_cols + 2 * HD)
+    gain_one, gain_two = gain_all[0, :1], gain_all[1, :1]
+    mixed_grad = mixed_grad.reshape(group_len, model_width)
+    ff_w = ff_w.reshape(model_width, 2 * ff_cols)
+    queries = queries.reshape(group_len, heads, HD)
+    both_kv = both_kv.reshape(2 * group_len, 2 * HD)
     keys = both_kv[:, :HD]
     values = both_kv[:, HD:]
-    query_index = token_index(side)
-    key_index = jnp.concatenate([query_index, token_index(1 - side)])
-    scores = jnp.einsum("tgd,jd->gtj", queries, keys, preferred_element_type=f32) * score_scale
-    allowed = key_index[None, :] <= query_index[:, None]
-    scores = jnp.where(allowed, scores, -1e30)
-    weights = jnp.exp(scores - jnp.max(scores, axis=-1, keepdims=True))
-    probabilities = weights / jnp.sum(weights, axis=-1, keepdims=True)
-    rounded_probs = probabilities.astype(bf16)
-    attended = jnp.einsum("gtj,jd->tgd", rounded_probs, values, preferred_element_type=f32)
-    own_attended = attended.reshape(group_len, q_cols).astype(bf16)
 
     def own_rows(values):
         return lax.dynamic_slice_in_dim(values, place * span_len, span_len, 0)
 
-    attended_rows, mixed_grad, ff_w = second_gather(
-        own_attended, (keep * upstream).astype(bf16), turned_ff, line
-    )
-    mixed_grad = mixed_grad.reshape(group_len, model_width)
-    ff_w = ff_w.reshape(model_width, 2 * ff_cols)
     branch = jnp.dot(attended_rows, out_w, preferred_element_type=f32)
     middle_all = inputs + keep * branch
     inverse_mid = lax.rsqrt(jnp.mean(middle_all * middle_all, axis=-1, keepdims=True) + epsilon)
@@ -1020,21 +1126,46 @@
     branch_grad = (keep * middle_grad).astype(bf16)
     own_grad = against(branch_grad, out_w).astype(bf16)
     attended_grad = turn_rows(own_grad, line).reshape(group_len, heads, HD)
-    mixed_parts = jnp.dot(hidden, down_w, preferred_element_type=f32)
-    mixed = ring_sum(split(after(mixed_parts, norm_grad)))
-    output = (middle + keep * mixed).astype(bf16)
+    mixed_parts = split(jnp.dot(hidden, after(down_w, norm_grad), preferred_element_type=f32))
+
+    def mixed_hop(total, hop, first):
+        total = after(shift(total.astype(bf16), "z", 1), first).astype(f32)
+        return total + pick(mixed_parts, (place - 1 - hop) % line, 0).astype(f32)
+
+    mixed = mixed_hop(pick(mixed_parts, (place - 1) % line, 0), 1, attended_grad)
+    inside = jnp.arange(span_len, dtype=jnp.int32)
+    block_first = jnp.arange(line, dtype=jnp.int32) * (2 * span_len)
+
+    def token_index(which):
+        return (block_first[:, None] + which * span_len + inside[None, :]).reshape(group_len)
+
+    query_index = token_index(side)
+    key_index = jnp.concatenate([query_index, token_index(1 - side)])
+    allowed = key_index[None, :] <= query_index[:, None]
+    scores = jnp.einsum("tgd,jd->gtj", queries, keys, preferred_element_type=f32) * score_scale
+    probabilities = jnp.where(allowed, jnp.exp(scores - log_total[:, :heads].T[..., None]), 0.0)
+    rounded_probs = probabilities.astype(bf16)
     prob_grad = jnp.einsum("tgd,jd->gtj", attended_grad, values, preferred_element_type=f32)
+    own_attended = lax.dynamic_slice_in_dim(attended_rows, place * q_cols, q_cols, 1)
+    attended = own_attended.reshape(group_len, heads, HD).astype(f32)
     delta = jnp.sum(attended_grad.astype(f32) * attended, axis=-1).T[..., None]
     score_grad = (probabilities * (prob_grad - delta)).astype(bf16)
+    for hop in range(2, line - 1):
+        mixed = mixed_hop(mixed, hop, score_grad)
     query_back = jnp.einsum("gtj,jd->tgd", score_grad, keys, preferred_element_type=f32) * score_scale
     key_back = jnp.einsum("gtj,tgd->jd", score_grad, queries, preferred_element_type=f32) * score_scale
     value_back = jnp.einsum("gtj,tgd->jd", rounded_probs, attended_grad, preferred_element_type=f32)
     kv_back = jnp.concatenate([key_back, value_back], axis=1)
     kv_back = kv_back[:group_len] + shift(kv_back[group_len:].astype(bf16), "x", 1).astype(f32)
+
+    def turn_back(vectors):
+        swapped = jnp.concatenate([vectors[..., HD // 2 :], vectors[..., : HD // 2]], axis=-1)
+        return vectors * turns[0][:, None] - swapped * turns[1][:, None]
+
     qkv_grad = jnp.concatenate(
         [
-            rotate(query_back, token_pos, -1.0).reshape(group_len, q_cols),
-            rotate(kv_back[:, None, :HD], token_pos, -1.0)[:, 0],
+            turn_back(query_back).reshape(group_len, q_cols),
+            turn_back(kv_back[:, None, :HD])[:, 0],
             kv_back[:, HD:],
         ],
         axis=1,
@@ -1048,10 +1179,12 @@
     input_norm_grad, ff_back, out_back, qkv_back = last_sum(
         split(against(qkv_grad, qkv_w)), by_place(grad_ff), by_place(grad_out), by_place(grad_qkv), line
     )
+    mixed = mixed_hop(mixed, line - 1, input_norm_grad)
+    output = (middle + keep * mixed).astype(bf16)
     ff_back = ff_back.astype(f32)
     qkv_back = qkv_back.astype(f32)
     grad_out = jnp.sum(out_back.astype(f32), axis=0)
-    inverse_one = own_rows(inverse_all)
+    inverse_one = lax.rsqrt(jnp.mean(own_x * own_x, axis=-1, keepdims=True) + epsilon)
     scaled_one = gain_one * input_norm_grad
     input_grad = (
         middle_grad

time: 552 us -> 590 us (1.069)
  Pallas kernels: 323 us -> 389 us
  other arithmetic: 40.4 us -> 25.5 us
  local copies, waits for them, and re-layouts: 34.7 us -> 25.7 us
  starting transfers between devices: 11.4 us -> 3.99 us
    pallas_call x5 -> x4, Pallas kernels: 323 us -> 389 us  [link_call(): pl.pallas_call(kernel, out_shape=shapes, in_specs=specs[:len(arguments)],...]
    unnamed x122 -> x85, local copies, waits for them, and re-layouts: 18.9 us -> 7.44 us
    sub x1 -> x0, matrix products: 8.01 us -> none  [line_body(): weights = jnp.exp(scores - jnp.max(scores, axis=-1, keepdims=True))]
    ppermute x8 -> x4, starting transfers between devices: 11.4 us -> 3.91 us  [shift(): lax.ppermute(values, axis, [(i, (i + step) % size) for i in range(size)])]
    ppermute x8 -> x4, waiting for transfers between devices: 27.2 us -> 27.8 us  [shift(): lax.ppermute(values, axis, [(i, (i + step) % size) for i in range(size)])]
  transfers between devices with their start and end apart: 10 -> 6, of which waited for: 3 -> 2; matrix products, arithmetic and copies ran while one was open for 16% -> 14% of each run, Pallas kernels for 29% -> 58%
where the time goes in v5:
time: 590 us; the launch traced here: 580 us
  Pallas kernels  389 us (66%)
  matrix products  91.7 us (16%)
  waiting for transfers between devices  29.2 us (5%)
  local copies, waits for them, and re-layouts  25.7 us (4%)
  other arithmetic  25.5 us (4%)
  between operations  15.8 us (3%)
    pallas_call x4, Pallas kernels, link_call(): pl.pallas_call(kernel, out_shape=shapes, in_specs=specs[:len(arguments)],...  389 us
    ppermute x4, waiting for transfers between devices, shift(): lax.ppermute(values, axis, [(i, (i + step) % size) for i in range(size)])  27.8 us
    dot_general x4, matrix products, against(): lax.dot_general(left, right, (((1,), (1,)), ((), ())), preferred_element_...  26.2 us
    dot_general x4, matrix products, over_rows(): lax.dot_general(left, right, (((0,), (0,)), ((), ())), preferred_element_...  23.1 us
  transfers between devices with their start and end apart: 6, of which 2 were waited for; matrix products, arithmetic and copies ran while one was open for 14% of the time, Pallas kernels for 58%

profile of v5, /device:TPU:0, one launch (start us, length us, event | category | flops | bytes accessed | tf_op | source)
XLA Modules:
  0.0 580.4 jit_solution(16691442371298637620)
XLA Ops:
  8.8 1.0 copy.147
  16.2 215.4 %shard_map.230 = (bf16[4,128,2048]{2,1,0:T(8,128)(2,1)}, bf16[4,8,80,768]{3,2,1,0:T(8,128)(2,1)}, f32[2,16,2048]{2,1,0:T(8,128)S(1)}, bf16[512,2048]{1,0:T(8,128...) custom-call(bf16[128,2048]{1,0:T(8,128)(2,1)S(1)} %bitcast.183, ...), custom_call_target="tpu_custom_call" | custom-call | tf_op jit(solution)/shard_map/pallas_call | solution.py:585
  231.6 2.2 dynamic-slice_convert_fusion
  233.8 2.6 reshape.242
  236.3 1.0 copy.127
  238.3 4.0 slice.89
  242.5 1.2 broadcast_compare_fusion
  243.6 4.5 fusion.37
  248.2 9.3 %multiply_reduce_fusion = (f32[512]{0:T(512)S(1)}, f32[512,2048]{1,0:T(8,128)S(1)}) fusion(bf16[512,2048]{1,0:T(8,128)(2,1)} %get-tuple-element.34, bf16[2048,2048]{1,0:T(8,128)(2,1)} %all-gather.3.cloned.1.call-done, f32[]{:T(128)} %bitcast.7, bf16[512,2048]{1,0:T(8,128)(2,1)} %bitcast.226), kind=kOutput, calls=%fused_computation.12 | convolution fusion | flops 4300209664 | bytes 16779268 | tf_op jit(solution)/shard_map/dot_general | solution.py:1093
  257.4 2.0 copy-done.12
  259.4 11.5 %fusion.47 = f32[512,2816]{1,0:T(8,128)} fusion(bf16[2048,2816]{1,0:T(8,128)(2,1)} %bitcast.220, f32[512,2048]{1,0:T(8,128)S(1)} %get-tuple-element.83, f32[2048]{0:T(1024)S(1)} %bitcast.216, f32[512]{0:T(512)S(1)} %add_rsqrt_fusion), kind=kOutput, calls=%fused_computation.132 | convolution fusion | flops 5908725760 | bytes 21506048 | tf_op jit(solution)/shard_map/dot_general | solution.py:1100
  270.9 10.5 %multiply_convert_fusion.2 = (bf16[512,1408]{1,0:T(8,128)(2,1)S(1)}, bf16[512,1408]{1,0:T(8,128)(2,1)}, bf16[512,1408]{1,0:T(8,128)(2,1)S(1)}) fusion(f32[512,2816]{1,0:T(8,128)} %fusion.47, bf16[512,2048]{1,0:T(8,128)(2,1)} %bitcast.224, bf16[1408,2048]{1,0:T(8,128)(2,1)} %all-gather.5.cloned.1.call-done), kind=kOutput, calls=%fused_computation.21 | convolution fusion | flops 2963603456 | bytes 17956864 | tf_op jit(solution)/shard_map/dot_general | solution.py:53
  281.4 3.4 convolution_convert_fusion.1
  284.9 9.6 %convolution_convert_fusion.5 = bf16[512,2048]{1,0:T(8,128)(2,1)S(1)} fusion(bf16[2048,2816]{1,0:T(8,128)(2,1)} %bitcast.221, bf16[512,1408]{1,0:T(8,128)(2,1)} %get-tuple-element.64, bf16[512,1408]{1,0:T(8,128)(2,1)S(1)} %get-tuple-element.63), kind=kOutput, calls=%fused_computation.17 | convolution fusion | flops 5912395776 | bytes 16515072 | tf_op jit(solution)/shard_map/dot_general | solution.py:53
  294.5 39.4 %shard_map.231 = (f32[128,2048]{1,0:T(8,128)S(1)}, bf16[176,2048]{1,0:T(8,128)(2,1)S(1)}) custom-call(bf16[4,128,2048]{2,1,0:T(8,128)(2,1)S(1)} %bitcast.184, bf16[2,2,2,176,2048]{4,3,2,1,0:T(8,128)(2,1)S(1)} %bitcast.182), custom_call_target="tpu_custom_call" | custom-call | tf_op jit(solution)/shard_map/pallas_call | solution.py:585
  333.9 1.4 multiply_reduce_fusion.4
  335.4 1.6 fusion.28
  337.0 2.9 convolution_convert_fusion.7.rows_ref
  339.9 15.0 %shard_map.232 = bf16[4,128,512]{2,1,0:T(8,128)(2,1)S(1)} custom-call(bf16[128,2048]{1,0:T(8,128)(2,1)S(1)} %convolution_convert_fusion.7.rows_ref), custom_call_target="tpu_custom_call" | custom-call | tf_op jit(solution)/shard_map/pallas_call | solution.py:585
  355.1 1.1 copy.109
  356.2 1.9 multiply_reduce_fusion.3
  358.2 5.3 fusion.9
  363.5 5.1 fusion.1
  368.6 1.8 broadcast_multiply_fusion
  370.4 1.2 fusion.12
  372.4 1.0 copy-done.2
  373.4 6.8 %convolution_convert_fusion.2 = bf16[2048,2048]{1,0:T(8,128)(2,1)} fusion(bf16[512,2048]{1,0:T(8,128)(2,1)} %get-tuple-element.34, s32[]{:T(128)S(6)} %select_n.57, f32[128,2048]{1,0:T(8,128)S(1)} %copy-done.2, f32[]{:T(128)} %bitcast.7), kind=kOutput, calls=%fused_computation.8 | convolution fusion | flops 1078460416 | bytes 9961988 | tf_op jit(solution)/shard_map/dot_general | solution.py:47
  380.2 1.7 collective-permute-start.3
  382.0 9.4 %convolution_convert_fusion = bf16[2048,2816]{1,0:T(8,128)(2,1)} fusion(bf16[512,2816]{1,0:T(8,128)(2,1)S(1)} %pad_maximum_fusion, f32[512,2048]{1,0:T(8,128)S(1)} %copy-done.13, f32[2048]{0:T(1024)S(1)} %bitcast.219, f32[512]{0:T(512)S(1)} %add_rsqrt_fusion), kind=kOutput, calls=%fused_computation | convolution fusion | flops 5914492928 | bytes 18622464 | tf_op jit(solution)/shard_map/dot_general | solution.py:47
  391.3 3.6 convolution_convert_fusion.6
  395.0 0.9 dynamic-slice_bitcast_fusion
  395.9 1.3 convert_element_type.210
  397.2 1.0 fusion.48
  399.3 1.1 copy.103
  400.4 1.0 copy.111
  401.5 1.7 fusion.19
  403.4 3.6 convolution_convert_fusion.3
  407.0 3.2 convolution_convert_fusion.4
  410.2 118.8 %shard_map.233 = (f32[128,2048]{1,0:T(8,128)}, bf16[4,64,2816]{2,1,0:T(8,128)(2,1)}, bf16[4,64,2048]{2,1,0:T(8,128)(2,1)}, bf16[4,64,768]{2,1,0:T(8,128)(2,1)}) custom-call(bf16[4,128,2048]{2,1,0:T(8,128)(2,1)} %bitcast.200, bf16[4,2,2,2,64,2816]{5,4,3,2,1,0:T(8,128)(2,1)} %bitcast.189, bf16[4,2,2,2,64,2048]{5,4,3,2,1,0:T(8,128)(2,1)} %bitcast.188, ...), custom_call_target="tpu_custom_call" | custom-call | tf_op jit(solution)/shard_map/pallas_call | solution.py:585
  529.0 1.6 convert_element_type.207
  531.0 1.1 copy-done.9
  535.2 1.0 convert_reduce_fusion
  537.1 1.2 fusion.24
  538.3 2.1 collective-permute-start.1
  541.9 13.7 %collective-permute-done.1 = bf16[128,2048]{1,0:T(8,128)(2,1)S(1)} collective-permute-done((bf16[128,2048]{1,0:T(8,128)(2,1)S(1)}, bf16[128,2048]{1,0:T(8,128)(2,1)S(1)}, u32[]{:S(2)}, u32[]{:S(2)}) %collective-permute-start.1) | collective-permute-done | bytes 524320 | tf_op jit(solution)/shard_map/ppermute | solution.py:1035
  555.8 1.1 fusion.32
  557.0 14.1 %collective-permute-done.2 = bf16[128,2048]{1,0:T(8,128)(2,1)S(1)} collective-permute-done((bf16[128,2048]{1,0:T(8,128)(2,1)S(1)}, bf16[128,2048]{1,0:T(8,128)(2,1)S(1)}, u32[]{:S(2)}, u32[]{:S(2)}) %collective-permute-start.2) | collective-permute-done | bytes 524320 | tf_op jit(solution)/shard_map/ppermute | solution.py:1035
  571.0 2.3 fusion.29
  (145 shorter events, 16.6 us)
Async XLA Ops:
  7.2 7.7 %copy-start.10 = (bf16[64,5632]{1,0:T(8,128)(2,1)S(1)}, bf16[64,5632]{1,0:T(8,128)(2,1)}, u32[]{:S(2)}) copy-start(bf16[64,5632]{1,0:T(8,128)(2,1)} %param.22) | copy-start | bytes 2162692
  7.2 7.7 %copy-start.8 = (bf16[64,5632]{1,0:T(8,128)(2,1)S(1)}, bf16[64,5632]{1,0:T(8,128)(2,1)}, u32[]{:S(2)}) copy-start(bf16[64,5632]{1,0:T(8,128)(2,1)} %param.23) | copy-start | bytes 2162692
  7.2 241.0 %all-gather.3.cloned.1.call-start = ((), (), s32[]{:S(2)}) async-start(), calls=%async_computation | async-start | bytes 8650752 | tf_op jit(solution)/shard_map/all_gather | solution.py:1046
  7.9 263.0 %all-gather.5.cloned.1.call-start = ((), (), s32[]{:S(2)}) async-start(), calls=%async_computation.1 | async-start | bytes 6488064 | tf_op jit(solution)/shard_map/all_gather | solution.py:1047
  14.9 1.0 copy-start.14
  14.9 1.2 copy-start
  238.3 5.3 copy-start.15
  257.4 2.0 copy-start.12
  270.9 10.5 %copy-start.34 = (bf16[4,128,2048]{2,1,0:T(8,128)(2,1)S(1)}, bf16[4,128,2048]{2,1,0:T(8,128)(2,1)}, u32[]{:S(2)}) copy-start(bf16[4,128,2048]{2,1,0:T(8,128)(2,1)} %get-tuple-element.37) | copy-start | bytes 6291460
  281.4 3.4 copy-start.35
  281.4 3.5 copy-start.20
  281.4 55.5 %slice-start = ((s8[8388608]{0:T(1024)(128)(4,1)}), s8[4194304]{0:T(1024)(128)(4,1)S(1)}, s32[]{:S(2)}) async-start(s8[8388608]{0:T(1024)(128)(4,1)} %bitcast.190), calls=%async_computation.2 | async-start | bytes 8388608
  284.9 52.0 %slice-start.1 = ((s8[8388608]{0:T(1024)(128)(4,1)}), s8[4194304]{0:T(1024)(128)(4,1)S(1)}, s32[]{:S(2)}) async-start(s8[8388608]{0:T(1024)(128)(4,1)} %bitcast.190), calls=%async_computation.3 | async-start | bytes 8388608
  337.0 2.9 copy-start.1
  358.1 5.3 copy-start.26
  358.1 5.3 copy-start.27
  368.6 1.8 copy-start.16
  370.4 1.4 copy-start.21
  370.4 1.8 copy-start.22
  372.2 1.2 copy-start.2
  373.4 8.5 %copy-start.13 = (f32[512,2048]{1,0:T(8,128)S(1)}, f32[512,2048]{1,0:T(8,128)}, u32[]{:S(2)}) copy-start(f32[512,2048]{1,0:T(8,128)} %copy-done.12) | copy-start | bytes 12582916
  380.2 11.1 %slice-start.2 = ((s8[5767168]{0:T(1024)(128)(4,1)}), s8[4194304]{0:T(1024)(128)(4,1)S(1)}, s32[]{:S(2)}) async-start(s8[5767168]{0:T(1024)(128)(4,1)} %bitcast.222), calls=%async_computation.4 | async-start | bytes 8388608
  380.2 11.1 %slice-start.3 = ((s8[5767168]{0:T(1024)(128)(4,1)}), s8[1572864]{0:T(1024)(128)(4,1)S(1)}, s32[]{:S(2)}) async-start(s8[5767168]{0:T(1024)(128)(4,1)} %bitcast.222), calls=%async_computation.5 | async-start | bytes 3145728
  380.2 11.1 %copy-start.36 = (bf16[512,1408]{1,0:T(8,128)(2,1)S(1)}, bf16[512,1408]{1,0:T(8,128)(2,1)}, u32[]{:S(2)}) copy-start(bf16[512,1408]{1,0:T(8,128)(2,1)} %copy-done.35) | copy-start | bytes 4325380
  380.2 18.0 %collective-permute-start.3 = (bf16[512,256]{1,0:T(8,128)(2,1)S(1)}, bf16[512,256]{1,0:T(8,128)(2,1)S(1)}, u32[]{:S(2)}, u32[]{:S(2)}) collective-permute-start(bf16[512,256]{1,0:T(8,128)(2,1)S(1)} %fusion.33), channel_id=1, source_target_pairs={{0,4},{4,0},{1,5},{5,1},{2,6},{6,2},{3,7},{7,3},{8,12},{12,8},{9,1... | collective-permute-start | bytes 786440 | tf_op jit(solution)/shard_map/ppermute | solution.py:1035
  395.0 3.3 copy-start.18
  395.9 141.2 %collective-permute-start = (bf16[128,2048]{1,0:T(8,128)(2,1)}, bf16[128,2048]{1,0:T(8,128)(2,1)}, u32[]{:S(2)}, u32[]{:S(2)}) collective-permute-start(bf16[128,2048]{1,0:T(8,128)(2,1)} %dynamic-slice_bitcast_fusion), channel_id=1, source_target_pairs={{0,8},{8,16},{16,24},{24,0},{1,9},{9,17},{17,25},{25,1},{2,10},{10... | collective-permute-start | bytes 1572872 | tf_op jit(solution)/shard_map/ppermute | solution.py:1035
  398.2 3.3 copy-start.5
  398.2 3.3 copy-start.23
  401.5 1.9 copy-start.33
  403.4 3.6 copy-start.7
  530.8 1.3 copy-start.9
  530.9 2.0 copy-start.3
  530.9 1.7 copy-start.11
  532.3 1.1 copy-start.28
  532.4 2.2 copy-start.4
  532.4 1.8 copy-start.6
  532.6 2.0 copy-start.32
  532.6 2.5 copy-start.24
  533.4 2.8 copy-start.29
  533.4 3.6 copy-start.19
  534.6 5.8 %copy-start.25 = (bf16[64,2048]{1,0:T(8,128)(2,1)S(1)}, bf16[64,2048]{1,0:T(8,128)(2,1)}, u32[]{:S(2)}) copy-start(bf16[64,2048]{1,0:T(8,128)(2,1)} %param.17) | copy-start | bytes 786436
  535.2 5.4 copy-start.30
  535.2 6.2 %copy-start.31 = (bf16[64]{0:T(256)(128)(2,1)S(1)}, bf16[64]{0:T(256)(128)(2,1)}, u32[]{:S(2)}) copy-start(bf16[64]{0:T(256)(128)(2,1)} %param.16) | copy-start | bytes 388
  536.2 20.8 %copy-start.17 = (f32[4,8,8,512]{3,2,0,1:T(8,128)}, f32[4,8,8,512]{3,2,0,1:T(8,128)S(1)}, u32[]{:S(2)}) copy-start(f32[4,8,8,512]{3,2,0,1:T(8,128)S(1)} %copy.133) | copy-start | bytes 1572868
  538.3 17.3 %collective-permute-start.1 = (bf16[128,2048]{1,0:T(8,128)(2,1)S(1)}, bf16[128,2048]{1,0:T(8,128)(2,1)S(1)}, u32[]{:S(2)}, u32[]{:S(2)}) collective-permute-start(bf16[128,2048]{1,0:T(8,128)(2,1)S(1)} %fusion.24), channel_id=1, source_target_pairs={{0,8},{8,16},{16,24},{24,0},{1,9},{9,17},{17,25},{25,1},{2,10},{10... | collective-permute-start | bytes 1572872 | tf_op jit(solution)/shard_map/ppermute | solution.py:1035
  555.7 15.3 %collective-permute-start.2 = (bf16[128,2048]{1,0:T(8,128)(2,1)S(1)}, bf16[128,2048]{1,0:T(8,128)(2,1)S(1)}, u32[]{:S(2)}, u32[]{:S(2)}) collective-permute-start(bf16[128,2048]{1,0:T(8,128)(2,1)S(1)} %fusion.23), channel_id=1, source_target_pairs={{0,8},{8,16},{16,24},{24,0},{1,9},{9,17},{17,25},{25,1},{2,10},{10... | collective-permute-start | bytes 1572872 | tf_op jit(solution)/shard_map/ppermute | solution.py:1035
Sparse Core Ops, SparseCore 0:
  10.9 131.2 all-gather.2
  144.0 62.7 all-gather.4

commit v6 on v5

--- a/solution.py
+++ b/solution.py
@@ -353,21 +353,22 @@
     mix_ring = RingGather(links, mix_ref, lambda block, rows: mixs_ref.at[block, rows])
     local.append(links.keep(att, place(links.z, pl.ds(0, group_len))))
     att_ring.step(0)
+    mix_ring.step(0)
     for k in far:
         turned_ff[k].wait_recv()
         far_ff.offer(k, ffs_ref.at[links.along(-k), here])
     far_ff.relay(0, "x")
     far_ff.close(0)
+    far_ff.relay(far[0], "x")
     att_ring.step(1)
-    mix_ring.step(0)
-    for k in far:
+    mix_ring.step(1)
+    for k in far[1:]:
         far_ff.relay(k, "x" if k < line // 2 else "y")
     att_ring.step(2)
-    mix_ring.step(1)
+    mix_ring.step(2)
     for k in far:
         far_ff.close(k)
     att_ring.step(3)
-    mix_ring.step(2)
     mix_ring.step(3)
     far_ff.wait(range(line))
     links.finish()
@@ -385,13 +386,15 @@
 
 
 class NearSum:
-    def __init__(self, links, source, own, from_core, from_first, from_second, first):
+    def __init__(self, links, source, own, from_core, from_first, from_second, first, in_place=False):
         self.links, self.source, self.own, self.first = links, source, own, first
+        self.in_place = in_place
         self.from_core, self.from_first, self.from_second = from_core, from_first, from_second
 
     def start(self):
         links = self.links
-        self.local = links.keep(self.source(links.c), self.own)
+        if not self.in_place:
+            self.local = links.keep(self.source(links.c), self.own)
         self.copy = links.send(self.source(1 - links.c), self.from_core, "c")
 
     def add(self, target, values):
@@ -400,7 +403,8 @@
     def core_done(self):
         links = self.links
         self.copy.wait_recv()
-        self.local.wait()
+        if not self.in_place:
+            self.local.wait()
         for x in range(2):
             for y in range(2):
                 self.add(self.own.at[x, y], self.from_core.at[x, y])
@@ -459,8 +463,9 @@
                 if number == links.line - 1:
                     self.total[where] = total
                     continue
-                self.made[number - 1, where] = total.astype(self.made.dtype)
-                source = self.made.at[number - 1, where]
+                made, place = (self.parts, block) if self.made is None else (self.made, number - 1)
+                made[place, where] = total.astype(made.dtype)
+                source = made.at[place, where]
             self.last[piece] = links.send(source, self.got.at[number, where], way)
 
 
@@ -505,76 +510,6 @@
     links.finish()
 
 
-def last_kernel(line, parts_ref, ff_ref, out_ref, qkv_ref, total_ref, ffs_ref, outs_ref, qkvs_ref, got, made, *scratch):
-    space, (send_sems, recv_sems) = scratch[:-2], scratch[-2:]
-    links = Links(send_sems, recv_sems, line)
-    far = [1, line - 1] + list(range(2, line - 1))
-    links.meet(["x", "y", "c"] + far)
-    ring = RingSum(links, parts_ref, total_ref, got, made)
-    ring.step(0)
-    items = []
-    for kind, (source, target) in enumerate(((ff_ref, ffs_ref), (out_ref, outs_ref), (qkv_ref, qkvs_ref))):
-        own, core, first, second = space[4 * kind : 4 * kind + 4]
-        for index, k in enumerate(far + [0]):
-            item = NearSum(
-                links,
-                lambda c, source=source, k=k: source.at[links.along(k), :, :, c],
-                own.at[index],
-                core.at[index],
-                first.at[index],
-                second.at[index],
-                "xy"[index % 2],
-            )
-            items.append((item, target, k))
-    for item, _, _ in items:
-        item.start()
-    arrived, local = [], []
-
-    def turn(item, target, k):
-        total = item.second_done()
-        if k == 0:
-            local.append(links.keep(total, target.at[links.z]))
-        else:
-            arrived.append(links.send(total, target.at[links.z], k))
-
-    pairs = [items[index : index + 2] for index in range(0, len(items), 2)]
-    for number in range(len(pairs) + 2):
-        if number < len(pairs):
-            for item in pairs[number]:
-                item[0].core_done()
-        if 1 <= number < line:
-            ring.step(number)
-        if 1 <= number <= len(pairs):
-            for item in pairs[number - 1]:
-                item[0].first_done()
-        if number >= 2:
-            for item in pairs[number - 2]:
-                turn(*item)
-    for copy in arrived:
-        copy.wait_recv()
-    links.finish()
-    for copy in local:
-        copy.wait()
-
-
-def turn_kernel(line, rows_ref, columns_ref, send_sems, recv_sems):
-    links = Links(send_sems, recv_sems, line)
-    far = [1, line - 1] + list(range(2, line - 1))
-    links.meet(far)
-    columns = columns_ref.shape[2]
-
-    def part(block):
-        return rows_ref.at[:, pl.ds(pl.multiple_of(block * columns, columns), columns)]
-
-    local = links.keep(part(links.z), columns_ref.at[links.z])
-    for k in far:
-        links.send(part(links.along(k)), columns_ref.at[links.z], k)
-    for copy in links.sent:
-        copy.wait_recv()
-    links.finish()
-    local.wait()
-
-
 def link_call(kernel, collective_id, copies, shapes, arguments, spaces=None, scratch=(), vmem=16):
     any_space = pl.BlockSpec(memory_space=pl.ANY)
     near_space = pl.BlockSpec(memory_space=pltpu.VMEM)
@@ -655,29 +590,313 @@
     )
 
 
-def last_sum(parts, grad_ff, grad_out, grad_qkv, line):
-    shape = parts.shape[1:]
-    grads = (grad_ff, grad_out, grad_qkv)
+def backward_kernel(
+    line,
+    up_ref,
+    middle_ref,
+    norm_grad_ref,
+    keep_ref,
+    gain_ref,
+    query,
+    kv,
+    peak,
+    turns,
+    mixed_ref,
+    out_ref,
+    atts_ref,
+    weight_ref,
+    norm_ref,
+    ff_ref,
+    middle_grad_ref,
+    mixed_total_ref,
+    total_ref,
+    ffs_ref,
+    outs_ref,
+    qkvs_ref,
+    big,
+    slim,
+    norm,
+    own_rows,
+    own_columns,
+    branch,
+    own_grad,
+    att_grad,
+    query_back,
+    kv_back,
+    kv_out,
+    kv_in,
+    flat,
+    parts,
+    *scratch,
+):
+    f32, bf16 = jnp.float32, jnp.bfloat16
+    send_sems, recv_sems = scratch[-2:]
+    rings, sums = scratch[:3], scratch[3:-2]
+    links = Links(send_sems, recv_sems, line)
+    far = [1, line - 1] + list(range(2, line - 1))
+    order = far + [0]
+    links.meet(["x", "y", "c"] + far)
+    span_len, width = up_ref.shape
+    group_len = line * span_len
+    q_cols = query.shape[1]
+    heads = q_cols // HD
+    rows_z = width // line
+    rows_each = rows_z // 8
+    scale = 1.0 / math.sqrt(HD)
+
+    def lanes_of(block):
+        return pl.ds(pl.multiple_of(block * q_cols, q_cols), q_cols)
+
+    here = pl.ds(pl.multiple_of(links.z * span_len, span_len), span_len)
+    loads = [
+        links.keep(out_ref, big),
+        links.keep(atts_ref.at[here], own_rows),
+        links.keep(atts_ref.at[:, lanes_of(links.z)], own_columns),
+        links.keep(norm_ref, norm),
+        links.keep(weight_ref.at[:, :, :, :, pl.ds(0, slim.shape[4])], slim),
+    ]
+    mixed_ring = RingSum(links, mixed_ref, mixed_total_ref, *rings[:2])
+    ring = RingSum(links, parts, total_ref, rings[2], None)
+
+    def items_of(source, space, in_place):
+        items = []
+        for index, k in enumerate(order):
+            block = links.along(k)
+            own = source.at[block, :, :, links.c] if in_place else space[0].at[index]
+            core, first, second = space[-3:]
+            items.append(
+                NearSum(
+                    links,
+                    lambda c, block=block: source.at[block, :, :, c],
+                    own,
+                    core.at[index],
+                    first.at[index],
+                    second.at[index],
+                    "xy"[index % 2],
+                    in_place,
+                )
+            )
+        return items
+
+    ff_items = items_of(ff_ref, sums[:4], False)
+    out_items = items_of(big, sums[4:7], True)
+    qkv_items = items_of(slim, sums[7:], True)
+    arrived, local = [], []
+
+    def turn(items, target, low, high):
+        for item, k in list(zip(items, order))[low:high]:
+            total = item.second_done()
+            if k == 0:
+                local.append(links.keep(total, target.at[links.z]))
+            else:
+                arrived.append(links.send(total, target.at[links.z], k))
+
+    def core_done(items, low, high):
+        for item in items[low:high]:
+            item.core_done()
+
+    def first_done(items, low, high):
+        for item in items[low:high]:
+            item.first_done()
+
+    half = line // 2
+    for item in ff_items:
+        item.start()
+    mixed_ring.step(0)
+
+    def d_middle(index, carry):
+        rows = pl.ds(pl.multiple_of(index * 16, 16), 16)
+        middle = middle_ref[rows]
+        inverse = lax.rsqrt(jnp.mean(middle * middle, axis=-1, keepdims=True) + epsilon)
+        scaled = gain_ref[1] * norm_grad_ref[rows]
+        grad = (
+            up_ref[rows]
+            + inverse * scaled
+            - middle
+            * (inverse * inverse * inverse)
+            * jnp.mean(scaled * middle, axis=-1, keepdims=True)
+        )
+        middle_grad_ref[rows] = grad
+        branch[rows] = (grad * keep_ref[0:1, 0:1]).astype(bf16)
+        return carry
+
+    lax.fori_loop(0, span_len // 16, d_middle, 0)
+    for copy in loads:
+        copy.wait()
+    for z in range(line):
+        weight = big[z].reshape(rows_z, width)
+        own_grad[:, z * rows_z : (z + 1) * rows_z] = lax.dot_general(
+            branch[...], weight, (((1,), (1,)), ((), ())), preferred_element_type=f32
+        ).astype(bf16)
+    turned = [links.send(own_grad.at[:, lanes_of(links.along(k))], att_grad.at[here], k) for k in far]
+    stayed = links.keep(own_grad.at[:, lanes_of(links.z)], att_grad.at[here])
+    core_done(ff_items, 0, half)
+    for z in range(line):
+        for part in range(4):
+            columns = slice(part * width // 4, (part + 1) * width // 4)
+            grad = lax.dot_general(
+                own_rows[:, z * rows_z : (z + 1) * rows_z],
+                branch[:, columns],
+                (((0,), (0,)), ((), ())),
+                preferred_element_type=f32,
+            )
+            big[z, :, :, :, :, columns] = grad.astype(bf16).reshape(2, 2, 2, rows_each, width // 4)
+    for item in out_items:
+        item.start()
+    core_done(ff_items, half, line)
+    mixed_ring.step(1)
+    kv_back[...] = jnp.zeros_like(kv_back)
+    for copy in turned:
+        copy.wait_recv()
+    stayed.wait()
+
+    def attend_back(head, carry):
+        lanes = pl.ds(pl.multiple_of(head * HD, HD), HD)
+        for block in range(line):
+            rows = slice(block * span_len, (block + 1) * span_len)
+            reach = (block + 1) * span_len
+            part, grad = query[rows, lanes], att_grad[rows, lanes]
+            row = lax.broadcasted_iota(jnp.int32, (span_len, reach), 0) + block * span_len
+            column = lax.broadcasted_iota(jnp.int32, (span_len, reach), 1)
+            allowed = (column <= row, column < (block + links.x) * span_len)
+            spot = lax.broadcasted_iota(jnp.int32, (span_len, HD), 1) == head
+            top = jnp.sum(jnp.where(spot, peak[rows], 0.0), axis=-1, keepdims=True)
+            delta = jnp.sum(
+                grad.astype(f32) * own_columns[rows, lanes].astype(f32), axis=-1, keepdims=True
+            )
+            total = None
+            for side in range(2):
+                keys, values = kv[side, :reach, :HD], kv[side, :reach, HD:]
+                score = lax.dot_general(
+                    part, keys, (((1,), (1,)), ((), ())), preferred_element_type=f32
+                )
+                weight = jnp.where(allowed[side], jnp.exp(score * scale - top), 0.0)
+                weight_grad = lax.dot_general(
+                    grad, values, (((1,), (1,)), ((), ())), preferred_element_type=f32
+                )
+                score_grad = (weight * (weight_grad - delta)).astype(bf16)
+                term = jnp.dot(score_grad, keys, preferred_element_type=f32)
+                total = term if total is None else total + term
+                kv_back[side, :reach, :HD] += lax.dot_general(
+                    score_grad, part, (((0,), (0,)), ((), ())), preferred_element_type=f32
+                )
+                kv_back[side, :reach, HD:] += lax.dot_general(
+                    weight.astype(bf16), grad, (((0,), (0,)), ((), ())), preferred_element_type=f32
+                )
+            query_back[rows, lanes] = total * scale
+        return carry
+
+    lax.fori_loop(0, heads, attend_back, 0)
+    kv_out[:, :HD] = (kv_back[1, :, :HD] * scale).astype(bf16)
+    kv_out[:, HD:] = kv_back[1, :, HD:].astype(bf16)
+    exchange = links.send(kv_out, kv_in, "x")
+
+    def turn_back(values, rows):
+        return values * turns[0, rows] - pltpu.roll(values, HD // 2, 1) * turns[1, rows]
+
+    for block in range(line):
+        rows = slice(block * span_len, (block + 1) * span_len)
+        for head in range(heads):
+            lanes = slice(head * HD, (head + 1) * HD)
+            flat[rows, lanes] = turn_back(query_back[rows, lanes], rows).astype(bf16)
+    first_done(ff_items, 0, half)
+    exchange.wait_recv()
+    for block in range(line):
+        rows = slice(block * span_len, (block + 1) * span_len)
+        key_grad = kv_back[0, rows, :HD] * scale + kv_in[rows, :HD].astype(f32)
+        flat[rows, q_cols : q_cols + HD] = turn_back(key_grad, rows).astype(bf16)
+        value_grad = kv_back[0, rows, HD:] + kv_in[rows, HD:].astype(f32)
+        flat[rows, q_cols + HD :] = value_grad.astype(bf16)
+    for z in range(line):
+        weight = slim[z].reshape(rows_z, flat.shape[1])
+        part = lax.dot_general(
+            flat[...], weight, (((1,), (1,)), ((), ())), preferred_element_type=f32
+        ).astype(bf16)
+        for block in range(line):
+            parts[block, :, z * rows_z : (z + 1) * rows_z] = part[
+                block * span_len : (block + 1) * span_len
+            ]
+    ring.step(0)
+    for z in range(line):
+        grad = lax.dot_general(
+            norm[:, z * rows_z : (z + 1) * rows_z],
+            flat[...],
+            (((0,), (0,)), ((), ())),
+            preferred_element_type=f32,
+        )
+        slim[z] = grad.astype(bf16).reshape(2, 2, 2, rows_each, flat.shape[1])
+    for item in qkv_items:
+        item.start()
+    core_done(out_items, 0, half)
+    mixed_ring.step(2)
+    first_done(ff_items, half, line)
+    turn(ff_items, ffs_ref, 0, half)
+    ring.step(1)
+    core_done(out_items, half, line)
+    first_done(out_items, 0, half)
+    turn(ff_items, ffs_ref, half, line)
+    ring.step(2)
+    core_done(qkv_items, 0, line)
+    first_done(out_items, half, line)
+    turn(out_items, outs_ref, 0, half)
+    mixed_ring.step(3)
+    ring.step(3)
+    first_done(qkv_items, 0, half)
+    turn(out_items, outs_ref, half, line)
+    first_done(qkv_items, half, line)
+    turn(qkv_items, qkvs_ref, 0, line)
+    for copy in arrived:
+        copy.wait_recv()
+    links.finish()
+    for copy in local:
+        copy.wait()
+
+
+def backward_call(small, mixed_parts, out_w, attended, weights, norm, grad_ff, line):
+    f32, bf16 = jnp.float32, jnp.bfloat16
+    span_len, width = small[0].shape
+    group_len = line * span_len
+    query = small[5]
+    q_cols, rows_each, qkv_cols = query.shape[1], width // line // 8, weights.shape[3]
+    weights = weights.reshape(line, 2, 2, 2, -1, qkv_cols)
+    wide = (line, 2, 2, 2, rows_each, width)
+    slim = (line, 2, 2, 2, rows_each, qkv_cols)
+    out_space = sum_space(line, rows_each, width)[1:]
+    qkv_space = sum_space(line, rows_each, qkv_cols)[1:]
+    token = jax.ShapeDtypeStruct((span_len, width), f32)
     return link_call(
-        functools.partial(last_kernel, line),
+        functools.partial(backward_kernel, line),
         4,
-        96,
-        (jax.ShapeDtypeStruct(shape, jnp.float32),)
-        + tuple(jax.ShapeDtypeStruct((line,) + grad.shape[4:], grad.dtype) for grad in grads),
-        (parts,) + grads,
-        "vhhhvhhh",
-        ring_space(line, shape) + sum((sum_space(line, *grad.shape[4:]) for grad in grads), []),
-        vmem=58,
-    )
-
-
-def turn_rows(values, line):
-    return link_call(
-        functools.partial(turn_kernel, line),
-        3,
-        line,
-        jax.ShapeDtypeStruct((line, values.shape[0], values.shape[1] // line), values.dtype),
-        (values,),
+        160,
+        (token, token, token)
+        + tuple(
+            jax.ShapeDtypeStruct((line, rows_each, columns), bf16)
+            for columns in (grad_ff.shape[5], width, qkv_cols)
+        ),
+        small + (mixed_parts, out_w.reshape(wide), attended, weights, norm, grad_ff),
+        "v" * 10 + "hhhhh" + "vvvhhh",
+        [
+            pltpu.VMEM(wide, bf16),
+            pltpu.VMEM(slim, bf16),
+            pltpu.VMEM((group_len, width), bf16),
+            pltpu.VMEM((span_len, width), bf16),
+            pltpu.VMEM((group_len, q_cols), bf16),
+            pltpu.VMEM((span_len, width), bf16),
+            pltpu.VMEM((span_len, width), bf16),
+            pltpu.VMEM((group_len, q_cols), bf16),
+            pltpu.VMEM((group_len, q_cols), f32),
+            pltpu.VMEM((2, group_len, 2 * HD), f32),
+            pltpu.VMEM((group_len, 2 * HD), bf16),
+            pltpu.VMEM((group_len, 2 * HD), bf16),
+            pltpu.VMEM((group_len, qkv_cols), bf16),
+            pltpu.VMEM((line, span_len, width), bf16),
+        ]
+        + ring_space(line, (span_len, width))
+        + ring_space(line, (span_len, width))[:1]
+        + sum_space(line, rows_each, grad_ff.shape[5])
+        + out_space
+        + qkv_space,
+        vmem=63,
     )
 
 
@@ -1021,24 +1240,10 @@
     _, span_len, model_width = tokens.shape
     line = lax.axis_size("z")
     place = lax.axis_index("z")
-    side = lax.axis_index("x")
-    near = lax.axis_size("x") * lax.axis_size("y") * lax.axis_size("c")
     rows_each = w_query.shape[0]
-    heads = HEADS // line
-    q_cols = heads * HD
+    q_cols = HEADS // line * HD
     ff_cols = w_gate.shape[1] // line
     group_len = span_len * line
-    score_scale = 1.0 / math.sqrt(HD)
-
-    def shift(values, axis, step):
-        size = lax.axis_size(axis)
-        return lax.ppermute(values, axis, [(i, (i + step) % size) for i in range(size)])
-
-    def after(values, first):
-        return lax.optimization_barrier((values, first))[0]
-
-    def pick(values, index, dim):
-        return lax.dynamic_index_in_dim(values, index, dim, keepdims=False)
 
     def by_columns(weight, columns):
         return weight.reshape(rows_each, line, columns).transpose(1, 0, 2)
@@ -1078,15 +1283,9 @@
         ff_w,
     ) = forward_call(tokens[0], table, pack_attn, pack_ff, (keep * upstream).astype(bf16), line)
     inputs = x_blocks.reshape(group_len, model_width).astype(f32)
-    qkv_w = near_w[:, :, :rows_each].reshape(model_width, q_cols + 2 * HD)
     gain_one, gain_two = gain_all[0, :1], gain_all[1, :1]
     mixed_grad = mixed_grad.reshape(group_len, model_width)
     ff_w = ff_w.reshape(model_width, 2 * ff_cols)
-    queries = queries.reshape(group_len, heads, HD)
-    both_kv = both_kv.reshape(2 * group_len, 2 * HD)
-    keys = both_kv[:, :HD]
-    values = both_kv[:, HD:]
-
     def own_rows(values):
         return lax.dynamic_slice_in_dim(values, place * span_len, span_len, 0)
 
@@ -1095,7 +1294,6 @@
     inverse_mid = lax.rsqrt(jnp.mean(middle_all * middle_all, axis=-1, keepdims=True) + epsilon)
     second_norm = (middle_all * inverse_mid * gain_two).astype(bf16)
     middle = own_rows(middle_all)
-    inverse_two = own_rows(inverse_mid)
 
     gate_up = jnp.dot(second_norm, ff_w, preferred_element_type=f32)
     gate_value = gate_up[:, :ff_cols]
@@ -1114,72 +1312,28 @@
     grad_down = over_rows(hidden, mixed_grad).astype(bf16).reshape(2, 2, 2, -1, model_width)
     norm_grad, grad_down = third_sum(split(against(both_grad, ff_w)), grad_down, line)
     grad_down = grad_down.astype(f32)
-    grad_ff = over_rows(second_norm, after(both_grad, norm_grad)).astype(bf16)
-    scaled_two = gain_two * norm_grad
-    middle_grad = (
-        upstream
-        + inverse_two * scaled_two
-        - middle
-        * (inverse_two * inverse_two * inverse_two)
-        * jnp.mean(scaled_two * middle, axis=-1, keepdims=True)
-    )
-    branch_grad = (keep * middle_grad).astype(bf16)
-    own_grad = against(branch_grad, out_w).astype(bf16)
-    attended_grad = turn_rows(own_grad, line).reshape(group_len, heads, HD)
-    mixed_parts = split(jnp.dot(hidden, after(down_w, norm_grad), preferred_element_type=f32))
-
-    def mixed_hop(total, hop, first):
-        total = after(shift(total.astype(bf16), "z", 1), first).astype(f32)
-        return total + pick(mixed_parts, (place - 1 - hop) % line, 0).astype(f32)
-
-    mixed = mixed_hop(pick(mixed_parts, (place - 1) % line, 0), 1, attended_grad)
-    inside = jnp.arange(span_len, dtype=jnp.int32)
-    block_first = jnp.arange(line, dtype=jnp.int32) * (2 * span_len)
-
-    def token_index(which):
-        return (block_first[:, None] + which * span_len + inside[None, :]).reshape(group_len)
-
-    query_index = token_index(side)
-    key_index = jnp.concatenate([query_index, token_index(1 - side)])
-    allowed = key_index[None, :] <= query_index[:, None]
-    scores = jnp.einsum("tgd,jd->gtj", queries, keys, preferred_element_type=f32) * score_scale
-    probabilities = jnp.where(allowed, jnp.exp(scores - log_total[:, :heads].T[..., None]), 0.0)
-    rounded_probs = probabilities.astype(bf16)
-    prob_grad = jnp.einsum("tgd,jd->gtj", attended_grad, values, preferred_element_type=f32)
-    own_attended = lax.dynamic_slice_in_dim(attended_rows, place * q_cols, q_cols, 1)
-    attended = own_attended.reshape(group_len, heads, HD).astype(f32)
-    delta = jnp.sum(attended_grad.astype(f32) * attended, axis=-1).T[..., None]
-    score_grad = (probabilities * (prob_grad - delta)).astype(bf16)
-    for hop in range(2, line - 1):
-        mixed = mixed_hop(mixed, hop, score_grad)
-    query_back = jnp.einsum("gtj,jd->tgd", score_grad, keys, preferred_element_type=f32) * score_scale
-    key_back = jnp.einsum("gtj,tgd->jd", score_grad, queries, preferred_element_type=f32) * score_scale
-    value_back = jnp.einsum("gtj,tgd->jd", rounded_probs, attended_grad, preferred_element_type=f32)
-    kv_back = jnp.concatenate([key_back, value_back], axis=1)
-    kv_back = kv_back[:group_len] + shift(kv_back[group_len:].astype(bf16), "x", 1).astype(f32)
-
-    def turn_back(vectors):
-        swapped = jnp.concatenate([vectors[..., HD // 2 :], vectors[..., : HD // 2]], axis=-1)
-        return vectors * turns[0][:, None] - swapped * turns[1][:, None]
-
-    qkv_grad = jnp.concatenate(
-        [
-            turn_back(query_back).reshape(group_len, q_cols),
-            turn_back(kv_back[:, None, :HD])[:, 0],
-            kv_back[:, HD:],
-        ],
-        axis=1,
-    ).astype(bf16)
-    grad_out = over_rows(own_rows(attended_rows), branch_grad).astype(bf16)
-    grad_qkv = over_rows(first_norm, qkv_grad).astype(bf16)
-
-    def by_place(grad):
-        return grad.reshape(line, 2, 2, 2, rows_each, grad.shape[1])
-
-    input_norm_grad, ff_back, out_back, qkv_back = last_sum(
-        split(against(qkv_grad, qkv_w)), by_place(grad_ff), by_place(grad_out), by_place(grad_qkv), line
-    )
-    mixed = mixed_hop(mixed, line - 1, input_norm_grad)
+    grad_ff = over_rows(second_norm, both_grad).astype(bf16)
+    mixed_parts = split(jnp.dot(hidden, down_w, preferred_element_type=f32))
+    middle_grad, mixed, input_norm_grad, ff_back, out_back, qkv_back = backward_call(
+        (
+            upstream,
+            middle,
+            norm_grad,
+            jnp.broadcast_to(keep, (8, HD)),
+            gain_all,
+            queries,
+            both_kv,
+            log_total,
+            turns,
+        ),
+        mixed_parts,
+        out_w,
+        attended_rows,
+        near_w,
+        first_norm,
+        grad_ff.reshape(line, 2, 2, 2, rows_each, 2 * ff_cols),
+        line,
+    )
     output = (middle + keep * mixed).astype(bf16)
     ff_back = ff_back.astype(f32)
     qkv_back = qkv_back.astype(f32)

time: 590 us -> 518 us (0.88)
  matrix products: 91.7 us -> 52.2 us
  waiting for transfers between devices: 29.2 us -> 1.4 us
  Pallas kernels: 389 us -> 412 us
  local copies, waits for them, and re-layouts: 25.7 us -> 13.8 us
  other arithmetic: 25.5 us -> 13.7 us
    ppermute x4 -> x0, waiting for transfers between devices: 27.8 us -> none  [shift(): lax.ppermute(values, axis, [(i, (i + step) % size) for i in range(size)])]
    pallas_call x4 -> x3, Pallas kernels: 389 us -> 412 us  [link_call(): pl.pallas_call(kernel, out_shape=shapes, in_specs=specs[:len(arguments)],...]
    dot_general x6 -> x1, matrix products: 21.6 us -> 4.63 us  [line_body(): mixed_parts = split(jnp.dot(hidden, down_w, preferred_element_type=f32))]
    dot_general x4 -> x2, matrix products: 23.1 us -> 12.6 us  [over_rows(): lax.dot_general(left, right, (((0,), (0,)), ((), ())), preferred_element_...]
    dot_general x4 -> x2, matrix products: 26.2 us -> 17.4 us  [against(): lax.dot_general(left, right, (((1,), (1,)), ((), ())), preferred_element_...]
  transfers between devices with their start and end apart: 6 -> 2, of which waited for: 2 -> 0; matrix products, arithmetic and copies ran while one was open for 14% -> 5% of each run, Pallas kernels for 58% -> 40%
where the time goes in v6:
time: 518 us; the launch traced here: 509 us
  Pallas kernels  412 us (80%)
  matrix products  52.2 us (10%)
  between operations  15.7 us (3%)
  local copies, waits for them, and re-layouts  13.8 us (3%)
  other arithmetic  13.7 us (3%)
    pallas_call x3, Pallas kernels, link_call(): pl.pallas_call(kernel, out_shape=shapes, in_specs=specs[:len(arguments)],...  412 us
    dot_general x2, matrix products, against(): lax.dot_general(left, right, (((1,), (1,)), ((), ())), preferred_element_...  17.4 us
    dot_general x2, matrix products, over_rows(): lax.dot_general(left, right, (((0,), (0,)), ((), ())), preferred_element_...  12.6 us
  transfers between devices with their start and end apart: 2, of which 0 were waited for; matrix products, arithmetic and copies ran while one was open for 5% of the time, Pallas kernels for 40%

profile of v6, /device:TPU:0, one launch (start us, length us, event | category | flops | bytes accessed | tf_op | source)
XLA Modules:
  0.0 509.0 jit_solution(16011667464375974586)
XLA Ops:
  7.2 0.7 all-gather.3.cloned.1.call-update
  8.0 0.7 all-gather.5.cloned.1.call-update
  9.3 1.0 copy.65
  10.3 0.8 dynamic_update_slice.6
  11.2 0.8 dynamic_update_slice.7
  12.0 0.8 fusion.8
  12.8 0.7 convert_bitcast_fusion
  13.4 0.3 multiply_cosine_fusion
  13.8 0.9 bitcast_bitcast_fusion.3
  14.8 0.1 bitcast_bitcast_fusion
  15.1 0.8 copy-done.24
  15.9 1.2 convert_multiply_fusion.3
  17.0 205.6 %shard_map.230 = (bf16[4,128,2048]{2,1,0:T(8,128)(2,1)}, bf16[4,8,80,768]{3,2,1,0:T(8,128)(2,1)}, f32[2,16,2048]{2,1,0:T(8,128)S(1)}, bf16[512,2048]{1,0:T(8,128...) custom-call(bf16[128,2048]{1,0:T(8,128)(2,1)S(1)} %bitcast.95, ...), custom_call_target="tpu_custom_call" | custom-call | tf_op jit(solution)/shard_map/pallas_call | solution.py:520
  222.6 0.8 copy-done.4
  223.4 0.8 copy-done.5
  224.2 0.8 copy-done.6
  225.0 0.7 copy-done.8
  225.8 9.4 %multiply_reduce_fusion = (f32[512]{0:T(512)S(1)}, f32[512,2048]{1,0:T(8,128)S(1)}) fusion(bf16[512,2048]{1,0:T(8,128)(2,1)} %get-tuple-element.31.atts_ref, bf16[2048,2048]{1,0:T(8,128)(2,1)} %all-gather.3.cloned.1.call-done, f32[]{:T(128)} %bitcast.7, bf16[512,2048]{1,0:T(8,128)(2,1)} %bitcast.121), kind=kOutput, calls=%fused_computation.4 | convolution fusion | flops 4300209664 | bytes 16779268 | tf_op jit(solution)/shard_map/dot_general | solution.py:1292
  235.2 1.9 copy-done.19
  237.1 8.1 %fusion.11 = f32[512,2816]{1,0:T(8,128)} fusion(bf16[2048,2816]{1,0:T(8,128)(2,1)S(1)} %bitcast.116, f32[512,2048]{1,0:T(8,128)S(1)} %get-tuple-element.71, f32[2048]{0:T(1024)S(1)} %bitcast.113, f32[512]{0:T(512)S(1)} %add_rsqrt_fusion), kind=kOutput, calls=%fused_computation.62 | convolution fusion | flops 5908725760 | bytes 21506048 | tf_op jit(solution)/shard_map/dot_general | solution.py:1298
  245.3 8.3 %multiply_convert_fusion.3 = (bf16[512,1408]{1,0:T(8,128)(2,1)S(1)}, bf16[512,1408]{1,0:T(8,128)(2,1)S(1)}, bf16[512,1408]{1,0:T(8,128)(2,1)S(1)}) fusion(f32[512,2816]{1,0:T(8,128)} %fusion.11, bf16[512,2048]{1,0:T(8,128)(2,1)S(1)} %bitcast.119, bf16[1408,2048]{1,0:T(8,128)(2,1)} %all-gather.5.cloned.1.call-done), kind=kOutput, calls=%fused_computation.10 | convolution fusion | flops 2963603456 | bytes 17956864 | tf_op jit(solution)/shard_map/dot_general | solution.py:53
  253.6 9.2 %convolution_convert_fusion.2 = bf16[512,2048]{1,0:T(8,128)(2,1)S(1)} fusion(bf16[2048,2816]{1,0:T(8,128)(2,1)} %bitcast.115, bf16[512,1408]{1,0:T(8,128)(2,1)S(1)} %get-tuple-element.56, bf16[512,1408]{1,0:T(8,128)(2,1)S(1)} %get-tuple-element.55), kind=kOutput, calls=%fused_computation.5 | convolution fusion | flops 5912395776 | bytes 16515072 | tf_op jit(solution)/shard_map/dot_general | solution.py:53
  262.8 9.2 %convolution_convert_fusion = bf16[2048,2816]{1,0:T(8,128)(2,1)} fusion(bf16[512,1408]{1,0:T(8,128)(2,1)S(1)} %get-tuple-element.56, bf16[512,1408]{1,0:T(8,128)(2,1)S(1)} %get-tuple-element.55, f32[512,2048]{1,0:T(8,128)S(1)} %copy-done.20, f32[2048]{0:T(1024)S(1)} %bitcast.114, f32[512]{0:T(512)S(1)} %add_rsqrt_fusion), kind=kOutput, calls=%fused_computation | convolution fusion | flops 5920260096 | bytes 18622464 | tf_op jit(solution)/shard_map/dot_general | solution.py:47
  271.9 1.0 constant_dynamic-slice_fusion.middle_ref
  273.0 3.4 convolution_convert_fusion.1
  276.4 37.4 %shard_map.231 = (f32[128,2048]{1,0:T(8,128)S(1)}, bf16[176,2048]{1,0:T(8,128)(2,1)S(1)}) custom-call(bf16[4,128,2048]{2,1,0:T(8,128)(2,1)S(1)} %bitcast.96, bf16[2,2,2,176,2048]{4,3,2,1,0:T(8,128)(2,1)S(1)} %bitcast.94), custom_call_target="tpu_custom_call" | custom-call | tf_op jit(solution)/shard_map/pallas_call | solution.py:520
  313.8 4.6 convolution_convert_fusion.3
  318.5 0.6 broadcast_in_dim.39.keep_ref
  319.1 169.1 %shard_map.232 = (f32[128,2048]{1,0:T(8,128)}, f32[128,2048]{1,0:T(8,128)}, f32[128,2048]{1,0:T(8,128)}, bf16[4,64,2816]{2,1,0:T(8,128)(2,1)}, bf16[4,64,2048]{2...) custom-call(f32[128,2048]{1,0:T(8,128)} %get-tuple-element.62.up_ref, f32[128,2048]{1,0:T(8,128)} %constant_dynamic-slice_fusion.middle_ref, ...), custom_call_target="tpu_custom_call" | custom-call | tf_op jit(solution)/shard_map/pallas_call | solution.py:520
  488.2 1.2 convert_element_type.111
  489.5 2.2 fusion.6
  491.8 0.3 fusion.1
  492.1 0.8 multiply_reduce_fusion.4
  492.9 0.2 multiply_reduce_fusion.3
  493.1 0.8 multiply_reduce_fusion.5
  493.9 1.0 convert_reduce_fusion
  494.9 0.2 convert_element_type.117
  495.1 0.2 slice_bitcast_fusion
  495.5 1.1 copy-done.13
  496.6 0.3 multiply_reduce_fusion.2
  496.9 0.1 copy.55
  497.1 0.1 copy-done.15
  497.2 0.2 multiply_reduce_fusion.1
  497.4 0.8 copy-done.3
  498.2 1.2 convert_element_type.120
  499.5 0.5 convert_divide_fusion
  500.0 0.5 convert_divide_fusion.1
  500.5 1.2 fusion.7
  (78 shorter events, 0.8 us)
Async XLA Ops:
  7.2 7.6 %copy-start.14 = (bf16[64,5632]{1,0:T(8,128)(2,1)S(1)}, bf16[64,5632]{1,0:T(8,128)(2,1)}, u32[]{:S(2)}) copy-start(bf16[64,5632]{1,0:T(8,128)(2,1)} %param.23) | copy-start | bytes 2162692
  7.2 7.6 %copy-start.12 = (bf16[64,5632]{1,0:T(8,128)(2,1)S(1)}, bf16[64,5632]{1,0:T(8,128)(2,1)}, u32[]{:S(2)}) copy-start(bf16[64,5632]{1,0:T(8,128)(2,1)} %param.22) | copy-start | bytes 2162692
  7.2 218.5 %all-gather.3.cloned.1.call-start = ((), (), s32[]{:S(2)}) async-start(), calls=%async_computation | async-start | bytes 8650752 | tf_op jit(solution)/shard_map/all_gather | solution.py:1251
  7.9 237.3 %all-gather.5.cloned.1.call-start = ((), (), s32[]{:S(2)}) async-start(), calls=%async_computation.1 | async-start | bytes 6488064 | tf_op jit(solution)/shard_map/all_gather | solution.py:1252
  14.8 1.0 copy-start.24
  15.0 2.1 copy-start
  222.6 0.8 copy-start.4
  223.4 0.8 copy-start.5
  224.2 0.8 copy-start.6
  225.0 0.7 copy-start.8
  225.7 9.5 %copy-start.7 = (f32[2,16,2048]{2,1,0:T(8,128)}, f32[2,16,2048]{2,1,0:T(8,128)S(1)}, u32[]{:S(2)}) copy-start(f32[2,16,2048]{2,1,0:T(8,128)S(1)} %get-tuple-element.33.gain_ref) | copy-start | bytes 786436
  225.8 11.4 %copy-start.29 = (bf16[4,8,64,2816]{3,2,1,0:T(8,128)(2,1)S(1)}, bf16[4,8,64,2816]{3,2,1,0:T(8,128)(2,1)}, u32[]{:S(2)}) copy-start(bf16[4,8,64,2816]{3,2,1,0:T(8,128)(2,1)} %get-tuple-element.34) | copy-start | bytes 34603012
  235.2 1.9 copy-start.19
  237.1 8.1 %copy-start.30 = (bf16[4,128,2048]{2,1,0:T(8,128)(2,1)S(1)}, bf16[4,128,2048]{2,1,0:T(8,128)(2,1)}, u32[]{:S(2)}) copy-start(bf16[4,128,2048]{2,1,0:T(8,128)(2,1)} %get-tuple-element.32) | copy-start | bytes 6291460
  253.5 9.2 %copy-start.20 = (f32[512,2048]{1,0:T(8,128)S(1)}, f32[512,2048]{1,0:T(8,128)}, u32[]{:S(2)}) copy-start(f32[512,2048]{1,0:T(8,128)} %copy-done.19) | copy-start | bytes 12582916
  262.7 10.2 %copy-start.31 = (bf16[4,128,2048]{2,1,0:T(8,128)(2,1)S(1)}, bf16[4,128,2048]{2,1,0:T(8,128)(2,1)}, u32[]{:S(2)}) copy-start(bf16[4,128,2048]{2,1,0:T(8,128)(2,1)} %get-tuple-element.32) | copy-start | bytes 6291460
  271.9 41.9 %slice-start = ((s8[5767168]{0:T(1024)(128)(4,1)}), s8[1572864]{0:T(1024)(128)(4,1)S(1)}, s32[]{:S(2)}) async-start(s8[5767168]{0:T(1024)(128)(4,1)} %bitcast.117), calls=%async_computation.2 | async-start | bytes 3145728
  273.0 40.8 %slice-start.1 = ((s8[5767168]{0:T(1024)(128)(4,1)}), s8[4194304]{0:T(1024)(128)(4,1)S(1)}, s32[]{:S(2)}) async-start(s8[5767168]{0:T(1024)(128)(4,1)} %bitcast.117), calls=%async_computation.3 | async-start | bytes 8388608
  313.8 4.7 copy-start.1
  313.8 4.6 copy-start.2
  488.1 1.3 copy-start.18
  488.2 3.6 copy-start.11
  489.4 2.7 copy-start.25
  489.5 3.5 copy-start.23
  489.5 3.6 copy-start.26
  489.5 4.4 copy-start.21
  491.8 3.1 copy-start.17
  492.9 2.2 copy-start.16
  495.3 1.3 copy-start.13
  495.5 2.0 copy-start.9
  495.5 1.7 copy-start.15
  496.9 1.3 copy-start.3
  497.0 4.7 copy-start.10
  497.0 2.4 copy-start.28
  497.0 3.0 copy-start.27
  497.1 3.5 copy-start.22
Sparse Core Ops, SparseCore 0:
  10.9 128.9 all-gather.2
  141.8 60.2 all-gather.4

commit v7 on v6

--- a/solution.py
+++ b/solution.py
@@ -176,7 +176,6 @@
     table_ref,
     pack_ref,
     ff_ref,
-    mix_ref,
     xs_ref,
     weight_ref,
     gain_ref,
@@ -186,7 +185,6 @@
     peak_ref,
     turn_ref,
     atts_ref,
-    mixs_ref,
     ffs_ref,
     x_all,
     tables,
@@ -227,7 +225,6 @@
     ring.step(0)
     near.offer(0, pack_ref.at[links.z])
     local.append(links.keep(ff_ref.at[links.z], ffs_ref.at[links.z, here]))
-    local.append(links.keep(mix_ref, mixs_ref.at[links.z]))
     for k in far:
         turned[k].wait_recv()
         near.offer(k, weights.at[links.along(-k), here])
@@ -350,10 +347,8 @@
         return atts_ref.at[rows, pl.ds(pl.multiple_of(block * q_cols, q_cols), q_cols)]
 
     att_ring = RingGather(links, att, place)
-    mix_ring = RingGather(links, mix_ref, lambda block, rows: mixs_ref.at[block, rows])
     local.append(links.keep(att, place(links.z, pl.ds(0, group_len))))
     att_ring.step(0)
-    mix_ring.step(0)
     for k in far:
         turned_ff[k].wait_recv()
         far_ff.offer(k, ffs_ref.at[links.along(-k), here])
@@ -361,15 +356,12 @@
     far_ff.close(0)
     far_ff.relay(far[0], "x")
     att_ring.step(1)
-    mix_ring.step(1)
     for k in far[1:]:
         far_ff.relay(k, "x" if k < line // 2 else "y")
     att_ring.step(2)
-    mix_ring.step(2)
     for k in far:
         far_ff.close(k)
     att_ring.step(3)
-    mix_ring.step(3)
     far_ff.wait(range(line))
     links.finish()
     for copy in local:
@@ -442,8 +434,8 @@
 
 
 class RingSum:
-    def __init__(self, links, parts, total, got, made, pieces=4):
-        self.links, self.parts, self.total, self.got, self.made = links, parts, total, got, made
+    def __init__(self, links, parts, total, got, pieces=4):
+        self.links, self.parts, self.total, self.got = links, parts, total, got
         self.pieces, self.last = pieces, [None] * pieces
         self.rows = parts.shape[1] // pieces
 
@@ -463,51 +455,9 @@
                 if number == links.line - 1:
                     self.total[where] = total
                     continue
-                made, place = (self.parts, block) if self.made is None else (self.made, number - 1)
-                made[place, where] = total.astype(made.dtype)
-                source = made.at[place, where]
+                self.parts[block, where] = total.astype(self.parts.dtype)
+                source = self.parts.at[block, where]
             self.last[piece] = links.send(source, self.got.at[number, where], way)
-
-
-def ring_space(line, shape):
-    return [pltpu.VMEM((line - 1,) + shape, jnp.bfloat16), pltpu.VMEM((line - 2,) + shape, jnp.bfloat16)]
-
-
-def third_kernel(
-    line, cuts, parts_ref, down_ref, total_ref, sum_ref, got, made, *scratch
-):
-    space, (send_sems, recv_sems) = scratch[:-2], scratch[-2:]
-    links = Links(send_sems, recv_sems, line)
-    links.meet(["x", "y", "c", 1, line - 1])
-    ring = RingSum(links, parts_ref, total_ref, got, made)
-    ring.step(0)
-    items = []
-    for index, (low, high) in enumerate(cuts):
-        rows = pl.ds(low, high - low)
-        own, core, first, second = space[4 * index : 4 * index + 4]
-        items.append(
-            NearSum(
-                links,
-                lambda c, rows=rows: down_ref.at[:, :, c, rows],
-                own.at[0],
-                core.at[0],
-                first.at[0],
-                second.at[0],
-                "xy"[index % 2],
-            )
-        )
-    for item in items:
-        item.start()
-    for item in items:
-        item.core_done()
-    ring.step(1)
-    for item in items:
-        item.first_done()
-    ring.step(2)
-    for item, (low, high) in zip(items, cuts):
-        sum_ref[low:high] = item.second_done()[...]
-    ring.step(3)
-    links.finish()
 
 
 def link_call(kernel, collective_id, copies, shapes, arguments, spaces=None, scratch=(), vmem=16):
@@ -530,7 +480,7 @@
     )(*arguments)
 
 
-def forward_call(tokens, table, pack, pack_ff, mixed, line):
+def forward_call(tokens, table, pack, pack_ff, line):
     span_len, width = tokens.shape
     group_len = line * span_len
     rows_each = pack_ff.shape[1]
@@ -547,7 +497,6 @@
         ((group_len, HD), f32),
         ((2, group_len, HD), f32),
         ((group_len, line * q_cols), bf16),
-        ((line, span_len, width), bf16),
         ((line, 8) + pack_ff.shape[1:], bf16),
     )
     return link_call(
@@ -555,7 +504,7 @@
         0,
         176,
         tuple(jax.ShapeDtypeStruct(*out) for out in outs),
-        (tokens, table, pack, pack_ff, mixed),
+        (tokens, table, pack, pack_ff),
         scratch=[
             pltpu.VMEM((line, span_len, width), bf16),
             pltpu.VMEM((line,) + table.shape, f32),
@@ -573,20 +522,250 @@
     )
 
 
-def third_sum(parts, grad_down, line):
-    shape = parts.shape[1:]
-    rows, columns = grad_down.shape[3:]
+def mlp_kernel(
+    line,
+    cuts,
+    keep_ref,
+    gain_ref,
+    mix_ref,
+    xs_ref,
+    atts_ref,
+    out_ref,
+    ff_ref,
+    down_ref,
+    middle_ref,
+    total_ref,
+    mixed_total_ref,
+    sum_ref,
+    grad_ff_ref,
+    big,
+    ff,
+    down,
+    norm,
+    parts,
+    mixed,
+    gate_up,
+    hidden,
+    both_grad,
+    got,
+    mixed_parts,
+    mixed_got,
+    *scratch,
+):
+    f32, bf16 = jnp.float32, jnp.bfloat16
+    space, (send_sems, recv_sems) = scratch[:-2], scratch[-2:]
+    links = Links(send_sems, recv_sems, line)
+    links.meet(["x", "y", "c", 1, line - 1])
+    span_len, width = mix_ref.shape
+    group_len = line * span_len
+    ff_cols = hidden.shape[1]
+    chunk = 2 * HD
+    stay = links.keep(mix_ref, mixed.at[links.z])
+    mix_ring = RingGather(links, mix_ref, lambda block, rows: mixed.at[block, rows])
+    mix_ring.step(0)
+    early = [
+        links.keep(out_ref, big),
+        links.keep(atts_ref, norm),
+        links.keep(xs_ref, parts),
+    ]
+    late = [links.keep(ff_ref, ff), links.keep(down_ref, down)]
+    ring = RingSum(links, parts, total_ref, got)
+    mixed_ring = RingSum(links, mixed_parts, mixed_total_ref, mixed_got)
+    items = []
+    for index, (low, high) in enumerate(cuts):
+        rows = pl.ds(low, high - low)
+        core, first, second = space[3 * index : 3 * index + 3]
+        items.append(
+            NearSum(
+                links,
+                lambda c, rows=rows: big.at[:, :, c, rows],
+                big.at[:, :, links.c, rows],
+                core.at[0],
+                first.at[0],
+                second.at[0],
+                "xy"[index % 2],
+                True,
+            )
+        )
+    for copy in early:
+        copy.wait()
+
+    half = group_len // 2
+    out_rows = width // 8
+    for part in range(2):
+        low = part * half
+        for column in range(4):
+            lanes = slice(column * width // 4, (column + 1) * width // 4)
+            value = None
+            for k in range(8):
+                term = jnp.dot(
+                    norm[low : low + half, k * out_rows : (k + 1) * out_rows],
+                    big[k // 4, k // 2 % 2, k % 2, :, lanes],
+                    preferred_element_type=f32,
+                )
+                value = term if value is None else value + term
+            gate_up[:half, lanes] = value * keep_ref[0:1, 0:1]
+
+        def normalise(index, carry, low=low):
+            block = (low // 16 + index) // (span_len // 16)
+            rows = pl.ds(pl.multiple_of(index * 16, 16), 16)
+            inside = pl.ds(pl.multiple_of(lax.rem(index, span_len // 16) * 16, 16), 16)
+            values = parts[block, inside].astype(f32) + gate_up[rows, :width]
+            gate_up[rows, :width] = values
+            inverse = lax.rsqrt(jnp.mean(values * values, axis=-1, keepdims=True) + epsilon)
+            target = pl.ds(pl.multiple_of(low + index * 16, 16), 16)
+            norm[target] = (values * inverse * gain_ref[1]).astype(bf16)
+            return carry
+
+        lax.fori_loop(0, half // 16, normalise, 0)
+
+        @pl.when(links.z // (line // 2) == part)
+        def _():
+            where = pl.multiple_of(lax.rem(links.z, line // 2) * span_len, span_len)
+            middle_ref[...] = gate_up[pl.ds(where, span_len), :width]
+
+    mix_ring.step(1)
+    for copy in late:
+        copy.wait()
+
+    def forward(low, size):
+        gates, ups = pl.ds(low, size), pl.ds(low + ff_cols, size)
+        gate = jnp.dot(norm[...], ff[:, gates], preferred_element_type=f32)
+        gate_up[:, gates] = gate
+        swish = gate * jax.nn.sigmoid(gate)
+        up = jnp.dot(norm[...], ff[:, ups], preferred_element_type=f32)
+        gate_up[:, ups] = up
+        hidden[:, gates] = (swish * up).astype(bf16)
+
+    def backward(low, size):
+        gates, ups = pl.ds(low, size), pl.ds(low + ff_cols, size)
+        grad = lax.dot_general(
+            mixed[...].reshape(group_len, width),
+            down[gates],
+            (((1,), (1,)), ((), ())),
+            preferred_element_type=f32,
+        )
+        gate, up = gate_up[:, gates], gate_up[:, ups]
+        sigmoid = jax.nn.sigmoid(gate)
+        both_grad[:, gates] = (grad * up * sigmoid * (1.0 + gate * (1.0 - sigmoid))).astype(bf16)
+        both_grad[:, ups] = (grad * (gate * sigmoid)).astype(bf16)
+
+    def over_chunks(work, extent):
+        def one(index, carry):
+            work(pl.multiple_of(index * chunk, chunk), chunk)
+            return carry
+
+        lax.fori_loop(0, extent // chunk, one, 0)
+        if extent % chunk:
+            work(extent // chunk * chunk, extent % chunk)
+
+    over_chunks(forward, ff_cols)
+    mix_ring.step(2)
+
+    def mixed_part(low, size):
+        lanes = pl.ds(low, size)
+        value = jnp.dot(hidden[...], down[:, lanes], preferred_element_type=f32).astype(bf16)
+        mixed_parts[:, :, lanes] = value.reshape(line, span_len, size)
+
+    over_chunks(mixed_part, width)
+    mixed_ring.step(0)
+    stay.wait()
+    mix_ring.step(3)
+    over_chunks(backward, ff_cols)
+
+    def norm_part(low, size):
+        value = lax.dot_general(
+            both_grad[...], ff[pl.ds(low, size)], (((1,), (1,)), ((), ())), preferred_element_type=f32
+        ).astype(bf16)
+        parts[:, :, pl.ds(low, size)] = value.reshape(line, span_len, size)
+
+    over_chunks(norm_part, width)
+    ring.step(0)
+    mixed_ring.step(1)
+    hidden_rows = hidden[...].T
+
+    def down_part(low, size):
+        lanes = pl.ds(low, size)
+        value = jnp.dot(
+            hidden_rows,
+            mixed[:, :, lanes].reshape(group_len, size),
+            preferred_element_type=f32,
+        ).astype(bf16)
+        big[:, :, :, : cuts[-1][1], lanes] = value.reshape(2, 2, 2, cuts[-1][1], size)
+
+    over_chunks(down_part, width)
+    for item in items:
+        item.start()
+    ring.step(1)
+    sent = []
+    block_rows = width // line
+    for z in range(line):
+        norm_rows = norm[:, z * block_rows : (z + 1) * block_rows].T
+
+        def ff_part(low, size, z=z, norm_rows=norm_rows):
+            lanes = pl.ds(low, size)
+            value = jnp.dot(norm_rows, both_grad[:, lanes], preferred_element_type=f32)
+            ff[z * block_rows : (z + 1) * block_rows, lanes] = value.astype(bf16)
+
+        over_chunks(ff_part, 2 * ff_cols)
+        rows = pl.ds(z * block_rows, block_rows)
+        sent.append(links.keep(ff.at[rows], grad_ff_ref.at[rows]))
+        if z == 0:
+            mixed_ring.step(2)
+            for item in items:
+                item.core_done()
+        if z == 1:
+            ring.step(2)
+    for item in items:
+        item.first_done()
+    ring.step(3)
+    mixed_ring.step(3)
+    for item, (low, high) in zip(items, cuts):
+        sum_ref[low:high] = item.second_done()[...]
+    links.finish()
+    for copy in sent:
+        copy.wait()
+
+
+def mlp_call(keep, gains, mixed, x_blocks, attended, out_w, ff_w, down_w, line):
+    f32, bf16 = jnp.float32, jnp.bfloat16
+    span_len, width = mixed.shape
+    group_len = line * span_len
+    ff_rows, both_cols = down_w.shape[0], ff_w.shape[1]
+    rows = ff_rows // 8
     half = (rows // 2 + 15) // 16 * 16
     cuts = ((0, half), (half, rows))
+    blocks = (line, span_len, width)
+    token = jax.ShapeDtypeStruct((span_len, width), f32)
     return link_call(
-        functools.partial(third_kernel, line, cuts),
+        functools.partial(mlp_kernel, line, cuts),
         2,
-        64,
-        (jax.ShapeDtypeStruct(shape, jnp.float32), jax.ShapeDtypeStruct((rows, columns), jnp.bfloat16)),
-        (parts, grad_down),
-        "vhvv",
-        ring_space(line, shape) + sum((sum_space(1, high - low, columns) for low, high in cuts), []),
-        vmem=40,
+        96,
+        (
+            token,
+            token,
+            token,
+            jax.ShapeDtypeStruct((rows, width), bf16),
+            jax.ShapeDtypeStruct(ff_w.shape, bf16),
+        ),
+        (keep, gains, mixed, x_blocks, attended, out_w.reshape(2, 2, 2, width // 8, width), ff_w, down_w),
+        "vvhhhhhh" + "vvvvh",
+        [
+            pltpu.VMEM((2, 2, 2, width // 8, width), bf16),
+            pltpu.VMEM(ff_w.shape, bf16),
+            pltpu.VMEM(down_w.shape, bf16),
+            pltpu.VMEM((group_len, width), bf16),
+            pltpu.VMEM(blocks, bf16),
+            pltpu.VMEM(blocks, bf16),
+            pltpu.VMEM((group_len, both_cols), f32),
+            pltpu.VMEM((group_len, ff_rows), bf16),
+            pltpu.VMEM((group_len, both_cols), bf16),
+            pltpu.VMEM((line - 1, span_len, width), bf16),
+            pltpu.VMEM(blocks, bf16),
+            pltpu.VMEM((line - 1, span_len, width), bf16),
+        ]
+        + sum((sum_space(1, high - low, width)[1:] for low, high in cuts), []),
+        vmem=63,
     )
 
 
@@ -601,14 +780,12 @@
     kv,
     peak,
     turns,
-    mixed_ref,
     out_ref,
     atts_ref,
     weight_ref,
     norm_ref,
     ff_ref,
     middle_grad_ref,
-    mixed_total_ref,
     total_ref,
     ffs_ref,
     outs_ref,
@@ -631,7 +808,7 @@
 ):
     f32, bf16 = jnp.float32, jnp.bfloat16
     send_sems, recv_sems = scratch[-2:]
-    rings, sums = scratch[:3], scratch[3:-2]
+    got, sums = scratch[0], scratch[1:-2]
     links = Links(send_sems, recv_sems, line)
     far = [1, line - 1] + list(range(2, line - 1))
     order = far + [0]
@@ -655,8 +832,7 @@
         links.keep(norm_ref, norm),
         links.keep(weight_ref.at[:, :, :, :, pl.ds(0, slim.shape[4])], slim),
     ]
-    mixed_ring = RingSum(links, mixed_ref, mixed_total_ref, *rings[:2])
-    ring = RingSum(links, parts, total_ref, rings[2], None)
+    ring = RingSum(links, parts, total_ref, got)
 
     def items_of(source, space, in_place):
         items = []
@@ -702,7 +878,6 @@
     half = line // 2
     for item in ff_items:
         item.start()
-    mixed_ring.step(0)
 
     def d_middle(index, carry):
         rows = pl.ds(pl.multiple_of(index * 16, 16), 16)
@@ -744,7 +919,6 @@
     for item in out_items:
         item.start()
     core_done(ff_items, half, line)
-    mixed_ring.step(1)
     kv_back[...] = jnp.zeros_like(kv_back)
     for copy in turned:
         copy.wait_recv()
@@ -828,7 +1002,6 @@
     for item in qkv_items:
         item.start()
     core_done(out_items, 0, half)
-    mixed_ring.step(2)
     first_done(ff_items, half, line)
     turn(ff_items, ffs_ref, 0, half)
     ring.step(1)
@@ -839,7 +1012,6 @@
     core_done(qkv_items, 0, line)
     first_done(out_items, half, line)
     turn(out_items, outs_ref, 0, half)
-    mixed_ring.step(3)
     ring.step(3)
     first_done(qkv_items, 0, half)
     turn(out_items, outs_ref, half, line)
@@ -852,7 +1024,7 @@
         copy.wait()
 
 
-def backward_call(small, mixed_parts, out_w, attended, weights, norm, grad_ff, line):
+def backward_call(small, out_w, attended, weights, norm, grad_ff, line):
     f32, bf16 = jnp.float32, jnp.bfloat16
     span_len, width = small[0].shape
     group_len = line * span_len
@@ -868,13 +1040,13 @@
         functools.partial(backward_kernel, line),
         4,
         160,
-        (token, token, token)
+        (token, token)
         + tuple(
             jax.ShapeDtypeStruct((line, rows_each, columns), bf16)
             for columns in (grad_ff.shape[5], width, qkv_cols)
         ),
-        small + (mixed_parts, out_w.reshape(wide), attended, weights, norm, grad_ff),
-        "v" * 10 + "hhhhh" + "vvvhhh",
+        small + (out_w.reshape(wide), attended, weights, norm, grad_ff),
+        "v" * 9 + "hhhhh" + "vvhhh",
         [
             pltpu.VMEM(wide, bf16),
             pltpu.VMEM(slim, bf16),
@@ -891,8 +1063,7 @@
             pltpu.VMEM((group_len, qkv_cols), bf16),
             pltpu.VMEM((line, span_len, width), bf16),
         ]
-        + ring_space(line, (span_len, width))
-        + ring_space(line, (span_len, width))[:1]
+        + [pltpu.VMEM((line - 1, span_len, width), bf16)]
         + sum_space(line, rows_each, grad_ff.shape[5])
         + out_space
         + qkv_space,
@@ -1239,7 +1410,6 @@
     bf16 = jnp.bfloat16
     _, span_len, model_width = tokens.shape
     line = lax.axis_size("z")
-    place = lax.axis_index("z")
     rows_each = w_query.shape[0]
     q_cols = HEADS // line * HD
     ff_cols = w_gate.shape[1] // line
@@ -1279,54 +1449,34 @@
         log_total,
         turns,
         attended_rows,
-        mixed_grad,
         ff_w,
-    ) = forward_call(tokens[0], table, pack_attn, pack_ff, (keep * upstream).astype(bf16), line)
-    inputs = x_blocks.reshape(group_len, model_width).astype(f32)
-    gain_one, gain_two = gain_all[0, :1], gain_all[1, :1]
-    mixed_grad = mixed_grad.reshape(group_len, model_width)
-    ff_w = ff_w.reshape(model_width, 2 * ff_cols)
-    def own_rows(values):
-        return lax.dynamic_slice_in_dim(values, place * span_len, span_len, 0)
-
-    branch = jnp.dot(attended_rows, out_w, preferred_element_type=f32)
-    middle_all = inputs + keep * branch
-    inverse_mid = lax.rsqrt(jnp.mean(middle_all * middle_all, axis=-1, keepdims=True) + epsilon)
-    second_norm = (middle_all * inverse_mid * gain_two).astype(bf16)
-    middle = own_rows(middle_all)
-
-    gate_up = jnp.dot(second_norm, ff_w, preferred_element_type=f32)
-    gate_value = gate_up[:, :ff_cols]
-    up_value = gate_up[:, ff_cols:]
-    gate_sigmoid = jax.nn.sigmoid(gate_value)
-    swish_value = gate_value * gate_sigmoid
-    hidden = (swish_value * up_value).astype(bf16)
-    hidden_grad = against(mixed_grad, down_w)
-    gate_grad = hidden_grad * up_value * gate_sigmoid * (1.0 + gate_value * (1.0 - gate_sigmoid))
-    up_grad = hidden_grad * swish_value
-    both_grad = jnp.concatenate([gate_grad, up_grad], axis=1).astype(bf16)
-
-    def split(values):
-        return values.astype(bf16).reshape(line, span_len, model_width)
-
-    grad_down = over_rows(hidden, mixed_grad).astype(bf16).reshape(2, 2, 2, -1, model_width)
-    norm_grad, grad_down = third_sum(split(against(both_grad, ff_w)), grad_down, line)
+    ) = forward_call(tokens[0], table, pack_attn, pack_ff, line)
+    keep_tile = jnp.broadcast_to(keep, (8, HD))
+    middle, norm_grad, mixed, grad_down, grad_ff = mlp_call(
+        keep_tile,
+        gain_all,
+        (keep * upstream).astype(bf16),
+        x_blocks,
+        attended_rows,
+        out_w,
+        ff_w.reshape(model_width, 2 * ff_cols),
+        down_w,
+        line,
+    )
     grad_down = grad_down.astype(f32)
-    grad_ff = over_rows(second_norm, both_grad).astype(bf16)
-    mixed_parts = split(jnp.dot(hidden, down_w, preferred_element_type=f32))
-    middle_grad, mixed, input_norm_grad, ff_back, out_back, qkv_back = backward_call(
+    output = (middle + keep * mixed).astype(bf16)
+    middle_grad, input_norm_grad, ff_back, out_back, qkv_back = backward_call(
         (
             upstream,
             middle,
             norm_grad,
-            jnp.broadcast_to(keep, (8, HD)),
+            keep_tile,
             gain_all,
             queries,
             both_kv,
             log_total,
             turns,
         ),
-        mixed_parts,
         out_w,
         attended_rows,
         near_w,
@@ -1334,10 +1484,10 @@
         grad_ff.reshape(line, 2, 2, 2, rows_each, 2 * ff_cols),
         line,
     )
-    output = (middle + keep * mixed).astype(bf16)
     ff_back = ff_back.astype(f32)
     qkv_back = qkv_back.astype(f32)
     grad_out = jnp.sum(out_back.astype(f32), axis=0)
+    gain_one = gain_all[0, :1]
     inverse_one = lax.rsqrt(jnp.mean(own_x * own_x, axis=-1, keepdims=True) + epsilon)
     scaled_one = gain_one * input_norm_grad
     input_grad = (

time: 518 us -> 469 us (0.905); the launches traced: 509 us -> 469 us
  matrix products: 52.2 us -> 0 us
  Pallas kernels: 412 us -> 429 us
    dot_general x7 -> x0, matrix products: 52.2 us -> none  [the longest x2 17.4 us: against(): lax.dot_general(left, right, (((1,), (1,)), ((), ())), preferred_element_...]
    pallas_call x3, Pallas kernels: 412 us -> 429 us  [link_call(): pl.pallas_call(kernel, out_shape=shapes, in_specs=specs[:len(arguments)],...]
  transfers between devices with their start and end apart: 2 -> 2, of which waited for: 0 -> 1; matrix products, arithmetic and copies ran while one was open for 5% -> 1% of each run, Pallas kernels for 40% -> 34%
where the time goes in v7:
time: 469 us
  Pallas kernels  429 us (91%)
  between operations  15.2 us (3%)
  other arithmetic  11.3 us (2%)
  local copies, waits for them, and re-layouts  10.2 us (2%)
    pallas_call x3, Pallas kernels, link_call(): pl.pallas_call(kernel, out_shape=shapes, in_specs=specs[:len(arguments)],...  429 us
  transfers between devices with their start and end apart: 2, of which 1 were waited for; matrix products, arithmetic and copies ran while one was open for 1% of the time, Pallas kernels for 34%

profile of v7, /device:TPU:0, one launch (start us, length us, event | category | flops | bytes accessed | tf_op | source)
XLA Modules:
  0.0 469.0 jit_solution(2434088000345370432)
XLA Ops:
  7.3 0.0 all-gather.5.cloned.1.call-start
  7.3 0.7 all-gather.5.cloned.1.call-update
  8.0 0.0 all-gather.3.cloned.1.call-start
  8.0 0.7 all-gather.3.cloned.1.call-update
  9.4 1.0 copy.65
  10.4 0.2 dynamic_update_slice.6
  10.6 0.2 dynamic_update_slice.7
  10.9 0.3 multiply_cosine_fusion
  11.2 0.1 pad_maximum_fusion.2.table_ref
  11.4 0.1 bitcast_bitcast_fusion
  11.5 0.0 copy-start
  11.5 0.1 pad_maximum_fusion.ff_ref
  11.7 0.9 copy-done
  12.6 159.3 %shard_map.230 = (bf16[4,128,2048]{2,1,0:T(8,128)(2,1)}, bf16[4,8,80,768]{3,2,1,0:T(8,128)(2,1)}, f32[2,16,2048]{2,1,0:T(8,128)S(1)}, bf16[512,2048]{1,0:T(8,128...) custom-call(bf16[128,2048]{1,0:T(8,128)(2,1)S(1)} %bitcast.78, ...), custom_call_target="tpu_custom_call" | custom-call | tf_op jit(solution)/shard_map/pallas_call | solution.py:470
  171.9 0.8 copy-done.2
  172.7 0.8 copy-done.3
  173.4 0.8 copy-done.4
  174.2 0.7 copy-done.5
  175.0 0.1 fusion.7
  175.0 1.4 convert_multiply_fusion.3
  176.4 2.2 all-gather.3.cloned.1.call-done
  178.6 0.6 broadcast_in_dim.34.keep_ref
  179.2 118.0 %shard_map.231 = (f32[128,2048]{1,0:T(8,128)}, f32[128,2048]{1,0:T(8,128)}, f32[128,2048]{1,0:T(8,128)}, bf16[176,2048]{1,0:T(8,128)(2,1)}, bf16[2048,2816]{1,0:T(8,128)(2,1)}) custom-call(f32[8,128]{1,0:T(8,128)} %broadcast_in_dim.34.keep_ref, f32[2,16,2048]{2,1,0:T(8,128)} %copy-done.1, bf16[128,2048]{1,0:T(8,128)(2,1)} %get-tuple-element.62.mix_ref, ...), custom_call_target="tpu_custom_call" | custom-call | tf_op jit(solution)/shard_map/pallas_call | solution.py:470
  297.2 151.4 %shard_map.232 = (f32[128,2048]{1,0:T(8,128)}, f32[128,2048]{1,0:T(8,128)}, bf16[4,64,2816]{2,1,0:T(8,128)(2,1)}, bf16[4,64,2048]{2,1,0:T(8,128)(2,1)}, bf16[4,64,768]{2,1,0:T(8,128)(2,1)}) custom-call(f32[128,2048]{1,0:T(8,128)} %get-tuple-element.61.up_ref, f32[128,2048]{1,0:T(8,128)} %get-tuple-element.35.middle_ref, ...), custom_call_target="tpu_custom_call" | custom-call | tf_op jit(solution)/shard_map/pallas_call | solution.py:470
  448.6 1.2 convert_element_type.78
  449.9 0.1 slice_bitcast_fusion.2
  449.9 0.0 copy-done.8
  450.0 0.3 copy-done.18
  450.3 0.9 fusion.5
  451.2 0.1 copy-done.9
  451.2 0.3 fusion
  451.6 0.8 copy-done.16
  452.4 0.9 convert_reduce_fusion
  453.4 0.2 multiply_reduce_fusion.2
  453.6 0.8 multiply_reduce_fusion.4
  454.4 0.8 multiply_reduce_fusion.3
  455.2 1.3 convert_element_type.87
  456.4 0.2 convert_element_type.84
  456.7 0.2 slice_bitcast_fusion
  456.9 0.1 copy.55
  457.1 1.1 copy-done.11
  458.2 0.3 multiply_reduce_fusion
  458.5 0.1 copy.54
  458.6 1.1 copy-done.13
  459.7 0.3 multiply_reduce_fusion.1
  460.0 0.5 convert_divide_fusion
  460.5 0.5 convert_divide_fusion.1
  461.0 1.2 fusion.6
  (58 shorter events, 0.3 us)
Async XLA Ops:
  7.2 3.2 copy-start.24
  7.2 3.4 copy-start.25
  7.2 3.6 copy-start.26
  7.2 4.1 copy-start.23
  7.2 4.1 copy-start.22
  7.2 4.1 copy-start.12
  7.2 4.1 copy-start.10
  7.3 169.2 %all-gather.5.cloned.1.call-start = ((), (), s32[]{:S(2)}) async-start(), calls=%async_computation.1 | async-start | bytes 6488064 | tf_op jit(solution)/shard_map/all_gather | solution.py:1422
  8.0 170.6 %all-gather.3.cloned.1.call-start = ((), (), s32[]{:S(2)}) async-start(), calls=%async_computation | async-start | bytes 8650752 | tf_op jit(solution)/shard_map/all_gather | solution.py:1421
  11.5 1.0 copy-start
  11.7 163.3 %copy-start.27 = (f32[2]{0:T(128)S(1)}, f32[2]{0:T(128)}, u32[]{:S(2)}) copy-start(f32[2]{0:T(128)} %param.28) | copy-start | bytes 28
  11.7 163.3 %copy-start.28 = (s32[1,128]{1,0:T(1,128)S(1)}, s32[1,128]{1,0:T(1,128)}, u32[]{:S(2)}) copy-start(s32[1,128]{1,0:T(1,128)} %param.26) | copy-start | bytes 1540
  11.7 163.4 %copy-start.21 = (bf16[1,128,2048]{2,1,0:T(8,128)(2,1)S(1)}, bf16[1,128,2048]{2,1,0:T(8,128)(2,1)}, u32[]{:S(2)}) copy-start(bf16[1,128,2048]{2,1,0:T(8,128)(2,1)} %param.29) | copy-start | bytes 1572868
  171.9 0.8 copy-start.2
  172.6 0.8 copy-start.3
  173.4 0.8 copy-start.4
  174.2 0.7 copy-start.5
  174.9 4.3 copy-start.1
  448.6 1.3 copy-start.8
  448.6 1.7 copy-start.18
  449.9 1.3 copy-start.9
  451.2 1.2 copy-start.16
  451.6 1.9 copy-start.19
  453.4 1.8 copy-start.20
  453.4 3.0 copy-start.14
  453.6 2.8 copy-start.15
  456.9 1.3 copy-start.11
  457.0 1.5 copy-start.6
  458.4 1.3 copy-start.13
  458.6 3.6 copy-start.7
  458.6 2.4 copy-start.17
Sparse Core Ops, SparseCore 0:
  10.0 63.5 all-gather.4
  76.4 102.1 all-gather.2

commit v8 on v7

--- a/solution.py
+++ b/solution.py
@@ -538,6 +538,7 @@
     mixed_total_ref,
     sum_ref,
     grad_ff_ref,
+    ff_half_ref,
     big,
     ff,
     down,
@@ -556,9 +557,12 @@
     space, (send_sems, recv_sems) = scratch[:-2], scratch[-2:]
     links = Links(send_sems, recv_sems, line)
     links.meet(["x", "y", "c", 1, line - 1])
+    far = [1, line - 1] + list(range(2, line - 1))
     span_len, width = mix_ref.shape
     group_len = line * span_len
     ff_cols = hidden.shape[1]
+    block_rows = width // line
+    rows_each = block_rows // 8
     chunk = 2 * HD
     stay = links.keep(mix_ref, mixed.at[links.z])
     mix_ring = RingGather(links, mix_ref, lambda block, rows: mixed.at[block, rows])
@@ -572,9 +576,25 @@
     ring = RingSum(links, parts, total_ref, got)
     mixed_ring = RingSum(links, mixed_parts, mixed_total_ref, mixed_got)
     items = []
+    ff_items = []
+    for index, k in enumerate(far[:2]):
+        block = links.along(k)
+        core, first, second = space[:3]
+        ff_items.append(
+            NearSum(
+                links,
+                lambda c, block=block: ff.at[block, :, :, c],
+                ff.at[block, :, :, links.c],
+                core.at[index],
+                first.at[index],
+                second.at[index],
+                "xy"[index % 2],
+                True,
+            )
+        )
     for index, (low, high) in enumerate(cuts):
         rows = pl.ds(low, high - low)
-        core, first, second = space[3 * index : 3 * index + 3]
+        core, first, second = space[3 * index + 3 : 3 * index + 6]
         items.append(
             NearSum(
                 links,
@@ -628,12 +648,15 @@
     for copy in late:
         copy.wait()
 
+    def columns_of(lanes, size):
+        return ff[:, :, :, :, :, lanes].reshape(width, size)
+
     def forward(low, size):
         gates, ups = pl.ds(low, size), pl.ds(low + ff_cols, size)
-        gate = jnp.dot(norm[...], ff[:, gates], preferred_element_type=f32)
+        gate = jnp.dot(norm[...], columns_of(gates, size), preferred_element_type=f32)
         gate_up[:, gates] = gate
         swish = gate * jax.nn.sigmoid(gate)
-        up = jnp.dot(norm[...], ff[:, ups], preferred_element_type=f32)
+        up = jnp.dot(norm[...], columns_of(ups, size), preferred_element_type=f32)
         gate_up[:, ups] = up
         hidden[:, gates] = (swish * up).astype(bf16)
 
@@ -673,15 +696,33 @@
     mix_ring.step(3)
     over_chunks(backward, ff_cols)
 
-    def norm_part(low, size):
+    def norm_part(index, carry):
+        size = 4 * rows_each
+        weight = ff[index // 2, lax.rem(index, 2)].reshape(size, 2 * ff_cols)
         value = lax.dot_general(
-            both_grad[...], ff[pl.ds(low, size)], (((1,), (1,)), ((), ())), preferred_element_type=f32
+            both_grad[...], weight, (((1,), (1,)), ((), ())), preferred_element_type=f32
         ).astype(bf16)
-        parts[:, :, pl.ds(low, size)] = value.reshape(line, span_len, size)
-
-    over_chunks(norm_part, width)
+        lanes = pl.ds(pl.multiple_of(index * size, size), size)
+        parts[:, :, lanes] = value.reshape(line, span_len, size)
+        return carry
+
+    lax.fori_loop(0, 2 * line, norm_part, 0)
     ring.step(0)
     mixed_ring.step(1)
+
+    def ff_block(block):
+        norm_rows = norm[:, pl.ds(pl.multiple_of(block * block_rows, block_rows), block_rows)].T
+
+        def ff_part(low, size):
+            lanes = pl.ds(low, size)
+            value = jnp.dot(norm_rows, both_grad[:, lanes], preferred_element_type=f32)
+            ff[block, :, :, :, :, lanes] = value.astype(bf16).reshape(2, 2, 2, rows_each, size)
+
+        over_chunks(ff_part, 2 * ff_cols)
+
+    for item, k in zip(ff_items, far):
+        ff_block(links.along(k))
+        item.start()
     hidden_rows = hidden[...].T
 
     def down_part(low, size):
@@ -693,32 +734,28 @@
         ).astype(bf16)
         big[:, :, :, : cuts[-1][1], lanes] = value.reshape(2, 2, 2, cuts[-1][1], size)
 
+    ring.step(1)
+    for item in ff_items:
+        item.core_done()
     over_chunks(down_part, width)
     for item in items:
         item.start()
-    ring.step(1)
+    mixed_ring.step(2)
+    ring.step(2)
+    for item in items:
+        item.core_done()
     sent = []
-    block_rows = width // line
-    for z in range(line):
-        norm_rows = norm[:, z * block_rows : (z + 1) * block_rows].T
-
-        def ff_part(low, size, z=z, norm_rows=norm_rows):
-            lanes = pl.ds(low, size)
-            value = jnp.dot(norm_rows, both_grad[:, lanes], preferred_element_type=f32)
-            ff[z * block_rows : (z + 1) * block_rows, lanes] = value.astype(bf16)
-
-        over_chunks(ff_part, 2 * ff_cols)
-        rows = pl.ds(z * block_rows, block_rows)
-        sent.append(links.keep(ff.at[rows], grad_ff_ref.at[rows]))
-        if z == 0:
-            mixed_ring.step(2)
-            for item in items:
-                item.core_done()
-        if z == 1:
-            ring.step(2)
+    for k in far[2:] + [0]:
+        block = links.along(k)
+        ff_block(block)
+        sent.append(links.keep(ff.at[block], grad_ff_ref.at[block]))
+    for item in ff_items:
+        item.first_done()
+    ring.step(3)
     for item in items:
         item.first_done()
-    ring.step(3)
+    for index, item in enumerate(ff_items):
+        sent.append(links.keep(item.second_done(), ff_half_ref.at[index]))
     mixed_ring.step(3)
     for item, (low, high) in zip(items, cuts):
         sum_ref[low:high] = item.second_done()[...]
@@ -731,7 +768,8 @@
     f32, bf16 = jnp.float32, jnp.bfloat16
     span_len, width = mixed.shape
     group_len = line * span_len
-    ff_rows, both_cols = down_w.shape[0], ff_w.shape[1]
+    ff_rows, both_cols, rows_each = down_w.shape[0], ff_w.shape[3], ff_w.shape[2]
+    ff_w = ff_w.reshape(line, 2, 2, 2, rows_each, both_cols)
     rows = ff_rows // 8
     half = (rows // 2 + 15) // 16 * 16
     cuts = ((0, half), (half, rows))
@@ -747,9 +785,10 @@
             token,
             jax.ShapeDtypeStruct((rows, width), bf16),
             jax.ShapeDtypeStruct(ff_w.shape, bf16),
+            jax.ShapeDtypeStruct((2, rows_each, both_cols), bf16),
         ),
         (keep, gains, mixed, x_blocks, attended, out_w.reshape(2, 2, 2, width // 8, width), ff_w, down_w),
-        "vvhhhhhh" + "vvvvh",
+        "vvhhhhhh" + "vvvvhh",
         [
             pltpu.VMEM((2, 2, 2, width // 8, width), bf16),
             pltpu.VMEM(ff_w.shape, bf16),
@@ -764,6 +803,7 @@
             pltpu.VMEM(blocks, bf16),
             pltpu.VMEM((line - 1, span_len, width), bf16),
         ]
+        + sum_space(2, rows_each, both_cols)[1:]
         + sum((sum_space(1, high - low, width)[1:] for low, high in cuts), []),
         vmem=63,
     )
@@ -776,15 +816,16 @@
     norm_grad_ref,
     keep_ref,
     gain_ref,
-    query,
-    kv,
-    peak,
-    turns,
+    query_ref,
+    kv_ref,
+    peak_ref,
+    turn_ref,
     out_ref,
     atts_ref,
     weight_ref,
     norm_ref,
     ff_ref,
+    ff_half_ref,
     middle_grad_ref,
     total_ref,
     ffs_ref,
@@ -804,6 +845,10 @@
     kv_in,
     flat,
     parts,
+    query,
+    kv,
+    peak,
+    turns,
     *scratch,
 ):
     f32, bf16 = jnp.float32, jnp.bfloat16
@@ -829,12 +874,16 @@
         links.keep(out_ref, big),
         links.keep(atts_ref.at[here], own_rows),
         links.keep(atts_ref.at[:, lanes_of(links.z)], own_columns),
+        links.keep(query_ref, query),
+        links.keep(kv_ref, kv),
+        links.keep(peak_ref, peak),
+        links.keep(turn_ref, turns),
         links.keep(norm_ref, norm),
         links.keep(weight_ref.at[:, :, :, :, pl.ds(0, slim.shape[4])], slim),
     ]
     ring = RingSum(links, parts, total_ref, got)
 
-    def items_of(source, space, in_place):
+    def items_of(source, space, in_place, order=order):
         items = []
         for index, k in enumerate(order):
             block = links.along(k)
@@ -854,12 +903,16 @@
             )
         return items
 
-    ff_items = items_of(ff_ref, sums[:4], False)
+    ff_order = order[2:]
+    ff_items = items_of(ff_ref, sums[:4], False, ff_order)
     out_items = items_of(big, sums[4:7], True)
     qkv_items = items_of(slim, sums[7:], True)
-    arrived, local = [], []
-
-    def turn(items, target, low, high):
+    local = []
+    arrived = [
+        links.send(ff_half_ref.at[index], ffs_ref.at[links.z], k) for index, k in enumerate(order[:2])
+    ]
+
+    def turn(items, target, low, high, order=order):
         for item, k in list(zip(items, order))[low:high]:
             total = item.second_done()
             if k == 0:
@@ -905,7 +958,7 @@
         ).astype(bf16)
     turned = [links.send(own_grad.at[:, lanes_of(links.along(k))], att_grad.at[here], k) for k in far]
     stayed = links.keep(own_grad.at[:, lanes_of(links.z)], att_grad.at[here])
-    core_done(ff_items, 0, half)
+    core_done(ff_items, 0, line)
     for z in range(line):
         for part in range(4):
             columns = slice(part * width // 4, (part + 1) * width // 4)
@@ -918,7 +971,6 @@
             big[z, :, :, :, :, columns] = grad.astype(bf16).reshape(2, 2, 2, rows_each, width // 4)
     for item in out_items:
         item.start()
-    core_done(ff_items, half, line)
     kv_back[...] = jnp.zeros_like(kv_back)
     for copy in turned:
         copy.wait_recv()
@@ -973,7 +1025,7 @@
         for head in range(heads):
             lanes = slice(head * HD, (head + 1) * HD)
             flat[rows, lanes] = turn_back(query_back[rows, lanes], rows).astype(bf16)
-    first_done(ff_items, 0, half)
+    first_done(ff_items, 0, line)
     exchange.wait_recv()
     for block in range(line):
         rows = slice(block * span_len, (block + 1) * span_len)
@@ -1002,12 +1054,10 @@
     for item in qkv_items:
         item.start()
     core_done(out_items, 0, half)
-    first_done(ff_items, half, line)
-    turn(ff_items, ffs_ref, 0, half)
+    turn(ff_items, ffs_ref, 0, line, ff_order)
     ring.step(1)
     core_done(out_items, half, line)
     first_done(out_items, 0, half)
-    turn(ff_items, ffs_ref, half, line)
     ring.step(2)
     core_done(qkv_items, 0, line)
     first_done(out_items, half, line)
@@ -1024,11 +1074,11 @@
         copy.wait()
 
 
-def backward_call(small, out_w, attended, weights, norm, grad_ff, line):
+def backward_call(small, saved, out_w, attended, weights, norm, grad_ff, ff_half, line):
     f32, bf16 = jnp.float32, jnp.bfloat16
     span_len, width = small[0].shape
     group_len = line * span_len
-    query = small[5]
+    query = saved[0]
     q_cols, rows_each, qkv_cols = query.shape[1], width // line // 8, weights.shape[3]
     weights = weights.reshape(line, 2, 2, 2, -1, qkv_cols)
     wide = (line, 2, 2, 2, rows_each, width)
@@ -1045,8 +1095,8 @@
             jax.ShapeDtypeStruct((line, rows_each, columns), bf16)
             for columns in (grad_ff.shape[5], width, qkv_cols)
         ),
-        small + (out_w.reshape(wide), attended, weights, norm, grad_ff),
-        "v" * 9 + "hhhhh" + "vvhhh",
+        small + saved + (out_w.reshape(wide), attended, weights, norm, grad_ff, ff_half),
+        "v" * 5 + "h" * 10 + "vvhhh",
         [
             pltpu.VMEM(wide, bf16),
             pltpu.VMEM(slim, bf16),
@@ -1063,8 +1113,9 @@
             pltpu.VMEM((group_len, qkv_cols), bf16),
             pltpu.VMEM((line, span_len, width), bf16),
         ]
+        + [pltpu.VMEM(value.shape, value.dtype) for value in saved]
         + [pltpu.VMEM((line - 1, span_len, width), bf16)]
-        + sum_space(line, rows_each, grad_ff.shape[5])
+        + sum_space(line - 2, rows_each, grad_ff.shape[5])
         + out_space
         + qkv_space,
         vmem=63,
@@ -1439,6 +1490,8 @@
     freqs = 10000.0 ** (-2.0 * jnp.arange(HD // 2, dtype=f32) / HD)
     angles = positions[0].astype(f32)[:, None] * freqs[None, :]
     table = jnp.concatenate([jnp.cos(angles), jnp.sin(angles)], axis=1)
+    own_mixed = (keep * upstream).astype(bf16)
+    first_tokens, own_mixed, upstream = lax.optimization_barrier((tokens[0], own_mixed, upstream))
     (
         x_blocks,
         near_w,
@@ -1450,16 +1503,16 @@
         turns,
         attended_rows,
         ff_w,
-    ) = forward_call(tokens[0], table, pack_attn, pack_ff, line)
+    ) = forward_call(first_tokens, table, pack_attn, pack_ff, line)
     keep_tile = jnp.broadcast_to(keep, (8, HD))
-    middle, norm_grad, mixed, grad_down, grad_ff = mlp_call(
+    middle, norm_grad, mixed, grad_down, grad_ff, ff_half = mlp_call(
         keep_tile,
         gain_all,
-        (keep * upstream).astype(bf16),
+        own_mixed,
         x_blocks,
         attended_rows,
         out_w,
-        ff_w.reshape(model_width, 2 * ff_cols),
+        ff_w,
         down_w,
         line,
     )
@@ -1472,16 +1525,14 @@
             norm_grad,
             keep_tile,
             gain_all,
-            queries,
-            both_kv,
-            log_total,
-            turns,
         ),
+        (queries, both_kv, log_total, turns),
         out_w,
         attended_rows,
         near_w,
         first_norm,
-        grad_ff.reshape(line, 2, 2, 2, rows_each, 2 * ff_cols),
+        grad_ff,
+        ff_half,
         line,
     )
     ff_back = ff_back.astype(f32)

time: 469 us -> 463 us (0.987)
  Pallas kernels: 429 us -> 418 us
    pallas_call x3, Pallas kernels: 429 us -> 418 us  [link_call(): pl.pallas_call(kernel, out_shape=shapes, in_specs=specs[:len(arguments)],...]
where the time goes in v8:
time: 463 us; the launch traced here: 462 us
  Pallas kernels  418 us (90%)
  between operations  15.1 us (3%)
  other arithmetic  11.3 us (2%)
  local copies, waits for them, and re-layouts  10.2 us (2%)
  waiting for transfers between devices  7.66 us (2%)
    pallas_call x3, Pallas kernels, link_call(): pl.pallas_call(kernel, out_shape=shapes, in_specs=specs[:len(arguments)],...  418 us
  transfers between devices with their start and end apart: 2, of which 1 were waited for; matrix products, arithmetic and copies ran while one was open for 1% of the time, Pallas kernels for 34%

profile of v8, /device:TPU:0, one launch (start us, length us, event | category | flops | bytes accessed | tf_op | source)
XLA Modules:
  0.0 462.4 jit_solution(14972759169514265186)
XLA Ops:
  7.2 0.0 all-gather.5.cloned.1.call-start
  7.3 0.7 all-gather.5.cloned.1.call-update
  8.0 0.0 all-gather.3.cloned.1.call-start
  8.0 0.7 all-gather.3.cloned.1.call-update
  9.4 1.0 copy.65
  10.4 0.1 fusion.7
  10.5 1.3 convert_multiply_fusion.3
  11.9 0.2 dynamic_update_slice.6
  12.1 0.2 dynamic_update_slice.7
  12.3 0.3 multiply_cosine_fusion
  12.6 0.1 pad_maximum_fusion.2.table_ref
  12.8 0.1 bitcast_bitcast_fusion
  13.0 0.1 pad_maximum_fusion.ff_ref
  13.1 0.9 copy-done
  14.0 157.2 %shard_map.230 = (bf16[4,128,2048]{2,1,0:T(8,128)(2,1)}, bf16[4,8,80,768]{3,2,1,0:T(8,128)(2,1)}, f32[2,16,2048]{2,1,0:T(8,128)S(1)}, bf16[512,2048]{1,0:T(8,128...) custom-call(bf16[128,2048]{1,0:T(8,128)(2,1)S(1)} %bitcast.77, ...), custom_call_target="tpu_custom_call" | custom-call | tf_op jit(solution)/shard_map/pallas_call | solution.py:470
  171.2 0.8 copy-done.2
  172.0 0.8 copy-done.3
  172.8 0.8 copy-done.4
  173.6 0.7 copy-done.5
  174.3 0.0 all-gather.5.cloned.1.call-done.down_ref
  174.3 6.3 %all-gather.3.cloned.1.call-done = bf16[2048,2048]{1,0:T(8,128)(2,1)} async-done(((bf16[64,2048]{1,0:T(8,128)(2,1)}), bf16[2048,2048]{1,0:T(8,128)(2,1)}) %all-gather.3.cloned.1.call-update) | async-done | bytes 8388624 | tf_op jit(solution)/shard_map/all_gather | solution.py:1472
  180.6 0.6 broadcast_in_dim.34.keep_ref
  181.2 126.3 %shard_map.231 = (f32[128,2048]{1,0:T(8,128)}, f32[128,2048]{1,0:T(8,128)}, f32[128,2048]{1,0:T(8,128)}, bf16[176,2048]{1,0:T(8,128)(2,1)}, bf16[4,2,2,2,64,2816...) custom-call(f32[8,128]{1,0:T(8,128)} %broadcast_in_dim.34.keep_ref, f32[2,16,2048]{2,1,0:T(8,128)} %copy-done.1, ...), custom_call_target="tpu_custom_call" | custom-call | tf_op jit(solution)/shard_map/pallas_call | solution.py:470
  307.5 134.6 %shard_map.232 = (f32[128,2048]{1,0:T(8,128)}, f32[128,2048]{1,0:T(8,128)}, bf16[4,64,2816]{2,1,0:T(8,128)(2,1)}, bf16[4,64,2048]{2,1,0:T(8,128)(2,1)}, bf16[4,64,768]{2,1,0:T(8,128)(2,1)}) custom-call(f32[128,2048]{1,0:T(8,128)} %get-tuple-element.43.up_ref, f32[128,2048]{1,0:T(8,128)} %get-tuple-element.41.middle_ref, ...), custom_call_target="tpu_custom_call" | custom-call | tf_op jit(solution)/shard_map/pallas_call | solution.py:470
  442.1 1.2 convert_element_type.78
  443.3 0.1 slice_bitcast_fusion.2
  443.4 0.0 copy-done.8
  443.4 0.3 copy-done.18
  443.7 0.9 fusion.5
  444.6 0.1 copy-done.9
  444.7 0.3 fusion
  445.0 0.8 copy-done.16
  445.9 0.9 convert_reduce_fusion
  446.9 0.2 multiply_reduce_fusion.2
  447.0 0.8 multiply_reduce_fusion.4
  447.8 0.8 multiply_reduce_fusion.3
  448.6 1.3 convert_element_type.87
  449.9 0.2 convert_element_type.84
  450.1 0.2 slice_bitcast_fusion
  450.3 0.1 copy.55
  450.5 1.1 copy-done.11
  451.6 0.3 multiply_reduce_fusion
  451.9 0.1 copy.54
  452.0 1.1 copy-done.13
  453.1 0.3 multiply_reduce_fusion.1
  453.4 0.5 convert_divide_fusion
  453.9 0.5 convert_divide_fusion.1
  454.4 1.2 fusion.6
  (58 shorter events, 0.3 us)
Async XLA Ops:
  7.2 3.2 copy-start.26
  7.2 3.2 copy-start.27
  7.2 3.3 copy-start.21
  7.2 167.1 %all-gather.5.cloned.1.call-start = ((), (), s32[]{:S(2)}) async-start(), calls=%async_computation.1 | async-start | bytes 6488064 | tf_op jit(solution)/shard_map/all_gather | solution.py:1473
  7.9 3.9 copy-start.24
  8.0 4.1 copy-start.25
  8.0 4.3 copy-start.28
  8.0 172.6 %all-gather.3.cloned.1.call-start = ((), (), s32[]{:S(2)}) async-start(), calls=%async_computation | async-start | bytes 8650752 | tf_op jit(solution)/shard_map/all_gather | solution.py:1472
  9.4 3.3 copy-start.22
  9.4 3.3 copy-start.23
  10.5 2.3 copy-start.10
  10.5 2.3 copy-start.12
  13.0 1.0 copy-start
  171.2 0.8 copy-start.2
  172.0 0.8 copy-start.3
  172.8 0.8 copy-start.4
  173.6 0.7 copy-start.5
  174.3 6.9 %copy-start.1 = (f32[2,16,2048]{2,1,0:T(8,128)}, f32[2,16,2048]{2,1,0:T(8,128)S(1)}, u32[]{:S(2)}) copy-start(f32[2,16,2048]{2,1,0:T(8,128)S(1)} %get-tuple-element.36.gain_ref) | copy-start | bytes 786436
  442.0 1.3 copy-start.8
  442.0 1.7 copy-start.18
  443.4 1.3 copy-start.9
  444.6 1.2 copy-start.16
  445.0 1.9 copy-start.19
  446.8 1.8 copy-start.20
  446.8 3.0 copy-start.14
  447.0 2.8 copy-start.15
  450.3 1.3 copy-start.11
  450.5 1.5 copy-start.6
  451.9 1.3 copy-start.13
  452.0 3.6 copy-start.7
  452.0 2.4 copy-start.17
Sparse Core Ops, SparseCore 0:
  9.9 64.9 all-gather.4
  77.8 102.7 all-gather.2

commit v9 on v8

--- a/solution.py
+++ b/solution.py
@@ -151,6 +151,12 @@
             for to in ("c", "xc", "yc", "xyc"):
                 self.got[block, to].wait_recv()
 
+    def settle(self):
+        for copy in self.got.values():
+            copy.wait_send()
+        mine = [id(copy) for copy in self.got.values()]
+        self.links.sent = [copy for copy in self.links.sent if id(copy) not in mine]
+
 
 class RingGather:
     def __init__(self, links, source, place, pieces=4):
@@ -172,10 +178,12 @@
 
 def first_kernel(
     line,
+    freq_ref,
     x_ref,
-    table_ref,
+    place_ref,
     pack_ref,
     ff_ref,
+    out_ref,
     xs_ref,
     weight_ref,
     gain_ref,
@@ -186,8 +194,9 @@
     turn_ref,
     atts_ref,
     ffs_ref,
+    outs_ref,
     x_all,
-    tables,
+    places,
     weights,
     gains,
     norm,
@@ -214,40 +223,59 @@
 
     near = NearGather(links, lambda block, place: weights.at[links.along(-block), place])
     far_ff = NearGather(links, lambda block, place: ffs_ref.at[links.along(-block), place])
+    far_out = NearGather(links, lambda block, place: outs_ref.at[links.along(-block), place])
     ring = RingGather(links, x_ref, lambda block, rows: x_all.at[block, rows])
     own = [
         links.keep(x_ref, x_all.at[links.z]),
-        links.keep(table_ref, tables.at[links.z]),
+        links.keep(place_ref, places.at[links.z]),
         links.keep(pack_ref.at[links.z], weights.at[links.z, here]),
     ]
     turned = {k: links.send(pack_ref.at[links.along(k)], weights.at[links.z, here], k) for k in far}
-    placed = [links.send(table_ref, tables.at[links.z], k) for k in far]
-    ring.step(0)
+    placed = [links.send(place_ref, places.at[links.z], k) for k in far]
+    turned_ff = {k: links.send(ff_ref.at[links.along(k)], ffs_ref.at[links.z, here], k) for k in far}
     near.offer(0, pack_ref.at[links.z])
+    far_ff.offer(0, ff_ref.at[links.z])
     local.append(links.keep(ff_ref.at[links.z], ffs_ref.at[links.z, here]))
+    local.append(links.keep(out_ref, outs_ref.at[links.z, here]))
+
+    def move_out(k):
+        moved.wait_recv()
+        block = outs_ref.at[links.along(-k), here]
+        onward = links.send(block, block, 1) if k < line - 1 else None
+        far_out.offer(k, block)
+        return onward
+
     for k in far:
         turned[k].wait_recv()
         near.offer(k, weights.at[links.along(-k), here])
+    ring.step(0)
+    for k in [0] + far:
+        near.relay(k, "x" if k < line // 2 else "y")
+    turned_ff[far[0]].wait_recv()
+    far_ff.offer(far[0], ffs_ref.at[links.along(-far[0]), here])
     ring.step(1)
     for k in [0] + far:
-        near.relay(k, "x" if k < line // 2 else "y")
-    far_ff.offer(0, ff_ref.at[links.z])
+        near.close(k)
+    far_ff.relay(0, "x")
     ring.step(2)
-    turned_ff = {k: links.send(ff_ref.at[links.along(k)], ffs_ref.at[links.z, here], k) for k in far}
-    for k in [0] + far:
-        near.close(k)
+    moved = links.send(out_ref, outs_ref.at[links.z, here], 1)
+    far_out.offer(0, out_ref)
     for copy in own:
         copy.wait()
     for copy in placed:
         copy.wait_recv()
 
     lane = lax.broadcasted_iota(jnp.int32, (span_len, HD), 1)
+    token = lax.broadcasted_iota(jnp.int32, (span_len, span_len), 0)
+    across = lax.broadcasted_iota(jnp.int32, (span_len, span_len), 1)
     for block in range(line):
-        table = tables[block]
-        swapped = pltpu.roll(table, HD // 2, 1)
+        row = jnp.broadcast_to(places[block, 0:1], (span_len, span_len))
+        column = jnp.sum(jnp.where(token == across, row, 0.0), axis=1, keepdims=True)
+        angles = column * freq_ref[0:1]
         rows = slice(block * span_len, (block + 1) * span_len)
-        turns[0, rows] = jnp.where(lane < HD // 2, table, swapped)
-        turns[1, rows] = jnp.where(lane < HD // 2, -swapped, table)
+        sine = jnp.sin(angles)
+        turns[0, rows] = jnp.cos(angles)
+        turns[1, rows] = jnp.where(lane < HD // 2, -sine, sine)
     local.append(links.keep(turns, turn_ref))
     near.wait(range(line))
     for index in range(line * 4):
@@ -258,6 +286,7 @@
             gains[which, :, index * HD : (index + 1) * HD] = both[0] + both[1]
     local.append(links.keep(weights, weight_ref))
     local.append(links.keep(gains, gain_ref))
+    far_ff.relay(far[0], "y")
     ring.step(3)
     local.append(links.keep(x_all, xs_ref))
 
@@ -305,6 +334,7 @@
             query[rows, lanes] = turn(flat[rows, lanes], rows).astype(bf16)
     local.append(links.keep(query, query_ref))
     exchange.wait_recv()
+    moved = move_out(1)
     local.append(links.keep(kv, kv_ref))
 
     scale = 1.0 / math.sqrt(HD)
@@ -349,20 +379,25 @@
     att_ring = RingGather(links, att, place)
     local.append(links.keep(att, place(links.z, pl.ds(0, group_len))))
     att_ring.step(0)
-    for k in far:
+    far_ff.close(0)
+    far_ff.close(far[0])
+    far_out.relay(0, "x")
+    moved = move_out(2)
+    far_out.relay(1, "x")
+    att_ring.step(1)
+    for k in range(3, line):
+        moved = move_out(k)
+    far_out.relay(2, "y")
+    att_ring.step(2)
+    for k in range(3, line):
+        far_out.relay(k, "y")
+    for k in range(line):
+        far_out.close(k)
+    att_ring.step(3)
+    far_out.wait(range(line))
+    far_ff.wait([0, far[0]])
+    for k in far[1:]:
         turned_ff[k].wait_recv()
-        far_ff.offer(k, ffs_ref.at[links.along(-k), here])
-    far_ff.relay(0, "x")
-    far_ff.close(0)
-    far_ff.relay(far[0], "x")
-    att_ring.step(1)
-    for k in far[1:]:
-        far_ff.relay(k, "x" if k < line // 2 else "y")
-    att_ring.step(2)
-    for k in far:
-        far_ff.close(k)
-    att_ring.step(3)
-    far_ff.wait(range(line))
     links.finish()
     for copy in local:
         copy.wait()
@@ -480,7 +515,7 @@
     )(*arguments)
 
 
-def forward_call(tokens, table, pack, pack_ff, line):
+def forward_call(freqs, tokens, places, pack, pack_ff, w_out, line):
     span_len, width = tokens.shape
     group_len = line * span_len
     rows_each = pack_ff.shape[1]
@@ -498,16 +533,18 @@
         ((2, group_len, HD), f32),
         ((group_len, line * q_cols), bf16),
         ((line, 8) + pack_ff.shape[1:], bf16),
+        ((line, 8) + w_out.shape, bf16),
     )
     return link_call(
         functools.partial(first_kernel, line),
         0,
         176,
         tuple(jax.ShapeDtypeStruct(*out) for out in outs),
-        (tokens, table, pack, pack_ff),
+        (freqs, tokens, places, pack, pack_ff, w_out),
+        "v" + "h" * 16,
         scratch=[
             pltpu.VMEM((line, span_len, width), bf16),
-            pltpu.VMEM((line,) + table.shape, f32),
+            pltpu.VMEM((line,) + places.shape, f32),
             pltpu.VMEM((line, 8) + pack.shape[1:], bf16),
             pltpu.VMEM((2, 16, width), f32),
             pltpu.VMEM((group_len, width), bf16),
@@ -572,7 +609,17 @@
         links.keep(atts_ref, norm),
         links.keep(xs_ref, parts),
     ]
-    late = [links.keep(ff_ref, ff), links.keep(down_ref, down)]
+    here = (links.x, links.y, links.c)
+    near = NearGather(
+        links, lambda block, place: ff.at[links.along(-block), place // 4, place // 2 % 2, place % 2]
+    )
+    late = [links.keep(down_ref, down)]
+    for k in (0, far[0]):
+        late.append(links.keep(ff_ref.at[links.along(-k)], ff.at[links.along(-k)]))
+    for k in far[1:]:
+        block = ff_ref.at[(links.along(-k),) + here]
+        late.append(links.keep(block, ff.at[(links.along(-k),) + here]))
+        near.offer(k, block)
     ring = RingSum(links, parts, total_ref, got)
     mixed_ring = RingSum(links, mixed_parts, mixed_total_ref, mixed_got)
     items = []
@@ -644,7 +691,13 @@
             where = pl.multiple_of(lax.rem(links.z, line // 2) * span_len, span_len)
             middle_ref[...] = gate_up[pl.ds(where, span_len), :width]
 
+        for index, k in enumerate(far[1:]):
+            if part == 0:
+                near.relay(k, "xy"[index % 2])
+            else:
+                near.close(k)
     mix_ring.step(1)
+    near.wait(far[1:])
     for copy in late:
         copy.wait()
 
@@ -707,6 +760,7 @@
         return carry
 
     lax.fori_loop(0, 2 * line, norm_part, 0)
+    near.settle()
     ring.step(0)
     mixed_ring.step(1)
 
@@ -1469,7 +1523,6 @@
     def by_columns(weight, columns):
         return weight.reshape(rows_each, line, columns).transpose(1, 0, 2)
 
-    out_w = lax.all_gather(w_out, ("z", "x", "y", "c"), axis=0, tiled=True)
     down_w = lax.all_gather(w_down, ("x", "y", "c"), axis=0, tiled=True)
     own_x = tokens[0].astype(f32)
     keep = keep_mask[0].astype(f32)
@@ -1488,8 +1541,8 @@
     pack_attn = jnp.concatenate([pack_attn, gain_rows], axis=1)
     pack_ff = jnp.concatenate([by_columns(w_gate, ff_cols), by_columns(w_up, ff_cols)], axis=2)
     freqs = 10000.0 ** (-2.0 * jnp.arange(HD // 2, dtype=f32) / HD)
-    angles = positions[0].astype(f32)[:, None] * freqs[None, :]
-    table = jnp.concatenate([jnp.cos(angles), jnp.sin(angles)], axis=1)
+    freqs = jnp.broadcast_to(jnp.concatenate([freqs, freqs])[None], (8, HD))
+    places = jnp.broadcast_to(positions[0].astype(f32)[None], (8, span_len))
     own_mixed = (keep * upstream).astype(bf16)
     first_tokens, own_mixed, upstream = lax.optimization_barrier((tokens[0], own_mixed, upstream))
     (
@@ -1503,7 +1556,8 @@
         turns,
         attended_rows,
         ff_w,
-    ) = forward_call(first_tokens, table, pack_attn, pack_ff, line)
+        out_w,
+    ) = forward_call(freqs, first_tokens, places, pack_attn, pack_ff, w_out, line)
     keep_tile = jnp.broadcast_to(keep, (8, HD))
     middle, norm_grad, mixed, grad_down, grad_ff, ff_half = mlp_call(
         keep_tile,

time: 463 us -> 457 us (0.987)
  waiting for transfers between devices: 7.66 us -> 0.7 us
    all_gather x1 -> x0, waiting for transfers between devices: 6.26 us -> none  [line_body(): out_w = lax.all_gather(w_out, ('z', 'x', 'y', 'c'), axis=0, tiled=True)]
  transfers between devices with their start and end apart: 2 -> 1, of which waited for: 1 -> 0; matrix products, arithmetic and copies ran while one was open for 1% -> 1% of each run, Pallas kernels for 34% -> 32%
where the time goes in v9:
time: 457 us; the launch traced here: 454 us
  Pallas kernels  416 us (91%)
  between operations  15.1 us (3%)
  other arithmetic  11.7 us (3%)
  local copies, waits for them, and re-layouts  10.3 us (2%)
    pallas_call x3, Pallas kernels, link_call(): pl.pallas_call(kernel, out_shape=shapes, in_specs=specs[:len(arguments)],...  416 us
  transfers between devices with their start and end apart: 1, of which 0 were waited for; matrix products, arithmetic and copies ran while one was open for 1% of the time, Pallas kernels for 32%

profile of v9, /device:TPU:0, one launch (start us, length us, event | category | flops | bytes accessed | tf_op | source)
XLA Modules:
  0.0 453.7 jit_solution(3187875885442274286)
XLA Ops:
  7.2 0.0 all-gather.2.cloned.1.call-start
  7.2 0.7 all-gather.2.cloned.1.call-update
  8.7 1.0 copy.65
  9.6 0.8 fusion.7
  10.4 1.3 convert_multiply_fusion.3
  11.8 0.2 dynamic_update_slice.6
  12.0 0.2 dynamic_update_slice.7
  12.2 0.1 pad_maximum_fusion.2
  12.4 0.1 bitcast_bitcast_fusion
  12.5 0.0 copy-start
  12.5 0.1 pad_maximum_fusion.ff_ref
  12.7 0.9 copy-done
  13.6 0.1 copy-done.6
  13.6 145.3 %shard_map.230 = (bf16[4,128,2048]{2,1,0:T(8,128)(2,1)}, bf16[4,8,80,768]{3,2,1,0:T(8,128)(2,1)}, f32[2,16,2048]{2,1,0:T(8,128)S(1)}, bf16[512,2048]{1,0:T(8,128...) custom-call(f32[8,128]{1,0:T(8,128)S(1)} %broadcast_in_dim.47.freq_r, ...), custom_call_target="tpu_custom_call" | custom-call | tf_op jit(solution)/shard_map/pallas_call | solution.py:505
  158.9 0.0 copy-start.2
  158.9 0.8 copy-done.2
  159.7 0.8 copy-done.3
  160.5 0.8 copy-done.4
  161.3 0.7 copy-done.5
  162.0 0.0 all-gather.2.cloned.1.call-done.down_ref
  162.0 0.6 broadcast_in_dim.46.keep_ref
  162.7 0.0 copy-done.1
  162.7 142.2 %shard_map.231 = (f32[128,2048]{1,0:T(8,128)}, f32[128,2048]{1,0:T(8,128)}, f32[128,2048]{1,0:T(8,128)}, bf16[176,2048]{1,0:T(8,128)(2,1)}, bf16[4,2,2,2,64,2816...) custom-call(f32[8,128]{1,0:T(8,128)} %broadcast_in_dim.46.keep_ref, f32[2,16,2048]{2,1,0:T(8,128)} %copy-done.1, ...), custom_call_target="tpu_custom_call" | custom-call | tf_op jit(solution)/shard_map/pallas_call | solution.py:505
  304.9 128.4 %shard_map.232 = (f32[128,2048]{1,0:T(8,128)}, f32[128,2048]{1,0:T(8,128)}, bf16[4,64,2816]{2,1,0:T(8,128)(2,1)}, bf16[4,64,2048]{2,1,0:T(8,128)(2,1)}, bf16[4,64,768]{2,1,0:T(8,128)(2,1)}) custom-call(f32[128,2048]{1,0:T(8,128)} %get-tuple-element.45.up_ref, f32[128,2048]{1,0:T(8,128)} %get-tuple-element.43.middle_ref, ...), custom_call_target="tpu_custom_call" | custom-call | tf_op jit(solution)/shard_map/pallas_call | solution.py:505
  433.3 1.2 convert_element_type.71
  434.5 0.1 slice_bitcast_fusion.2
  434.6 0.0 copy-done.9
  434.6 0.3 copy-done.19
  434.9 0.9 fusion.5
  435.8 0.1 copy-done.10
  435.9 0.3 fusion
  436.2 0.8 copy-done.17
  437.1 0.9 convert_reduce_fusion
  438.1 0.2 multiply_reduce_fusion.2
  438.3 0.8 multiply_reduce_fusion.4
  439.0 0.8 multiply_reduce_fusion.3
  439.8 1.3 convert_element_type.80
  441.1 0.2 convert_element_type.77
  441.3 0.2 slice_bitcast_fusion
  441.6 0.1 copy.55
  441.7 1.1 copy-done.12
  442.8 0.3 multiply_reduce_fusion
  443.1 0.1 copy.54
  443.3 1.1 copy-done.14
  444.3 0.3 multiply_reduce_fusion.1
  444.6 0.5 convert_divide_fusion
  445.1 0.5 convert_divide_fusion.1
  445.7 1.2 fusion.6
  (54 shorter events, 0.3 us)
Async XLA Ops:
  7.2 3.2 copy-start.22
  7.2 154.8 %all-gather.2.cloned.1.call-start = ((), (), s32[]{:S(2)}) async-start(), calls=%async_computation | async-start | bytes 6488064 | tf_op jit(solution)/shard_map/all_gather | solution.py:1526
  7.9 3.8 copy-start.25
  7.9 4.0 copy-start.26
  7.9 4.3 copy-start.23
  8.0 4.3 copy-start.24
  10.4 2.0 copy-start.27
  10.4 2.0 copy-start.11
  10.4 2.0 copy-start.13
  12.5 1.0 copy-start
  12.5 1.1 copy-start.6
  158.9 0.8 copy-start.2
  159.7 0.8 copy-start.3
  160.5 0.8 copy-start.4
  161.3 0.7 copy-start.5
  162.0 0.7 copy-start.1
  433.3 1.3 copy-start.9
  433.3 1.7 copy-start.19
  434.6 1.3 copy-start.10
  435.8 1.2 copy-start.17
  436.2 1.9 copy-start.20
  438.0 1.8 copy-start.21
  438.1 3.0 copy-start.15
  438.3 2.8 copy-start.16
  441.5 1.3 copy-start.12
  441.7 1.5 copy-start.7
  443.1 1.3 copy-start.14
  443.2 3.6 copy-start.8
  443.2 2.4 copy-start.18
Sparse Core Ops, SparseCore 0:
  9.9 69.4 all-gather.1

commit v10 on v9

--- a/solution.py
+++ b/solution.py
@@ -150,12 +150,6 @@
         for block in blocks:
             for to in ("c", "xc", "yc", "xyc"):
                 self.got[block, to].wait_recv()
-
-    def settle(self):
-        for copy in self.got.values():
-            copy.wait_send()
-        mine = [id(copy) for copy in self.got.values()]
-        self.links.sent = [copy for copy in self.links.sent if id(copy) not in mine]
 
 
 class RingGather:
@@ -251,8 +245,9 @@
     ring.step(0)
     for k in [0] + far:
         near.relay(k, "x" if k < line // 2 else "y")
-    turned_ff[far[0]].wait_recv()
-    far_ff.offer(far[0], ffs_ref.at[links.along(-far[0]), here])
+    for k in far:
+        turned_ff[k].wait_recv()
+        far_ff.offer(k, ffs_ref.at[links.along(-k), here])
     ring.step(1)
     for k in [0] + far:
         near.close(k)
@@ -286,7 +281,7 @@
             gains[which, :, index * HD : (index + 1) * HD] = both[0] + both[1]
     local.append(links.keep(weights, weight_ref))
     local.append(links.keep(gains, gain_ref))
-    far_ff.relay(far[0], "y")
+    far_ff.relay(far[0], "x")
     ring.step(3)
     local.append(links.keep(x_all, xs_ref))
 
@@ -333,6 +328,8 @@
             lanes = slice(head * HD, (head + 1) * HD)
             query[rows, lanes] = turn(flat[rows, lanes], rows).astype(bf16)
     local.append(links.keep(query, query_ref))
+    for k in far[1:]:
+        far_ff.relay(k, "x" if k < line // 2 else "y")
     exchange.wait_recv()
     moved = move_out(1)
     local.append(links.keep(kv, kv_ref))
@@ -379,8 +376,8 @@
     att_ring = RingGather(links, att, place)
     local.append(links.keep(att, place(links.z, pl.ds(0, group_len))))
     att_ring.step(0)
-    far_ff.close(0)
-    far_ff.close(far[0])
+    for k in [0] + far:
+        far_ff.close(k)
     far_out.relay(0, "x")
     moved = move_out(2)
     far_out.relay(1, "x")
@@ -395,9 +392,7 @@
         far_out.close(k)
     att_ring.step(3)
     far_out.wait(range(line))
-    far_ff.wait([0, far[0]])
-    for k in far[1:]:
-        turned_ff[k].wait_recv()
+    far_ff.wait(range(line))
     links.finish()
     for copy in local:
         copy.wait()
@@ -555,7 +550,7 @@
             pltpu.VMEM((group_len, HD), f32),
             pltpu.VMEM((group_len, q_cols), bf16),
         ],
-        vmem=48,
+        vmem=63,
     )
 
 
@@ -609,17 +604,7 @@
         links.keep(atts_ref, norm),
         links.keep(xs_ref, parts),
     ]
-    here = (links.x, links.y, links.c)
-    near = NearGather(
-        links, lambda block, place: ff.at[links.along(-block), place // 4, place // 2 % 2, place % 2]
-    )
-    late = [links.keep(down_ref, down)]
-    for k in (0, far[0]):
-        late.append(links.keep(ff_ref.at[links.along(-k)], ff.at[links.along(-k)]))
-    for k in far[1:]:
-        block = ff_ref.at[(links.along(-k),) + here]
-        late.append(links.keep(block, ff.at[(links.along(-k),) + here]))
-        near.offer(k, block)
+    late = [links.keep(ff_ref, ff), links.keep(down_ref, down)]
     ring = RingSum(links, parts, total_ref, got)
     mixed_ring = RingSum(links, mixed_parts, mixed_total_ref, mixed_got)
     items = []
@@ -690,14 +675,9 @@
         def _():
             where = pl.multiple_of(lax.rem(links.z, line // 2) * span_len, span_len)
             middle_ref[...] = gate_up[pl.ds(where, span_len), :width]
-
-        for index, k in enumerate(far[1:]):
-            if part == 0:
-                near.relay(k, "xy"[index % 2])
-            else:
-                near.close(k)
-    mix_ring.step(1)
-    near.wait(far[1:])
+        if part == 0:
+            mix_ring.step(1)
+
     for copy in late:
         copy.wait()
 
@@ -747,7 +727,24 @@
     mixed_ring.step(0)
     stay.wait()
     mix_ring.step(3)
+    hidden_rows = hidden[...].T
+
+    def down_part(low, size):
+        lanes = pl.ds(low, size)
+        value = jnp.dot(
+            hidden_rows,
+            mixed[:, :, lanes].reshape(group_len, size),
+            preferred_element_type=f32,
+        ).astype(bf16)
+        big[:, :, :, : cuts[-1][1], lanes] = value.reshape(2, 2, 2, cuts[-1][1], size)
+
+    over_chunks(down_part, width)
+    for item in items:
+        item.start()
     over_chunks(backward, ff_cols)
+    mixed_ring.step(1)
+    for item in items:
+        item.core_done()
 
     def norm_part(index, carry):
         size = 4 * rows_each
@@ -760,9 +757,7 @@
         return carry
 
     lax.fori_loop(0, 2 * line, norm_part, 0)
-    near.settle()
     ring.step(0)
-    mixed_ring.step(1)
 
     def ff_block(block):
         norm_rows = norm[:, pl.ds(pl.multiple_of(block * block_rows, block_rows), block_rows)].T
@@ -777,42 +772,26 @@
     for item, k in zip(ff_items, far):
         ff_block(links.along(k))
         item.start()
-    hidden_rows = hidden[...].T
-
-    def down_part(low, size):
-        lanes = pl.ds(low, size)
-        value = jnp.dot(
-            hidden_rows,
-            mixed[:, :, lanes].reshape(group_len, size),
-            preferred_element_type=f32,
-        ).astype(bf16)
-        big[:, :, :, : cuts[-1][1], lanes] = value.reshape(2, 2, 2, cuts[-1][1], size)
-
+    for item in items:
+        item.first_done()
     ring.step(1)
     for item in ff_items:
         item.core_done()
-    over_chunks(down_part, width)
-    for item in items:
-        item.start()
     mixed_ring.step(2)
-    ring.step(2)
-    for item in items:
-        item.core_done()
     sent = []
     for k in far[2:] + [0]:
         block = links.along(k)
         ff_block(block)
         sent.append(links.keep(ff.at[block], grad_ff_ref.at[block]))
+    for item, (low, high) in zip(items, cuts):
+        sum_ref[low:high] = item.second_done()[...]
+    ring.step(2)
     for item in ff_items:
         item.first_done()
+    mixed_ring.step(3)
     ring.step(3)
-    for item in items:
-        item.first_done()
     for index, item in enumerate(ff_items):
         sent.append(links.keep(item.second_done(), ff_half_ref.at[index]))
-    mixed_ring.step(3)
-    for item, (low, high) in zip(items, cuts):
-        sum_ref[low:high] = item.second_done()[...]
     links.finish()
     for copy in sent:
         copy.wait()

time: 457 us -> 436 us (0.954)
  Pallas kernels: 416 us -> 399 us
    pallas_call x3, Pallas kernels: 416 us -> 399 us  [link_call(): pl.pallas_call(kernel, out_shape=shapes, in_specs=specs[:len(arguments)],...]
    unnamed x59 -> x45, local copies, waits for them, and re-layouts: 7.86 us -> 2.86 us
  transfers between devices with their start and end apart: 1 -> 1, of which waited for: 0 -> 0; matrix products, arithmetic and copies ran while one was open for 1% -> 2% of each run, Pallas kernels for 32% -> 34%
where the time goes in v10:
time: 436 us; the launch traced here: 435 us
  Pallas kernels  399 us (92%)
  between operations  15 us (3%)
  other arithmetic  13.5 us (3%)
  local copies, waits for them, and re-layouts  7.29 us (2%)
    pallas_call x3, Pallas kernels, link_call(): pl.pallas_call(kernel, out_shape=shapes, in_specs=specs[:len(arguments)],...  399 us
  transfers between devices with their start and end apart: 1, of which 0 were waited for; matrix products, arithmetic and copies ran while one was open for 2% of the time, Pallas kernels for 34%

profile of v10, /device:TPU:0, one launch (start us, length us, event | category | flops | bytes accessed | tf_op | source)
XLA Modules:
  0.0 435.3 jit_solution(12001998878937673211)
XLA Ops:
  7.2 0.0 all-gather.2.cloned.1.call-start
  7.2 0.7 all-gather.2.cloned.1.call-update
  8.7 1.0 copy.65
  9.6 0.8 fusion.7
  10.4 0.0 copy-start.5
  10.4 0.0 copy-start.6
  10.4 1.3 convert_multiply_fusion.3
  11.8 0.2 dynamic_update_slice.6
  12.0 0.2 dynamic_update_slice.7
  12.2 0.1 pad_maximum_fusion.2
  12.3 0.8 pad_maximum_fusion.1.pack_ref
  13.1 0.1 bitcast_bitcast_fusion
  13.3 1.2 pad_maximum_fusion.ff_ref
  14.5 0.6 broadcast_in_dim.47.freq_ref
  15.1 0.6 broadcast_in_dim.51.place_ref
  15.7 147.4 %shard_map.230 = (bf16[4,128,2048]{2,1,0:T(8,128)(2,1)}, bf16[4,8,80,768]{3,2,1,0:T(8,128)(2,1)}, f32[2,16,2048]{2,1,0:T(8,128)}, bf16[512,2048]{1,0:T(8,128)(2,...) custom-call(f32[8,128]{1,0:T(8,128)} %broadcast_in_dim.47.freq_ref, ...), custom_call_target="tpu_custom_call" | custom-call | tf_op jit(solution)/shard_map/pallas_call | solution.py:500
  163.1 0.8 slice.18
  163.9 0.6 broadcast_in_dim.46.keep_ref
  164.5 115.8 %shard_map.231 = (f32[128,2048]{1,0:T(8,128)}, f32[128,2048]{1,0:T(8,128)}, f32[128,2048]{1,0:T(8,128)}, bf16[176,2048]{1,0:T(8,128)(2,1)}, bf16[4,2,2,2,64,2816...) custom-call(f32[8,128]{1,0:T(8,128)} %broadcast_in_dim.46.keep_ref, f32[2,16,2048]{2,1,0:T(8,128)} %get-tuple-element.37.gain_ref, ...), custom_call_target="tpu_custom_call" | custom-call | tf_op jit(solution)/shard_map/pallas_call | solution.py:500
  280.3 135.6 %shard_map.232 = (f32[128,2048]{1,0:T(8,128)}, f32[128,2048]{1,0:T(8,128)}, bf16[4,64,2816]{2,1,0:T(8,128)(2,1)}, bf16[4,64,2048]{2,1,0:T(8,128)(2,1)}, bf16[4,64,768]{2,1,0:T(8,128)(2,1)}) custom-call(f32[128,2048]{1,0:T(8,128)} %get-tuple-element.45.up_ref, f32[128,2048]{1,0:T(8,128)} %get-tuple-element.43.middle_ref, ...), custom_call_target="tpu_custom_call" | custom-call | tf_op jit(solution)/shard_map/pallas_call | solution.py:500
  415.9 1.2 convert_element_type.71
  417.2 0.1 slice_bitcast_fusion.2
  417.2 0.0 copy-start.2
  417.3 0.0 copy-done.3
  417.3 0.3 copy-done.12
  417.6 0.9 fusion.5
  418.5 0.2 copy-done.4
  418.7 0.3 fusion
  419.0 0.7 copy-done.10
  419.8 0.9 convert_reduce_fusion
  420.8 0.0 copy-start.8
  420.8 0.2 multiply_reduce_fusion.2
  421.0 0.8 multiply_reduce_fusion.4
  421.7 0.8 multiply_reduce_fusion.3
  422.5 1.3 convert_element_type.80
  423.8 0.2 convert_element_type.77
  424.0 0.2 slice_bitcast_fusion
  424.2 0.1 copy.55
  424.4 0.0 copy-start
  424.4 0.2 multiply_reduce_fusion
  424.6 0.0 copy-start.7
  424.6 0.1 copy.54
  424.8 0.7 copy-done
  425.5 0.5 copy-done.7
  426.0 0.3 multiply_reduce_fusion.1
  426.3 0.5 convert_divide_fusion
  426.8 0.5 convert_divide_fusion.1
  427.3 1.2 fusion.6
  (40 shorter events, 0.2 us)
Async XLA Ops:
  7.2 3.2 copy-start.15
  7.2 156.7 %all-gather.2.cloned.1.call-start = ((), (), s32[]{:S(2)}) async-start(), calls=%async_computation | async-start | bytes 6488064 | tf_op jit(solution)/shard_map/all_gather | solution.py:1505
  7.9 3.8 copy-start.18
  7.9 4.0 copy-start.19
  7.9 4.3 copy-start.16
  8.0 4.3 copy-start.17
  10.4 2.7 copy-start.20
  10.4 2.7 copy-start.5
  10.4 2.7 copy-start.6
  415.9 1.3 copy-start.3
  415.9 1.7 copy-start.12
  417.2 1.3 copy-start.2
  417.3 1.5 copy-start.4
  418.5 1.3 copy-start.10
  419.0 1.8 copy-start.13
  420.7 1.8 copy-start.14
  420.8 3.0 copy-start.8
  421.0 2.8 copy-start.9
  424.4 1.1 copy-start
  424.6 1.4 copy-start.7
  425.5 3.0 copy-start.1
  425.5 1.9 copy-start.11
Sparse Core Ops, SparseCore 0:
  9.9 69.3 all-gather.1

commit v11 on v10

--- a/solution.py
+++ b/solution.py
@@ -175,8 +175,12 @@
     freq_ref,
     x_ref,
     place_ref,
-    pack_ref,
-    ff_ref,
+    gain_rows_ref,
+    query_w_ref,
+    key_w_ref,
+    value_w_ref,
+    gate_w_ref,
+    up_w_ref,
     out_ref,
     xs_ref,
     weight_ref,
@@ -210,8 +214,9 @@
     here = links.slot
     span_len, width = x_ref.shape
     group_len = line * span_len
-    rows_each = ff_ref.shape[1]
+    rows_each = gate_w_ref.shape[0]
     q_cols = query.shape[1]
+    ff_cols = gate_w_ref.shape[1] // line
     heads = q_cols // HD
     local = []
 
@@ -219,17 +224,46 @@
     far_ff = NearGather(links, lambda block, place: ffs_ref.at[links.along(-block), place])
     far_out = NearGather(links, lambda block, place: outs_ref.at[links.along(-block), place])
     ring = RingGather(links, x_ref, lambda block, rows: x_all.at[block, rows])
-    own = [
-        links.keep(x_ref, x_all.at[links.z]),
-        links.keep(place_ref, places.at[links.z]),
-        links.keep(pack_ref.at[links.z], weights.at[links.z, here]),
-    ]
-    turned = {k: links.send(pack_ref.at[links.along(k)], weights.at[links.z, here], k) for k in far}
+
+    def columns(weight, block, size):
+        return weight.at[:, pl.ds(pl.multiple_of(block * size, HD), size)]
+
+    def near_pieces(block):
+        target = weights.at[links.z, here]
+        rows = pl.ds(0, rows_each)
+        return [
+            (columns(query_w_ref, block, q_cols), target.at[rows, pl.ds(0, q_cols)]),
+            (columns(key_w_ref, block, HD), target.at[rows, pl.ds(q_cols, HD)]),
+            (columns(value_w_ref, block, HD), target.at[rows, pl.ds(q_cols + HD, HD)]),
+            (gain_rows_ref, target.at[pl.ds(rows_each, 16)]),
+        ]
+
+    def ff_pieces(block):
+        target = ffs_ref.at[links.z, here]
+        return [
+            (columns(gate_w_ref, block, ff_cols), target.at[:, pl.ds(0, ff_cols)]),
+            (columns(up_w_ref, block, ff_cols), target.at[:, pl.ds(ff_cols, ff_cols)]),
+        ]
+
+    def turn_out(pieces):
+        return {k: [links.send(*piece, k) for piece in pieces(links.along(k))] for k in far}
+
+    def arrived(copies):
+        for copy in copies:
+            copy.wait_recv()
+
+    own = [links.keep(*piece) for piece in near_pieces(links.z)]
+    own_ff = [links.keep(*piece) for piece in ff_pieces(links.z)]
+    turned = turn_out(near_pieces)
     placed = [links.send(place_ref, places.at[links.z], k) for k in far]
-    turned_ff = {k: links.send(ff_ref.at[links.along(k)], ffs_ref.at[links.z, here], k) for k in far}
-    near.offer(0, pack_ref.at[links.z])
-    far_ff.offer(0, ff_ref.at[links.z])
-    local.append(links.keep(ff_ref.at[links.z], ffs_ref.at[links.z, here]))
+    turned_ff = turn_out(ff_pieces)
+    for copy in own:
+        copy.wait()
+    near.offer(0, weights.at[links.z, here])
+    for copy in own_ff:
+        copy.wait()
+    far_ff.offer(0, ffs_ref.at[links.z, here])
+    own = [links.keep(x_ref, x_all.at[links.z]), links.keep(place_ref, places.at[links.z])]
     local.append(links.keep(out_ref, outs_ref.at[links.z, here]))
 
     def move_out(k):
@@ -240,13 +274,13 @@
         return onward
 
     for k in far:
-        turned[k].wait_recv()
+        arrived(turned[k])
         near.offer(k, weights.at[links.along(-k), here])
     ring.step(0)
     for k in [0] + far:
         near.relay(k, "x" if k < line // 2 else "y")
     for k in far:
-        turned_ff[k].wait_recv()
+        arrived(turned_ff[k])
         far_ff.offer(k, ffs_ref.at[links.along(-k), here])
     ring.step(1)
     for k in [0] + far:
@@ -510,16 +544,17 @@
     )(*arguments)
 
 
-def forward_call(freqs, tokens, places, pack, pack_ff, w_out, line):
+def forward_call(freqs, tokens, places, gain_rows, weights, line):
     span_len, width = tokens.shape
     group_len = line * span_len
-    rows_each = pack_ff.shape[1]
-    qkv_cols = pack.shape[2]
+    rows_each, qkv_cols = weights[0].shape[0], gain_rows.shape[1]
     q_cols = qkv_cols - 2 * HD
+    both_cols = 2 * weights[3].shape[1] // line
     f32, bf16 = jnp.float32, jnp.bfloat16
+    near = (line, 8, rows_each + 16, qkv_cols)
     outs = (
         ((line, span_len, width), bf16),
-        ((line, 8) + pack.shape[1:], bf16),
+        (near, bf16),
         ((2, 16, width), f32),
         ((group_len, width), bf16),
         ((group_len, q_cols), bf16),
@@ -527,20 +562,20 @@
         ((group_len, HD), f32),
         ((2, group_len, HD), f32),
         ((group_len, line * q_cols), bf16),
-        ((line, 8) + pack_ff.shape[1:], bf16),
-        ((line, 8) + w_out.shape, bf16),
+        ((line, 8, rows_each, both_cols), bf16),
+        ((line, 8, rows_each, width), bf16),
     )
     return link_call(
         functools.partial(first_kernel, line),
         0,
-        176,
+        208,
         tuple(jax.ShapeDtypeStruct(*out) for out in outs),
-        (freqs, tokens, places, pack, pack_ff, w_out),
-        "v" + "h" * 16,
+        (freqs, tokens, places, gain_rows) + weights,
+        "v" + "h" * 20,
         scratch=[
             pltpu.VMEM((line, span_len, width), bf16),
             pltpu.VMEM((line,) + places.shape, f32),
-            pltpu.VMEM((line, 8) + pack.shape[1:], bf16),
+            pltpu.VMEM(near, bf16),
             pltpu.VMEM((2, 16, width), f32),
             pltpu.VMEM((group_len, width), bf16),
             pltpu.VMEM((2, group_len, HD), f32),
@@ -604,7 +639,18 @@
         links.keep(atts_ref, norm),
         links.keep(xs_ref, parts),
     ]
-    late = [links.keep(ff_ref, ff), links.keep(down_ref, down)]
+    late = [links.keep(ff_ref, ff)]
+    down_rows = down_ref.shape[0]
+
+    def down_place(block, place):
+        low, high = cuts[block]
+        return down.at[pl.ds(pl.multiple_of(place * down_rows + low, 16), high - low)]
+
+    near = NearGather(links, down_place)
+    for block, (low, high) in enumerate(cuts):
+        rows = down_ref.at[pl.ds(low, high - low)]
+        late.append(links.keep(rows, down_place(block, links.slot)))
+        near.offer(block, rows)
     ring = RingSum(links, parts, total_ref, got)
     mixed_ring = RingSum(links, mixed_parts, mixed_total_ref, mixed_got)
     items = []
@@ -678,6 +724,8 @@
         if part == 0:
             mix_ring.step(1)
 
+    for block in range(2):
+        near.relay(block, "xy"[block])
     for copy in late:
         copy.wait()
 
@@ -717,6 +765,9 @@
 
     over_chunks(forward, ff_cols)
     mix_ring.step(2)
+    for block in range(2):
+        near.close(block)
+    near.wait(range(2))
 
     def mixed_part(low, size):
         lanes = pl.ds(low, size)
@@ -797,13 +848,13 @@
         copy.wait()
 
 
-def mlp_call(keep, gains, mixed, x_blocks, attended, out_w, ff_w, down_w, line):
+def mlp_call(keep, gains, mixed, x_blocks, attended, out_w, ff_w, w_down, line):
     f32, bf16 = jnp.float32, jnp.bfloat16
     span_len, width = mixed.shape
     group_len = line * span_len
-    ff_rows, both_cols, rows_each = down_w.shape[0], ff_w.shape[3], ff_w.shape[2]
+    rows, both_cols, rows_each = w_down.shape[0], ff_w.shape[3], ff_w.shape[2]
+    ff_rows = 8 * rows
     ff_w = ff_w.reshape(line, 2, 2, 2, rows_each, both_cols)
-    rows = ff_rows // 8
     half = (rows // 2 + 15) // 16 * 16
     cuts = ((0, half), (half, rows))
     blocks = (line, span_len, width)
@@ -811,7 +862,7 @@
     return link_call(
         functools.partial(mlp_kernel, line, cuts),
         2,
-        96,
+        112,
         (
             token,
             token,
@@ -820,12 +871,12 @@
             jax.ShapeDtypeStruct(ff_w.shape, bf16),
             jax.ShapeDtypeStruct((2, rows_each, both_cols), bf16),
         ),
-        (keep, gains, mixed, x_blocks, attended, out_w.reshape(2, 2, 2, width // 8, width), ff_w, down_w),
+        (keep, gains, mixed, x_blocks, attended, out_w.reshape(2, 2, 2, width // 8, width), ff_w, w_down),
         "vvhhhhhh" + "vvvvhh",
         [
             pltpu.VMEM((2, 2, 2, width // 8, width), bf16),
             pltpu.VMEM(ff_w.shape, bf16),
-            pltpu.VMEM(down_w.shape, bf16),
+            pltpu.VMEM((ff_rows, width), bf16),
             pltpu.VMEM((group_len, width), bf16),
             pltpu.VMEM(blocks, bf16),
             pltpu.VMEM(blocks, bf16),
@@ -940,18 +991,31 @@
     ff_items = items_of(ff_ref, sums[:4], False, ff_order)
     out_items = items_of(big, sums[4:7], True)
     qkv_items = items_of(slim, sums[7:], True)
-    local = []
-    arrived = [
-        links.send(ff_half_ref.at[index], ffs_ref.at[links.z], k) for index, k in enumerate(order[:2])
-    ]
-
-    def turn(items, target, low, high, order=order):
+    local, arrived = [], []
+    ff_cols = ff_ref.shape[5] // 2
+    ff_pieces = ((0, ff_cols), (ff_cols, ff_cols))
+    qkv_pieces = ((0, q_cols), (q_cols, HD), (q_cols + HD, HD))
+
+    def deliver(total, target, k, pieces):
+        for low, size in pieces:
+            if pieces == out_pieces:
+                place = target.at[links.z]
+            else:
+                lanes = pl.multiple_of(line * low + links.z * size, HD)
+                place = target.at[:, pl.ds(lanes, size)]
+            part = total.at[:, pl.ds(low, size)]
+            if k == 0:
+                local.append(links.keep(part, place))
+            else:
+                arrived.append(links.send(part, place, k))
+
+    out_pieces = ((0, width),)
+    for index, k in enumerate(order[:2]):
+        deliver(ff_half_ref.at[index], ffs_ref, k, ff_pieces)
+
+    def turn(items, target, low, high, pieces, order=order):
         for item, k in list(zip(items, order))[low:high]:
-            total = item.second_done()
-            if k == 0:
-                local.append(links.keep(total, target.at[links.z]))
-            else:
-                arrived.append(links.send(total, target.at[links.z], k))
+            deliver(item.second_done(), target, k, pieces)
 
     def core_done(items, low, high):
         for item in items[low:high]:
@@ -1087,19 +1151,19 @@
     for item in qkv_items:
         item.start()
     core_done(out_items, 0, half)
-    turn(ff_items, ffs_ref, 0, line, ff_order)
+    turn(ff_items, ffs_ref, 0, line, ff_pieces, ff_order)
     ring.step(1)
     core_done(out_items, half, line)
     first_done(out_items, 0, half)
     ring.step(2)
     core_done(qkv_items, 0, line)
     first_done(out_items, half, line)
-    turn(out_items, outs_ref, 0, half)
+    turn(out_items, outs_ref, 0, half, out_pieces)
     ring.step(3)
     first_done(qkv_items, 0, half)
-    turn(out_items, outs_ref, half, line)
+    turn(out_items, outs_ref, half, line, out_pieces)
     first_done(qkv_items, half, line)
-    turn(qkv_items, qkvs_ref, 0, line)
+    turn(qkv_items, qkvs_ref, 0, line, qkv_pieces)
     for copy in arrived:
         copy.wait_recv()
     links.finish()
@@ -1124,9 +1188,10 @@
         4,
         160,
         (token, token)
-        + tuple(
-            jax.ShapeDtypeStruct((line, rows_each, columns), bf16)
-            for columns in (grad_ff.shape[5], width, qkv_cols)
+        + (
+            jax.ShapeDtypeStruct((rows_each, line * grad_ff.shape[5]), bf16),
+            jax.ShapeDtypeStruct((line, rows_each, width), bf16),
+            jax.ShapeDtypeStruct((rows_each, line * qkv_cols), bf16),
         ),
         small + saved + (out_w.reshape(wide), attended, weights, norm, grad_ff, ff_half),
         "v" * 5 + "h" * 10 + "vvhhh",
@@ -1496,13 +1561,7 @@
     line = lax.axis_size("z")
     rows_each = w_query.shape[0]
     q_cols = HEADS // line * HD
-    ff_cols = w_gate.shape[1] // line
-    group_len = span_len * line
-
-    def by_columns(weight, columns):
-        return weight.reshape(rows_each, line, columns).transpose(1, 0, 2)
-
-    down_w = lax.all_gather(w_down, ("x", "y", "c"), axis=0, tiled=True)
+
     own_x = tokens[0].astype(f32)
     keep = keep_mask[0].astype(f32)
     group_match = group_ids[0][:, None] == jnp.arange(exit_scale.shape[0], dtype=jnp.int32)[None, :]
@@ -1513,12 +1572,7 @@
     gain_row = jnp.zeros((q_cols + 2 * HD,), bf16)
     gain_row = lax.dynamic_update_slice_in_dim(gain_row, attn_gain, core * rows_each, 0)
     gain_row = lax.dynamic_update_slice_in_dim(gain_row, mlp_gain, HD + core * rows_each, 0)
-    gain_rows = jnp.broadcast_to(gain_row, (line, 16, gain_row.shape[0]))
-    pack_attn = jnp.concatenate(
-        [by_columns(w_query, q_cols), by_columns(w_key, HD), by_columns(w_value, HD)], axis=2
-    )
-    pack_attn = jnp.concatenate([pack_attn, gain_rows], axis=1)
-    pack_ff = jnp.concatenate([by_columns(w_gate, ff_cols), by_columns(w_up, ff_cols)], axis=2)
+    gain_rows = jnp.broadcast_to(gain_row, (16, gain_row.shape[0]))
     freqs = 10000.0 ** (-2.0 * jnp.arange(HD // 2, dtype=f32) / HD)
     freqs = jnp.broadcast_to(jnp.concatenate([freqs, freqs])[None], (8, HD))
     places = jnp.broadcast_to(positions[0].astype(f32)[None], (8, span_len))
@@ -1536,7 +1590,14 @@
         attended_rows,
         ff_w,
         out_w,
-    ) = forward_call(freqs, first_tokens, places, pack_attn, pack_ff, w_out, line)
+    ) = forward_call(
+        freqs,
+        first_tokens,
+        places,
+        gain_rows,
+        (w_query, w_key, w_value, w_gate, w_up, w_out),
+        line,
+    )
     keep_tile = jnp.broadcast_to(keep, (8, HD))
     middle, norm_grad, mixed, grad_down, grad_ff, ff_half = mlp_call(
         keep_tile,
@@ -1546,7 +1607,7 @@
         attended_rows,
         out_w,
         ff_w,
-        down_w,
+        w_down,
         line,
     )
     grad_down = grad_down.astype(f32)
@@ -1582,14 +1643,12 @@
         * jnp.mean(scaled_one * own_x, axis=-1, keepdims=True)
     )
 
-    def side_by_side(blocks):
-        return blocks.transpose(1, 0, 2).reshape(rows_each, -1)
-
-    grad_query = side_by_side(qkv_back[:, :, :q_cols])
-    grad_key = side_by_side(qkv_back[:, :, q_cols : q_cols + HD])
-    grad_value = side_by_side(qkv_back[:, :, q_cols + HD :])
-    grad_gate = side_by_side(ff_back[:, :, :ff_cols])
-    grad_up = side_by_side(ff_back[:, :, ff_cols:])
+    heads_end, keys_end = w_query.shape[1], w_query.shape[1] + w_key.shape[1]
+    grad_query = qkv_back[:, :heads_end]
+    grad_key = qkv_back[:, heads_end:keys_end]
+    grad_value = qkv_back[:, keys_end:]
+    grad_gate = ff_back[:, : w_gate.shape[1]]
+    grad_up = ff_back[:, w_gate.shape[1] :]
 
     def gain_grad(pairs, gain):
         total = sum(jnp.sum(weight.astype(f32) * grad, axis=1) for weight, grad in pairs)

time: 436 us -> 416 us (0.954)
  between operations: 15 us -> 1.52 us
  Pallas kernels: 399 us -> 394 us
    pallas_call x3, Pallas kernels: 399 us -> 394 us  [link_call(): pl.pallas_call(kernel, out_shape=shapes, in_specs=specs[:len(arguments)],...]
  transfers between devices with their start and end apart: 1 -> 0, of which waited for: 0 -> 0; matrix products, arithmetic and copies ran while one was open for 2% -> 0% of each run, Pallas kernels for 34% -> 0%
where the time goes in v11:
time: 416 us
  Pallas kernels  394 us (95%)
  other arithmetic  13.8 us (3%)
  local copies, waits for them, and re-layouts  5.89 us (1%)
    pallas_call x3, Pallas kernels, link_call(): pl.pallas_call(kernel, out_shape=shapes, in_specs=specs[:len(arguments)],...  394 us

profile of v11, /device:TPU:0, one launch (start us, length us, event | category | flops | bytes accessed | tf_op | source)
XLA Modules:
  0.0 415.6 jit_solution(15466478775175725229)
XLA Ops:
  0.6 0.0 copy-start.14
  0.7 0.9 dynamic_update_slice.6
  1.5 0.8 dynamic_update_slice.7
  2.3 0.6 broadcast_in_dim.53.gain_rows_ref
  3.6 0.8 fusion.7
  4.4 2.4 convert_multiply_fusion.3
  6.7 0.1 pad_maximum_fusion
  6.8 0.6 broadcast_in_dim.47.freq_ref
  7.4 0.0 copy-done.14
  7.4 0.6 broadcast_in_dim.51.place_ref
  8.0 146.9 %shard_map.230 = (bf16[4,128,2048]{2,1,0:T(8,128)(2,1)}, bf16[4,8,80,768]{3,2,1,0:T(8,128)(2,1)}, f32[2,16,2048]{2,1,0:T(8,128)}, bf16[512,2048]{1,0:T(8,128)(2,...) custom-call(f32[8,128]{1,0:T(8,128)} %broadcast_in_dim.47.freq_ref, ...), custom_call_target="tpu_custom_call" | custom-call | tf_op jit(solution)/shard_map/pallas_call | solution.py:534
  154.9 0.6 broadcast_in_dim.46.keep_ref
  155.5 116.8 %shard_map.231 = (f32[128,2048]{1,0:T(8,128)}, f32[128,2048]{1,0:T(8,128)}, f32[128,2048]{1,0:T(8,128)}, bf16[176,2048]{1,0:T(8,128)(2,1)}, bf16[4,2,2,2,64,2816...) custom-call(f32[8,128]{1,0:T(8,128)} %broadcast_in_dim.46.keep_ref, f32[2,16,2048]{2,1,0:T(8,128)} %get-tuple-element.37.gain_ref, ...), custom_call_target="tpu_custom_call" | custom-call | tf_op jit(solution)/shard_map/pallas_call | solution.py:534
  272.3 0.0 copy-start.3
  272.3 130.7 %shard_map.232 = (f32[128,2048]{1,0:T(8,128)}, f32[128,2048]{1,0:T(8,128)}, bf16[64,11264]{1,0:T(8,128)(2,1)}, bf16[4,64,2048]{2,1,0:T(8,128)(2,1)}, bf16[64,3072]{1,0:T(8,128)(2,1)}) custom-call(f32[128,2048]{1,0:T(8,128)} %get-tuple-element.45.up_ref, f32[128,2048]{1,0:T(8,128)} %get-tuple-element.43.middle_ref, ...), custom_call_target="tpu_custom_call" | custom-call | tf_op jit(solution)/shard_map/pallas_call | solution.py:534
  403.1 0.0 copy-done.3
  403.1 0.0 copy-start.4
  403.1 0.0 copy-start.8
  403.1 0.0 copy-start.10
  403.1 0.0 copy-start.11
  403.1 3.7 multiply_reduce_fusion
  406.8 0.0 copy-start.12
  406.9 0.0 copy-start.13
  406.9 0.0 copy-start
  406.9 0.0 copy-start.2
  406.9 0.0 copy-done.4
  406.9 0.0 copy-done.8
  406.9 1.0 multiply_reduce_fusion.2
  407.9 0.0 copy-start.7
  407.9 0.0 copy-done.10
  407.9 0.0 copy-done.11
  407.9 0.8 multiply_reduce_fusion.4
  408.7 0.0 copy-done.12
  408.8 0.0 copy-done.13
  408.8 0.5 convert_divide_fusion
  409.3 0.8 slice.18
  410.1 0.0 copy-done
  410.1 0.0 copy-done.2
  410.1 0.3 fusion
  410.4 0.0 copy-done.7
  410.5 1.1 fusion.6
  411.6 0.1 copy-done.5
  411.7 1.0 convert_reduce_fusion
  412.6 0.1 copy-done.9
  412.7 1.3 convert_element_type.80
  414.0 0.0 copy-done.1
  414.0 0.7 copy-done.6
  414.7 0.9 fusion.5
  (8 shorter events, 0.0 us)
Async XLA Ops:
  0.6 6.8 %copy-start.14 = (s32[1,128]{1,0:T(1,128)S(1)}, s32[1,128]{1,0:T(1,128)}, u32[]{:S(2)}) copy-start(s32[1,128]{1,0:T(1,128)} %param.27) | copy-start | bytes 1540
  272.3 130.8 %copy-start.3 = (bf16[64,5632]{1,0:T(8,128)(2,1)S(1)}, bf16[64,5632]{1,0:T(8,128)(2,1)}, u32[]{:S(2)}) copy-start(bf16[64,5632]{1,0:T(8,128)(2,1)} %gate_w_ref.1) | copy-start | bytes 2162692
  403.1 3.8 copy-start.4
  403.1 3.8 copy-start.8
  403.1 4.8 %copy-start.10 = (bf16[64,512]{1,0:T(8,128)(2,1)S(1)}, bf16[64,512]{1,0:T(8,128)(2,1)}, u32[]{:S(2)}) copy-start(bf16[64,512]{1,0:T(8,128)(2,1)} %key_w_ref.1) | copy-start | bytes 196612
  403.1 4.8 %copy-start.11 = (bf16[64,512]{1,0:T(8,128)(2,1)S(1)}, bf16[64,512]{1,0:T(8,128)(2,1)}, u32[]{:S(2)}) copy-start(bf16[64,512]{1,0:T(8,128)(2,1)} %value_w_ref.1) | copy-start | bytes 196612
  406.8 1.9 copy-start.12
  406.9 1.9 copy-start.13
  406.9 3.3 copy-start
  406.9 3.3 copy-start.2
  407.9 2.6 copy-start.7
  410.5 1.2 copy-start.5
  411.6 1.1 copy-start.9
  412.6 1.4 copy-start.1
  412.6 2.1 copy-start.6

commit v12 on v11

--- a/solution.py
+++ b/solution.py
@@ -153,28 +153,42 @@
 
 
 class RingGather:
-    def __init__(self, links, source, place, pieces=4):
-        self.links, self.source, self.place, self.pieces = links, source, place, pieces
-        self.rows = source.shape[0] // pieces
+    def __init__(self, links, rows, origin, place, first=0, pieces=4):
+        self.links, self.origin, self.place, self.first = links, origin, place, first
+        self.pieces, self.rows = pieces, rows // pieces
         self.last = [None] * pieces
 
     def step(self, number):
+        if number > self.first:
+            self.wait()
+        if number == self.links.line - 1:
+            return
         for piece in range(self.pieces):
             way = 1 if piece < self.pieces // 2 else -1
             rows = pl.ds(piece * self.rows, self.rows)
-            place = self.place(self.links.along(-way * number), rows)
-            if number > 0:
-                self.last[piece].wait_recv()
-            if number < self.links.line - 1:
-                origin = self.source.at[rows] if number == 0 else place
-                self.last[piece] = self.links.send(origin, place, way)
+            block = self.links.along(-way * number)
+            place = self.place(block, rows)
+            source = self.origin(block, rows) if number == self.first else place
+            self.last[piece] = self.links.send(source, place, way)
+
+    def wait(self):
+        for copy in self.last:
+            copy.wait_recv()
+
+
+def column_of(row):
+    size = row.shape[1]
+    down = lax.broadcasted_iota(jnp.int32, (size, size), 0)
+    across = lax.broadcasted_iota(jnp.int32, (size, size), 1)
+    values = jnp.where(down == across, jnp.broadcast_to(row, (size, size)), 0.0)
+    return jnp.sum(values, axis=1, keepdims=True)
 
 
 def first_kernel(
     line,
-    freq_ref,
+    small_ref,
     x_ref,
-    place_ref,
+    grad_ref,
     gain_rows_ref,
     query_w_ref,
     key_w_ref,
@@ -193,7 +207,10 @@
     atts_ref,
     ffs_ref,
     outs_ref,
+    mixs_ref,
     x_all,
+    grad,
+    mix,
     places,
     weights,
     gains,
@@ -223,7 +240,10 @@
     near = NearGather(links, lambda block, place: weights.at[links.along(-block), place])
     far_ff = NearGather(links, lambda block, place: ffs_ref.at[links.along(-block), place])
     far_out = NearGather(links, lambda block, place: outs_ref.at[links.along(-block), place])
-    ring = RingGather(links, x_ref, lambda block, rows: x_all.at[block, rows])
+    ring = RingGather(
+        links, span_len, lambda block, rows: x_ref.at[rows], lambda block, rows: x_all.at[block, rows]
+    )
+    place_ref = small_ref.at[0]
 
     def columns(weight, block, size):
         return weight.at[:, pl.ds(pl.multiple_of(block * size, HD), size)]
@@ -263,7 +283,11 @@
     for copy in own_ff:
         copy.wait()
     far_ff.offer(0, ffs_ref.at[links.z, here])
-    own = [links.keep(x_ref, x_all.at[links.z]), links.keep(place_ref, places.at[links.z])]
+    own = [
+        links.keep(x_ref, x_all.at[links.z]),
+        links.keep(place_ref, places.at[links.z]),
+        links.keep(grad_ref, grad),
+    ]
     local.append(links.keep(out_ref, outs_ref.at[links.z, here]))
 
     def move_out(k):
@@ -295,17 +319,19 @@
         copy.wait_recv()
 
     lane = lax.broadcasted_iota(jnp.int32, (span_len, HD), 1)
-    token = lax.broadcasted_iota(jnp.int32, (span_len, span_len), 0)
-    across = lax.broadcasted_iota(jnp.int32, (span_len, span_len), 1)
     for block in range(line):
-        row = jnp.broadcast_to(places[block, 0:1], (span_len, span_len))
-        column = jnp.sum(jnp.where(token == across, row, 0.0), axis=1, keepdims=True)
-        angles = column * freq_ref[0:1]
+        angles = column_of(places[block, 0:1]) * small_ref[2, 0:1]
         rows = slice(block * span_len, (block + 1) * span_len)
         sine = jnp.sin(angles)
         turns[0, rows] = jnp.cos(angles)
         turns[1, rows] = jnp.where(lane < HD // 2, -sine, sine)
     local.append(links.keep(turns, turn_ref))
+    token_scale = column_of(small_ref[1, 0:1])
+    for low in range(0, span_len, 16):
+        rows = slice(low, low + 16)
+        upstream = grad[rows].astype(f32) * token_scale[rows]
+        mix[rows] = (upstream * small_ref[3, 0:1, 0:1]).astype(bf16)
+    local.append(links.keep(mix, mixs_ref.at[links.z]))
     near.wait(range(line))
     for index in range(line * 4):
         z, q = divmod(index, 4)
@@ -407,7 +433,10 @@
     def place(block, rows):
         return atts_ref.at[rows, pl.ds(pl.multiple_of(block * q_cols, q_cols), q_cols)]
 
-    att_ring = RingGather(links, att, place)
+    att_ring = RingGather(links, group_len, lambda block, rows: att.at[rows], place)
+    mix_ring = RingGather(
+        links, span_len, lambda block, rows: mix.at[rows], lambda block, rows: mixs_ref.at[block, rows]
+    )
     local.append(links.keep(att, place(links.z, pl.ds(0, group_len))))
     att_ring.step(0)
     for k in [0] + far:
@@ -420,11 +449,13 @@
         moved = move_out(k)
     far_out.relay(2, "y")
     att_ring.step(2)
+    mix_ring.step(0)
     for k in range(3, line):
         far_out.relay(k, "y")
     for k in range(line):
         far_out.close(k)
     att_ring.step(3)
+    mix_ring.wait()
     far_out.wait(range(line))
     far_ff.wait(range(line))
     links.finish()
@@ -503,7 +534,7 @@
         self.pieces, self.last = pieces, [None] * pieces
         self.rows = parts.shape[1] // pieces
 
-    def step(self, number):
+    def step(self, number, carry=None):
         links = self.links
         for piece in range(self.pieces):
             way = 1 if piece < self.pieces // 2 else -1
@@ -518,6 +549,9 @@
                 ].astype(jnp.float32)
                 if number == links.line - 1:
                     self.total[where] = total
+                    continue
+                if carry is not None:
+                    carry[where] = total.astype(carry.dtype)
                     continue
                 self.parts[block, where] = total.astype(self.parts.dtype)
                 source = self.parts.at[block, where]
@@ -544,7 +578,7 @@
     )(*arguments)
 
 
-def forward_call(freqs, tokens, places, gain_rows, weights, line):
+def forward_call(small, tokens, out_grad, gain_rows, weights, line):
     span_len, width = tokens.shape
     group_len = line * span_len
     rows_each, qkv_cols = weights[0].shape[0], gain_rows.shape[1]
@@ -564,17 +598,20 @@
         ((group_len, line * q_cols), bf16),
         ((line, 8, rows_each, both_cols), bf16),
         ((line, 8, rows_each, width), bf16),
+        ((line, span_len, width), bf16),
     )
     return link_call(
         functools.partial(first_kernel, line),
         0,
         208,
         tuple(jax.ShapeDtypeStruct(*out) for out in outs),
-        (freqs, tokens, places, gain_rows) + weights,
-        "v" + "h" * 20,
+        (small, tokens, out_grad, gain_rows) + weights,
+        "v" + "h" * 21,
         scratch=[
             pltpu.VMEM((line, span_len, width), bf16),
-            pltpu.VMEM((line,) + places.shape, f32),
+            pltpu.VMEM((span_len, width), bf16),
+            pltpu.VMEM((span_len, width), bf16),
+            pltpu.VMEM((line,) + small.shape[1:], f32),
             pltpu.VMEM(near, bf16),
             pltpu.VMEM((2, 16, width), f32),
             pltpu.VMEM((group_len, width), bf16),
@@ -592,9 +629,9 @@
 def mlp_kernel(
     line,
     cuts,
-    keep_ref,
+    small_ref,
     gain_ref,
-    mix_ref,
+    mixs_ref,
     xs_ref,
     atts_ref,
     out_ref,
@@ -602,7 +639,8 @@
     down_ref,
     middle_ref,
     total_ref,
-    mixed_total_ref,
+    carry_ref,
+    mixed_own_ref,
     sum_ref,
     grad_ff_ref,
     ff_half_ref,
@@ -625,15 +663,24 @@
     links = Links(send_sems, recv_sems, line)
     links.meet(["x", "y", "c", 1, line - 1])
     far = [1, line - 1] + list(range(2, line - 1))
-    span_len, width = mix_ref.shape
+    span_len, width = mixs_ref.shape[1:]
     group_len = line * span_len
     ff_cols = hidden.shape[1]
     block_rows = width // line
     rows_each = block_rows // 8
     chunk = 2 * HD
-    stay = links.keep(mix_ref, mixed.at[links.z])
-    mix_ring = RingGather(links, mix_ref, lambda block, rows: mixed.at[block, rows])
-    mix_ring.step(0)
+    mix_ring = RingGather(
+        links,
+        span_len,
+        lambda block, rows: mixs_ref.at[block, rows],
+        lambda block, rows: mixed.at[block, rows],
+        1,
+    )
+    mix_ring.step(1)
+    stay = [links.keep(mixs_ref.at[links.z], mixed.at[links.z])]
+    for low, step in ((0, -1), (span_len // 2, 1)):
+        rows = pl.ds(low, span_len // 2)
+        stay.append(links.keep(mixs_ref.at[links.along(step), rows], mixed.at[links.along(step), rows]))
     early = [
         links.keep(out_ref, big),
         links.keep(atts_ref, norm),
@@ -652,7 +699,7 @@
         late.append(links.keep(rows, down_place(block, links.slot)))
         near.offer(block, rows)
     ring = RingSum(links, parts, total_ref, got)
-    mixed_ring = RingSum(links, mixed_parts, mixed_total_ref, mixed_got)
+    mixed_ring = RingSum(links, mixed_parts, None, mixed_got)
     items = []
     ff_items = []
     for index, k in enumerate(far[:2]):
@@ -702,7 +749,7 @@
                     preferred_element_type=f32,
                 )
                 value = term if value is None else value + term
-            gate_up[:half, lanes] = value * keep_ref[0:1, 0:1]
+            gate_up[:half, lanes] = value * small_ref[3, 0:1, 0:1]
 
         def normalise(index, carry, low=low):
             block = (low // 16 + index) // (span_len // 16)
@@ -722,7 +769,7 @@
             where = pl.multiple_of(lax.rem(links.z, line // 2) * span_len, span_len)
             middle_ref[...] = gate_up[pl.ds(where, span_len), :width]
         if part == 0:
-            mix_ring.step(1)
+            mix_ring.step(2)
 
     for block in range(2):
         near.relay(block, "xy"[block])
@@ -764,7 +811,6 @@
             work(extent // chunk * chunk, extent % chunk)
 
     over_chunks(forward, ff_cols)
-    mix_ring.step(2)
     for block in range(2):
         near.close(block)
     near.wait(range(2))
@@ -776,7 +822,9 @@
 
     over_chunks(mixed_part, width)
     mixed_ring.step(0)
-    stay.wait()
+    mixed_own_ref[...] = mixed_parts[links.z]
+    for copy in stay:
+        copy.wait()
     mix_ring.step(3)
     hidden_rows = hidden[...].T
 
@@ -828,7 +876,7 @@
     ring.step(1)
     for item in ff_items:
         item.core_done()
-    mixed_ring.step(2)
+    mixed_ring.step(2, carry_ref)
     sent = []
     for k in far[2:] + [0]:
         block = links.along(k)
@@ -839,7 +887,6 @@
     ring.step(2)
     for item in ff_items:
         item.first_done()
-    mixed_ring.step(3)
     ring.step(3)
     for index, item in enumerate(ff_items):
         sent.append(links.keep(item.second_done(), ff_half_ref.at[index]))
@@ -848,9 +895,9 @@
         copy.wait()
 
 
-def mlp_call(keep, gains, mixed, x_blocks, attended, out_w, ff_w, w_down, line):
+def mlp_call(small, gains, mixed, x_blocks, attended, out_w, ff_w, w_down, line):
     f32, bf16 = jnp.float32, jnp.bfloat16
-    span_len, width = mixed.shape
+    span_len, width = mixed.shape[1:]
     group_len = line * span_len
     rows, both_cols, rows_each = w_down.shape[0], ff_w.shape[3], ff_w.shape[2]
     ff_rows = 8 * rows
@@ -866,13 +913,14 @@
         (
             token,
             token,
-            token,
+            jax.ShapeDtypeStruct((span_len, width), bf16),
+            jax.ShapeDtypeStruct((span_len, width), bf16),
             jax.ShapeDtypeStruct((rows, width), bf16),
             jax.ShapeDtypeStruct(ff_w.shape, bf16),
             jax.ShapeDtypeStruct((2, rows_each, both_cols), bf16),
         ),
-        (keep, gains, mixed, x_blocks, attended, out_w.reshape(2, 2, 2, width // 8, width), ff_w, w_down),
-        "vvhhhhhh" + "vvvvhh",
+        (small, gains, mixed, x_blocks, attended, out_w.reshape(2, 2, 2, width // 8, width), ff_w, w_down),
+        "vvhhhhhh" + "vvvvvhh",
         [
             pltpu.VMEM((2, 2, 2, width // 8, width), bf16),
             pltpu.VMEM(ff_w.shape, bf16),
@@ -885,7 +933,7 @@
             pltpu.VMEM((group_len, both_cols), bf16),
             pltpu.VMEM((line - 1, span_len, width), bf16),
             pltpu.VMEM(blocks, bf16),
-            pltpu.VMEM((line - 1, span_len, width), bf16),
+            pltpu.VMEM((line - 2, span_len, width), bf16),
         ]
         + sum_space(2, rows_each, both_cols)[1:]
         + sum((sum_space(1, high - low, width)[1:] for low, high in cuts), []),
@@ -895,11 +943,14 @@
 
 def backward_kernel(
     line,
-    up_ref,
+    small_ref,
+    gain_ref,
     middle_ref,
     norm_grad_ref,
-    keep_ref,
-    gain_ref,
+    x_ref,
+    grad_ref,
+    carry_ref,
+    mixed_own_ref,
     query_ref,
     kv_ref,
     peak_ref,
@@ -910,11 +961,17 @@
     norm_ref,
     ff_ref,
     ff_half_ref,
-    middle_grad_ref,
-    total_ref,
+    output_ref,
+    token_ref,
     ffs_ref,
     outs_ref,
     qkvs_ref,
+    x_own,
+    grad_own,
+    mixed_own,
+    mixed_in,
+    middle_grad,
+    total,
     big,
     slim,
     norm,
@@ -942,7 +999,7 @@
     far = [1, line - 1] + list(range(2, line - 1))
     order = far + [0]
     links.meet(["x", "y", "c"] + far)
-    span_len, width = up_ref.shape
+    span_len, width = x_ref.shape
     group_len = line * span_len
     q_cols = query.shape[1]
     heads = q_cols // HD
@@ -958,6 +1015,9 @@
         links.keep(out_ref, big),
         links.keep(atts_ref.at[here], own_rows),
         links.keep(atts_ref.at[:, lanes_of(links.z)], own_columns),
+        links.keep(grad_ref, grad_own),
+        links.keep(x_ref, x_own),
+        links.keep(mixed_own_ref, mixed_own),
         links.keep(query_ref, query),
         links.keep(kv_ref, kv),
         links.keep(peak_ref, peak),
@@ -965,7 +1025,7 @@
         links.keep(norm_ref, norm),
         links.keep(weight_ref.at[:, :, :, :, pl.ds(0, slim.shape[4])], slim),
     ]
-    ring = RingSum(links, parts, total_ref, got)
+    ring = RingSum(links, parts, total, got)
 
     def items_of(source, space, in_place, order=order):
         items = []
@@ -1012,6 +1072,11 @@
     out_pieces = ((0, width),)
     for index, k in enumerate(order[:2]):
         deliver(ff_half_ref.at[index], ffs_ref, k, ff_pieces)
+    mixed_last = []
+    for piece in range(4):
+        rows = pl.ds(piece * (span_len // 4), span_len // 4)
+        way = 1 if piece < 2 else -1
+        mixed_last.append(links.send(carry_ref.at[rows], mixed_in.at[rows], way))
 
     def turn(items, target, low, high, pieces, order=order):
         for item, k in list(zip(items, order))[low:high]:
@@ -1029,25 +1094,24 @@
     for item in ff_items:
         item.start()
 
-    def d_middle(index, carry):
-        rows = pl.ds(pl.multiple_of(index * 16, 16), 16)
-        middle = middle_ref[rows]
-        inverse = lax.rsqrt(jnp.mean(middle * middle, axis=-1, keepdims=True) + epsilon)
-        scaled = gain_ref[1] * norm_grad_ref[rows]
-        grad = (
-            up_ref[rows]
-            + inverse * scaled
-            - middle
-            * (inverse * inverse * inverse)
-            * jnp.mean(scaled * middle, axis=-1, keepdims=True)
-        )
-        middle_grad_ref[rows] = grad
-        branch[rows] = (grad * keep_ref[0:1, 0:1]).astype(bf16)
-        return carry
-
-    lax.fori_loop(0, span_len // 16, d_middle, 0)
     for copy in loads:
         copy.wait()
+    keep = small_ref[3, 0:1, 0:1]
+    token_scale = column_of(small_ref[1, 0:1])
+
+    def norm_back(values, grad, gain):
+        inverse = lax.rsqrt(jnp.mean(values * values, axis=-1, keepdims=True) + epsilon)
+        scaled = gain * grad
+        return inverse * scaled - values * (inverse * inverse * inverse) * jnp.mean(
+            scaled * values, axis=-1, keepdims=True
+        )
+
+    for low in range(0, span_len, 16):
+        rows = slice(low, low + 16)
+        upstream = grad_own[rows].astype(f32) * token_scale[rows]
+        grad = upstream + norm_back(middle_ref[rows], norm_grad_ref[rows], gain_ref[1])
+        middle_grad[rows] = grad
+        branch[rows] = (grad * keep).astype(bf16)
     for z in range(line):
         weight = big[z].reshape(rows_z, width)
         own_grad[:, z * rows_z : (z + 1) * rows_z] = lax.dot_general(
@@ -1087,7 +1151,7 @@
             delta = jnp.sum(
                 grad.astype(f32) * own_columns[rows, lanes].astype(f32), axis=-1, keepdims=True
             )
-            total = None
+            back = None
             for side in range(2):
                 keys, values = kv[side, :reach, :HD], kv[side, :reach, HD:]
                 score = lax.dot_general(
@@ -1099,14 +1163,14 @@
                 )
                 score_grad = (weight * (weight_grad - delta)).astype(bf16)
                 term = jnp.dot(score_grad, keys, preferred_element_type=f32)
-                total = term if total is None else total + term
+                back = term if back is None else back + term
                 kv_back[side, :reach, :HD] += lax.dot_general(
                     score_grad, part, (((0,), (0,)), ((), ())), preferred_element_type=f32
                 )
                 kv_back[side, :reach, HD:] += lax.dot_general(
                     weight.astype(bf16), grad, (((0,), (0,)), ((), ())), preferred_element_type=f32
                 )
-            query_back[rows, lanes] = total * scale
+            query_back[rows, lanes] = back * scale
         return carry
 
     lax.fori_loop(0, heads, attend_back, 0)
@@ -1152,6 +1216,12 @@
         item.start()
     core_done(out_items, 0, half)
     turn(ff_items, ffs_ref, 0, line, ff_pieces, ff_order)
+    for copy in mixed_last:
+        copy.wait_recv()
+    for low in range(0, span_len, 16):
+        rows = slice(low, low + 16)
+        mixed = mixed_in[rows].astype(f32) + mixed_own[rows].astype(f32)
+        output_ref[rows] = (middle_ref[rows] + keep * mixed).astype(bf16)
     ring.step(1)
     core_done(out_items, half, line)
     first_done(out_items, 0, half)
@@ -1160,6 +1230,10 @@
     first_done(out_items, half, line)
     turn(out_items, outs_ref, 0, half, out_pieces)
     ring.step(3)
+    for low in range(0, span_len, 16):
+        rows = slice(low, low + 16)
+        grad = middle_grad[rows] + norm_back(x_own[rows].astype(f32), total[rows], gain_ref[0])
+        token_ref[rows] = grad.astype(bf16)
     first_done(qkv_items, 0, half)
     turn(out_items, outs_ref, half, line, out_pieces)
     first_done(qkv_items, half, line)
@@ -1171,9 +1245,9 @@
         copy.wait()
 
 
-def backward_call(small, saved, out_w, attended, weights, norm, grad_ff, ff_half, line):
+def backward_call(near, tokens, saved, out_w, attended, weights, norm, grad_ff, ff_half, line):
     f32, bf16 = jnp.float32, jnp.bfloat16
-    span_len, width = small[0].shape
+    span_len, width = tokens[0].shape
     group_len = line * span_len
     query = saved[0]
     q_cols, rows_each, qkv_cols = query.shape[1], width // line // 8, weights.shape[3]
@@ -1182,7 +1256,7 @@
     slim = (line, 2, 2, 2, rows_each, qkv_cols)
     out_space = sum_space(line, rows_each, width)[1:]
     qkv_space = sum_space(line, rows_each, qkv_cols)[1:]
-    token = jax.ShapeDtypeStruct((span_len, width), f32)
+    token = jax.ShapeDtypeStruct((span_len, width), bf16)
     return link_call(
         functools.partial(backward_kernel, line),
         4,
@@ -1193,9 +1267,11 @@
             jax.ShapeDtypeStruct((line, rows_each, width), bf16),
             jax.ShapeDtypeStruct((rows_each, line * qkv_cols), bf16),
         ),
-        small + saved + (out_w.reshape(wide), attended, weights, norm, grad_ff, ff_half),
-        "v" * 5 + "h" * 10 + "vvhhh",
-        [
+        near + tokens + saved + (out_w.reshape(wide), attended, weights, norm, grad_ff, ff_half),
+        "v" * 4 + "h" * 14 + "vvhhh",
+        [pltpu.VMEM((span_len, width), bf16)] * 4
+        + [pltpu.VMEM((span_len, width), f32)] * 2
+        + [
             pltpu.VMEM(wide, bf16),
             pltpu.VMEM(slim, bf16),
             pltpu.VMEM((group_len, width), bf16),
@@ -1562,22 +1638,24 @@
     rows_each = w_query.shape[0]
     q_cols = HEADS // line * HD
 
-    own_x = tokens[0].astype(f32)
-    keep = keep_mask[0].astype(f32)
     group_match = group_ids[0][:, None] == jnp.arange(exit_scale.shape[0], dtype=jnp.int32)[None, :]
-    token_scale = jnp.sum(jnp.where(group_match, exit_scale[None, :], 0.0), axis=1, keepdims=True)
-    upstream = out_grad[0].astype(f32) * token_scale
+    token_scale = jnp.sum(jnp.where(group_match, exit_scale[None, :], 0.0), axis=1)
+    freqs = 10000.0 ** (-2.0 * jnp.arange(HD // 2, dtype=f32) / HD)
+    small = jnp.stack(
+        [
+            positions[0].astype(f32),
+            token_scale,
+            jnp.concatenate([freqs, freqs]),
+            jnp.broadcast_to(keep_mask.astype(f32), (span_len,)),
+        ]
+    )
+    small = jnp.broadcast_to(small[:, None], (4, 8, span_len))
 
     core = lax.axis_index("c")
     gain_row = jnp.zeros((q_cols + 2 * HD,), bf16)
     gain_row = lax.dynamic_update_slice_in_dim(gain_row, attn_gain, core * rows_each, 0)
     gain_row = lax.dynamic_update_slice_in_dim(gain_row, mlp_gain, HD + core * rows_each, 0)
     gain_rows = jnp.broadcast_to(gain_row, (16, gain_row.shape[0]))
-    freqs = 10000.0 ** (-2.0 * jnp.arange(HD // 2, dtype=f32) / HD)
-    freqs = jnp.broadcast_to(jnp.concatenate([freqs, freqs])[None], (8, HD))
-    places = jnp.broadcast_to(positions[0].astype(f32)[None], (8, span_len))
-    own_mixed = (keep * upstream).astype(bf16)
-    first_tokens, own_mixed, upstream = lax.optimization_barrier((tokens[0], own_mixed, upstream))
     (
         x_blocks,
         near_w,
@@ -1590,19 +1668,19 @@
         attended_rows,
         ff_w,
         out_w,
+        mixed_blocks,
     ) = forward_call(
-        freqs,
-        first_tokens,
-        places,
+        small,
+        tokens[0],
+        out_grad[0],
         gain_rows,
         (w_query, w_key, w_value, w_gate, w_up, w_out),
         line,
     )
-    keep_tile = jnp.broadcast_to(keep, (8, HD))
-    middle, norm_grad, mixed, grad_down, grad_ff, ff_half = mlp_call(
-        keep_tile,
+    middle, norm_grad, carry, mixed_own, grad_down, grad_ff, ff_half = mlp_call(
+        small,
         gain_all,
-        own_mixed,
+        mixed_blocks,
         x_blocks,
         attended_rows,
         out_w,
@@ -1611,15 +1689,9 @@
         line,
     )
     grad_down = grad_down.astype(f32)
-    output = (middle + keep * mixed).astype(bf16)
-    middle_grad, input_norm_grad, ff_back, out_back, qkv_back = backward_call(
-        (
-            upstream,
-            middle,
-            norm_grad,
-            keep_tile,
-            gain_all,
-        ),
+    output, token_grad, ff_back, out_back, qkv_back = backward_call(
+        (small, gain_all, middle, norm_grad),
+        (tokens[0], out_grad[0], carry, mixed_own),
         (queries, both_kv, log_total, turns),
         out_w,
         attended_rows,
@@ -1632,17 +1704,6 @@
     ff_back = ff_back.astype(f32)
     qkv_back = qkv_back.astype(f32)
     grad_out = jnp.sum(out_back.astype(f32), axis=0)
-    gain_one = gain_all[0, :1]
-    inverse_one = lax.rsqrt(jnp.mean(own_x * own_x, axis=-1, keepdims=True) + epsilon)
-    scaled_one = gain_one * input_norm_grad
-    input_grad = (
-        middle_grad
-        + inverse_one * scaled_one
-        - own_x
-        * (inverse_one * inverse_one * inverse_one)
-        * jnp.mean(scaled_one * own_x, axis=-1, keepdims=True)
-    )
-
     heads_end, keys_end = w_query.shape[1], w_query.shape[1] + w_key.shape[1]
     grad_query = qkv_back[:, :heads_end]
     grad_key = qkv_back[:, heads_end:keys_end]
@@ -1656,7 +1717,7 @@
 
     return (
         output[None],
-        input_grad.astype(bf16)[None],
+        token_grad[None],
         gain_grad([(w_query, grad_query), (w_key, grad_key), (w_value, grad_value)], attn_gain),
         grad_query,
         grad_key,

time: 416 us -> 431 us (1.036)
  Pallas kernels: 394 us -> 414 us
    pallas_call x3, Pallas kernels: 394 us -> 414 us  [link_call(): pl.pallas_call(kernel, out_shape=shapes, in_specs=specs[:len(arguments)],...]
where the time goes in v12:
time: 431 us
  Pallas kernels  414 us (96%)
  other arithmetic  10.2 us (2%)
  local copies, waits for them, and re-layouts  5.45 us (1%)
    pallas_call x3, Pallas kernels, link_call(): pl.pallas_call(kernel, out_shape=shapes, in_specs=specs[:len(arguments)],...  414 us

profile of v12, /device:TPU:0, one launch (start us, length us, event | category | flops | bytes accessed | tf_op | source)
XLA Modules:
  0.0 430.9 jit_solution(6968405984198789964)
XLA Ops:
  1.3 0.1 pad.3.clone
  1.4 0.8 fusion
  2.1 0.7 convert_element_type.42
  2.8 0.1 maximum_bitcast_fusion
  2.9 0.1 maximum_maximum_fusion
  2.9 0.8 dynamic_update_slice.6
  3.8 0.8 dynamic_update_slice.7
  4.6 0.6 broadcast_in_dim.34.small_ref
  5.2 0.6 broadcast_in_dim.36.gain_rows_ref
  5.8 164.1 %shard_map.230 = (bf16[4,128,2048]{2,1,0:T(8,128)(2,1)}, bf16[4,8,80,768]{3,2,1,0:T(8,128)(2,1)}, f32[2,16,2048]{2,1,0:T(8,128)}, bf16[512,2048]{1,0:T(8,128)(2,...) custom-call(f32[4,8,128]{2,1,0:T(8,128)} %broadcast_in_dim.34.small_, ...), custom_call_target="tpu_custom_call" | custom-call | tf_op jit(solution)/shard_map/pallas_call | solution.py:568
  169.9 109.7 %shard_map.231 = (f32[128,2048]{1,0:T(8,128)}, f32[128,2048]{1,0:T(8,128)}, bf16[128,2048]{1,0:T(8,128)(2,1)}, bf16[128,2048]{1,0:T(8,128)(2,1)}, bf16[176,2048]...) custom-call(f32[4,8,128]{2,1,0:T(8,128)} %broadcast_in_dim.34.small_ref, ...), custom_call_target="tpu_custom_call" | custom-call | tf_op jit(solution)/shard_map/pallas_call | solution.py:568
  279.6 0.0 copy-start.8
  279.6 0.0 copy-start.9
  279.6 0.0 copy-start.3
  279.6 140.1 %shard_map.232 = (bf16[128,2048]{1,0:T(8,128)(2,1)}, bf16[128,2048]{1,0:T(8,128)(2,1)}, bf16[64,11264]{1,0:T(8,128)(2,1)}, bf16[4,64,2048]{2,1,0:T(8,128)(2,1)}, bf16[64,3072]{1,0:T(8,128)(2,1)}) custom-call(f32[4,8,128]{2,1,0:T(8,128)} %broadcast_in_dim.34.small_ref, f32[2,16,2048]{2,1,0:T(8,128)} %get-tuple-element.35.gain_ref, ...), custom_call_target="tpu_custom_call" | custom-call | tf_op jit(solution)/shard_map/pallas_call | solution.py:568
  419.7 0.0 copy-start.4
  419.7 0.0 copy-done.8
  419.7 0.0 copy-done.9
  419.7 1.8 multiply_reduce_fusion.4
  421.5 0.0 copy-done.3
  421.5 0.0 copy-start.5
  421.6 2.0 multiply_reduce_fusion.2
  423.5 0.0 copy-done.4
  423.5 0.0 copy-start.2
  423.6 1.0 convert_reduce_fusion
  424.5 0.0 copy-done.5
  424.5 0.0 copy-start
  424.5 0.0 copy-start.1
  424.5 1.3 convert_element_type.55
  425.8 0.0 copy-done.2
  425.8 0.7 copy-done
  426.4 0.2 copy-done.1
  426.6 0.0 copy-start.10
  426.6 0.0 copy-start.11
  426.6 0.0 copy-start.7
  426.6 0.0 copy-start.6
  426.6 2.1 multiply_reduce_fusion
  428.7 0.0 copy-done.10
  428.8 0.0 copy-done.11
  428.8 0.5 convert_divide_fusion
  429.3 0.0 copy-done.7
  429.3 0.8 copy.31
  430.1 0.0 copy-done.6
  430.1 0.8 copy.32
  (2 shorter events, 0.0 us)
Async XLA Ops:
  279.6 140.1 %copy-start.8 = (bf16[64,512]{1,0:T(8,128)(2,1)S(1)}, bf16[64,512]{1,0:T(8,128)(2,1)}, u32[]{:S(2)}) copy-start(bf16[64,512]{1,0:T(8,128)(2,1)} %key_w_ref.1) | copy-start | bytes 196612
  279.6 140.1 %copy-start.9 = (bf16[64,512]{1,0:T(8,128)(2,1)S(1)}, bf16[64,512]{1,0:T(8,128)(2,1)}, u32[]{:S(2)}) copy-start(bf16[64,512]{1,0:T(8,128)(2,1)} %value_w_ref.1) | copy-start | bytes 196612
  279.6 141.9 %copy-start.3 = (bf16[64,2048]{1,0:T(8,128)(2,1)S(1)}, bf16[64,2048]{1,0:T(8,128)(2,1)}, u32[]{:S(2)}) copy-start(bf16[64,2048]{1,0:T(8,128)(2,1)} %query_w_ref.1) | copy-start | bytes 786436
  419.7 3.8 copy-start.4
  421.5 3.0 copy-start.5
  423.5 2.2 copy-start.2
  424.5 1.9 copy-start
  424.5 2.1 copy-start.1
  426.6 2.1 copy-start.10
  426.6 2.1 copy-start.11
  426.6 2.7 copy-start.7
  426.6 3.4 copy-start.6

commit v13 on v12

--- a/solution.py
+++ b/solution.py
@@ -153,14 +153,15 @@
 
 
 class RingGather:
-    def __init__(self, links, rows, origin, place, first=0, pieces=4):
-        self.links, self.origin, self.place, self.first = links, origin, place, first
+    def __init__(self, links, rows, origin, place, pieces=4):
+        self.links, self.origin, self.place = links, origin, place
         self.pieces, self.rows = pieces, rows // pieces
         self.last = [None] * pieces
 
     def step(self, number):
-        if number > self.first:
-            self.wait()
+        if number > 0:
+            for copy in self.last:
+                copy.wait_recv()
         if number == self.links.line - 1:
             return
         for piece in range(self.pieces):
@@ -168,12 +169,8 @@
             rows = pl.ds(piece * self.rows, self.rows)
             block = self.links.along(-way * number)
             place = self.place(block, rows)
-            source = self.origin(block, rows) if number == self.first else place
+            source = self.origin(rows) if number == 0 else place
             self.last[piece] = self.links.send(source, place, way)
-
-    def wait(self):
-        for copy in self.last:
-            copy.wait_recv()
 
 
 def column_of(row):
@@ -207,7 +204,7 @@
     atts_ref,
     ffs_ref,
     outs_ref,
-    mixs_ref,
+    mix_ref,
     x_all,
     grad,
     mix,
@@ -241,7 +238,7 @@
     far_ff = NearGather(links, lambda block, place: ffs_ref.at[links.along(-block), place])
     far_out = NearGather(links, lambda block, place: outs_ref.at[links.along(-block), place])
     ring = RingGather(
-        links, span_len, lambda block, rows: x_ref.at[rows], lambda block, rows: x_all.at[block, rows]
+        links, span_len, lambda rows: x_ref.at[rows], lambda block, rows: x_all.at[block, rows]
     )
     place_ref = small_ref.at[0]
 
@@ -331,7 +328,7 @@
         rows = slice(low, low + 16)
         upstream = grad[rows].astype(f32) * token_scale[rows]
         mix[rows] = (upstream * small_ref[3, 0:1, 0:1]).astype(bf16)
-    local.append(links.keep(mix, mixs_ref.at[links.z]))
+    local.append(links.keep(mix, mix_ref))
     near.wait(range(line))
     for index in range(line * 4):
         z, q = divmod(index, 4)
@@ -433,10 +430,7 @@
     def place(block, rows):
         return atts_ref.at[rows, pl.ds(pl.multiple_of(block * q_cols, q_cols), q_cols)]
 
-    att_ring = RingGather(links, group_len, lambda block, rows: att.at[rows], place)
-    mix_ring = RingGather(
-        links, span_len, lambda block, rows: mix.at[rows], lambda block, rows: mixs_ref.at[block, rows]
-    )
+    att_ring = RingGather(links, group_len, lambda rows: att.at[rows], place)
     local.append(links.keep(att, place(links.z, pl.ds(0, group_len))))
     att_ring.step(0)
     for k in [0] + far:
@@ -449,13 +443,11 @@
         moved = move_out(k)
     far_out.relay(2, "y")
     att_ring.step(2)
-    mix_ring.step(0)
     for k in range(3, line):
         far_out.relay(k, "y")
     for k in range(line):
         far_out.close(k)
     att_ring.step(3)
-    mix_ring.wait()
     far_out.wait(range(line))
     far_ff.wait(range(line))
     links.finish()
@@ -534,7 +526,7 @@
         self.pieces, self.last = pieces, [None] * pieces
         self.rows = parts.shape[1] // pieces
 
-    def step(self, number, carry=None):
+    def step(self, number):
         links = self.links
         for piece in range(self.pieces):
             way = 1 if piece < self.pieces // 2 else -1
@@ -549,9 +541,6 @@
                 ].astype(jnp.float32)
                 if number == links.line - 1:
                     self.total[where] = total
-                    continue
-                if carry is not None:
-                    carry[where] = total.astype(carry.dtype)
                     continue
                 self.parts[block, where] = total.astype(self.parts.dtype)
                 source = self.parts.at[block, where]
@@ -598,7 +587,7 @@
         ((group_len, line * q_cols), bf16),
         ((line, 8, rows_each, both_cols), bf16),
         ((line, 8, rows_each, width), bf16),
-        ((line, span_len, width), bf16),
+        ((span_len, width), bf16),
     )
     return link_call(
         functools.partial(first_kernel, line),
@@ -631,7 +620,7 @@
     cuts,
     small_ref,
     gain_ref,
-    mixs_ref,
+    mix_ref,
     xs_ref,
     atts_ref,
     out_ref,
@@ -639,8 +628,7 @@
     down_ref,
     middle_ref,
     total_ref,
-    carry_ref,
-    mixed_own_ref,
+    output_ref,
     sum_ref,
     grad_ff_ref,
     ff_half_ref,
@@ -656,6 +644,7 @@
     got,
     mixed_parts,
     mixed_got,
+    mixed_total,
     *scratch,
 ):
     f32, bf16 = jnp.float32, jnp.bfloat16
@@ -663,24 +652,17 @@
     links = Links(send_sems, recv_sems, line)
     links.meet(["x", "y", "c", 1, line - 1])
     far = [1, line - 1] + list(range(2, line - 1))
-    span_len, width = mixs_ref.shape[1:]
+    span_len, width = mix_ref.shape
     group_len = line * span_len
     ff_cols = hidden.shape[1]
     block_rows = width // line
     rows_each = block_rows // 8
     chunk = 2 * HD
     mix_ring = RingGather(
-        links,
-        span_len,
-        lambda block, rows: mixs_ref.at[block, rows],
-        lambda block, rows: mixed.at[block, rows],
-        1,
-    )
-    mix_ring.step(1)
-    stay = [links.keep(mixs_ref.at[links.z], mixed.at[links.z])]
-    for low, step in ((0, -1), (span_len // 2, 1)):
-        rows = pl.ds(low, span_len // 2)
-        stay.append(links.keep(mixs_ref.at[links.along(step), rows], mixed.at[links.along(step), rows]))
+        links, span_len, lambda rows: mix_ref.at[rows], lambda block, rows: mixed.at[block, rows]
+    )
+    mix_ring.step(0)
+    stay = links.keep(mix_ref, mixed.at[links.z])
     early = [
         links.keep(out_ref, big),
         links.keep(atts_ref, norm),
@@ -699,7 +681,7 @@
         late.append(links.keep(rows, down_place(block, links.slot)))
         near.offer(block, rows)
     ring = RingSum(links, parts, total_ref, got)
-    mixed_ring = RingSum(links, mixed_parts, None, mixed_got)
+    mixed_ring = RingSum(links, mixed_parts, mixed_total, mixed_got)
     items = []
     ff_items = []
     for index, k in enumerate(far[:2]):
@@ -769,7 +751,7 @@
             where = pl.multiple_of(lax.rem(links.z, line // 2) * span_len, span_len)
             middle_ref[...] = gate_up[pl.ds(where, span_len), :width]
         if part == 0:
-            mix_ring.step(2)
+            mix_ring.step(1)
 
     for block in range(2):
         near.relay(block, "xy"[block])
@@ -811,6 +793,7 @@
             work(extent // chunk * chunk, extent % chunk)
 
     over_chunks(forward, ff_cols)
+    mix_ring.step(2)
     for block in range(2):
         near.close(block)
     near.wait(range(2))
@@ -822,9 +805,7 @@
 
     over_chunks(mixed_part, width)
     mixed_ring.step(0)
-    mixed_own_ref[...] = mixed_parts[links.z]
-    for copy in stay:
-        copy.wait()
+    stay.wait()
     mix_ring.step(3)
     hidden_rows = hidden[...].T
 
@@ -876,7 +857,7 @@
     ring.step(1)
     for item in ff_items:
         item.core_done()
-    mixed_ring.step(2, carry_ref)
+    mixed_ring.step(2)
     sent = []
     for k in far[2:] + [0]:
         block = links.along(k)
@@ -887,6 +868,10 @@
     ring.step(2)
     for item in ff_items:
         item.first_done()
+    mixed_ring.step(3)
+    for low in range(0, span_len, 16):
+        rows = slice(low, low + 16)
+        output_ref[rows] = (middle_ref[rows] + small_ref[3, 0:1, 0:1] * mixed_total[rows]).astype(bf16)
     ring.step(3)
     for index, item in enumerate(ff_items):
         sent.append(links.keep(item.second_done(), ff_half_ref.at[index]))
@@ -897,7 +882,7 @@
 
 def mlp_call(small, gains, mixed, x_blocks, attended, out_w, ff_w, w_down, line):
     f32, bf16 = jnp.float32, jnp.bfloat16
-    span_len, width = mixed.shape[1:]
+    span_len, width = mixed.shape
     group_len = line * span_len
     rows, both_cols, rows_each = w_down.shape[0], ff_w.shape[3], ff_w.shape[2]
     ff_rows = 8 * rows
@@ -914,13 +899,12 @@
             token,
             token,
             jax.ShapeDtypeStruct((span_len, width), bf16),
-            jax.ShapeDtypeStruct((span_len, width), bf16),
             jax.ShapeDtypeStruct((rows, width), bf16),
             jax.ShapeDtypeStruct(ff_w.shape, bf16),
             jax.ShapeDtypeStruct((2, rows_each, both_cols), bf16),
         ),
         (small, gains, mixed, x_blocks, attended, out_w.reshape(2, 2, 2, width // 8, width), ff_w, w_down),
-        "vvhhhhhh" + "vvvvvhh",
+        "vvhhhhhh" + "vvvvhh",
         [
             pltpu.VMEM((2, 2, 2, width // 8, width), bf16),
             pltpu.VMEM(ff_w.shape, bf16),
@@ -933,7 +917,8 @@
             pltpu.VMEM((group_len, both_cols), bf16),
             pltpu.VMEM((line - 1, span_len, width), bf16),
             pltpu.VMEM(blocks, bf16),
-            pltpu.VMEM((line - 2, span_len, width), bf16),
+            pltpu.VMEM((line - 1, span_len, width), bf16),
+            pltpu.VMEM((span_len, width), f32),
         ]
         + sum_space(2, rows_each, both_cols)[1:]
         + sum((sum_space(1, high - low, width)[1:] for low, high in cuts), []),
@@ -949,8 +934,6 @@
     norm_grad_ref,
     x_ref,
     grad_ref,
-    carry_ref,
-    mixed_own_ref,
     query_ref,
     kv_ref,
     peak_ref,
@@ -961,15 +944,12 @@
     norm_ref,
     ff_ref,
     ff_half_ref,
-    output_ref,
     token_ref,
     ffs_ref,
     outs_ref,
     qkvs_ref,
     x_own,
     grad_own,
-    mixed_own,
-    mixed_in,
     middle_grad,
     total,
     big,
@@ -1011,13 +991,12 @@
         return pl.ds(pl.multiple_of(block * q_cols, q_cols), q_cols)
 
     here = pl.ds(pl.multiple_of(links.z * span_len, span_len), span_len)
+    first_load = links.keep(grad_ref, grad_own)
     loads = [
         links.keep(out_ref, big),
         links.keep(atts_ref.at[here], own_rows),
         links.keep(atts_ref.at[:, lanes_of(links.z)], own_columns),
-        links.keep(grad_ref, grad_own),
         links.keep(x_ref, x_own),
-        links.keep(mixed_own_ref, mixed_own),
         links.keep(query_ref, query),
         links.keep(kv_ref, kv),
         links.keep(peak_ref, peak),
@@ -1072,12 +1051,6 @@
     out_pieces = ((0, width),)
     for index, k in enumerate(order[:2]):
         deliver(ff_half_ref.at[index], ffs_ref, k, ff_pieces)
-    mixed_last = []
-    for piece in range(4):
-        rows = pl.ds(piece * (span_len // 4), span_len // 4)
-        way = 1 if piece < 2 else -1
-        mixed_last.append(links.send(carry_ref.at[rows], mixed_in.at[rows], way))
-
     def turn(items, target, low, high, pieces, order=order):
         for item, k in list(zip(items, order))[low:high]:
             deliver(item.second_done(), target, k, pieces)
@@ -1094,8 +1067,7 @@
     for item in ff_items:
         item.start()
 
-    for copy in loads:
-        copy.wait()
+    first_load.wait()
     keep = small_ref[3, 0:1, 0:1]
     token_scale = column_of(small_ref[1, 0:1])
 
@@ -1112,6 +1084,8 @@
         grad = upstream + norm_back(middle_ref[rows], norm_grad_ref[rows], gain_ref[1])
         middle_grad[rows] = grad
         branch[rows] = (grad * keep).astype(bf16)
+    for copy in loads:
+        copy.wait()
     for z in range(line):
         weight = big[z].reshape(rows_z, width)
         own_grad[:, z * rows_z : (z + 1) * rows_z] = lax.dot_general(
@@ -1216,12 +1190,6 @@
         item.start()
     core_done(out_items, 0, half)
     turn(ff_items, ffs_ref, 0, line, ff_pieces, ff_order)
-    for copy in mixed_last:
-        copy.wait_recv()
-    for low in range(0, span_len, 16):
-        rows = slice(low, low + 16)
-        mixed = mixed_in[rows].astype(f32) + mixed_own[rows].astype(f32)
-        output_ref[rows] = (middle_ref[rows] + keep * mixed).astype(bf16)
     ring.step(1)
     core_done(out_items, half, line)
     first_done(out_items, 0, half)
@@ -1261,15 +1229,15 @@
         functools.partial(backward_kernel, line),
         4,
         160,
-        (token, token)
+        (token,)
         + (
             jax.ShapeDtypeStruct((rows_each, line * grad_ff.shape[5]), bf16),
             jax.ShapeDtypeStruct((line, rows_each, width), bf16),
             jax.ShapeDtypeStruct((rows_each, line * qkv_cols), bf16),
         ),
         near + tokens + saved + (out_w.reshape(wide), attended, weights, norm, grad_ff, ff_half),
-        "v" * 4 + "h" * 14 + "vvhhh",
-        [pltpu.VMEM((span_len, width), bf16)] * 4
+        "v" * 4 + "h" * 12 + "vhhh",
+        [pltpu.VMEM((span_len, width), bf16)] * 2
         + [pltpu.VMEM((span_len, width), f32)] * 2
         + [
             pltpu.VMEM(wide, bf16),
@@ -1668,7 +1636,7 @@
         attended_rows,
         ff_w,
         out_w,
-        mixed_blocks,
+        own_mixed,
     ) = forward_call(
         small,
         tokens[0],
@@ -1677,10 +1645,10 @@
         (w_query, w_key, w_value, w_gate, w_up, w_out),
         line,
     )
-    middle, norm_grad, carry, mixed_own, grad_down, grad_ff, ff_half = mlp_call(
+    middle, norm_grad, output, grad_down, grad_ff, ff_half = mlp_call(
         small,
         gain_all,
-        mixed_blocks,
+        own_mixed,
         x_blocks,
         attended_rows,
         out_w,
@@ -1689,9 +1657,9 @@
         line,
     )
     grad_down = grad_down.astype(f32)
-    output, token_grad, ff_back, out_back, qkv_back = backward_call(
+    token_grad, ff_back, out_back, qkv_back = backward_call(
         (small, gain_all, middle, norm_grad),
-        (tokens[0], out_grad[0], carry, mixed_own),
+        (tokens[0], out_grad[0]),
         (queries, both_kv, log_total, turns),
         out_w,
         attended_rows,

time: 431 us -> 416 us (0.965)
  Pallas kernels: 414 us -> 399 us
    pallas_call x3, Pallas kernels: 414 us -> 399 us  [link_call(): pl.pallas_call(kernel, out_shape=shapes, in_specs=specs[:len(arguments)],...]
where the time goes in v13:
time: 416 us
  Pallas kernels  399 us (96%)
  other arithmetic  10.2 us (2%)
  local copies, waits for them, and re-layouts  5.45 us (1%)
    pallas_call x3, Pallas kernels, link_call(): pl.pallas_call(kernel, out_shape=shapes, in_specs=specs[:len(arguments)],...  399 us

profile of v13, /device:TPU:0, one launch (start us, length us, event | category | flops | bytes accessed | tf_op | source)
XLA Modules:
  0.0 415.8 jit_solution(6440898632430588269)
XLA Ops:
  1.3 0.1 pad.3.clone
  1.4 0.8 fusion
  2.1 0.7 convert_element_type.42
  2.8 0.1 maximum_bitcast_fusion
  2.9 0.1 maximum_maximum_fusion
  2.9 0.8 dynamic_update_slice.6
  3.8 0.8 dynamic_update_slice.7
  4.6 0.6 broadcast_in_dim.34.small_ref
  5.2 0.6 broadcast_in_dim.36.gain_rows_ref
  5.8 152.8 %shard_map.230 = (bf16[4,128,2048]{2,1,0:T(8,128)(2,1)}, bf16[4,8,80,768]{3,2,1,0:T(8,128)(2,1)}, f32[2,16,2048]{2,1,0:T(8,128)}, bf16[512,2048]{1,0:T(8,128)(2,...) custom-call(f32[4,8,128]{2,1,0:T(8,128)} %broadcast_in_dim.34.small_, ...), custom_call_target="tpu_custom_call" | custom-call | tf_op jit(solution)/shard_map/pallas_call | solution.py:557
  158.6 113.2 %shard_map.231 = (f32[128,2048]{1,0:T(8,128)}, f32[128,2048]{1,0:T(8,128)}, bf16[128,2048]{1,0:T(8,128)(2,1)}, bf16[176,2048]{1,0:T(8,128)(2,1)}, bf16[4,2,2,2,6...) custom-call(f32[4,8,128]{2,1,0:T(8,128)} %broadcast_in_dim.34.small_ref, ...), custom_call_target="tpu_custom_call" | custom-call | tf_op jit(solution)/shard_map/pallas_call | solution.py:557
  271.9 0.0 copy-start.8
  271.9 0.0 copy-start.9
  271.9 0.0 copy-start.3
  271.9 132.7 %shard_map.232 = (bf16[128,2048]{1,0:T(8,128)(2,1)}, bf16[64,11264]{1,0:T(8,128)(2,1)}, bf16[4,64,2048]{2,1,0:T(8,128)(2,1)}, bf16[64,3072]{1,0:T(8,128)(2,1)}) custom-call(f32[4,8,128]{2,1,0:T(8,128)} %broadcast_in_dim.34.small_ref, f32[2,16,2048]{2,1,0:T(8,128)} %get-tuple-element.33.gain_ref, f32[128,2048]{1,0:T(8,128)} %get-tuple-element.40.middle_ref, ...), custom_call_target="tpu_custom_call" | custom-call | tf_op jit(solution)/shard_map/pallas_call | solution.py:557
  404.7 0.0 copy-start.4
  404.7 0.0 copy-done.8
  404.7 0.0 copy-done.9
  404.7 1.8 multiply_reduce_fusion.4
  406.5 0.0 copy-done.3
  406.5 0.0 copy-start.5
  406.5 2.0 multiply_reduce_fusion.2
  408.5 0.0 copy-done.4
  408.5 0.0 copy-start.2
  408.5 1.0 convert_reduce_fusion
  409.5 0.0 copy-done.5
  409.5 0.0 copy-start
  409.5 0.0 copy-start.1
  409.5 1.3 convert_element_type.55
  410.7 0.0 copy-done.2
  410.7 0.7 copy-done
  411.4 0.2 copy-done.1
  411.6 0.0 copy-start.10
  411.6 0.0 copy-start.11
  411.6 0.0 copy-start.6
  411.6 0.0 copy-start.7
  411.6 2.1 multiply_reduce_fusion
  413.7 0.0 copy-done.10
  413.7 0.0 copy-done.11
  413.7 0.5 convert_divide_fusion
  414.2 0.0 copy-done.6
  414.2 0.8 copy.31
  415.0 0.0 copy-done.7
  415.0 0.8 copy.32
  (2 shorter events, 0.0 us)
Async XLA Ops:
  271.9 132.8 %copy-start.8 = (bf16[64,512]{1,0:T(8,128)(2,1)S(1)}, bf16[64,512]{1,0:T(8,128)(2,1)}, u32[]{:S(2)}) copy-start(bf16[64,512]{1,0:T(8,128)(2,1)} %key_w_ref.1) | copy-start | bytes 196612
  271.9 132.8 %copy-start.9 = (bf16[64,512]{1,0:T(8,128)(2,1)S(1)}, bf16[64,512]{1,0:T(8,128)(2,1)}, u32[]{:S(2)}) copy-start(bf16[64,512]{1,0:T(8,128)(2,1)} %value_w_ref.1) | copy-start | bytes 196612
  271.9 134.6 %copy-start.3 = (bf16[64,2048]{1,0:T(8,128)(2,1)S(1)}, bf16[64,2048]{1,0:T(8,128)(2,1)}, u32[]{:S(2)}) copy-start(bf16[64,2048]{1,0:T(8,128)(2,1)} %query_w_ref.1) | copy-start | bytes 786436
  404.7 3.8 copy-start.4
  406.5 3.0 copy-start.5
  408.5 2.2 copy-start.2
  409.5 1.9 copy-start
  409.5 2.1 copy-start.1
  411.6 2.1 copy-start.10
  411.6 2.1 copy-start.11
  411.6 2.7 copy-start.6
  411.6 3.4 copy-start.7

commit v14 on v13

--- a/solution.py
+++ b/solution.py
@@ -63,6 +63,13 @@
 AXES = ("z", "x", "y", "c")
 
 
+def only(when, act):
+    if when is None:
+        act()
+    else:
+        pl.when(when)(act)
+
+
 class Links:
     def __init__(self, send_sems, recv_sems, line):
         self.send_sems, self.recv_sems, self.line = send_sems, recv_sems, line
@@ -97,7 +104,7 @@
             pl.semaphore_signal(barrier, inc=1, device_id=self.device(to), device_id_type=MESH)
         pl.semaphore_wait(barrier, len(targets))
 
-    def send(self, source, target, to):
+    def send(self, source, target, to, when=None):
         copy = pltpu.make_async_remote_copy(
             src_ref=source,
             dst_ref=target,
@@ -106,9 +113,9 @@
             device_id=self.device(to),
             device_id_type=MESH,
         )
-        copy.start()
+        only(when, copy.start)
         self.used += 1
-        self.sent.append(copy)
+        self.sent.append((copy, when))
         return copy
 
     def keep(self, source, target):
@@ -118,8 +125,8 @@
         return copy
 
     def finish(self):
-        for copy in self.sent:
-            copy.wait_send()
+        for copy, when in self.sent:
+            only(when, copy.wait_send)
 
 
 class NearGather:
@@ -152,25 +159,29 @@
                 self.got[block, to].wait_recv()
 
 
-class RingGather:
-    def __init__(self, links, rows, origin, place, pieces=4):
+class LineGather:
+    def __init__(self, links, rows, origin, place, pieces=2):
         self.links, self.origin, self.place = links, origin, place
         self.pieces, self.rows = pieces, rows // pieces
-        self.last = [None] * pieces
+        self.last = {}
+
+    def inside(self, block):
+        return jnp.logical_and(block >= 0, block < self.links.line)
 
     def step(self, number):
-        if number > 0:
-            for copy in self.last:
-                copy.wait_recv()
-        if number == self.links.line - 1:
-            return
+        z = self.links.z
         for piece in range(self.pieces):
-            way = 1 if piece < self.pieces // 2 else -1
-            rows = pl.ds(piece * self.rows, self.rows)
-            block = self.links.along(-way * number)
-            place = self.place(block, rows)
-            source = self.origin(rows) if number == 0 else place
-            self.last[piece] = self.links.send(source, place, way)
+            for way in (1, -1):
+                held = self.inside(z - way * number)
+                if number > 0:
+                    only(held, self.last[piece, way].wait_recv)
+                if number == self.links.line - 1:
+                    continue
+                rows = pl.ds(piece * self.rows, self.rows)
+                place = self.place(self.links.along(-way * number), rows)
+                source = self.origin(rows) if number == 0 else place
+                when = jnp.logical_and(held, self.inside(z + way))
+                self.last[piece, way] = self.links.send(source, place, way, when)
 
 
 def column_of(row):
@@ -237,7 +248,7 @@
     near = NearGather(links, lambda block, place: weights.at[links.along(-block), place])
     far_ff = NearGather(links, lambda block, place: ffs_ref.at[links.along(-block), place])
     far_out = NearGather(links, lambda block, place: outs_ref.at[links.along(-block), place])
-    ring = RingGather(
+    ring = LineGather(
         links, span_len, lambda rows: x_ref.at[rows], lambda block, rows: x_all.at[block, rows]
     )
     place_ref = small_ref.at[0]
@@ -430,7 +441,7 @@
     def place(block, rows):
         return atts_ref.at[rows, pl.ds(pl.multiple_of(block * q_cols, q_cols), q_cols)]
 
-    att_ring = RingGather(links, group_len, lambda rows: att.at[rows], place)
+    att_ring = LineGather(links, group_len, lambda rows: att.at[rows], place)
     local.append(links.keep(att, place(links.z, pl.ds(0, group_len))))
     att_ring.step(0)
     for k in [0] + far:
@@ -658,7 +669,7 @@
     block_rows = width // line
     rows_each = block_rows // 8
     chunk = 2 * HD
-    mix_ring = RingGather(
+    mix_ring = LineGather(
         links, span_len, lambda rows: mix_ref.at[rows], lambda block, rows: mixed.at[block, rows]
     )
     mix_ring.step(0)
@@ -1606,24 +1617,21 @@
     rows_each = w_query.shape[0]
     q_cols = HEADS // line * HD
 
-    group_match = group_ids[0][:, None] == jnp.arange(exit_scale.shape[0], dtype=jnp.int32)[None, :]
-    token_scale = jnp.sum(jnp.where(group_match, exit_scale[None, :], 0.0), axis=1)
-    freqs = 10000.0 ** (-2.0 * jnp.arange(HD // 2, dtype=f32) / HD)
-    small = jnp.stack(
-        [
-            positions[0].astype(f32),
-            token_scale,
-            jnp.concatenate([freqs, freqs]),
-            jnp.broadcast_to(keep_mask.astype(f32), (span_len,)),
-        ]
-    )
-    small = jnp.broadcast_to(small[:, None], (4, 8, span_len))
+    token_scale = jnp.zeros((span_len,), f32)
+    for group in range(exit_scale.shape[0]):
+        token_scale = jnp.where(group_ids[0] == group, exit_scale[group], token_scale)
+    lane = jnp.arange(span_len, dtype=jnp.int32)
+    rates = 10000.0 ** (-2.0 * (lane % (HD // 2)).astype(f32) / HD)
+    row = lax.broadcasted_iota(jnp.int32, (4, 8, span_len), 0)
+    small = jnp.where(row == 2, rates, keep_mask[0].astype(f32))
+    small = jnp.where(row == 1, token_scale, small)
+    small = jnp.where(row == 0, positions[0].astype(f32), small)
 
     core = lax.axis_index("c")
-    gain_row = jnp.zeros((q_cols + 2 * HD,), bf16)
-    gain_row = lax.dynamic_update_slice_in_dim(gain_row, attn_gain, core * rows_each, 0)
-    gain_row = lax.dynamic_update_slice_in_dim(gain_row, mlp_gain, HD + core * rows_each, 0)
-    gain_rows = jnp.broadcast_to(gain_row, (16, gain_row.shape[0]))
+    spot = lax.broadcasted_iota(jnp.int32, (16, q_cols + 2 * HD), 1) // rows_each
+    repeats = (q_cols + 2 * HD) // rows_each
+    gain_rows = jnp.where(spot == 2 + core, jnp.tile(mlp_gain, repeats), 0)
+    gain_rows = jnp.where(spot == core, jnp.tile(attn_gain, repeats), gain_rows).astype(bf16)
     (
         x_blocks,
         near_w,

time: 416 us -> 416 us (level)
  Pallas kernels: 399 us -> 393 us
    pallas_call x3, Pallas kernels: 399 us -> 393 us  [link_call(): pl.pallas_call(kernel, out_shape=shapes, in_specs=specs[:len(arguments)],...]
where the time goes in v14:
time: 416 us; the launch traced here: 413 us
  Pallas kernels  393 us (94%)
  other arithmetic  13.1 us (3%)
  local copies, waits for them, and re-layouts  5.29 us (1%)
    pallas_call x3, Pallas kernels, link_call(): pl.pallas_call(kernel, out_shape=shapes, in_specs=specs[:len(arguments)],...  393 us

profile of v14, /device:TPU:0, one launch (start us, length us, event | category | flops | bytes accessed | tf_op | source)
XLA Modules:
  0.0 413.2 jit_solution(8020400574443331784)
XLA Ops:
  1.3 0.7 convert_bitcast_fusion
  2.0 1.3 fusion.9
  3.3 2.0 fusion.5
  5.2 0.7 tile.8
  5.9 0.1 tile.9
  6.0 0.7 tile.20
  6.7 0.1 tile.21
  6.7 0.6 fusion.gain_rows_ref
  7.4 0.7 select_select_fusion.small_ref
  8.1 143.4 %shard_map.230 = (bf16[4,128,2048]{2,1,0:T(8,128)(2,1)}, bf16[4,8,80,768]{3,2,1,0:T(8,128)(2,1)}, f32[2,16,2048]{2,1,0:T(8,128)}, bf16[512,2048]{1,0:T(8,128)(2,...) custom-call(f32[4,8,128]{2,1,0:T(8,128)} %select_select_fusion.small, ...), custom_call_target="tpu_custom_call" | custom-call | tf_op jit(solution)/shard_map/pallas_call | solution.py:568
  151.5 118.2 %shard_map.231 = (f32[128,2048]{1,0:T(8,128)}, f32[128,2048]{1,0:T(8,128)}, bf16[128,2048]{1,0:T(8,128)(2,1)}, bf16[176,2048]{1,0:T(8,128)(2,1)}, bf16[4,2,2,2,6...) custom-call(f32[4,8,128]{2,1,0:T(8,128)} %select_select_fusion.small_ref, ...), custom_call_target="tpu_custom_call" | custom-call | tf_op jit(solution)/shard_map/pallas_call | solution.py:568
  269.6 0.0 copy-start.8
  269.6 0.0 copy-start.9
  269.7 0.0 copy-start.3
  269.7 131.8 %shard_map.232 = (bf16[128,2048]{1,0:T(8,128)(2,1)}, bf16[64,11264]{1,0:T(8,128)(2,1)}, bf16[4,64,2048]{2,1,0:T(8,128)(2,1)}, bf16[64,3072]{1,0:T(8,128)(2,1)}) custom-call(f32[4,8,128]{2,1,0:T(8,128)} %select_select_fusion.small_ref, f32[2,16,2048]{2,1,0:T(8,128)} %get-tuple-element.33.gain_ref, f32[128,2048]{1,0:T(8,128)} %get-tuple-element.40.middle_ref, ...), custom_call_target="tpu_custom_call" | custom-call | tf_op jit(solution)/shard_map/pallas_call | solution.py:568
  401.5 0.0 copy-start.10
  401.5 0.0 copy-start.4
  401.5 0.0 copy-done.8
  401.5 0.0 copy-done.9
  401.6 1.8 multiply_reduce_fusion.4
  403.3 0.0 copy-done.3
  403.4 0.0 copy-start.5
  403.4 2.0 multiply_reduce_fusion.2
  405.3 0.0 copy-done.10
  405.4 0.5 convert_divide_fusion.1
  405.9 0.0 copy-done.4
  405.9 0.0 copy-start.2
  405.9 0.9 convert_reduce_fusion
  406.8 0.0 copy-done.5
  406.8 0.0 copy-start
  406.8 0.0 copy-start.1
  406.8 1.3 convert_element_type.65
  408.1 0.0 copy-done.2
  408.1 0.7 copy-done
  408.8 0.2 copy-done.1
  409.0 0.0 copy-start.11
  409.0 0.0 copy-start.6
  409.0 0.0 copy-start.7
  409.0 2.1 multiply_reduce_fusion
  411.1 0.0 copy-done.11
  411.1 0.5 convert_divide_fusion
  411.6 0.0 copy-done.6
  411.6 0.8 copy.29
  412.4 0.0 copy-done.7
  412.4 0.8 copy.30
  (5 shorter events, 0.0 us)
Async XLA Ops:
  269.6 131.9 %copy-start.8 = (bf16[64,512]{1,0:T(8,128)(2,1)S(1)}, bf16[64,512]{1,0:T(8,128)(2,1)}, u32[]{:S(2)}) copy-start(bf16[64,512]{1,0:T(8,128)(2,1)} %key_w_ref.1) | copy-start | bytes 196612
  269.6 131.9 %copy-start.9 = (bf16[64,512]{1,0:T(8,128)(2,1)S(1)}, bf16[64,512]{1,0:T(8,128)(2,1)}, u32[]{:S(2)}) copy-start(bf16[64,512]{1,0:T(8,128)(2,1)} %value_w_ref.1) | copy-start | bytes 196612
  269.7 133.7 %copy-start.3 = (bf16[64,2048]{1,0:T(8,128)(2,1)S(1)}, bf16[64,2048]{1,0:T(8,128)(2,1)}, u32[]{:S(2)}) copy-start(bf16[64,2048]{1,0:T(8,128)(2,1)} %query_w_ref.1) | copy-start | bytes 786436
  401.5 3.8 copy-start.10
  401.5 4.4 %copy-start.4 = (bf16[4,64,2048]{2,1,0:T(8,128)(2,1)S(1)}, bf16[4,64,2048]{2,1,0:T(8,128)(2,1)}, u32[]{:S(2)}) copy-start(bf16[4,64,2048]{2,1,0:T(8,128)(2,1)} %get-tuple-element.52) | copy-start | bytes 3145732
  403.4 3.5 copy-start.5
  405.9 2.2 copy-start.2
  406.8 1.9 copy-start
  406.8 2.1 copy-start.1
  409.0 2.1 copy-start.11
  409.0 2.6 copy-start.6
  409.0 3.4 copy-start.7

commit v15 on v13

--- a/solution.py
+++ b/solution.py
@@ -63,6 +63,13 @@
 AXES = ("z", "x", "y", "c")
 
 
+def only(when, act):
+    if when is None:
+        act()
+    else:
+        pl.when(when)(act)
+
+
 class Links:
     def __init__(self, send_sems, recv_sems, line):
         self.send_sems, self.recv_sems, self.line = send_sems, recv_sems, line
@@ -97,7 +104,7 @@
             pl.semaphore_signal(barrier, inc=1, device_id=self.device(to), device_id_type=MESH)
         pl.semaphore_wait(barrier, len(targets))
 
-    def send(self, source, target, to):
+    def send(self, source, target, to, when=None):
         copy = pltpu.make_async_remote_copy(
             src_ref=source,
             dst_ref=target,
@@ -106,9 +113,9 @@
             device_id=self.device(to),
             device_id_type=MESH,
         )
-        copy.start()
+        only(when, copy.start)
         self.used += 1
-        self.sent.append(copy)
+        self.sent.append((copy, when))
         return copy
 
     def keep(self, source, target):
@@ -118,8 +125,8 @@
         return copy
 
     def finish(self):
-        for copy in self.sent:
-            copy.wait_send()
+        for copy, when in self.sent:
+            only(when, copy.wait_send)
 
 
 class NearGather:
@@ -150,6 +157,31 @@
         for block in blocks:
             for to in ("c", "xc", "yc", "xyc"):
                 self.got[block, to].wait_recv()
+
+
+class LineGather:
+    def __init__(self, links, rows, origin, place, pieces=2):
+        self.links, self.origin, self.place = links, origin, place
+        self.pieces, self.rows = pieces, rows // pieces
+        self.last = {}
+
+    def inside(self, block):
+        return jnp.logical_and(block >= 0, block < self.links.line)
+
+    def step(self, number):
+        z = self.links.z
+        for piece in range(self.pieces):
+            for way in (1, -1):
+                held = self.inside(z - way * number)
+                if number > 0:
+                    only(held, self.last[piece, way].wait_recv)
+                if number == self.links.line - 1:
+                    continue
+                rows = pl.ds(piece * self.rows, self.rows)
+                place = self.place(self.links.along(-way * number), rows)
+                source = self.origin(rows) if number == 0 else place
+                when = jnp.logical_and(held, self.inside(z + way))
+                self.last[piece, way] = self.links.send(source, place, way, when)
 
 
 class RingGather:
@@ -237,7 +269,7 @@
     near = NearGather(links, lambda block, place: weights.at[links.along(-block), place])
     far_ff = NearGather(links, lambda block, place: ffs_ref.at[links.along(-block), place])
     far_out = NearGather(links, lambda block, place: outs_ref.at[links.along(-block), place])
-    ring = RingGather(
+    ring = LineGather(
         links, span_len, lambda rows: x_ref.at[rows], lambda block, rows: x_all.at[block, rows]
     )
     place_ref = small_ref.at[0]
@@ -430,7 +462,7 @@
     def place(block, rows):
         return atts_ref.at[rows, pl.ds(pl.multiple_of(block * q_cols, q_cols), q_cols)]
 
-    att_ring = RingGather(links, group_len, lambda rows: att.at[rows], place)
+    att_ring = LineGather(links, group_len, lambda rows: att.at[rows], place)
     local.append(links.keep(att, place(links.z, pl.ds(0, group_len))))
     att_ring.step(0)
     for k in [0] + far:
@@ -1049,8 +1081,7 @@
                 arrived.append(links.send(part, place, k))
 
     out_pieces = ((0, width),)
-    for index, k in enumerate(order[:2]):
-        deliver(ff_half_ref.at[index], ffs_ref, k, ff_pieces)
+    deliver(ff_half_ref.at[0], ffs_ref, order[0], ff_pieces)
     def turn(items, target, low, high, pieces, order=order):
         for item, k in list(zip(items, order))[low:high]:
             deliver(item.second_done(), target, k, pieces)
@@ -1084,8 +1115,7 @@
         grad = upstream + norm_back(middle_ref[rows], norm_grad_ref[rows], gain_ref[1])
         middle_grad[rows] = grad
         branch[rows] = (grad * keep).astype(bf16)
-    for copy in loads:
-        copy.wait()
+    loads[0].wait()
     for z in range(line):
         weight = big[z].reshape(rows_z, width)
         own_grad[:, z * rows_z : (z + 1) * rows_z] = lax.dot_general(
@@ -1093,6 +1123,9 @@
         ).astype(bf16)
     turned = [links.send(own_grad.at[:, lanes_of(links.along(k))], att_grad.at[here], k) for k in far]
     stayed = links.keep(own_grad.at[:, lanes_of(links.z)], att_grad.at[here])
+    for copy in loads[1:]:
+        copy.wait()
+    deliver(ff_half_ref.at[1], ffs_ref, order[1], ff_pieces)
     core_done(ff_items, 0, line)
     for z in range(line):
         for part in range(4):
@@ -1111,7 +1144,7 @@
         copy.wait_recv()
     stayed.wait()
 
-    def attend_back(head, carry):
+    def attend_back(side, head, carry):
         lanes = pl.ds(pl.multiple_of(head * HD, HD), HD)
         for block in range(line):
             rows = slice(block * span_len, (block + 1) * span_len)
@@ -1119,38 +1152,34 @@
             part, grad = query[rows, lanes], att_grad[rows, lanes]
             row = lax.broadcasted_iota(jnp.int32, (span_len, reach), 0) + block * span_len
             column = lax.broadcasted_iota(jnp.int32, (span_len, reach), 1)
-            allowed = (column <= row, column < (block + links.x) * span_len)
+            allowed = column <= row if side == 0 else column < (block + links.x) * span_len
             spot = lax.broadcasted_iota(jnp.int32, (span_len, HD), 1) == head
             top = jnp.sum(jnp.where(spot, peak[rows], 0.0), axis=-1, keepdims=True)
             delta = jnp.sum(
                 grad.astype(f32) * own_columns[rows, lanes].astype(f32), axis=-1, keepdims=True
             )
-            back = None
-            for side in range(2):
-                keys, values = kv[side, :reach, :HD], kv[side, :reach, HD:]
-                score = lax.dot_general(
-                    part, keys, (((1,), (1,)), ((), ())), preferred_element_type=f32
-                )
-                weight = jnp.where(allowed[side], jnp.exp(score * scale - top), 0.0)
-                weight_grad = lax.dot_general(
-                    grad, values, (((1,), (1,)), ((), ())), preferred_element_type=f32
-                )
-                score_grad = (weight * (weight_grad - delta)).astype(bf16)
-                term = jnp.dot(score_grad, keys, preferred_element_type=f32)
-                back = term if back is None else back + term
-                kv_back[side, :reach, :HD] += lax.dot_general(
-                    score_grad, part, (((0,), (0,)), ((), ())), preferred_element_type=f32
-                )
-                kv_back[side, :reach, HD:] += lax.dot_general(
-                    weight.astype(bf16), grad, (((0,), (0,)), ((), ())), preferred_element_type=f32
-                )
-            query_back[rows, lanes] = back * scale
+            keys, values = kv[side, :reach, :HD], kv[side, :reach, HD:]
+            score = lax.dot_general(part, keys, (((1,), (1,)), ((), ())), preferred_element_type=f32)
+            weight = jnp.where(allowed, jnp.exp(score * scale - top), 0.0)
+            weight_grad = lax.dot_general(
+                grad, values, (((1,), (1,)), ((), ())), preferred_element_type=f32
+            )
+            score_grad = (weight * (weight_grad - delta)).astype(bf16)
+            back = jnp.dot(score_grad, keys, preferred_element_type=f32) * scale
+            kv_back[side, :reach, :HD] += lax.dot_general(
+                score_grad, part, (((0,), (0,)), ((), ())), preferred_element_type=f32
+            )
+            kv_back[side, :reach, HD:] += lax.dot_general(
+                weight.astype(bf16), grad, (((0,), (0,)), ((), ())), preferred_element_type=f32
+            )
+            query_back[rows, lanes] = back if side == 1 else query_back[rows, lanes] + back
         return carry
 
-    lax.fori_loop(0, heads, attend_back, 0)
+    lax.fori_loop(0, heads, functools.partial(attend_back, 1), 0)
     kv_out[:, :HD] = (kv_back[1, :, :HD] * scale).astype(bf16)
     kv_out[:, HD:] = kv_back[1, :, HD:].astype(bf16)
     exchange = links.send(kv_out, kv_in, "x")
+    lax.fori_loop(0, heads, functools.partial(attend_back, 0), 0)
 
     def turn_back(values, rows):
         return values * turns[0, rows] - pltpu.roll(values, HD // 2, 1) * turns[1, rows]
@@ -1161,6 +1190,7 @@
             lanes = slice(head * HD, (head + 1) * HD)
             flat[rows, lanes] = turn_back(query_back[rows, lanes], rows).astype(bf16)
     first_done(ff_items, 0, line)
+    core_done(out_items, 0, half)
     exchange.wait_recv()
     for block in range(line):
         rows = slice(block * span_len, (block + 1) * span_len)
@@ -1178,6 +1208,7 @@
                 block * span_len : (block + 1) * span_len
             ]
     ring.step(0)
+    turn(ff_items, ffs_ref, 0, line, ff_pieces, ff_order)
     for z in range(line):
         grad = lax.dot_general(
             norm[:, z * rows_z : (z + 1) * rows_z],
@@ -1188,23 +1219,21 @@
         slim[z] = grad.astype(bf16).reshape(2, 2, 2, rows_each, flat.shape[1])
     for item in qkv_items:
         item.start()
-    core_done(out_items, 0, half)
-    turn(ff_items, ffs_ref, 0, line, ff_pieces, ff_order)
-    ring.step(1)
     core_done(out_items, half, line)
     first_done(out_items, 0, half)
+    ring.step(1)
+    core_done(qkv_items, 0, line)
+    turn(out_items, outs_ref, 0, half, out_pieces)
+    first_done(out_items, half, line)
     ring.step(2)
-    core_done(qkv_items, 0, line)
-    first_done(out_items, half, line)
-    turn(out_items, outs_ref, 0, half, out_pieces)
+    first_done(qkv_items, 0, half)
+    turn(out_items, outs_ref, half, line, out_pieces)
+    first_done(qkv_items, half, line)
     ring.step(3)
     for low in range(0, span_len, 16):
         rows = slice(low, low + 16)
         grad = middle_grad[rows] + norm_back(x_own[rows].astype(f32), total[rows], gain_ref[0])
         token_ref[rows] = grad.astype(bf16)
-    first_done(qkv_items, 0, half)
-    turn(out_items, outs_ref, half, line, out_pieces)
-    first_done(qkv_items, half, line)
     turn(qkv_items, qkvs_ref, 0, line, qkv_pieces)
     for copy in arrived:
         copy.wait_recv()

time: 416 us -> 402 us (0.966)
  Pallas kernels: 399 us -> 385 us
    pallas_call x3, Pallas kernels: 399 us -> 385 us  [link_call(): pl.pallas_call(kernel, out_shape=shapes, in_specs=specs[:len(arguments)],...]
where the time goes in v15:
time: 402 us
  Pallas kernels  385 us (96%)
  other arithmetic  10.2 us (3%)
  local copies, waits for them, and re-layouts  5.45 us (1%)
    pallas_call x3, Pallas kernels, link_call(): pl.pallas_call(kernel, out_shape=shapes, in_specs=specs[:len(arguments)],...  385 us

profile of v15, /device:TPU:0, one launch (start us, length us, event | category | flops | bytes accessed | tf_op | source)
XLA Modules:
  0.0 401.6 jit_solution(12353699085874531253)
XLA Ops:
  1.3 0.1 pad.3.clone
  1.4 0.8 fusion
  2.1 0.7 convert_element_type.42
  2.8 0.1 maximum_bitcast_fusion
  2.9 0.1 maximum_maximum_fusion
  2.9 0.8 dynamic_update_slice.6
  3.8 0.8 dynamic_update_slice.7
  4.6 0.6 broadcast_in_dim.34.small_ref
  5.2 0.6 broadcast_in_dim.36.gain_rows_ref
  5.8 143.4 %shard_map.230 = (bf16[4,128,2048]{2,1,0:T(8,128)(2,1)}, bf16[4,8,80,768]{3,2,1,0:T(8,128)(2,1)}, f32[2,16,2048]{2,1,0:T(8,128)}, bf16[512,2048]{1,0:T(8,128)(2,...) custom-call(f32[4,8,128]{2,1,0:T(8,128)} %broadcast_in_dim.34.small_, ...), custom_call_target="tpu_custom_call" | custom-call | tf_op jit(solution)/shard_map/pallas_call | solution.py:589
  149.2 117.2 %shard_map.231 = (f32[128,2048]{1,0:T(8,128)}, f32[128,2048]{1,0:T(8,128)}, bf16[128,2048]{1,0:T(8,128)(2,1)}, bf16[176,2048]{1,0:T(8,128)(2,1)}, bf16[4,2,2,2,6...) custom-call(f32[4,8,128]{2,1,0:T(8,128)} %broadcast_in_dim.34.small_ref, ...), custom_call_target="tpu_custom_call" | custom-call | tf_op jit(solution)/shard_map/pallas_call | solution.py:589
  266.5 0.0 copy-start.8
  266.5 0.0 copy-start.9
  266.5 0.0 copy-start.3
  266.5 124.0 %shard_map.232 = (bf16[128,2048]{1,0:T(8,128)(2,1)}, bf16[64,11264]{1,0:T(8,128)(2,1)}, bf16[4,64,2048]{2,1,0:T(8,128)(2,1)}, bf16[64,3072]{1,0:T(8,128)(2,1)}) custom-call(f32[4,8,128]{2,1,0:T(8,128)} %broadcast_in_dim.34.small_ref, f32[2,16,2048]{2,1,0:T(8,128)} %get-tuple-element.33.gain_ref, f32[128,2048]{1,0:T(8,128)} %get-tuple-element.40.middle_ref, ...), custom_call_target="tpu_custom_call" | custom-call | tf_op jit(solution)/shard_map/pallas_call | solution.py:589
  390.5 0.0 copy-start.4
  390.5 0.0 copy-done.8
  390.5 0.0 copy-done.9
  390.5 1.8 multiply_reduce_fusion.4
  392.3 0.0 copy-done.3
  392.3 0.0 copy-start.5
  392.3 2.0 multiply_reduce_fusion.2
  394.3 0.0 copy-done.4
  394.3 0.0 copy-start.2
  394.3 1.0 convert_reduce_fusion
  395.3 0.0 copy-done.5
  395.3 0.0 copy-start
  395.3 0.0 copy-start.1
  395.3 1.3 convert_element_type.55
  396.5 0.0 copy-done.2
  396.5 0.7 copy-done
  397.2 0.2 copy-done.1
  397.4 0.0 copy-start.10
  397.4 0.0 copy-start.11
  397.4 0.0 copy-start.6
  397.4 0.0 copy-start.7
  397.4 2.1 multiply_reduce_fusion
  399.5 0.0 copy-done.10
  399.5 0.0 copy-done.11
  399.5 0.5 convert_divide_fusion
  400.1 0.0 copy-done.6
  400.1 0.8 copy.31
  400.9 0.0 copy-done.7
  400.9 0.8 copy.32
  (2 shorter events, 0.0 us)
Async XLA Ops:
  266.5 124.0 %copy-start.8 = (bf16[64,512]{1,0:T(8,128)(2,1)S(1)}, bf16[64,512]{1,0:T(8,128)(2,1)}, u32[]{:S(2)}) copy-start(bf16[64,512]{1,0:T(8,128)(2,1)} %key_w_ref.1) | copy-start | bytes 196612
  266.5 124.0 %copy-start.9 = (bf16[64,512]{1,0:T(8,128)(2,1)S(1)}, bf16[64,512]{1,0:T(8,128)(2,1)}, u32[]{:S(2)}) copy-start(bf16[64,512]{1,0:T(8,128)(2,1)} %value_w_ref.1) | copy-start | bytes 196612
  266.5 125.8 %copy-start.3 = (bf16[64,2048]{1,0:T(8,128)(2,1)S(1)}, bf16[64,2048]{1,0:T(8,128)(2,1)}, u32[]{:S(2)}) copy-start(bf16[64,2048]{1,0:T(8,128)(2,1)} %query_w_ref.1) | copy-start | bytes 786436
  390.5 3.8 copy-start.4
  392.3 3.0 copy-start.5
  394.3 2.2 copy-start.2
  395.3 1.9 copy-start
  395.3 2.1 copy-start.1
  397.4 2.1 copy-start.10
  397.4 2.1 copy-start.11
  397.4 2.7 copy-start.6
  397.4 3.4 copy-start.7

commit v16 on v15

--- a/solution.py
+++ b/solution.py
@@ -268,7 +268,14 @@
 
     near = NearGather(links, lambda block, place: weights.at[links.along(-block), place])
     far_ff = NearGather(links, lambda block, place: ffs_ref.at[links.along(-block), place])
-    far_out = NearGather(links, lambda block, place: outs_ref.at[links.along(-block), place])
+    out_half = out_ref.shape[0] // 2
+
+    def out_part(block, place):
+        k, part = block
+        rows = pl.ds(part * out_half, out_half)
+        return outs_ref.at[links.along(k if part else -k), place, rows]
+
+    far_out = NearGather(links, out_part)
     ring = LineGather(
         links, span_len, lambda rows: x_ref.at[rows], lambda block, rows: x_all.at[block, rows]
     )
@@ -320,12 +327,25 @@
     local.append(links.keep(out_ref, outs_ref.at[links.z, here]))
 
     def move_out(k):
-        moved.wait_recv()
-        block = outs_ref.at[links.along(-k), here]
-        onward = links.send(block, block, 1) if k < line - 1 else None
-        far_out.offer(k, block)
-        return onward
-
+        for part in range(2):
+            if k == 0:
+                block = out_ref.at[pl.ds(part * out_half, out_half)]
+            else:
+                moved[part].wait_recv()
+                block = out_part((k, part), here)
+            if k < line - 1:
+                moved[part] = links.send(block, out_part((0, part), here) if k == 0 else block, 1 - 2 * part)
+            far_out.offer((k, part), block)
+
+    def relay_out(k):
+        for part in range(2):
+            far_out.relay((k, part), "xy"[part])
+
+    def close_out(k):
+        for part in range(2):
+            far_out.close((k, part))
+
+    moved = [None, None]
     for k in far:
         arrived(turned[k])
         near.offer(k, weights.at[links.along(-k), here])
@@ -340,8 +360,7 @@
         near.close(k)
     far_ff.relay(0, "x")
     ring.step(2)
-    moved = links.send(out_ref, outs_ref.at[links.z, here], 1)
-    far_out.offer(0, out_ref)
+    move_out(0)
     for copy in own:
         copy.wait()
     for copy in placed:
@@ -373,6 +392,7 @@
     far_ff.relay(far[0], "x")
     ring.step(3)
     local.append(links.keep(x_all, xs_ref))
+    move_out(1)
 
     def normalise(index, carry):
         block = index // (span_len // 16)
@@ -419,8 +439,9 @@
     local.append(links.keep(query, query_ref))
     for k in far[1:]:
         far_ff.relay(k, "x" if k < line // 2 else "y")
+    relay_out(0)
+    move_out(2)
     exchange.wait_recv()
-    moved = move_out(1)
     local.append(links.keep(kv, kv_ref))
 
     scale = 1.0 / math.sqrt(HD)
@@ -467,20 +488,18 @@
     att_ring.step(0)
     for k in [0] + far:
         far_ff.close(k)
-    far_out.relay(0, "x")
-    moved = move_out(2)
-    far_out.relay(1, "x")
+    for k in range(3, line):
+        move_out(k)
+    relay_out(1)
     att_ring.step(1)
-    for k in range(3, line):
-        moved = move_out(k)
-    far_out.relay(2, "y")
+    relay_out(2)
     att_ring.step(2)
     for k in range(3, line):
-        far_out.relay(k, "y")
+        relay_out(k)
     for k in range(line):
-        far_out.close(k)
+        close_out(k)
     att_ring.step(3)
-    far_out.wait(range(line))
+    far_out.wait([(k, part) for k in range(line) for part in range(2)])
     far_ff.wait(range(line))
     links.finish()
     for copy in local:
@@ -624,7 +643,7 @@
     return link_call(
         functools.partial(first_kernel, line),
         0,
-        208,
+        256,
         tuple(jax.ShapeDtypeStruct(*out) for out in outs),
         (small, tokens, out_grad, gain_rows) + weights,
         "v" + "h" * 21,

time: 402 us -> 399 us (level)
  no operation moved by 1% of the time
where the time goes in v16:
time: 399 us; the launch traced here: 398 us
  Pallas kernels  381 us (95%)
  other arithmetic  10.2 us (3%)
  local copies, waits for them, and re-layouts  5.45 us (1%)
    pallas_call x3, Pallas kernels, link_call(): pl.pallas_call(kernel, out_shape=shapes, in_specs=specs[:len(arguments)],...  381 us

profile of v16, /device:TPU:0, one launch (start us, length us, event | category | flops | bytes accessed | tf_op | source)
XLA Modules:
  0.0 398.3 jit_solution(5708986864190099936)
XLA Ops:
  1.3 0.1 pad.3.clone
  1.4 0.8 fusion
  2.1 0.7 convert_element_type.42
  2.8 0.1 maximum_bitcast_fusion
  2.9 0.1 maximum_maximum_fusion
  2.9 0.8 dynamic_update_slice.6
  3.8 0.8 dynamic_update_slice.7
  4.6 0.6 broadcast_in_dim.34.small_ref
  5.2 0.6 broadcast_in_dim.36.gain_rows_ref
  5.8 138.8 %shard_map.230 = (bf16[4,128,2048]{2,1,0:T(8,128)(2,1)}, bf16[4,8,80,768]{3,2,1,0:T(8,128)(2,1)}, f32[2,16,2048]{2,1,0:T(8,128)}, bf16[512,2048]{1,0:T(8,128)(2,...) custom-call(f32[4,8,128]{2,1,0:T(8,128)} %broadcast_in_dim.34.small_, ...), custom_call_target="tpu_custom_call" | custom-call | tf_op jit(solution)/shard_map/pallas_call | solution.py:608
  144.6 118.4 %shard_map.231 = (f32[128,2048]{1,0:T(8,128)}, f32[128,2048]{1,0:T(8,128)}, bf16[128,2048]{1,0:T(8,128)(2,1)}, bf16[176,2048]{1,0:T(8,128)(2,1)}, bf16[4,2,2,2,6...) custom-call(f32[4,8,128]{2,1,0:T(8,128)} %broadcast_in_dim.34.small_ref, ...), custom_call_target="tpu_custom_call" | custom-call | tf_op jit(solution)/shard_map/pallas_call | solution.py:608
  263.0 0.0 copy-start.8
  263.1 0.0 copy-start.9
  263.1 0.0 copy-start.3
  263.1 124.1 %shard_map.232 = (bf16[128,2048]{1,0:T(8,128)(2,1)}, bf16[64,11264]{1,0:T(8,128)(2,1)}, bf16[4,64,2048]{2,1,0:T(8,128)(2,1)}, bf16[64,3072]{1,0:T(8,128)(2,1)}) custom-call(f32[4,8,128]{2,1,0:T(8,128)} %broadcast_in_dim.34.small_ref, f32[2,16,2048]{2,1,0:T(8,128)} %get-tuple-element.33.gain_ref, f32[128,2048]{1,0:T(8,128)} %get-tuple-element.40.middle_ref, ...), custom_call_target="tpu_custom_call" | custom-call | tf_op jit(solution)/shard_map/pallas_call | solution.py:608
  387.2 0.0 copy-start.4
  387.2 0.0 copy-done.8
  387.2 0.0 copy-done.9
  387.2 1.8 multiply_reduce_fusion.4
  389.0 0.0 copy-done.3
  389.0 0.0 copy-start.5
  389.0 2.0 multiply_reduce_fusion.2
  391.0 0.0 copy-done.4
  391.0 0.0 copy-start.2
  391.0 1.0 convert_reduce_fusion
  392.0 0.0 copy-done.5
  392.0 0.0 copy-start
  392.0 0.0 copy-start.1
  392.0 1.3 convert_element_type.55
  393.2 0.0 copy-done.2
  393.2 0.7 copy-done
  393.9 0.2 copy-done.1
  394.1 0.0 copy-start.10
  394.1 0.0 copy-start.11
  394.1 0.0 copy-start.6
  394.1 0.0 copy-start.7
  394.1 2.1 multiply_reduce_fusion
  396.2 0.0 copy-done.10
  396.2 0.0 copy-done.11
  396.2 0.5 convert_divide_fusion
  396.7 0.0 copy-done.6
  396.7 0.8 copy.31
  397.5 0.0 copy-done.7
  397.5 0.8 copy.32
  (2 shorter events, 0.0 us)
Async XLA Ops:
  263.0 124.1 %copy-start.8 = (bf16[64,512]{1,0:T(8,128)(2,1)S(1)}, bf16[64,512]{1,0:T(8,128)(2,1)}, u32[]{:S(2)}) copy-start(bf16[64,512]{1,0:T(8,128)(2,1)} %key_w_ref.1) | copy-start | bytes 196612
  263.1 124.1 %copy-start.9 = (bf16[64,512]{1,0:T(8,128)(2,1)S(1)}, bf16[64,512]{1,0:T(8,128)(2,1)}, u32[]{:S(2)}) copy-start(bf16[64,512]{1,0:T(8,128)(2,1)} %value_w_ref.1) | copy-start | bytes 196612
  263.1 125.9 %copy-start.3 = (bf16[64,2048]{1,0:T(8,128)(2,1)S(1)}, bf16[64,2048]{1,0:T(8,128)(2,1)}, u32[]{:S(2)}) copy-start(bf16[64,2048]{1,0:T(8,128)(2,1)} %query_w_ref.1) | copy-start | bytes 786436
  387.2 3.8 copy-start.4
  389.0 3.0 copy-start.5
  391.0 2.2 copy-start.2
  392.0 1.9 copy-start
  392.0 2.1 copy-start.1
  394.1 2.1 copy-start.10
  394.1 2.1 copy-start.11
  394.1 2.7 copy-start.6
  394.1 3.4 copy-start.7

commit v17 on v16

--- a/solution.py
+++ b/solution.py
@@ -386,7 +386,8 @@
         for which in range(2):
             lanes = slice(which * HD, (which + 1) * HD)
             both = [weights[z, 2 * q + c, rows_each : rows_each + 16, lanes].astype(f32) for c in range(2)]
-            gains[which, :, index * HD : (index + 1) * HD] = both[0] + both[1]
+            first = lax.broadcasted_iota(jnp.int32, both[0].shape, 1) < rows_each
+            gains[which, :, index * HD : (index + 1) * HD] = jnp.where(first, both[0], both[1])
     local.append(links.keep(weights, weight_ref))
     local.append(links.keep(gains, gain_ref))
     far_ff.relay(far[0], "x")
@@ -701,7 +702,6 @@
     f32, bf16 = jnp.float32, jnp.bfloat16
     space, (send_sems, recv_sems) = scratch[:-2], scratch[-2:]
     links = Links(send_sems, recv_sems, line)
-    links.meet(["x", "y", "c", 1, line - 1])
     far = [1, line - 1] + list(range(2, line - 1))
     span_len, width = mix_ref.shape
     group_len = line * span_len
@@ -709,16 +709,17 @@
     block_rows = width // line
     rows_each = block_rows // 8
     chunk = 2 * HD
-    mix_ring = RingGather(
-        links, span_len, lambda rows: mix_ref.at[rows], lambda block, rows: mixed.at[block, rows]
-    )
-    mix_ring.step(0)
-    stay = links.keep(mix_ref, mixed.at[links.z])
     early = [
         links.keep(out_ref, big),
         links.keep(atts_ref, norm),
         links.keep(xs_ref, parts),
     ]
+    links.meet(["x", "y", "c", 1, line - 1])
+    mix_ring = RingGather(
+        links, span_len, lambda rows: mix_ref.at[rows], lambda block, rows: mixed.at[block, rows]
+    )
+    mix_ring.step(0)
+    stay = links.keep(mix_ref, mixed.at[links.z])
     late = [links.keep(ff_ref, ff)]
     down_rows = down_ref.shape[0]
 
@@ -981,8 +982,8 @@
     line,
     small_ref,
     gain_ref,
-    middle_ref,
-    norm_grad_ref,
+    middle_hbm,
+    norm_grad_hbm,
     x_ref,
     grad_ref,
     query_ref,
@@ -999,6 +1000,8 @@
     ffs_ref,
     outs_ref,
     qkvs_ref,
+    middle_ref,
+    norm_grad_ref,
     x_own,
     grad_own,
     middle_grad,
@@ -1029,7 +1032,6 @@
     links = Links(send_sems, recv_sems, line)
     far = [1, line - 1] + list(range(2, line - 1))
     order = far + [0]
-    links.meet(["x", "y", "c"] + far)
     span_len, width = x_ref.shape
     group_len = line * span_len
     q_cols = query.shape[1]
@@ -1042,7 +1044,11 @@
         return pl.ds(pl.multiple_of(block * q_cols, q_cols), q_cols)
 
     here = pl.ds(pl.multiple_of(links.z * span_len, span_len), span_len)
-    first_load = links.keep(grad_ref, grad_own)
+    first_loads = [
+        links.keep(grad_ref, grad_own),
+        links.keep(middle_hbm, middle_ref),
+        links.keep(norm_grad_hbm, norm_grad_ref),
+    ]
     loads = [
         links.keep(out_ref, big),
         links.keep(atts_ref.at[here], own_rows),
@@ -1055,6 +1061,7 @@
         links.keep(norm_ref, norm),
         links.keep(weight_ref.at[:, :, :, :, pl.ds(0, slim.shape[4])], slim),
     ]
+    links.meet(["x", "y", "c"] + far)
     ring = RingSum(links, parts, total, got)
 
     def items_of(source, space, in_place, order=order):
@@ -1117,7 +1124,8 @@
     for item in ff_items:
         item.start()
 
-    first_load.wait()
+    for copy in first_loads:
+        copy.wait()
     keep = small_ref[3, 0:1, 0:1]
     token_scale = column_of(small_ref[1, 0:1])
 
@@ -1284,8 +1292,9 @@
             jax.ShapeDtypeStruct((rows_each, line * qkv_cols), bf16),
         ),
         near + tokens + saved + (out_w.reshape(wide), attended, weights, norm, grad_ff, ff_half),
-        "v" * 4 + "h" * 12 + "vhhh",
-        [pltpu.VMEM((span_len, width), bf16)] * 2
+        "v" * 2 + "h" * 14 + "vhhh",
+        [pltpu.VMEM((span_len, width), f32)] * 2
+        + [pltpu.VMEM((span_len, width), bf16)] * 2
         + [pltpu.VMEM((span_len, width), f32)] * 2
         + [
             pltpu.VMEM(wide, bf16),
@@ -1667,10 +1676,8 @@
     )
     small = jnp.broadcast_to(small[:, None], (4, 8, span_len))
 
-    core = lax.axis_index("c")
-    gain_row = jnp.zeros((q_cols + 2 * HD,), bf16)
-    gain_row = lax.dynamic_update_slice_in_dim(gain_row, attn_gain, core * rows_each, 0)
-    gain_row = lax.dynamic_update_slice_in_dim(gain_row, mlp_gain, HD + core * rows_each, 0)
+    gain_row = jnp.concatenate([attn_gain, attn_gain, mlp_gain, mlp_gain])
+    gain_row = jnp.pad(gain_row, (0, q_cols + 2 * HD - gain_row.shape[0]))
     gain_rows = jnp.broadcast_to(gain_row, (16, gain_row.shape[0]))
     (
         x_blocks,

time: 399 us -> 397 us (level)
  no operation moved by 1% of the time
where the time goes in v17:
time: 397 us
  Pallas kernels  381 us (96%)
  other arithmetic  11 us (3%)
    pallas_call x3, Pallas kernels, link_call(): pl.pallas_call(kernel, out_shape=shapes, in_specs=specs[:len(arguments)],...  381 us

profile of v17, /device:TPU:0, one launch (start us, length us, event | category | flops | bytes accessed | tf_op | source)
XLA Modules:
  0.0 396.8 jit_solution(15685350757849051019)
XLA Ops:
  1.3 0.1 pad.12.clone
  1.4 0.8 fusion.7
  2.1 0.7 convert_element_type.44
  2.8 0.1 maximum_bitcast_fusion
  2.9 0.1 maximum_maximum_fusion
  2.9 0.8 fusion.6
  3.8 0.6 broadcast_in_dim.31.small_ref
  4.4 0.6 broadcast_in_dim.32.gain_rows_ref
  5.0 138.8 %shard_map.230 = (bf16[4,128,2048]{2,1,0:T(8,128)(2,1)}, bf16[4,8,80,768]{3,2,1,0:T(8,128)(2,1)}, f32[2,16,2048]{2,1,0:T(8,128)}, bf16[512,2048]{1,0:T(8,128)(2,...) custom-call(f32[4,8,128]{2,1,0:T(8,128)} %broadcast_in_dim.31.small_, ...), custom_call_target="tpu_custom_call" | custom-call | tf_op jit(solution)/shard_map/pallas_call | solution.py:609
  143.8 118.4 %shard_map.231 = (f32[128,2048]{1,0:T(8,128)}, f32[128,2048]{1,0:T(8,128)}, bf16[128,2048]{1,0:T(8,128)(2,1)}, bf16[176,2048]{1,0:T(8,128)(2,1)}, bf16[4,2,2,2,6...) custom-call(f32[4,8,128]{2,1,0:T(8,128)} %broadcast_in_dim.31.small_ref, ...), custom_call_target="tpu_custom_call" | custom-call | tf_op jit(solution)/shard_map/pallas_call | solution.py:609
  262.2 0.0 copy-start.8
  262.2 0.0 copy-start.9
  262.2 0.0 copy-start.3
  262.2 123.4 %shard_map.232 = (bf16[128,2048]{1,0:T(8,128)(2,1)}, bf16[64,11264]{1,0:T(8,128)(2,1)}, bf16[4,64,2048]{2,1,0:T(8,128)(2,1)}, bf16[64,3072]{1,0:T(8,128)(2,1)}) custom-call(f32[4,8,128]{2,1,0:T(8,128)} %broadcast_in_dim.31.small_ref, f32[2,16,2048]{2,1,0:T(8,128)} %get-tuple-element.33.gain_ref, f32[128,2048]{1,0:T(8,128)} %get-tuple-element.40.middle_hbm, ...), custom_call_target="tpu_custom_call" | custom-call | tf_op jit(solution)/shard_map/pallas_call | solution.py:609
  385.6 0.0 copy-start.4
  385.6 0.0 copy-done.8
  385.6 0.0 copy-done.9
  385.6 1.8 multiply_reduce_fusion.4
  387.4 0.0 copy-done.3
  387.4 0.0 copy-start.5
  387.5 2.0 multiply_reduce_fusion.2
  389.4 0.0 copy-done.4
  389.4 0.0 copy-start.2
  389.5 1.0 convert_reduce_fusion
  390.4 0.0 copy-done.5
  390.4 0.0 copy-start
  390.4 0.0 copy-start.1
  390.4 1.3 convert_element_type.57
  391.7 0.0 copy-done.2
  391.7 0.7 copy-done
  392.3 0.2 copy-done.1
  392.5 0.0 copy-start.10
  392.5 0.0 copy-start.11
  392.5 0.0 copy-start.6
  392.5 0.0 copy-start.7
  392.5 2.1 multiply_reduce_fusion
  394.6 0.0 copy-done.10
  394.6 0.0 copy-done.11
  394.7 0.5 convert_divide_fusion
  395.2 0.0 copy-done.6
  395.2 0.8 copy.29
  396.0 0.0 copy-done.7
  396.0 0.8 copy.30
  (1 shorter events, 0.0 us)
Async XLA Ops:
  262.2 123.4 %copy-start.8 = (bf16[64,512]{1,0:T(8,128)(2,1)S(1)}, bf16[64,512]{1,0:T(8,128)(2,1)}, u32[]{:S(2)}) copy-start(bf16[64,512]{1,0:T(8,128)(2,1)} %key_w_ref.1) | copy-start | bytes 196612
  262.2 123.4 %copy-start.9 = (bf16[64,512]{1,0:T(8,128)(2,1)S(1)}, bf16[64,512]{1,0:T(8,128)(2,1)}, u32[]{:S(2)}) copy-start(bf16[64,512]{1,0:T(8,128)(2,1)} %value_w_ref.1) | copy-start | bytes 196612
  262.2 125.2 %copy-start.3 = (bf16[64,2048]{1,0:T(8,128)(2,1)S(1)}, bf16[64,2048]{1,0:T(8,128)(2,1)}, u32[]{:S(2)}) copy-start(bf16[64,2048]{1,0:T(8,128)(2,1)} %query_w_ref.1) | copy-start | bytes 786436
  385.6 3.8 copy-start.4
  387.4 3.0 copy-start.5
  389.4 2.2 copy-start.2
  390.4 1.9 copy-start
  390.4 2.1 copy-start.1
  392.5 2.1 copy-start.10
  392.5 2.1 copy-start.11
  392.5 2.7 copy-start.6
  392.5 3.4 copy-start.7

commit v18 on v17

--- a/solution.py
+++ b/solution.py
@@ -256,7 +256,6 @@
     f32, bf16 = jnp.float32, jnp.bfloat16
     links = Links(send_sems, recv_sems, line)
     far = [1, line - 1] + list(range(2, line - 1))
-    links.meet(["x", "y", "c"] + far)
     here = links.slot
     span_len, width = x_ref.shape
     group_len = line * span_len
@@ -310,6 +309,12 @@
 
     own = [links.keep(*piece) for piece in near_pieces(links.z)]
     own_ff = [links.keep(*piece) for piece in ff_pieces(links.z)]
+    own_tokens = [
+        links.keep(x_ref, x_all.at[links.z]),
+        links.keep(place_ref, places.at[links.z]),
+        links.keep(grad_ref, grad),
+    ]
+    links.meet(["x", "y", "c"] + far)
     turned = turn_out(near_pieces)
     placed = [links.send(place_ref, places.at[links.z], k) for k in far]
     turned_ff = turn_out(ff_pieces)
@@ -319,11 +324,7 @@
     for copy in own_ff:
         copy.wait()
     far_ff.offer(0, ffs_ref.at[links.z, here])
-    own = [
-        links.keep(x_ref, x_all.at[links.z]),
-        links.keep(place_ref, places.at[links.z]),
-        links.keep(grad_ref, grad),
-    ]
+    own = own_tokens
     local.append(links.keep(out_ref, outs_ref.at[links.z, here]))
 
     def move_out(k):

time: 397 us -> 397 us (level)
  no operation moved by 1% of the time
where the time goes in v18:
time: 397 us
  Pallas kernels  381 us (96%)
  other arithmetic  11 us (3%)
    pallas_call x3, Pallas kernels, link_call(): pl.pallas_call(kernel, out_shape=shapes, in_specs=specs[:len(arguments)],...  381 us

profile of v18, /device:TPU:0, one launch (start us, length us, event | category | flops | bytes accessed | tf_op | source)
XLA Modules:
  0.0 396.8 jit_solution(7240091365112430832)
XLA Ops:
  1.3 0.1 pad.12.clone
  1.4 0.8 fusion.7
  2.1 0.7 convert_element_type.44
  2.8 0.1 maximum_bitcast_fusion
  2.9 0.1 maximum_maximum_fusion
  2.9 0.8 fusion.6
  3.8 0.6 broadcast_in_dim.31.small_ref
  4.4 0.6 broadcast_in_dim.32.gain_rows_ref
  5.0 138.8 %shard_map.230 = (bf16[4,128,2048]{2,1,0:T(8,128)(2,1)}, bf16[4,8,80,768]{3,2,1,0:T(8,128)(2,1)}, f32[2,16,2048]{2,1,0:T(8,128)}, bf16[512,2048]{1,0:T(8,128)(2,...) custom-call(f32[4,8,128]{2,1,0:T(8,128)} %broadcast_in_dim.31.small_, ...), custom_call_target="tpu_custom_call" | custom-call | tf_op jit(solution)/shard_map/pallas_call | solution.py:610
  143.8 118.4 %shard_map.231 = (f32[128,2048]{1,0:T(8,128)}, f32[128,2048]{1,0:T(8,128)}, bf16[128,2048]{1,0:T(8,128)(2,1)}, bf16[176,2048]{1,0:T(8,128)(2,1)}, bf16[4,2,2,2,6...) custom-call(f32[4,8,128]{2,1,0:T(8,128)} %broadcast_in_dim.31.small_ref, ...), custom_call_target="tpu_custom_call" | custom-call | tf_op jit(solution)/shard_map/pallas_call | solution.py:610
  262.2 0.0 copy-start.8
  262.2 0.0 copy-start.9
  262.2 0.0 copy-start.3
  262.3 123.4 %shard_map.232 = (bf16[128,2048]{1,0:T(8,128)(2,1)}, bf16[64,11264]{1,0:T(8,128)(2,1)}, bf16[4,64,2048]{2,1,0:T(8,128)(2,1)}, bf16[64,3072]{1,0:T(8,128)(2,1)}) custom-call(f32[4,8,128]{2,1,0:T(8,128)} %broadcast_in_dim.31.small_ref, f32[2,16,2048]{2,1,0:T(8,128)} %get-tuple-element.33.gain_ref, f32[128,2048]{1,0:T(8,128)} %get-tuple-element.40.middle_hbm, ...), custom_call_target="tpu_custom_call" | custom-call | tf_op jit(solution)/shard_map/pallas_call | solution.py:610
  385.7 0.0 copy-start.4
  385.7 0.0 copy-done.8
  385.7 0.0 copy-done.9
  385.7 1.8 multiply_reduce_fusion.4
  387.5 0.0 copy-done.3
  387.5 0.0 copy-start.5
  387.5 2.0 multiply_reduce_fusion.2
  389.5 0.0 copy-done.4
  389.5 0.0 copy-start.2
  389.5 1.0 convert_reduce_fusion
  390.5 0.0 copy-done.5
  390.5 0.0 copy-start
  390.5 0.0 copy-start.1
  390.5 1.3 convert_element_type.57
  391.7 0.0 copy-done.2
  391.7 0.7 copy-done
  392.4 0.2 copy-done.1
  392.6 0.0 copy-start.10
  392.6 0.0 copy-start.11
  392.6 0.0 copy-start.6
  392.6 0.0 copy-start.7
  392.6 2.1 multiply_reduce_fusion
  394.7 0.0 copy-done.10
  394.7 0.0 copy-done.11
  394.7 0.5 convert_divide_fusion
  395.3 0.0 copy-done.6
  395.3 0.8 copy.29
  396.1 0.0 copy-done.7
  396.1 0.8 copy.30
  (1 shorter events, 0.0 us)
Async XLA Ops:
  262.2 123.5 %copy-start.8 = (bf16[64,512]{1,0:T(8,128)(2,1)S(1)}, bf16[64,512]{1,0:T(8,128)(2,1)}, u32[]{:S(2)}) copy-start(bf16[64,512]{1,0:T(8,128)(2,1)} %key_w_ref.1) | copy-start | bytes 196612
  262.2 123.5 %copy-start.9 = (bf16[64,512]{1,0:T(8,128)(2,1)S(1)}, bf16[64,512]{1,0:T(8,128)(2,1)}, u32[]{:S(2)}) copy-start(bf16[64,512]{1,0:T(8,128)(2,1)} %value_w_ref.1) | copy-start | bytes 196612
  262.2 125.3 %copy-start.3 = (bf16[64,2048]{1,0:T(8,128)(2,1)S(1)}, bf16[64,2048]{1,0:T(8,128)(2,1)}, u32[]{:S(2)}) copy-start(bf16[64,2048]{1,0:T(8,128)(2,1)} %query_w_ref.1) | copy-start | bytes 786436
  385.7 3.8 copy-start.4
  387.5 3.0 copy-start.5
  389.5 2.2 copy-start.2
  390.5 1.9 copy-start
  390.5 2.1 copy-start.1
  392.6 2.1 copy-start.10
  392.6 2.1 copy-start.11
  392.6 2.7 copy-start.6
  392.6 3.4 copy-start.7
